TPU v7x, 32 devices: a whole 2x2x4 slice. The times are simulated.
32 devices in a mesh: groups: 2 (over y), dp: 4 (over x, core), tensor: 4 (over z).
Axes of the slice: x: 2, y: 2, z: 4, core: 2. Of those that a mesh axis runs over, the one named last changes fastest.
Arguments:
- inputs: bfloat16 [16384, 8192], P(('groups', 'dp', 'tensor')), parts along dimension 0, may hold values from -6 to 6
- in_proj: bfloat16 [64, 8192], replicated, as said below
- out_grads: bfloat16 [16384, 28672], P(('groups', 'dp'), 'tensor'), parts along dimension 0, may hold values from -6 to 6
- out_proj: bfloat16 [64, 28672], P(None, 'tensor'), may hold values from -0.03125 to 0.03125
- prior: float32 [8192, 4096], P(('groups', 'dp', 'tensor')), parts along dimension 0, as said below
- queries: bfloat16 [1024, 4096], P(('groups', 'dp', 'tensor')), parts along dimension 0, may hold values from -6 to 6
Outputs:
- scores: float32 [16, 512], P('groups', ('dp', 'tensor')), parts along dimension 0
There are 2 independent parts, one for each index of `groups`. A program takes and returns all parts, laid end to end along the dimension named above; an argument that names none is the same for every part. Nothing has to cross between parts.
Inputs may be any that keep to these rules, and one draw needn't show every extreme that they name: `in_proj`: a projection from 8192 input features to 64, entries up to about ten over the square root of 8192. `prior`: symmetric and positive definite, smallest eigenvalue above 0.1, entries of order one at most on the diagonal.
All inputs are finite; a program needn't handle non-finite values.
Results may differ from a plain program's by a relative error of at most 0.0003.
Values sent between devices are 32-bit elements; how exact they have to be, the bound alone decides.
No kernel may reach another device: no remote copies, remote signals or barrier semaphores. Data moves between devices by JAX's collectives and lax.ppermute only.
A program may use at most 128 MiB of HBM per device.

v0:
```python
import jax
import jax.numpy as jnp
from jax import lax
from jax.sharding import PartitionSpec as P

R_IN = 64
R_OUT = 64
SEQ = 1024
ITERS = 4


def on_device(inputs, in_proj, out_grads, out_proj, prior, queries):
    highest = lax.Precision.HIGHEST
    width = R_IN * R_OUT
    in_local = lax.dot_general(
        in_proj, inputs, (((1,), (1,)), ((), ())), preferred_element_type=jnp.float32
    )
    in_feats = lax.all_gather(in_local, "tensor", axis=1, tiled=True)
    out_local = lax.dot_general(
        out_proj, out_grads, (((1,), (1,)), ((), ())), preferred_element_type=jnp.float32
    )
    seq_count = in_feats.shape[1] // SEQ
    in_tokens = in_feats.reshape(R_IN, seq_count, SEQ)
    out_feats = lax.psum(out_local, "tensor")
    out_tokens = out_feats.reshape(R_OUT, seq_count, SEQ)
    own_vectors = jnp.einsum("ast,bst->sab", in_tokens, out_tokens, precision=highest)
    own_vectors = own_vectors.reshape(seq_count, width) / SEQ
    vectors = lax.all_gather(own_vectors, "dp", axis=0, tiled=True)
    train_count = vectors.shape[0]
    row_count = prior.shape[0]
    row_start = (
        lax.axis_index("dp") * lax.axis_size("tensor") + lax.axis_index("tensor")
    ) * row_count

    def gather_rows(values):
        return lax.all_gather(values, ("dp", "tensor"), axis=1, tiled=True)

    def global_sum(values):
        return lax.psum(values, ("dp", "tensor"))

    own_columns = lax.dynamic_slice_in_dim(vectors, row_start, row_count, 1)
    fisher_rows = (
        prior
        + lax.dot_general(
            own_columns,
            vectors,
            (((0,), (0,)), ((), ())),
            precision=highest,
            preferred_element_type=jnp.float32,
        )
        / train_count
    )
    solution = jnp.zeros_like(own_columns)
    residual = own_columns
    direction = own_columns
    norm_now = global_sum(jnp.sum(residual * residual, axis=1))
    for iteration in range(ITERS):
        gathered = gather_rows(direction)
        applied = lax.dot_general(
            gathered,
            fisher_rows,
            (((1,), (1,)), ((), ())),
            precision=highest,
            preferred_element_type=jnp.float32,
        )
        step_size = norm_now / global_sum(jnp.sum(direction * applied, axis=1))
        solution = solution + step_size[:, None] * direction
        residual = residual - step_size[:, None] * applied
        norm_next = global_sum(jnp.sum(residual * residual, axis=1))
        direction = residual + (norm_next / norm_now)[:, None] * direction
        norm_now = norm_next
    whole_solution = gather_rows(solution)
    return lax.dot_general(
        whole_solution,
        queries.astype(jnp.float32),
        (((1,), (1,)), ((), ())),
        precision=highest,
        preferred_element_type=jnp.float32,
    )


def solution(mesh):
    return jax.shard_map(
        on_device,
        mesh=mesh,
        in_specs=(
            P(("groups", "dp", "tensor"), None),
            P(),
            P(("groups", "dp"), "tensor"),
            P(None, "tensor"),
            P(("groups", "dp", "tensor"), None),
            P(("groups", "dp", "tensor"), None),
        ),
        out_specs=P("groups", ("dp", "tensor")),
        check_vma=False,
    )
```

profile of v0, /device:TPU:0, one launch (start us, length us, event | category | flops | bytes accessed | tf_op | source)
XLA Modules:
  0.0 482.6 jit_solution(15077708447934698771)
XLA Ops:
  6.5 14.6 %fusion.5 = f32[64,2048]{1,0:T(8,128)S(1)} fusion(bf16[64,7168]{1,0:T(8,128)(2,1)} %param.9, bf16[2048,7168]{1,0:T(8,128)(2,1)} %param.8), kind=kOutput, calls=%fused_computation.24 | convolution fusion | flops 1879048192 | bytes 30801920 | tf_op jit(solution)/shard_map/dot_general | solution.py:19
  22.0 6.0 %fusion.4 = f32[64,512]{1,0:T(8,128)S(1)} fusion(bf16[64,8192]{1,0:T(8,128)(2,1)S(1)} %copy-done, bf16[512,8192]{1,0:T(8,128)(2,1)} %param.6), kind=kOutput, calls=%fused_computation.23 | convolution fusion | flops 536870912 | bytes 9568256 | tf_op jit(solution)/shard_map/dot_general | solution.py:15
  28.1 23.4 %all_gather.21 = f32[64,2048]{1,0:T(8,128)S(1)} all-gather(f32[64,512]{1,0:T(8,128)S(1)} %fusion.4), channel_id=1, replica_groups=mesh['groups'=2,'dp'=4,'tensor'=4] {'tensor'}, dimensions={1}, use_global_device_ids=true | all-gather | bytes 655360 | tf_op jit(solution)/shard_map/all_gather | solution.py:18
  51.4 17.6 %all-reduce.3.cloned.1.call-done = f32[64,2,1024]{2,0,1:T(8,128)} async-done(((f32[64,2,1024]{2,0,1:T(8,128)}), f32[64,2,1024]{2,0,1:T(8,128)}) %all-reduce.3.cloned.1.call-update) | async-done | bytes 524304 | tf_op jit(solution)/shard_map/psum | solution.py:24
  69.0 1.6 convolution_multiply_fusion.1
  70.8 5.4 %all-gather = f32[4,2,4096]{2,1,0:T(2,128)S(1)} all-gather(f32[1,2,4096]{2,1,0:T(2,128)S(1)} %reshape.18), channel_id=1, replica_groups=mesh['groups'=2,'dp'=4,'tensor'=4] {'dp'}, dimensions={0}, use_global_device_ids=true | all-gather | bytes 163840 | tf_op jit(solution)/shard_map/all_gather | solution.py:28
  76.3 32.7 %all_gather.23 = f32[8,4096]{1,0:T(8,128)S(1)} all-gather(f32[8,256]{1,0:T(8,128)S(1)} %constant_dynamic-slice_fusion), channel_id=1, replica_groups=mesh['groups'=2,'dp'=4,'tensor'=4] {'dp','tensor'}, dimensions={1}, use_global_device_ids=true | all-gather | bytes 139264 | tf_op jit(solution)/shard_map/all_gather | solution.py:36
  109.0 5.5 %fusion = f32[256,4096]{1,0:T(8,128)S(1)} fusion(f32[256,4096]{1,0:T(8,128)} %param.10, f32[8,256]{1,0:T(8,128)S(1)} %constant_dynamic-slice_fusion, f32[8,4096]{1,0:T(8,128)S(1)} %reshape.19), kind=kOutput, calls=%fused_computation.1 | convolution fusion | flops 102760448 | bytes 8527872 | tf_op jit(solution)/shard_map/dot_general | solution.py:44
  114.6 1.9 copy-done.1
  116.5 3.5 multiply_reduce_fusion.5
  120.0 29.7 %all-reduce = (f32[8]{0:T(128)S(1)}, f32[8]{0:T(128)S(1)}) all-reduce(f32[8]{0:T(128)S(1)} %get-tuple-element.6, f32[8]{0:T(128)S(1)} %get-tuple-element.5), channel_id=1, replica_groups=mesh['groups'=2,'dp'=4,'tensor'=4] {'dp','tensor'}, use_global_device_ids=true, to_apply=%region_2.0 | all-reduce | flops 16 | bytes 128 | tf_op jit(solution)/shard_map/psum | solution.py:39
  149.9 31.9 %psum.66 = f32[8]{0:T(128)S(1)} all-reduce(f32[8]{0:T(128)S(1)} %multiply_reduce_fusion.4), channel_id=1, replica_groups=mesh['groups'=2,'dp'=4,'tensor'=4] {'dp','tensor'}, use_global_device_ids=true, to_apply=%region_6.0 | all-reduce | flops 8 | bytes 64 | tf_op jit(solution)/shard_map/psum | solution.py:39
  181.8 29.7 %all_gather.24 = f32[8,4096]{1,0:T(8,128)S(1)} all-gather(f32[8,256]{1,0:T(8,128)S(1)} %multiply_add_fusion.3), channel_id=1, replica_groups=mesh['groups'=2,'dp'=4,'tensor'=4] {'dp','tensor'}, dimensions={1}, use_global_device_ids=true | all-gather | bytes 139264 | tf_op jit(solution)/shard_map/all_gather | solution.py:36
  211.5 5.6 %multiply_reduce_fusion.3 = (f32[8]{0:T(128)S(1)}, f32[8,256]{1,0:T(8,128)S(1)}) fusion(f32[8,256]{1,0:T(8,128)S(1)} %multiply_add_fusion.3, f32[8,4096]{1,0:T(8,128)S(1)} %all_gather.24, f32[256,4096]{1,0:T(8,128)} %copy-done.1), kind=kOutput, calls=%fused_computation.16 | convolution fusion | flops 100667384 | bytes 4341792 | tf_op jit(solution)/shard_map/dot_general | solution.py:59
  217.2 31.8 %psum.67 = f32[8]{0:T(128)S(1)} all-reduce(f32[8]{0:T(128)S(1)} %get-tuple-element.12), channel_id=1, replica_groups=mesh['groups'=2,'dp'=4,'tensor'=4] {'dp','tensor'}, use_global_device_ids=true, to_apply=%region_8.0 | all-reduce | flops 8 | bytes 64 | tf_op jit(solution)/shard_map/psum | solution.py:39
  249.2 29.8 %psum.68 = f32[8]{0:T(128)S(1)} all-reduce(f32[8]{0:T(128)S(1)} %get-tuple-element.9), channel_id=1, replica_groups=mesh['groups'=2,'dp'=4,'tensor'=4] {'dp','tensor'}, use_global_device_ids=true, to_apply=%region_10.0 | all-reduce | flops 8 | bytes 64 | tf_op jit(solution)/shard_map/psum | solution.py:39
  279.0 31.6 %all_gather.25 = f32[8,4096]{1,0:T(8,128)S(1)} all-gather(f32[8,256]{1,0:T(8,128)S(1)} %multiply_add_fusion.2), channel_id=1, replica_groups=mesh['groups'=2,'dp'=4,'tensor'=4] {'dp','tensor'}, dimensions={1}, use_global_device_ids=true | all-gather | bytes 139264 | tf_op jit(solution)/shard_map/all_gather | solution.py:36
  310.7 5.7 %multiply_reduce_fusion.1 = (f32[8]{0:T(128)S(1)}, f32[8,256]{1,0:T(8,128)S(1)}) fusion(f32[8,256]{1,0:T(8,128)S(1)} %multiply_add_fusion.2, f32[8,4096]{1,0:T(8,128)S(1)} %all_gather.25, f32[256,4096]{1,0:T(8,128)} %copy-done.1), kind=kOutput, calls=%fused_computation.12 | convolution fusion | flops 100667384 | bytes 4341792 | tf_op jit(solution)/shard_map/dot_general | solution.py:59
  316.3 29.8 %psum.69 = f32[8]{0:T(128)S(1)} all-reduce(f32[8]{0:T(128)S(1)} %get-tuple-element.14), channel_id=1, replica_groups=mesh['groups'=2,'dp'=4,'tensor'=4] {'dp','tensor'}, use_global_device_ids=true, to_apply=%region_12.0 | all-reduce | flops 8 | bytes 64 | tf_op jit(solution)/shard_map/psum | solution.py:39
  346.3 31.8 %psum.70 = f32[8]{0:T(128)S(1)} all-reduce(f32[8]{0:T(128)S(1)} %multiply_reduce_fusion), channel_id=1, replica_groups=mesh['groups'=2,'dp'=4,'tensor'=4] {'dp','tensor'}, use_global_device_ids=true, to_apply=%region_14.0 | all-reduce | flops 8 | bytes 64 | tf_op jit(solution)/shard_map/psum | solution.py:39
  378.2 29.5 %all_gather.26 = f32[8,4096]{1,0:T(8,128)S(1)} all-gather(f32[8,256]{1,0:T(8,128)S(1)} %multiply_add_fusion.1), channel_id=1, replica_groups=mesh['groups'=2,'dp'=4,'tensor'=4] {'dp','tensor'}, dimensions={1}, use_global_device_ids=true | all-gather | bytes 139264 | tf_op jit(solution)/shard_map/all_gather | solution.py:36
  407.7 5.6 %fusion.1 = f32[8]{0:T(128)S(1)} fusion(f32[8,256]{1,0:T(8,128)S(1)} %multiply_add_fusion.1, f32[8,4096]{1,0:T(8,128)S(1)} %all_gather.26, f32[256,4096]{1,0:T(8,128)} %copy-done.1), kind=kOutput, calls=%fused_computation.4 | convolution fusion | flops 100667384 | bytes 4333600 | tf_op jit(solution)/shard_map/dot_general | solution.py:59
  413.4 31.8 %psum.71 = f32[8]{0:T(128)S(1)} all-reduce(f32[8]{0:T(128)S(1)} %fusion.1), channel_id=1, replica_groups=mesh['groups'=2,'dp'=4,'tensor'=4] {'dp','tensor'}, use_global_device_ids=true, to_apply=%region_16.0 | all-reduce | flops 8 | bytes 64 | tf_op jit(solution)/shard_map/psum | solution.py:39
  445.2 29.6 %all_gather.27 = f32[8,4096]{1,0:T(8,128)S(1)} all-gather(f32[8,256]{1,0:T(8,128)S(1)} %multiply_add_fusion), channel_id=1, replica_groups=mesh['groups'=2,'dp'=4,'tensor'=4] {'dp','tensor'}, dimensions={1}, use_global_device_ids=true | all-gather | bytes 139264 | tf_op jit(solution)/shard_map/all_gather | solution.py:36
  (26 shorter events, 2.9 us)
Async XLA Ops:
  6.5 15.5 %copy-start = (bf16[64,8192]{1,0:T(8,128)(2,1)S(1)}, bf16[64,8192]{1,0:T(8,128)(2,1)}, u32[]{:S(2)}) copy-start(bf16[64,8192]{1,0:T(8,128)(2,1)} %param.7) | copy-start | bytes 3145732
  6.5 62.5 %all-reduce.3.cloned.1.call-start = ((), (), s32[]{:S(2)}) async-start(), calls=%async_computation | async-start | bytes 1048576 | tf_op jit(solution)/shard_map/psum | solution.py:24
  114.6 1.9 copy-start.1
  310.7 164.2 %copy-start.2 = (bf16[32,4096]{1,0:T(8,128)(2,1)S(1)}, bf16[32,4096]{1,0:T(8,128)(2,1)}, u32[]{:S(2)}) copy-start(bf16[32,4096]{1,0:T(8,128)(2,1)} %param.11) | copy-start | bytes 786436
Sparse Core Ops, SparseCore 0:
  22.1 46.8 all-reduce.2
where the time goes:
time: 483 us
  blocking collectives  399 us (83%)
  matrix products  49.2 us (10%)
  waiting for transfers between devices  17.6 us (4%)
  between operations  13.5 us (3%)
    psum x7, blocking collectives, global_sum(): return lax.psum(values, ('dp', 'tensor'))  217 us
    all_gather x5, blocking collectives, gather_rows(): return lax.all_gather(values, ('dp', 'tensor'), axis=1, tiled=True)  153 us
    all_gather x1, blocking collectives, on_device(): in_feats = lax.all_gather(in_local, 'tensor', axis=1, tiled=True)  23.4 us
    dot_general x4, matrix products, on_device(): lax.dot_general(gathered, fisher_rows, (((1,), (1,)), ((), ())), precisio...  20.5 us
    psum x1, waiting for transfers between devices, on_device(): out_feats = lax.psum(out_local, 'tensor')  17.6 us
    dot_general x1, matrix products, on_device(): lax.dot_general(out_proj, out_grads, (((1,), (1,)), ((), ())), preferred_...  14.6 us
  transfers between devices with their start and end apart: 1, of which 1 were waited for; matrix products, arithmetic and copies ran while one was open for 1% of the time, Pallas kernels for 0%

commit v1 on v0

v1 whole, which is shorter than its diff:
```python
import jax
import jax.numpy as jnp
from jax import lax
from jax.sharding import PartitionSpec as P

R_IN = 64
R_OUT = 64
SEQ = 1024
ITERS = 4


def on_device(inputs, in_proj, out_grads, out_proj, prior, queries):
    highest = lax.Precision.HIGHEST
    width = R_IN * R_OUT
    in_local = lax.dot_general(
        in_proj, inputs, (((1,), (1,)), ((), ())), preferred_element_type=jnp.float32
    )
    in_all = lax.all_gather(in_local, "tensor", axis=0)
    out_local = lax.dot_general(
        out_proj, out_grads, (((1,), (1,)), ((), ())), preferred_element_type=jnp.float32
    )
    tokens = out_local.shape[1]
    seq_count = tokens // SEQ
    in_tokens = in_all.transpose(1, 0, 2).reshape(R_IN, seq_count, SEQ)
    out_tokens = out_local.reshape(R_OUT, seq_count, SEQ)
    partial = jnp.einsum("ast,bst->sab", in_tokens, out_tokens, precision=highest)
    partial = partial.reshape(seq_count, width) / SEQ
    own_vectors = jnp.sum(lax.all_gather(partial, "tensor", axis=0), axis=0)
    vectors = lax.all_gather(own_vectors, "dp", axis=0, tiled=True)
    train_count = vectors.shape[0]
    row_count = prior.shape[0]
    row_start = (
        lax.axis_index("dp") * lax.axis_size("tensor") + lax.axis_index("tensor")
    ) * row_count

    def gather_rows(values):
        held = lax.all_gather(values, "tensor", axis=0)
        held = lax.all_gather(held, "dp", axis=0)
        return held.transpose(2, 0, 1, 3).reshape(values.shape[0], width)

    def own_rows(values):
        return lax.dynamic_slice_in_dim(values, row_start, row_count, 1)

    fisher_rows = (
        prior
        + lax.dot_general(
            own_rows(vectors),
            vectors,
            (((0,), (0,)), ((), ())),
            precision=highest,
            preferred_element_type=jnp.float32,
        )
        / train_count
    )

    def apply_rows(direction):
        return lax.dot_general(
            direction,
            fisher_rows,
            (((1,), (1,)), ((), ())),
            precision=highest,
            preferred_element_type=jnp.float32,
        )

    solution = jnp.zeros_like(vectors)
    residual = vectors
    direction = vectors
    norm_now = jnp.sum(residual * residual, axis=1)
    for iteration in range(ITERS):
        applied_rows = apply_rows(direction)
        if iteration == ITERS - 1:
            own = jnp.sum(own_rows(direction) * applied_rows, axis=1)
            own = jnp.broadcast_to(own[:, None], (train_count, 128))
            held = jnp.sum(lax.all_gather(own, "tensor", axis=0), axis=0)
            curvature = jnp.sum(lax.all_gather(held, "dp", axis=0), axis=0)[:, 0]
            step_size = norm_now / curvature
            solution = solution + step_size[:, None] * direction
            break
        applied = gather_rows(applied_rows)
        step_size = norm_now / jnp.sum(direction * applied, axis=1)
        solution = solution + step_size[:, None] * direction
        residual = residual - step_size[:, None] * applied
        norm_next = jnp.sum(residual * residual, axis=1)
        direction = residual + (norm_next / norm_now)[:, None] * direction
        norm_now = norm_next
    return lax.dot_general(
        solution,
        queries.astype(jnp.float32),
        (((1,), (1,)), ((), ())),
        precision=highest,
        preferred_element_type=jnp.float32,
    )


def solution(mesh):
    return jax.shard_map(
        on_device,
        mesh=mesh,
        in_specs=(
            P(("groups", "dp", "tensor"), None),
            P(),
            P(("groups", "dp"), "tensor"),
            P(None, "tensor"),
            P(("groups", "dp", "tensor"), None),
            P(("groups", "dp", "tensor"), None),
        ),
        out_specs=P("groups", ("dp", "tensor")),
        check_vma=False,
    )
```

time: 483 us -> 157 us (0.33)
  blocking collectives: 399 us -> 110 us
  waiting for transfers between devices: 17.6 us -> 0 us
  between operations: 13.5 us -> 0.81 us
  matrix products: 49.2 us -> 41.2 us
    psum x7 -> x0, blocking collectives: 217 us -> none  [global_sum(): return lax.psum(values, ('dp', 'tensor'))]
    all_gather x6 -> x9, blocking collectives: 177 us -> 92.2 us  [the longest x3 39.4 us: gather_rows(): held = lax.all_gather(values, 'tensor', axis=0)]
    psum x1 -> x0, waiting for transfers between devices: 17.6 us -> none  [on_device(): out_feats = lax.psum(out_local, 'tensor')]
    unnamed x0 -> x1, blocking collectives: none -> 12.1 us
    dot_general x6, matrix products: 26.9 us -> 20 us  [the longest x4 13.5 us: apply_rows(): lax.dot_general(direction, fisher_rows, (((1,), (1,)), ((), ())), precisi...]
  transfers between devices with their start and end apart: 1 -> 0, of which waited for: 1 -> 0; matrix products, arithmetic and copies ran while one was open for 1% -> 0% of each run, Pallas kernels for 0% -> 0%
where the time goes in v1:
time: 157 us
  blocking collectives  110 us (70%)
  matrix products  41.2 us (26%)
  local copies, waits for them, and re-layouts  3.26 us (2%)
  other arithmetic  1.72 us (1%)
    all_gather x3, blocking collectives, gather_rows(): held = lax.all_gather(values, 'tensor', axis=0)  39.4 us
    all_gather x1, blocking collectives, on_device(): in_all = lax.all_gather(in_local, 'tensor', axis=0)  17.4 us
    all_gather x3, blocking collectives, gather_rows(): held = lax.all_gather(held, 'dp', axis=0)  16.5 us
    dot_general x1, matrix products, on_device(): lax.dot_general(out_proj, out_grads, (((1,), (1,)), ((), ())), preferred_...  14.3 us
    all_gather x1, blocking collectives, on_device(): own_vectors = jnp.sum(lax.all_gather(partial, 'tensor', axis=0), axis=0)  13.8 us
    dot_general x4, matrix products, apply_rows(): lax.dot_general(direction, fisher_rows, (((1,), (1,)), ((), ())), precisi...  13.5 us
    unnamed x1, blocking collectives  12.1 us
    dot_general x1, matrix products, on_device(): lax.dot_general(in_proj, inputs, (((1,), (1,)), ((), ())), preferred_elem...  6.12 us

profile of v1, /device:TPU:0, one launch (start us, length us, event | category | flops | bytes accessed | tf_op | source)
XLA Modules:
  0.0 156.8 jit_solution(12387387869968031011)
XLA Ops:
  0.0 1.2 copy-done
  1.2 6.1 %fusion.19 = f32[64,512]{1,0:T(8,128)S(1)} fusion(bf16[64,8192]{1,0:T(8,128)(2,1)S(1)} %copy-done, bf16[512,8192]{1,0:T(8,128)(2,1)} %param.6), kind=kOutput, calls=%fused_computation.39 | convolution fusion | flops 536870912 | bytes 9568256 | tf_op jit(solution)/shard_map/dot_general | solution.py:15
  7.3 17.4 %all-gather = f32[256,512]{1,0:T(8,128)S(1)} all-gather(f32[64,512]{1,0:T(8,128)S(1)} %fusion.19), channel_id=3, replica_groups=mesh['groups'=2,'dp'=4,'tensor'=4] {'tensor'}, dimensions={0}, use_global_device_ids=true | all-gather | bytes 655360 | tf_op jit(solution)/shard_map/all_gather | solution.py:18
  24.7 0.3 copy.30
  25.1 0.5 reshape.59
  25.6 14.3 %fusion.20 = f32[64,2048]{1,0:T(8,128)S(1)} fusion(bf16[64,7168]{1,0:T(8,128)(2,1)S(1)} %copy-done.1, bf16[2048,7168]{1,0:T(8,128)(2,1)} %param.8), kind=kOutput, calls=%fused_computation.40 | convolution fusion | flops 1879048192 | bytes 30801920 | tf_op jit(solution)/shard_map/dot_general | solution.py:19
  39.9 0.8 convolution_multiply_fusion.1
  40.7 13.8 %all_gather.60 = f32[4,2,4096]{2,1,0:T(2,128)S(1)} all-gather(f32[1,2,4096]{2,1,0:T(2,128)S(1)} %div.62), channel_id=1, replica_groups=mesh['groups'=2,'dp'=4,'tensor'=4] {'tensor'}, dimensions={0}, use_global_device_ids=true | all-gather | bytes 163840 | tf_op jit(solution)/shard_map/all_gather | solution.py:28
  54.6 5.6 %all-gather.9 = f32[4,2,4096]{2,1,0:T(2,128)S(1)} all-gather(f32[1,2,4096]{2,1,0:T(2,128)S(1)} %bitcast.57), channel_id=1, replica_groups=mesh['groups'=2,'dp'=4,'tensor'=4] {'dp'}, dimensions={0}, use_global_device_ids=true | all-gather | bytes 163840 | tf_op jit(solution)/shard_map/all_gather | solution.py:29
  60.3 5.5 %fusion = f32[256,4096]{1,0:T(8,128)S(1)} fusion(f32[256,4096]{1,0:T(8,128)} %param.10, f32[8,4096]{1,0:T(8,128)S(1)} %reshape.79, s32[]{:T(128)S(6)} %select_n.4), kind=kOutput, calls=%fused_computation.1 | convolution fusion | flops 102760448 | bytes 8527876 | tf_op jit(solution)/shard_map/dot_general | solution.py:46
  65.8 3.3 %fusion.21 = f32[8,256]{1,0:T(8,128)S(1)} fusion(f32[8,4096]{1,0:T(8,128)S(1)} %reshape.79, f32[256,4096]{1,0:T(8,128)S(1)} %fusion), kind=kOutput, calls=%fused_computation.41 | convolution fusion | flops 100663296 | bytes 4333568 | tf_op jit(solution)/shard_map/dot_general | solution.py:57
  69.2 13.1 %all-gather.1 = f32[32,256]{1,0:T(8,128)S(1)} all-gather(f32[8,256]{1,0:T(8,128)S(1)} %fusion.21), channel_id=4, replica_groups=mesh['groups'=2,'dp'=4,'tensor'=4] {'tensor'}, dimensions={0}, use_global_device_ids=true | all-gather | bytes 40960 | tf_op jit(solution)/shard_map/all_gather | solution.py:37
  82.3 5.4 %all-gather.2 = f32[16,8,256]{2,1,0:T(8,128)S(1)} all-gather(f32[4,8,256]{2,1,0:T(8,128)S(1)} %bitcast.58), channel_id=5, replica_groups=mesh['groups'=2,'dp'=4,'tensor'=4] {'dp'}, dimensions={0}, use_global_device_ids=true | all-gather | bytes 163840 | tf_op jit(solution)/shard_map/all_gather | solution.py:38
  88.2 3.3 %fusion.22 = f32[8,256]{1,0:T(8,128)S(1)} fusion(f32[8,4096]{1,0:T(8,128)S(1)} %multiply_add_fusion.2, f32[256,4096]{1,0:T(8,128)S(1)} %fusion), kind=kOutput, calls=%fused_computation.42 | convolution fusion | flops 100663296 | bytes 4333568 | tf_op jit(solution)/shard_map/dot_general | solution.py:57
  91.6 13.1 %all-gather.3 = f32[32,256]{1,0:T(8,128)S(1)} all-gather(f32[8,256]{1,0:T(8,128)S(1)} %fusion.22), channel_id=6, replica_groups=mesh['groups'=2,'dp'=4,'tensor'=4] {'tensor'}, dimensions={0}, use_global_device_ids=true | all-gather | bytes 40960 | tf_op jit(solution)/shard_map/all_gather | solution.py:37
  104.7 5.6 %all-gather.4 = f32[16,8,256]{2,1,0:T(8,128)S(1)} all-gather(f32[4,8,256]{2,1,0:T(8,128)S(1)} %bitcast.59), channel_id=7, replica_groups=mesh['groups'=2,'dp'=4,'tensor'=4] {'dp'}, dimensions={0}, use_global_device_ids=true | all-gather | bytes 163840 | tf_op jit(solution)/shard_map/all_gather | solution.py:38
  110.9 3.3 %fusion.23 = f32[8,256]{1,0:T(8,128)S(1)} fusion(f32[8,4096]{1,0:T(8,128)S(1)} %multiply_add_fusion.1, f32[256,4096]{1,0:T(8,128)S(1)} %fusion), kind=kOutput, calls=%fused_computation.43 | convolution fusion | flops 100663296 | bytes 4333568 | tf_op jit(solution)/shard_map/dot_general | solution.py:57
  114.2 13.1 %all-gather.5 = f32[32,256]{1,0:T(8,128)S(1)} all-gather(f32[8,256]{1,0:T(8,128)S(1)} %fusion.23), channel_id=8, replica_groups=mesh['groups'=2,'dp'=4,'tensor'=4] {'tensor'}, dimensions={0}, use_global_device_ids=true | all-gather | bytes 40960 | tf_op jit(solution)/shard_map/all_gather | solution.py:37
  127.3 5.4 %all-gather.6 = f32[16,8,256]{2,1,0:T(8,128)S(1)} all-gather(f32[4,8,256]{2,1,0:T(8,128)S(1)} %bitcast.60), channel_id=9, replica_groups=mesh['groups'=2,'dp'=4,'tensor'=4] {'dp'}, dimensions={0}, use_global_device_ids=true | all-gather | bytes 163840 | tf_op jit(solution)/shard_map/all_gather | solution.py:38
  133.3 3.5 %fusion.1 = f32[8]{0:T(128)S(1)} fusion(f32[8,4096]{1,0:T(8,128)S(1)} %multiply_add_fusion, f32[256,4096]{1,0:T(8,128)S(1)} %fusion, s32[]{:T(128)S(6)} %select_n.4), kind=kOutput, calls=%fused_computation.4 | convolution fusion | flops 100667384 | bytes 4333604 | tf_op jit(solution)/shard_map/dot_general | solution.py:57
  136.7 0.6 dynamic-slice
  138.2 12.1 %all-reduce = f32[32]{0:T(128)S(1)} all-reduce(f32[32]{0:T(128)S(1)} %dynamic-update-slice), channel_id=10, replica_groups=mesh['groups'=2,'dp'=4,'tensor'=4] {'tensor'}, use_global_device_ids=true, to_apply=%add | all-reduce | flops 32 | bytes 256
  150.5 5.2 %all-gather.8 = f32[32,128]{1,0:T(8,128)S(1)} all-gather(f32[8,128]{1,0:T(8,128)S(1)} %broadcast_reduce_fusion), channel_id=11, replica_groups=mesh['groups'=2,'dp'=4,'tensor'=4] {'dp'}, dimensions={0}, use_global_device_ids=true | all-gather | bytes 20480 | tf_op jit(solution)/shard_map/all_gather | solution.py:75
  155.8 1.0 fusion.5
  (32 shorter events, 2.3 us)
Async XLA Ops:
  0.0 1.2 copy-start
  1.2 24.3 %copy-start.1 = (bf16[64,7168]{1,0:T(8,128)(2,1)S(1)}, bf16[64,7168]{1,0:T(8,128)(2,1)}, u32[]{:S(2)}) copy-start(bf16[64,7168]{1,0:T(8,128)(2,1)} %param.9) | copy-start | bytes 2752516
  110.8 25.9 %copy-start.3 = (u32[32]{0:T(128)S(1)}, u32[32]{0:T(128)}, u32[]{:S(2)}) copy-start(u32[32]{0:T(128)} %constant.25) | copy-start | bytes 388
  110.9 45.0 %copy-start.2 = (bf16[32,4096]{1,0:T(8,128)(2,1)S(1)}, bf16[32,4096]{1,0:T(8,128)(2,1)}, u32[]{:S(2)}) copy-start(bf16[32,4096]{1,0:T(8,128)(2,1)} %param.11) | copy-start | bytes 786436

commit v2 on v0

v2 whole, which is shorter than its diff:
```python
import functools

import jax
import jax.numpy as jnp
from jax import lax
from jax.experimental import pallas as pl
from jax.experimental.pallas import tpu as pltpu
from jax.sharding import PartitionSpec as P

R_IN = 64
R_OUT = 64
SEQ = 1024
ITERS = 4
LANES = 128
DIRECT_LIMIT = 16
NT = (((1,), (1,)), ((), ()))
HIGHEST = lax.Precision.HIGHEST
VMEM_SPEC = pl.BlockSpec(memory_space=pltpu.VMEM)
ANY_SPEC = pl.BlockSpec(memory_space=pl.ANY)


def exchange(value, axes, size):
    held = [value]
    for k in range(1, size):
        held.append(lax.ppermute(value, axes, [(i, i ^ k) for i in range(size)]))
    return held


def dot_nt(a, b):
    return lax.dot_general(a, b, NT, precision=HIGHEST, preferred_element_type=jnp.float32)


def row_sum(values):
    return jnp.sum(values, axis=1, keepdims=True)


def partial_kernel(size, *refs):
    blocks, out_ref, part_ref, held = refs[:size], refs[size], refs[size + 1], refs[size + 2]
    me = lax.axis_index("tensor")
    tokens = blocks[0].shape[1]
    for k, block in enumerate(blocks):
        start = pl.multiple_of((me ^ k) * tokens, LANES)
        held[:, pl.ds(start, tokens)] = block[...]
    for s in range(part_ref.shape[0]):
        span = slice(s * SEQ, (s + 1) * SEQ)
        part_ref[s] = dot_nt(held[:, span], out_ref[:, span]) * (1.0 / SEQ)


def partial_vectors(blocks, out_local):
    seq_count = out_local.shape[1] // SEQ
    return pl.pallas_call(
        functools.partial(partial_kernel, len(blocks)),
        out_shape=jax.ShapeDtypeStruct((seq_count, R_IN, R_OUT), jnp.float32),
        in_specs=[VMEM_SPEC] * (len(blocks) + 1),
        out_specs=VMEM_SPEC,
        scratch_shapes=[pltpu.VMEM(out_local.shape, jnp.float32)],
        name="partial_vectors",
    )(*blocks, out_local)


def prior_copies(prior_ref, prior_vmem, sems):
    chunk = prior_ref.shape[1] // sems.shape[0]
    copies = []
    for c in range(sems.shape[0]):
        span = pl.ds(c * chunk, chunk)
        copies.append(
            pltpu.make_async_copy(prior_ref.at[:, span], prior_vmem.at[:, span], sems.at[c])
        )
    return copies


def own_columns(ref, me, count):
    if count % LANES == 0:
        return ref[:, pl.ds(pl.multiple_of(me * count, LANES), count)]
    per = LANES // count
    held = ref[:, pl.ds(pl.multiple_of((me // per) * LANES, LANES), LANES)]
    return pltpu.roll(held, LANES - (me % per) * count, 1)[:, :count]


def apply_fisher(direction, vectors_ref, copies, prior_vmem, me):
    seqs, width = direction.shape
    rows = prior_vmem.shape[0]
    upper = direction.astype(jnp.bfloat16)
    lower = (direction - upper.astype(jnp.float32)).astype(jnp.bfloat16)
    both = jnp.concatenate([upper, lower], axis=0)
    weights = dot_nt(direction, vectors_ref[...]) * (1.0 / seqs)
    applied = jnp.dot(
        weights, own_columns(vectors_ref, me, rows), precision=HIGHEST, preferred_element_type=jnp.float32
    )
    chunk = width // len(copies)
    for c, copy in enumerate(copies):
        copy.wait()
        span = slice(c * chunk, (c + 1) * chunk)
        block = prior_vmem[:, span]
        block_upper = block.astype(jnp.bfloat16)
        block_lower = (block - block_upper.astype(jnp.float32)).astype(jnp.bfloat16)
        first = lax.dot_general(both[:, span], block_upper, NT, preferred_element_type=jnp.float32)
        second = lax.dot_general(upper[:, span], block_lower, NT, preferred_element_type=jnp.float32)
        applied = applied + (first[:seqs] + first[seqs:] + second)
    return applied


def flat_index(tensor_size):
    return lax.axis_index("dp") * tensor_size + lax.axis_index("tensor")


def start_kernel(size, tensor_size, *refs):
    pieces, prior_ref = refs[:size], refs[size]
    vectors_ref, applied_ref, norm_ref, held, prior_vmem, sems = refs[size + 1 :]
    copies = prior_copies(prior_ref, prior_vmem, sems)
    for copy in copies:
        copy.start()
    dp = lax.axis_index("dp")
    for k, piece in enumerate(pieces):
        held[dp ^ k] = piece[...]
    vectors = jnp.concatenate([held[k] for k in range(size)], axis=0)
    vectors_ref[...] = vectors
    norm_ref[...] = jnp.broadcast_to(row_sum(vectors * vectors), norm_ref.shape)
    applied_ref[...] = apply_fisher(vectors, vectors_ref, copies, prior_vmem, flat_index(tensor_size))


def start_cg(pieces, prior, tensor_size):
    seqs = len(pieces) * pieces[0].shape[0]
    rows, width = prior.shape
    shape = functools.partial(jax.ShapeDtypeStruct, dtype=jnp.float32)
    return pl.pallas_call(
        functools.partial(start_kernel, len(pieces), tensor_size),
        out_shape=(shape((seqs, width)), shape((seqs, rows)), shape((seqs, LANES))),
        in_specs=[VMEM_SPEC] * len(pieces) + [ANY_SPEC],
        out_specs=(VMEM_SPEC,) * 3,
        scratch_shapes=[
            pltpu.VMEM((len(pieces),) + pieces[0].shape, jnp.float32),
            pltpu.VMEM(prior.shape, jnp.float32),
            pltpu.SemaphoreType.DMA((4,)),
        ],
        compiler_params=pltpu.CompilerParams(vmem_limit_bytes=16 * 2**20),
        name="cg_start",
    )(*pieces, prior)


def step_kernel(size, tensor_size, first, last, *refs):
    blocks, refs = refs[:size], refs[size:]
    if first:
        prior_ref, vectors_ref, norm_ref = refs[:3]
        refs = refs[3:]
    else:
        prior_ref, vectors_ref, norm_ref, direction_ref, residual_ref, solution_ref = refs[:6]
        refs = refs[6:]
    if last:
        queries_ref, curvature_out, norm_out, solved_out, along_out = refs[:5]
        refs = refs[5:]
    else:
        applied_out, norm_out, direction_out, residual_out, solution_out = refs[:5]
        refs = refs[5:]
    held, prior_vmem, sems = refs
    copies = prior_copies(prior_ref, prior_vmem, sems)
    for copy in copies:
        copy.start()
    me = flat_index(tensor_size)
    if size == 1:
        applied = blocks[0][...]
    else:
        rows = blocks[0].shape[1]
        for k, block in enumerate(blocks):
            held[:, pl.ds(pl.multiple_of((me ^ k) * rows, LANES), rows)] = block[...]
        applied = held[...]
    direction = vectors_ref[...] if first else direction_ref[...]
    residual = direction if first else residual_ref[...]
    norm = norm_ref[...][:, :1]
    step = norm / row_sum(direction * applied)
    solution = step * direction
    if not first:
        solution = solution_ref[...] + solution
    residual = residual - step * applied
    norm_next = row_sum(residual * residual)
    direction = residual + (norm_next / norm) * direction
    norm_out[...] = jnp.broadcast_to(norm_next, norm_out.shape)
    applied_rows = apply_fisher(direction, vectors_ref, copies, prior_vmem, me)
    if last:
        held[...] = direction
        own = own_columns(held, me, applied_rows.shape[1])
        curvature_out[...] = jnp.broadcast_to(row_sum(own * applied_rows), curvature_out.shape)
        queries = queries_ref[...].astype(jnp.float32)
        solved_out[...] = dot_nt(solution, queries)
        along_out[...] = dot_nt(direction, queries)
    else:
        applied_out[...] = applied_rows
        direction_out[...] = direction
        residual_out[...] = residual
        solution_out[...] = solution


def step_cg(blocks, prior, vectors, norm, state, queries, tensor_size):
    first, last = state is None, queries is not None
    shape = functools.partial(jax.ShapeDtypeStruct, dtype=jnp.float32)
    whole, column = shape(vectors.shape), shape(norm.shape)
    seqs = vectors.shape[0]
    operands = list(blocks) + [prior, vectors, norm] + list(state or ()) + ([queries] if last else [])
    specs = [VMEM_SPEC] * len(operands)
    specs[len(blocks)] = ANY_SPEC
    if last:
        scores = shape((seqs, queries.shape[0]))
        out_shape = (column, column, scores, scores)
    else:
        out_shape = (shape((seqs, prior.shape[0])), column, whole, whole, whole)
    return pl.pallas_call(
        functools.partial(step_kernel, len(blocks), tensor_size, first, last),
        out_shape=out_shape,
        in_specs=specs,
        out_specs=(VMEM_SPEC,) * len(out_shape),
        scratch_shapes=[
            pltpu.VMEM(vectors.shape, jnp.float32),
            pltpu.VMEM(prior.shape, jnp.float32),
            pltpu.SemaphoreType.DMA((4,)),
        ],
        compiler_params=pltpu.CompilerParams(vmem_limit_bytes=16 * 2**20),
        name="cg_step",
    )(*operands)


def on_device(dp_size, tensor_size, inputs, in_proj, out_grads, out_proj, prior, queries):
    width = R_IN * R_OUT
    both, devices = ("dp", "tensor"), dp_size * tensor_size
    in_local = lax.dot_general(in_proj, inputs, NT, preferred_element_type=jnp.float32)
    in_blocks = exchange(in_local, "tensor", tensor_size)
    out_local = lax.dot_general(out_proj, out_grads, NT, preferred_element_type=jnp.float32)
    partial = partial_vectors(in_blocks, out_local).reshape(-1, width)
    own_vectors = sum(exchange(partial, "tensor", tensor_size))
    pieces = exchange(own_vectors, "dp", dp_size)

    def gather_rows(values):
        if devices <= DIRECT_LIMIT:
            return exchange(values, both, devices)
        held = lax.all_gather(lax.all_gather(values, "tensor", axis=0), "dp", axis=0)
        return [held.transpose(2, 0, 1, 3).reshape(values.shape[0], width)]

    def global_sum(values):
        if devices <= DIRECT_LIMIT:
            return sum(exchange(values, both, devices))
        return lax.psum(values, both)

    vectors, applied_rows, norm = start_cg(pieces, prior, tensor_size)
    state = None
    for iteration in range(1, ITERS - 1):
        blocks = gather_rows(applied_rows)
        applied_rows, norm, *state = step_cg(blocks, prior, vectors, norm, state, None, tensor_size)
    blocks = gather_rows(applied_rows)
    curvature, norm, solved, along = step_cg(blocks, prior, vectors, norm, state, queries, tensor_size)
    curvature = global_sum(curvature)
    return solved + (norm / curvature)[:, :1] * along


def solution(mesh):
    return jax.shard_map(
        functools.partial(on_device, mesh.shape["dp"], mesh.shape["tensor"]),
        mesh=mesh,
        in_specs=(
            P(("groups", "dp", "tensor"), None),
            P(),
            P(("groups", "dp"), "tensor"),
            P(None, "tensor"),
            P(("groups", "dp", "tensor"), None),
            P(("groups", "dp", "tensor"), None),
        ),
        out_specs=P("groups", ("dp", "tensor")),
        check_vma=False,
    )
```

time: 483 us -> 159 us (0.33)
  blocking collectives: 399 us -> 0 us
  starting transfers between devices: 0.01 us -> 97.5 us
  matrix products: 49.2 us -> 21.1 us
  Pallas kernels: 0 us -> 15.5 us
  between operations: 13.5 us -> 0.18 us
  local copies, waits for them, and re-layouts: 2.97 us -> 7.98 us
    psum x7 -> x0, blocking collectives: 217 us -> none  [global_sum(): return lax.psum(values, ('dp', 'tensor'))]
    all_gather x7 -> x0, blocking collectives: 182 us -> none  [the longest x5 153 us: gather_rows(): return lax.all_gather(values, ('dp', 'tensor'), axis=1, tiled=True)]
    ppermute x0 -> x69, starting transfers between devices: none -> 97.5 us  [exchange(): held.append(lax.ppermute(value, axes, [(i, i ^ k) for i in range(size)]))]
    dot_general x9 -> x2, matrix products: 49.2 us -> 21.1 us  [the longest x1 15 us: on_device(): lax.dot_general(out_proj, out_grads, NT, preferred_element_type=jnp.float32)]
    psum x1 -> x0, waiting for transfers between devices: 17.6 us -> none  [on_device(): out_feats = lax.psum(out_local, 'tensor')]
    ppermute x0 -> x69, waiting for transfers between devices: none -> 15.8 us  [exchange(): held.append(lax.ppermute(value, axes, [(i, i ^ k) for i in range(size)]))]
    pallas_call x0 -> x5, Pallas kernels: none -> 15.5 us  [the longest x3 10.2 us: step_cg(): pl.pallas_call(functools.partial(step_kernel, len(blocks), tensor_size, f...]
  transfers between devices with their start and end apart: 1 -> 69, of which waited for: 1 -> 15; matrix products, arithmetic and copies ran while one was open for 1% -> 9% of each run, Pallas kernels for 0% -> 0%
where the time goes in v2:
time: 159 us
  starting transfers between devices  97.5 us (61%)
  matrix products  21.1 us (13%)
  waiting for transfers between devices  15.8 us (10%)
  Pallas kernels  15.5 us (10%)
  local copies, waits for them, and re-layouts  7.98 us (5%)
    ppermute x69, starting transfers between devices, exchange(): held.append(lax.ppermute(value, axes, [(i, i ^ k) for i in range(size)]))  97.5 us
    ppermute x69, waiting for transfers between devices, exchange(): held.append(lax.ppermute(value, axes, [(i, i ^ k) for i in range(size)]))  15.8 us
    dot_general x1, matrix products, on_device(): lax.dot_general(out_proj, out_grads, NT, preferred_element_type=jnp.float32)  15 us
    pallas_call x3, Pallas kernels, step_cg(): pl.pallas_call(functools.partial(step_kernel, len(blocks), tensor_size, f...  10.2 us
    unnamed x18, local copies, waits for them, and re-layouts  6.93 us
    dot_general x1, matrix products, on_device(): lax.dot_general(in_proj, inputs, NT, preferred_element_type=jnp.float32)  6.04 us
  transfers between devices with their start and end apart: 69, of which 15 were waited for; matrix products, arithmetic and copies ran while one was open for 9% of the time, Pallas kernels for 0%

profile of v2, /device:TPU:0, one launch (start us, length us, event | category | flops | bytes accessed | tf_op | source)
XLA Modules:
  0.0 158.7 jit_solution(2464144426364186222)
XLA Ops:
  1.2 6.0 %fusion.refs_0_ = f32[64,512]{1,0:T(8,128)S(1)} fusion(bf16[64,8192]{1,0:T(8,128)(2,1)S(1)} %copy-done, bf16[512,8192]{1,0:T(8,128)(2,1)} %param.6), kind=kOutput, calls=%fused_computation.4 | convolution fusion | flops 536870912 | bytes 9568256 | tf_op jit(solution)/shard_map/dot_general | solution.py:224
  7.3 5.1 %collective-permute-start.2 = (f32[64,512]{1,0:T(8,128)S(1)}, f32[64,512]{1,0:T(8,128)S(1)}, u32[]{:S(2)}, u32[]{:S(2)}) collective-permute-start(f32[64,512]{1,0:T(8,128)S(1)} %fusion.refs_0_), channel_id=1, source_target_pairs={{0,3},{1,2},{2,1},{3,0},{4,7},{5,6},{6,5},{7,4},{8,11},{9,10},{10,... | collective-permute-start | bytes 393224 | tf_op jit(solution)/shard_map/ppermute | solution.py:25
  13.0 15.0 %fusion.1.refs_4_ = f32[64,2048]{1,0:T(8,128)} fusion(bf16[64,7168]{1,0:T(8,128)(2,1)S(1)} %copy-done.4, bf16[2048,7168]{1,0:T(8,128)(2,1)} %param.8), kind=kOutput, calls=%fused_computation.5 | convolution fusion | flops 1879048192 | bytes 30801920 | tf_op jit(solution)/shard_map/dot_general | solution.py:226
  29.4 2.5 %partial_vectors.1 = f32[2,64,64]{2,1,0:T(8,128)} custom-call(f32[64,512]{1,0:T(8,128)} %copy-done.5, f32[64,512]{1,0:T(8,128)} %copy-done.8, f32[64,512]{1,0:T(8,128)} %copy-done.7, f32[64,512]{1,0:T(8,128)} %copy-done.6, f32[64,2048]{1,0:T(8,128)} %fusion.1.refs_4_), custom_call_target="tpu_custom_call" | custom-call | tf_op jit(solution)/shard_map/partial_vectors/pallas_call | solution.py:51
  32.9 3.8 %collective-permute-start.5 = (f32[2,4096]{1,0:T(2,128)S(1)}, f32[2,4096]{1,0:T(2,128)S(1)}, u32[]{:S(2)}, u32[]{:S(2)}) collective-permute-start(f32[2,4096]{1,0:T(2,128)S(1)} %reshape.3), channel_id=1, source_target_pairs={{0,3},{1,2},{2,1},{3,0},{4,7},{5,6},{6,5},{7,4},{8,11},{9,10},{10,... | collective-permute-start | bytes 98312 | tf_op jit(solution)/shard_map/ppermute | solution.py:25
  38.7 2.8 %collective-permute-done.4 = f32[2,4096]{1,0:T(2,128)S(1)} collective-permute-done((f32[2,4096]{1,0:T(2,128)S(1)}, f32[2,4096]{1,0:T(2,128)S(1)}, u32[]{:S(2)}, u32[]{:S(2)}) %collective-permute-start.4) | collective-permute-done | bytes 32800 | tf_op jit(solution)/shard_map/ppermute | solution.py:25
  47.9 2.7 %cg_start.1 = (f32[8,4096]{1,0:T(8,128)S(1)}, f32[8,256]{1,0:T(8,128)S(1)}, f32[8,128]{1,0:T(8,128)S(1)}) custom-call(f32[2,4096]{1,0:T(2,128)S(1)} %add_add_fusion.refs_0_, f32[2,4096]{1,0:T(2,128)S(1)} %collective-permute-done.6.refs_1_, f32[2,4096]{1,0:T(2,128)S(1)} %collective-permute-done.7.refs_2_, f32[2,4096]{1,0:T(2,128)S(1)} %collective-permute-done.8.refs_3_, ...), custom_call_target="tpu_custom_call" | custom-call | tf_op jit(solution)/shard_map/cg_start/pallas_call | solution.py:126
  53.1 2.9 %collective-permute-start.21 = (f32[8,256]{1,0:T(8,128)S(1)}, f32[8,256]{1,0:T(8,128)S(1)}, u32[]{:S(2)}, u32[]{:S(2)}) collective-permute-start(f32[8,256]{1,0:T(8,128)S(1)} %get-tuple-element.22.refs_0_), channel_id=1, source_target_pairs={{0,13},{1,12},{2,15},{3,14},{4,9},{5,8},{6,11},{7,10},{8,5},{9,4},... | collective-permute-start | bytes 24584 | tf_op jit(solution)/shard_map/ppermute | solution.py:25
  56.8 2.4 %collective-permute-start.19 = (f32[8,256]{1,0:T(8,128)S(1)}, f32[8,256]{1,0:T(8,128)S(1)}, u32[]{:S(2)}, u32[]{:S(2)}) collective-permute-start(f32[8,256]{1,0:T(8,128)S(1)} %get-tuple-element.22.refs_0_), channel_id=1, source_target_pairs={{0,11},{1,10},{2,9},{3,8},{4,15},{5,14},{6,13},{7,12},{8,3},{9,2},... | collective-permute-start | bytes 24584 | tf_op jit(solution)/shard_map/ppermute | solution.py:25
  59.2 3.8 %collective-permute-start.17 = (f32[8,256]{1,0:T(8,128)S(1)}, f32[8,256]{1,0:T(8,128)S(1)}, u32[]{:S(2)}, u32[]{:S(2)}) collective-permute-start(f32[8,256]{1,0:T(8,128)S(1)} %get-tuple-element.22.refs_0_), channel_id=1, source_target_pairs={{0,9},{1,8},{2,11},{3,10},{4,13},{5,12},{6,15},{7,14},{8,1},{9,0},... | collective-permute-start | bytes 24584 | tf_op jit(solution)/shard_map/ppermute | solution.py:25
  69.3 2.9 %collective-permute-start.9 = (f32[8,256]{1,0:T(8,128)S(1)}, f32[8,256]{1,0:T(8,128)S(1)}, u32[]{:S(2)}, u32[]{:S(2)}) collective-permute-start(f32[8,256]{1,0:T(8,128)S(1)} %get-tuple-element.22.refs_0_), channel_id=1, source_target_pairs={{0,1},{1,0},{2,3},{3,2},{4,5},{5,4},{6,7},{7,6},{8,9},{9,8},{10,11... | collective-permute-start | bytes 24584 | tf_op jit(solution)/shard_map/ppermute | solution.py:25
  76.1 3.1 %cg_step.3 = (f32[8,256]{1,0:T(8,128)S(1)}, f32[8,128]{1,0:T(8,128)S(1)}, f32[8,4096]{1,0:T(8,128)S(1)}, f32[8,4096]{1,0:T(8,128)S(1)}, f32[8,4096]{1,0:T(8,128)S(1)}) custom-call(f32[8,256]{1,0:T(8,128)S(1)} %get-tuple-element.22.refs_0_, f32[8,256]{1,0:T(8,128)S(1)} %collective-permute-done.9.refs_1_, f32[8,256]{1,0:T(8,128)S(1)} %collective-permute-done.10.refs_2_, ...), custom_call_target="tpu_custom_call" | custom-call | tf_op jit(solution)/shard_map/cg_step/pallas_call | solution.py:206
  80.7 2.6 %collective-permute-start.37 = (f32[8,256]{1,0:T(8,128)S(1)}, f32[8,256]{1,0:T(8,128)S(1)}, u32[]{:S(2)}, u32[]{:S(2)}) collective-permute-start(f32[8,256]{1,0:T(8,128)S(1)} %get-tuple-element.25.refs_0_), channel_id=1, source_target_pairs={{0,14},{1,15},{2,12},{3,13},{4,10},{5,11},{6,8},{7,9},{8,6},{9,7},... | collective-permute-start | bytes 24584 | tf_op jit(solution)/shard_map/ppermute | solution.py:25
  85.5 3.2 %collective-permute-start.34 = (f32[8,256]{1,0:T(8,128)S(1)}, f32[8,256]{1,0:T(8,128)S(1)}, u32[]{:S(2)}, u32[]{:S(2)}) collective-permute-start(f32[8,256]{1,0:T(8,128)S(1)} %get-tuple-element.25.refs_0_), channel_id=1, source_target_pairs={{0,11},{1,10},{2,9},{3,8},{4,15},{5,14},{6,13},{7,12},{8,3},{9,2},... | collective-permute-start | bytes 24584 | tf_op jit(solution)/shard_map/ppermute | solution.py:25
  88.9 2.8 %collective-permute-start.32 = (f32[8,256]{1,0:T(8,128)S(1)}, f32[8,256]{1,0:T(8,128)S(1)}, u32[]{:S(2)}, u32[]{:S(2)}) collective-permute-start(f32[8,256]{1,0:T(8,128)S(1)} %get-tuple-element.25.refs_0_), channel_id=1, source_target_pairs={{0,9},{1,8},{2,11},{3,10},{4,13},{5,12},{6,15},{7,14},{8,1},{9,0},... | collective-permute-start | bytes 24584 | tf_op jit(solution)/shard_map/ppermute | solution.py:25
  103.3 3.1 %cg_step.4 = (f32[8,256]{1,0:T(8,128)S(1)}, f32[8,128]{1,0:T(8,128)S(1)}, f32[8,4096]{1,0:T(8,128)S(1)}, f32[8,4096]{1,0:T(8,128)S(1)}, f32[8,4096]{1,0:T(8,128)S(1)}) custom-call(f32[8,256]{1,0:T(8,128)S(1)} %get-tuple-element.25.refs_0_, f32[8,256]{1,0:T(8,128)S(1)} %collective-permute-done.24.refs_1_, f32[8,256]{1,0:T(8,128)S(1)} %collective-permute-done.25.refs_2_, ...), custom_call_target="tpu_custom_call" | custom-call | tf_op jit(solution)/shard_map/cg_step/pallas_call | solution.py:206
  107.4 2.3 %collective-permute-start.52 = (f32[8,256]{1,0:T(8,128)S(1)}, f32[8,256]{1,0:T(8,128)S(1)}, u32[]{:S(2)}, u32[]{:S(2)}) collective-permute-start(f32[8,256]{1,0:T(8,128)S(1)} %get-tuple-element.30.refs_0_), channel_id=1, source_target_pairs={{0,14},{1,15},{2,12},{3,13},{4,10},{5,11},{6,8},{7,9},{8,6},{9,7},... | collective-permute-start | bytes 24584 | tf_op jit(solution)/shard_map/ppermute | solution.py:25
  112.6 2.5 %collective-permute-start.49 = (f32[8,256]{1,0:T(8,128)S(1)}, f32[8,256]{1,0:T(8,128)S(1)}, u32[]{:S(2)}, u32[]{:S(2)}) collective-permute-start(f32[8,256]{1,0:T(8,128)S(1)} %get-tuple-element.30.refs_0_), channel_id=1, source_target_pairs={{0,11},{1,10},{2,9},{3,8},{4,15},{5,14},{6,13},{7,12},{8,3},{9,2},... | collective-permute-start | bytes 24584 | tf_op jit(solution)/shard_map/ppermute | solution.py:25
  115.3 3.5 %collective-permute-start.47 = (f32[8,256]{1,0:T(8,128)S(1)}, f32[8,256]{1,0:T(8,128)S(1)}, u32[]{:S(2)}, u32[]{:S(2)}) collective-permute-start(f32[8,256]{1,0:T(8,128)S(1)} %get-tuple-element.30.refs_0_), channel_id=1, source_target_pairs={{0,9},{1,8},{2,11},{3,10},{4,13},{5,12},{6,15},{7,14},{8,1},{9,0},... | collective-permute-start | bytes 24584 | tf_op jit(solution)/shard_map/ppermute | solution.py:25
  125.2 2.8 %collective-permute-start.39 = (f32[8,256]{1,0:T(8,128)S(1)}, f32[8,256]{1,0:T(8,128)S(1)}, u32[]{:S(2)}, u32[]{:S(2)}) collective-permute-start(f32[8,256]{1,0:T(8,128)S(1)} %get-tuple-element.30.refs_0_), channel_id=1, source_target_pairs={{0,1},{1,0},{2,3},{3,2},{4,5},{5,4},{6,7},{7,6},{8,9},{9,8},{10,11... | collective-permute-start | bytes 24584 | tf_op jit(solution)/shard_map/ppermute | solution.py:25
  129.8 4.1 %cg_step.5 = (f32[8,128]{1,0:T(8,128)S(1)}, f32[8,128]{1,0:T(8,128)S(1)}, f32[8,32]{1,0:T(8,128)S(1)}, f32[8,32]{1,0:T(8,128)S(1)}) custom-call(f32[8,256]{1,0:T(8,128)S(1)} %get-tuple-element.30.refs_0_, f32[8,256]{1,0:T(8,128)S(1)} %collective-permute-done.39.refs_1_, f32[8,256]{1,0:T(8,128)S(1)} %collective-permute-done.40.refs_2_, ...), custom_call_target="tpu_custom_call" | custom-call | tf_op jit(solution)/shard_map/cg_step/pallas_call | solution.py:206
  135.5 2.5 %collective-permute-start.67 = (f32[8,128]{1,0:T(8,128)S(1)}, f32[8,128]{1,0:T(8,128)S(1)}, u32[]{:S(2)}, u32[]{:S(2)}) collective-permute-start(f32[8,128]{1,0:T(8,128)S(1)} %get-tuple-element.37), channel_id=1, source_target_pairs={{0,14},{1,15},{2,12},{3,13},{4,10},{5,11},{6,8},{7,9},{8,6},{9,7},... | collective-permute-start | bytes 12296 | tf_op jit(solution)/shard_map/ppermute | solution.py:25
  140.1 3.2 %collective-permute-start.64 = (f32[8,128]{1,0:T(8,128)S(1)}, f32[8,128]{1,0:T(8,128)S(1)}, u32[]{:S(2)}, u32[]{:S(2)}) collective-permute-start(f32[8,128]{1,0:T(8,128)S(1)} %get-tuple-element.37), channel_id=1, source_target_pairs={{0,11},{1,10},{2,9},{3,8},{4,15},{5,14},{6,13},{7,12},{8,3},{9,2},... | collective-permute-start | bytes 12296 | tf_op jit(solution)/shard_map/ppermute | solution.py:25
  143.5 2.8 %collective-permute-start.62 = (f32[8,128]{1,0:T(8,128)S(1)}, f32[8,128]{1,0:T(8,128)S(1)}, u32[]{:S(2)}, u32[]{:S(2)}) collective-permute-start(f32[8,128]{1,0:T(8,128)S(1)} %get-tuple-element.37), channel_id=1, source_target_pairs={{0,9},{1,8},{2,11},{3,10},{4,13},{5,12},{6,15},{7,14},{8,1},{9,0},... | collective-permute-start | bytes 12296 | tf_op jit(solution)/shard_map/ppermute | solution.py:25
  (144 shorter events, 70.0 us)
Async XLA Ops:
  7.3 20.8 %collective-permute-start.2 = (f32[64,512]{1,0:T(8,128)S(1)}, f32[64,512]{1,0:T(8,128)S(1)}, u32[]{:S(2)}, u32[]{:S(2)}) collective-permute-start(f32[64,512]{1,0:T(8,128)S(1)} %fusion.refs_0_), channel_id=1, source_target_pairs={{0,3},{1,2},{2,1},{3,0},{4,7},{5,6},{6,5},{7,4},{8,11},{9,10},{10,... | collective-permute-start | bytes 393224 | tf_op jit(solution)/shard_map/ppermute | solution.py:25
  12.4 15.7 %collective-permute-start.1 = (f32[64,512]{1,0:T(8,128)S(1)}, f32[64,512]{1,0:T(8,128)S(1)}, u32[]{:S(2)}, u32[]{:S(2)}) collective-permute-start(f32[64,512]{1,0:T(8,128)S(1)} %fusion.refs_0_), channel_id=1, source_target_pairs={{0,2},{1,3},{2,0},{3,1},{4,6},{5,7},{6,4},{7,5},{8,10},{9,11},{10,... | collective-permute-start | bytes 393224 | tf_op jit(solution)/shard_map/ppermute | solution.py:25
  12.4 15.7 %collective-permute-start = (f32[64,512]{1,0:T(8,128)S(1)}, f32[64,512]{1,0:T(8,128)S(1)}, u32[]{:S(2)}, u32[]{:S(2)}) collective-permute-start(f32[64,512]{1,0:T(8,128)S(1)} %fusion.refs_0_), channel_id=1, source_target_pairs={{0,1},{1,0},{2,3},{3,2},{4,5},{5,4},{6,7},{7,6},{8,9},{9,8},{10,11... | collective-permute-start | bytes 393224 | tf_op jit(solution)/shard_map/ppermute | solution.py:25
  50.6 8.6 %collective-permute-start.23 = (f32[8,256]{1,0:T(8,128)S(1)}, f32[8,256]{1,0:T(8,128)S(1)}, u32[]{:S(2)}, u32[]{:S(2)}) collective-permute-start(f32[8,256]{1,0:T(8,128)S(1)} %get-tuple-element.22.refs_0_), channel_id=1, source_target_pairs={{0,15},{1,14},{2,13},{3,12},{4,11},{5,10},{6,9},{7,8},{8,7},{9,6},... | collective-permute-start | bytes 24584 | tf_op jit(solution)/shard_map/ppermute | solution.py:25
  53.1 9.9 %collective-permute-start.21 = (f32[8,256]{1,0:T(8,128)S(1)}, f32[8,256]{1,0:T(8,128)S(1)}, u32[]{:S(2)}, u32[]{:S(2)}) collective-permute-start(f32[8,256]{1,0:T(8,128)S(1)} %get-tuple-element.22.refs_0_), channel_id=1, source_target_pairs={{0,13},{1,12},{2,15},{3,14},{4,9},{5,8},{6,11},{7,10},{8,5},{9,4},... | collective-permute-start | bytes 24584 | tf_op jit(solution)/shard_map/ppermute | solution.py:25
  56.0 7.6 %collective-permute-start.20 = (f32[8,256]{1,0:T(8,128)S(1)}, f32[8,256]{1,0:T(8,128)S(1)}, u32[]{:S(2)}, u32[]{:S(2)}) collective-permute-start(f32[8,256]{1,0:T(8,128)S(1)} %get-tuple-element.22.refs_0_), channel_id=1, source_target_pairs={{0,12},{1,13},{2,14},{3,15},{4,8},{5,9},{6,10},{7,11},{8,4},{9,5},... | collective-permute-start | bytes 24584 | tf_op jit(solution)/shard_map/ppermute | solution.py:25
  56.8 7.0 %collective-permute-start.19 = (f32[8,256]{1,0:T(8,128)S(1)}, f32[8,256]{1,0:T(8,128)S(1)}, u32[]{:S(2)}, u32[]{:S(2)}) collective-permute-start(f32[8,256]{1,0:T(8,128)S(1)} %get-tuple-element.22.refs_0_), channel_id=1, source_target_pairs={{0,11},{1,10},{2,9},{3,8},{4,15},{5,14},{6,13},{7,12},{8,3},{9,2},... | collective-permute-start | bytes 24584 | tf_op jit(solution)/shard_map/ppermute | solution.py:25
  59.2 7.3 %collective-permute-start.17 = (f32[8,256]{1,0:T(8,128)S(1)}, f32[8,256]{1,0:T(8,128)S(1)}, u32[]{:S(2)}, u32[]{:S(2)}) collective-permute-start(f32[8,256]{1,0:T(8,128)S(1)} %get-tuple-element.22.refs_0_), channel_id=1, source_target_pairs={{0,9},{1,8},{2,11},{3,10},{4,13},{5,12},{6,15},{7,14},{8,1},{9,0},... | collective-permute-start | bytes 24584 | tf_op jit(solution)/shard_map/ppermute | solution.py:25
  64.9 7.4 %collective-permute-start.13 = (f32[8,256]{1,0:T(8,128)S(1)}, f32[8,256]{1,0:T(8,128)S(1)}, u32[]{:S(2)}, u32[]{:S(2)}) collective-permute-start(f32[8,256]{1,0:T(8,128)S(1)} %get-tuple-element.22.refs_0_), channel_id=1, source_target_pairs={{0,5},{1,4},{2,7},{3,6},{4,1},{5,0},{6,3},{7,2},{8,13},{9,12},{10,... | collective-permute-start | bytes 24584 | tf_op jit(solution)/shard_map/ppermute | solution.py:25
  79.2 9.5 %collective-permute-start.38 = (f32[8,256]{1,0:T(8,128)S(1)}, f32[8,256]{1,0:T(8,128)S(1)}, u32[]{:S(2)}, u32[]{:S(2)}) collective-permute-start(f32[8,256]{1,0:T(8,128)S(1)} %get-tuple-element.25.refs_0_), channel_id=1, source_target_pairs={{0,15},{1,14},{2,13},{3,12},{4,11},{5,10},{6,9},{7,8},{8,7},{9,6},... | collective-permute-start | bytes 24584 | tf_op jit(solution)/shard_map/ppermute | solution.py:25
  80.7 8.1 %collective-permute-start.37 = (f32[8,256]{1,0:T(8,128)S(1)}, f32[8,256]{1,0:T(8,128)S(1)}, u32[]{:S(2)}, u32[]{:S(2)}) collective-permute-start(f32[8,256]{1,0:T(8,128)S(1)} %get-tuple-element.25.refs_0_), channel_id=1, source_target_pairs={{0,14},{1,15},{2,12},{3,13},{4,10},{5,11},{6,8},{7,9},{8,6},{9,7},... | collective-permute-start | bytes 24584 | tf_op jit(solution)/shard_map/ppermute | solution.py:25
  83.3 8.4 %collective-permute-start.36 = (f32[8,256]{1,0:T(8,128)S(1)}, f32[8,256]{1,0:T(8,128)S(1)}, u32[]{:S(2)}, u32[]{:S(2)}) collective-permute-start(f32[8,256]{1,0:T(8,128)S(1)} %get-tuple-element.25.refs_0_), channel_id=1, source_target_pairs={{0,13},{1,12},{2,15},{3,14},{4,9},{5,8},{6,11},{7,10},{8,5},{9,4},... | collective-permute-start | bytes 24584 | tf_op jit(solution)/shard_map/ppermute | solution.py:25
  83.7 8.5 %collective-permute-start.35 = (f32[8,256]{1,0:T(8,128)S(1)}, f32[8,256]{1,0:T(8,128)S(1)}, u32[]{:S(2)}, u32[]{:S(2)}) collective-permute-start(f32[8,256]{1,0:T(8,128)S(1)} %get-tuple-element.25.refs_0_), channel_id=1, source_target_pairs={{0,12},{1,13},{2,14},{3,15},{4,8},{5,9},{6,10},{7,11},{8,4},{9,5},... | collective-permute-start | bytes 24584 | tf_op jit(solution)/shard_map/ppermute | solution.py:25
  85.5 7.4 %collective-permute-start.34 = (f32[8,256]{1,0:T(8,128)S(1)}, f32[8,256]{1,0:T(8,128)S(1)}, u32[]{:S(2)}, u32[]{:S(2)}) collective-permute-start(f32[8,256]{1,0:T(8,128)S(1)} %get-tuple-element.25.refs_0_), channel_id=1, source_target_pairs={{0,11},{1,10},{2,9},{3,8},{4,15},{5,14},{6,13},{7,12},{8,3},{9,2},... | collective-permute-start | bytes 24584 | tf_op jit(solution)/shard_map/ppermute | solution.py:25
  106.4 8.7 %collective-permute-start.53 = (f32[8,256]{1,0:T(8,128)S(1)}, f32[8,256]{1,0:T(8,128)S(1)}, u32[]{:S(2)}, u32[]{:S(2)}) collective-permute-start(f32[8,256]{1,0:T(8,128)S(1)} %get-tuple-element.30.refs_0_), channel_id=1, source_target_pairs={{0,15},{1,14},{2,13},{3,12},{4,11},{5,10},{6,9},{7,8},{8,7},{9,6},... | collective-permute-start | bytes 24584 | tf_op jit(solution)/shard_map/ppermute | solution.py:25
  107.4 7.9 %collective-permute-start.52 = (f32[8,256]{1,0:T(8,128)S(1)}, f32[8,256]{1,0:T(8,128)S(1)}, u32[]{:S(2)}, u32[]{:S(2)}) collective-permute-start(f32[8,256]{1,0:T(8,128)S(1)} %get-tuple-element.30.refs_0_), channel_id=1, source_target_pairs={{0,14},{1,15},{2,12},{3,13},{4,10},{5,11},{6,8},{7,9},{8,6},{9,7},... | collective-permute-start | bytes 24584 | tf_op jit(solution)/shard_map/ppermute | solution.py:25
  109.7 9.1 %collective-permute-start.51 = (f32[8,256]{1,0:T(8,128)S(1)}, f32[8,256]{1,0:T(8,128)S(1)}, u32[]{:S(2)}, u32[]{:S(2)}) collective-permute-start(f32[8,256]{1,0:T(8,128)S(1)} %get-tuple-element.30.refs_0_), channel_id=1, source_target_pairs={{0,13},{1,12},{2,15},{3,14},{4,9},{5,8},{6,11},{7,10},{8,5},{9,4},... | collective-permute-start | bytes 24584 | tf_op jit(solution)/shard_map/ppermute | solution.py:25
  110.7 8.7 %collective-permute-start.50 = (f32[8,256]{1,0:T(8,128)S(1)}, f32[8,256]{1,0:T(8,128)S(1)}, u32[]{:S(2)}, u32[]{:S(2)}) collective-permute-start(f32[8,256]{1,0:T(8,128)S(1)} %get-tuple-element.30.refs_0_), channel_id=1, source_target_pairs={{0,12},{1,13},{2,14},{3,15},{4,8},{5,9},{6,10},{7,11},{8,4},{9,5},... | collective-permute-start | bytes 24584 | tf_op jit(solution)/shard_map/ppermute | solution.py:25
  120.7 7.3 %collective-permute-start.43 = (f32[8,256]{1,0:T(8,128)S(1)}, f32[8,256]{1,0:T(8,128)S(1)}, u32[]{:S(2)}, u32[]{:S(2)}) collective-permute-start(f32[8,256]{1,0:T(8,128)S(1)} %get-tuple-element.30.refs_0_), channel_id=1, source_target_pairs={{0,5},{1,4},{2,7},{3,6},{4,1},{5,0},{6,3},{7,2},{8,13},{9,12},{10,... | collective-permute-start | bytes 24584 | tf_op jit(solution)/shard_map/ppermute | solution.py:25
  133.9 9.5 %collective-permute-start.68 = (f32[8,128]{1,0:T(8,128)S(1)}, f32[8,128]{1,0:T(8,128)S(1)}, u32[]{:S(2)}, u32[]{:S(2)}) collective-permute-start(f32[8,128]{1,0:T(8,128)S(1)} %get-tuple-element.37), channel_id=1, source_target_pairs={{0,15},{1,14},{2,13},{3,12},{4,11},{5,10},{6,9},{7,8},{8,7},{9,6},... | collective-permute-start | bytes 12296 | tf_op jit(solution)/shard_map/ppermute | solution.py:25
  135.5 8.0 %collective-permute-start.67 = (f32[8,128]{1,0:T(8,128)S(1)}, f32[8,128]{1,0:T(8,128)S(1)}, u32[]{:S(2)}, u32[]{:S(2)}) collective-permute-start(f32[8,128]{1,0:T(8,128)S(1)} %get-tuple-element.37), channel_id=1, source_target_pairs={{0,14},{1,15},{2,12},{3,13},{4,10},{5,11},{6,8},{7,9},{8,6},{9,7},... | collective-permute-start | bytes 12296 | tf_op jit(solution)/shard_map/ppermute | solution.py:25
  137.9 8.4 %collective-permute-start.66 = (f32[8,128]{1,0:T(8,128)S(1)}, f32[8,128]{1,0:T(8,128)S(1)}, u32[]{:S(2)}, u32[]{:S(2)}) collective-permute-start(f32[8,128]{1,0:T(8,128)S(1)} %get-tuple-element.37), channel_id=1, source_target_pairs={{0,13},{1,12},{2,15},{3,14},{4,9},{5,8},{6,11},{7,10},{8,5},{9,4},... | collective-permute-start | bytes 12296 | tf_op jit(solution)/shard_map/ppermute | solution.py:25
  138.3 8.6 %collective-permute-start.65 = (f32[8,128]{1,0:T(8,128)S(1)}, f32[8,128]{1,0:T(8,128)S(1)}, u32[]{:S(2)}, u32[]{:S(2)}) collective-permute-start(f32[8,128]{1,0:T(8,128)S(1)} %get-tuple-element.37), channel_id=1, source_target_pairs={{0,12},{1,13},{2,14},{3,15},{4,8},{5,9},{6,10},{7,11},{8,4},{9,5},... | collective-permute-start | bytes 12296 | tf_op jit(solution)/shard_map/ppermute | solution.py:25
  140.1 7.4 %collective-permute-start.64 = (f32[8,128]{1,0:T(8,128)S(1)}, f32[8,128]{1,0:T(8,128)S(1)}, u32[]{:S(2)}, u32[]{:S(2)}) collective-permute-start(f32[8,128]{1,0:T(8,128)S(1)} %get-tuple-element.37), channel_id=1, source_target_pairs={{0,11},{1,10},{2,9},{3,8},{4,15},{5,14},{6,13},{7,12},{8,3},{9,2},... | collective-permute-start | bytes 12296 | tf_op jit(solution)/shard_map/ppermute | solution.py:25
  (54 other events, 385.2 us)

commit v3 on v2

v3 whole, which is shorter than its diff:
```python
import functools

import jax
import jax.numpy as jnp
from jax import lax
from jax.experimental import pallas as pl
from jax.experimental.pallas import tpu as pltpu
from jax.sharding import PartitionSpec as P

R_IN = 64
R_OUT = 64
SEQ = 1024
ITERS = 4
LANES = 128
NT = (((1,), (1,)), ((), ()))
HIGHEST = lax.Precision.HIGHEST
VMEM_SPEC = pl.BlockSpec(memory_space=pltpu.VMEM)
PARAMS = pltpu.CompilerParams(vmem_limit_bytes=16 * 2**20)
F32 = functools.partial(jax.ShapeDtypeStruct, dtype=jnp.float32)


def gather(value, axes, size):
    return lax.all_to_all(jnp.broadcast_to(value[None], (size,) + value.shape), axes, 0, 0)


def dot_nt(a, b):
    return lax.dot_general(a, b, NT, precision=HIGHEST, preferred_element_type=jnp.float32)


def row_sum(values):
    return jnp.sum(values, axis=1, keepdims=True)


def partial_kernel(in_ref, out_ref, part_ref, held):
    count, _, tokens = in_ref.shape
    for k in range(count):
        held[:, k * tokens : (k + 1) * tokens] = in_ref[k]
    for s in range(part_ref.shape[0]):
        span = slice(s * SEQ, (s + 1) * SEQ)
        part_ref[s] = dot_nt(held[:, span], out_ref[:, span]) * (1.0 / SEQ)


def partial_vectors(in_all, out_local):
    seq_count = out_local.shape[1] // SEQ
    return pl.pallas_call(
        partial_kernel,
        out_shape=F32((seq_count, R_IN, R_OUT)),
        in_specs=[VMEM_SPEC] * 2,
        out_specs=VMEM_SPEC,
        scratch_shapes=[pltpu.VMEM(out_local.shape, jnp.float32)],
        compiler_params=PARAMS,
        name="partial_vectors",
    )(in_all, out_local)


def split_kernel(prior_ref, upper_ref, lower_ref):
    block = prior_ref[...]
    upper = block.astype(jnp.bfloat16)
    upper_ref[...] = upper
    lower_ref[...] = (block - upper.astype(jnp.float32)).astype(jnp.bfloat16)


def split_prior(prior):
    rows, width = prior.shape
    spec = pl.BlockSpec((rows, width // 8), lambda i: (0, i))
    return pl.pallas_call(
        split_kernel,
        grid=(8,),
        out_shape=(jax.ShapeDtypeStruct(prior.shape, jnp.bfloat16),) * 2,
        in_specs=[spec],
        out_specs=(spec, spec),
        compiler_params=PARAMS,
        name="split_prior",
    )(prior)


def own_columns(ref, me, count):
    if count % LANES == 0:
        return ref[:, pl.ds(pl.multiple_of(me * count, LANES), count)]
    per = LANES // count
    held = ref[:, pl.ds(pl.multiple_of((me // per) * LANES, LANES), LANES)]
    return pltpu.roll(held, LANES - (me % per) * count, 1)[:, :count]


def apply_fisher(direction, vectors_ref, upper_ref, lower_ref, me):
    seqs = direction.shape[0]
    upper = direction.astype(jnp.bfloat16)
    lower = (direction - upper.astype(jnp.float32)).astype(jnp.bfloat16)
    both = jnp.concatenate([upper, lower], axis=0)
    weights = dot_nt(direction, vectors_ref[...]) * (1.0 / seqs)
    own = own_columns(vectors_ref, me, upper_ref.shape[0])
    applied = jnp.dot(weights, own, precision=HIGHEST, preferred_element_type=jnp.float32)
    first = lax.dot_general(both, upper_ref[...], NT, preferred_element_type=jnp.float32)
    second = lax.dot_general(upper, lower_ref[...], NT, preferred_element_type=jnp.float32)
    return applied + (first[:seqs] + first[seqs:] + second)


def flat_index(tensor_size):
    return lax.axis_index("dp") * tensor_size + lax.axis_index("tensor")


def start_kernel(tensor_size, pieces_ref, upper_ref, lower_ref, vectors_ref, applied_ref, norm_ref):
    count, seqs, columns = pieces_ref.shape
    for i in range(count):
        dp, tensor = i // tensor_size, i % tensor_size
        vectors_ref[dp * seqs : (dp + 1) * seqs, tensor * columns : (tensor + 1) * columns] = pieces_ref[i]
    vectors = vectors_ref[...]
    norm_ref[...] = jnp.broadcast_to(row_sum(vectors * vectors), norm_ref.shape)
    applied_ref[...] = apply_fisher(vectors, vectors_ref, upper_ref, lower_ref, flat_index(tensor_size))


def start_cg(pieces, prior_pieces, tensor_size):
    seqs = pieces.shape[0] // tensor_size * pieces.shape[1]
    rows, width = prior_pieces[0].shape
    return pl.pallas_call(
        functools.partial(start_kernel, tensor_size),
        out_shape=(F32((seqs, width)), F32((seqs, rows)), F32((seqs, LANES))),
        in_specs=[VMEM_SPEC] * 3,
        out_specs=(VMEM_SPEC,) * 3,
        compiler_params=PARAMS,
        name="cg_start",
    )(pieces, *prior_pieces)


def step_kernel(tensor_size, first, last, *refs):
    blocks_ref, upper_ref, lower_ref, vectors_ref, norm_ref = refs[:5]
    refs = refs[5:]
    if not first:
        direction_ref, residual_ref, solution_ref = refs[:3]
        refs = refs[3:]
    if last:
        queries_ref, curvature_out, norm_out, solved_out, along_out, held = refs
    else:
        applied_out, norm_out, direction_out, residual_out, solution_out, held = refs
    me = flat_index(tensor_size)
    count, _, rows = blocks_ref.shape
    for i in range(count):
        held[:, i * rows : (i + 1) * rows] = blocks_ref[i]
    applied = held[...]
    direction = vectors_ref[...] if first else direction_ref[...]
    residual = direction if first else residual_ref[...]
    norm = norm_ref[...][:, :1]
    step = norm / row_sum(direction * applied)
    solution = step * direction
    if not first:
        solution = solution_ref[...] + solution
    residual = residual - step * applied
    norm_next = row_sum(residual * residual)
    direction = residual + (norm_next / norm) * direction
    norm_out[...] = jnp.broadcast_to(norm_next, norm_out.shape)
    applied_rows = apply_fisher(direction, vectors_ref, upper_ref, lower_ref, me)
    if last:
        held[...] = direction
        own = own_columns(held, me, rows)
        curvature_out[...] = jnp.broadcast_to(row_sum(own * applied_rows), curvature_out.shape)
        queries = queries_ref[...].astype(jnp.float32)
        solved_out[...] = dot_nt(solution, queries)
        along_out[...] = dot_nt(direction, queries)
    else:
        applied_out[...] = applied_rows
        direction_out[...] = direction
        residual_out[...] = residual
        solution_out[...] = solution


def step_cg(blocks, prior_pieces, vectors, norm, state, queries, tensor_size):
    first, last = state is None, queries is not None
    whole, column = F32(vectors.shape), F32(norm.shape)
    seqs = vectors.shape[0]
    operands = [blocks, *prior_pieces, vectors, norm, *(state or ())] + ([queries] if last else [])
    if last:
        scores = F32((seqs, queries.shape[0]))
        out_shape = (column, column, scores, scores)
    else:
        out_shape = (F32((seqs, blocks.shape[2])), column, whole, whole, whole)
    return pl.pallas_call(
        functools.partial(step_kernel, tensor_size, first, last),
        out_shape=out_shape,
        in_specs=[VMEM_SPEC] * len(operands),
        out_specs=(VMEM_SPEC,) * len(out_shape),
        scratch_shapes=[pltpu.VMEM(vectors.shape, jnp.float32)],
        compiler_params=PARAMS,
        name="cg_step",
    )(*operands)


def on_device(dp_size, tensor_size, inputs, in_proj, out_grads, out_proj, prior, queries):
    width = R_IN * R_OUT
    both, devices = ("dp", "tensor"), dp_size * tensor_size
    in_local = lax.dot_general(in_proj, inputs, NT, preferred_element_type=jnp.float32)
    in_all = gather(in_local, "tensor", tensor_size)
    out_local = lax.dot_general(out_proj, out_grads, NT, preferred_element_type=jnp.float32)
    partial = partial_vectors(in_all, out_local).reshape(-1, tensor_size, width // tensor_size)
    partial = lax.all_to_all(partial.transpose(1, 0, 2), "tensor", 0, 0)
    pieces = gather(jnp.sum(partial, axis=0), both, devices)
    prior_pieces = split_prior(prior)
    vectors, applied_rows, norm = start_cg(pieces, prior_pieces, tensor_size)
    state = None
    for iteration in range(1, ITERS - 1):
        blocks = gather(applied_rows, both, devices)
        applied_rows, norm, *state = step_cg(blocks, prior_pieces, vectors, norm, state, None, tensor_size)
    blocks = gather(applied_rows, both, devices)
    curvature, norm, solved, along = step_cg(blocks, prior_pieces, vectors, norm, state, queries, tensor_size)
    curvature = jnp.sum(gather(curvature, both, devices), axis=0)
    return solved + (norm / curvature)[:, :1] * along


def solution(mesh):
    return jax.shard_map(
        functools.partial(on_device, mesh.shape["dp"], mesh.shape["tensor"]),
        mesh=mesh,
        in_specs=(
            P(("groups", "dp", "tensor"), None),
            P(),
            P(("groups", "dp"), "tensor"),
            P(None, "tensor"),
            P(("groups", "dp", "tensor"), None),
            P(("groups", "dp", "tensor"), None),
        ),
        out_specs=P("groups", ("dp", "tensor")),
        check_vma=False,
    )
```

time: 159 us -> 104 us (0.65)
  starting transfers between devices: 97.5 us -> 9.83 us
  blocking collectives: 0 us -> 51.6 us
  waiting for transfers between devices: 15.8 us -> 2.53 us
  Pallas kernels: 15.5 us -> 10.3 us
    ppermute x69 -> x0, starting transfers between devices: 97.5 us -> none  [exchange(): held.append(lax.ppermute(value, axes, [(i, i ^ k) for i in range(size)]))]
    all_to_all x0 -> x5, blocking collectives: none -> 51.6 us  [the longest x4 41.2 us: gather(): lax.all_to_all(jnp.broadcast_to(value[None], (size,) + value.shape), axes...]
    ppermute x69 -> x0, waiting for transfers between devices: 15.8 us -> none  [exchange(): held.append(lax.ppermute(value, axes, [(i, i ^ k) for i in range(size)]))]
    all_to_all x0 -> x2, starting transfers between devices: none -> 9.83 us  [gather(): lax.all_to_all(jnp.broadcast_to(value[None], (size,) + value.shape), axes...]
    pallas_call x5 -> x6, Pallas kernels: 15.5 us -> 10.3 us  [the longest x3 6.74 us: step_cg(): pl.pallas_call(functools.partial(step_kernel, tensor_size, first, last),...]
    all_to_all x0 -> x2, waiting for transfers between devices: none -> 2.53 us  [gather(): lax.all_to_all(jnp.broadcast_to(value[None], (size,) + value.shape), axes...]
    broadcast_in_dim x0 -> x6, local copies, waits for them, and re-layouts: none -> 1.65 us  [gather(): jnp.broadcast_to(value[None], (size,) + value.shape)]
    unnamed x18 -> x12, local copies, waits for them, and re-layouts: 6.93 us -> 6.35 us
  transfers between devices with their start and end apart: 69 -> 2, of which waited for: 15 -> 2; matrix products, arithmetic and copies ran while one was open for 9% -> 14% of each run, Pallas kernels for 0% -> 1%
where the time goes in v3:
time: 104 us
  blocking collectives  51.6 us (50%)
  matrix products  20.3 us (20%)
  Pallas kernels  10.3 us (10%)
  starting transfers between devices  9.83 us (9%)
  local copies, waits for them, and re-layouts  8.24 us (8%)
  waiting for transfers between devices  2.53 us (2%)
    all_to_all x4, blocking collectives, gather(): lax.all_to_all(jnp.broadcast_to(value[None], (size,) + value.shape), axes...  41.2 us
    dot_general x1, matrix products, on_device(): lax.dot_general(out_proj, out_grads, NT, preferred_element_type=jnp.float32)  14.3 us
    all_to_all x1, blocking collectives, on_device(): partial = lax.all_to_all(partial.transpose(1, 0, 2), 'tensor', 0, 0)  10.4 us
    all_to_all x2, starting transfers between devices, gather(): lax.all_to_all(jnp.broadcast_to(value[None], (size,) + value.shape), axes...  9.83 us
    pallas_call x3, Pallas kernels, step_cg(): pl.pallas_call(functools.partial(step_kernel, tensor_size, first, last),...  6.74 us
    unnamed x12, local copies, waits for them, and re-layouts  6.35 us
    dot_general x1, matrix products, on_device(): lax.dot_general(in_proj, inputs, NT, preferred_element_type=jnp.float32)  6.04 us
    all_to_all x2, waiting for transfers between devices, gather(): lax.all_to_all(jnp.broadcast_to(value[None], (size,) + value.shape), axes...  2.53 us
  transfers between devices with their start and end apart: 2, of which 2 were waited for; matrix products, arithmetic and copies ran while one was open for 14% of the time, Pallas kernels for 1%

profile of v3, /device:TPU:0, one launch (start us, length us, event | category | flops | bytes accessed | tf_op | source)
XLA Modules:
  0.0 103.6 jit_solution(12860597008333319973)
XLA Ops:
  0.0 1.2 %copy-done = bf16[64,8192]{1,0:T(8,128)(2,1)S(1)} copy-done((bf16[64,8192]{1,0:T(8,128)(2,1)S(1)}, bf16[64,8192]{1,0:T(8,128)(2,1)}, u32[]{:S(2)}) %copy-start) | copy-done | bytes 1048600
  1.2 6.0 %fusion = f32[64,512]{1,0:T(8,128)S(1)} fusion(bf16[64,8192]{1,0:T(8,128)(2,1)S(1)} %copy-done, bf16[512,8192]{1,0:T(8,128)(2,1)} %param.6), kind=kOutput, calls=%fused_computation.3 | convolution fusion | flops 536870912 | bytes 9568256 | tf_op jit(solution)/shard_map/dot_general | solution.py:190
  7.3 0.9 broadcast_in_dim.12
  8.1 6.3 %all-to-all-start = ((f32[4,64,512]{2,1,0:T(8,128)}), f32[4,64,512]{2,1,0:T(8,128)S(1)}, u32[]{:S(2)}, u32[]{:S(2)}) async-start(f32[4,64,512]{2,1,0:T(8,128)} %broadcast_in_dim.12), calls=%async_computation | async-start | bytes 1048576 | tf_op jit(solution)/shard_map/all_to_all | solution.py:23
  14.4 14.3 %fusion.1.out_ref = f32[64,2048]{1,0:T(8,128)S(1)} fusion(bf16[64,7168]{1,0:T(8,128)(2,1)S(1)} %copy-done.5, bf16[2048,7168]{1,0:T(8,128)(2,1)} %param.8), kind=kOutput, calls=%fused_computation.4 | convolution fusion | flops 1879048192 | bytes 30801920 | tf_op jit(solution)/shard_map/dot_general | solution.py:192
  28.8 0.2 all-to-all-done.in_ref
  28.9 0.6 partial_vectors.1
  29.6 10.4 %all_to_all.35 = f32[4,2,1024]{2,1,0:T(2,128)S(1)} all-to-all(f32[4,2,1024]{2,1,0:T(2,128)S(1)} %bitcast.7), channel_id=1, replica_groups=mesh['groups'=2,'dp'=4,'tensor'=4] {'tensor'}, dimensions={0} | all-to-all | bytes 65536 | tf_op jit(solution)/shard_map/all_to_all | solution.py:194
  40.0 0.7 broadcast_in_dim.13
  40.7 3.5 %all-to-all-start.2 = ((f32[16,2,1024]{2,1,0:T(2,128)}), f32[16,2,1024]{2,1,0:T(2,128)S(1)}, u32[]{:S(2)}, u32[]{:S(2)}) async-start(f32[16,2,1024]{2,1,0:T(2,128)} %broadcast_in_dim.13), calls=%async_computation.2 | async-start | bytes 262144 | tf_op jit(solution)/shard_map/all_to_all | solution.py:23
  44.3 2.2 %copy-done.3 = f32[256,4096]{1,0:T(8,128)S(1)} copy-done((f32[256,4096]{1,0:T(8,128)S(1)}, f32[256,4096]{1,0:T(8,128)}, u32[]{:S(2)}) %copy-start.3) | copy-done | bytes 4194328
  46.4 1.4 %split_prior.1 = (bf16[256,4096]{1,0:T(8,128)(2,1)S(1)}, bf16[256,4096]{1,0:T(8,128)(2,1)S(1)}) custom-call(f32[256,4096]{1,0:T(8,128)S(1)} %copy-done.3), custom_call_target="tpu_custom_call" | custom-call | tf_op jit(solution)/shard_map/split_prior/pallas_call | solution.py:66
  47.9 1.3 %copy-done.1 = bf16[256,4096]{1,0:T(8,128)(2,1)} copy-done((bf16[256,4096]{1,0:T(8,128)(2,1)}, bf16[256,4096]{1,0:T(8,128)(2,1)S(1)}, u32[]{:S(2)}) %copy-start.1) | copy-done | bytes 2097176
  49.2 2.4 %all-to-all-done.2.pieces_ref = f32[16,2,1024]{2,1,0:T(2,128)S(1)} async-done(((f32[16,2,1024]{2,1,0:T(2,128)}), f32[16,2,1024]{2,1,0:T(2,128)S(1)}, u32[]{:S(2)}, u32[]{:S(2)}) %all-to-all-start.2) | async-done | bytes 131104 | tf_op jit(solution)/shard_map/all_to_all | solution.py:23
  51.6 1.6 %copy-done.2 = bf16[256,4096]{1,0:T(8,128)(2,1)S(1)} copy-done((bf16[256,4096]{1,0:T(8,128)(2,1)S(1)}, bf16[256,4096]{1,0:T(8,128)(2,1)}, u32[]{:S(2)}) %copy-start.2) | copy-done | bytes 2097176
  53.1 1.6 %cg_start.1 = (f32[8,4096]{1,0:T(8,128)S(1)}, f32[8,256]{1,0:T(8,128)S(1)}, f32[8,128]{1,0:T(8,128)S(1)}) custom-call(f32[16,2,1024]{2,1,0:T(2,128)S(1)} %all-to-all-done.2.pieces_ref, bf16[256,4096]{1,0:T(8,128)(2,1)S(1)} %get-tuple-element.24.upper_ref.refs_1_, bf16[256,4096]{1,0:T(8,128)(2,1)S(1)} %copy-done.2), custom_call_target="tpu_custom_call" | custom-call | tf_op jit(solution)/shard_map/cg_start/pallas_call | solution.py:115
  54.8 10.7 %all_to_all.36.refs_0_ = f32[16,8,256]{2,1,0:T(8,128)S(1)} all-to-all(f32[16,8,256]{2,1,0:T(8,128)S(1)} %broadcast_in_dim.14), channel_id=1, replica_groups=mesh['groups'=2,'dp'=4,'tensor'=4] {'dp','tensor'}, dimensions={0} | all-to-all | bytes 262144 | tf_op jit(solution)/shard_map/all_to_all | solution.py:23
  65.5 2.0 %cg_step.3 = (f32[8,256]{1,0:T(8,128)S(1)}, f32[8,128]{1,0:T(8,128)S(1)}, f32[8,4096]{1,0:T(8,128)S(1)}, f32[8,4096]{1,0:T(8,128)S(1)}, f32[8,4096]{1,0:T(8,128)S(1)}) custom-call(f32[16,8,256]{2,1,0:T(8,128)S(1)} %all_to_all.36.refs_0_, bf16[256,4096]{1,0:T(8,128)(2,1)S(1)} %get-tuple-element.24.upper_ref.refs_1_, bf16[256,4096]{1,0:T(8,128)(2,1)S(1)} %copy-done.2, ...), custom_call_target="tpu_custom_call" | custom-call | tf_op jit(solution)/shard_map/cg_step/pallas_call | solution.py:176
  67.5 10.4 %all_to_all.37.refs_0_ = f32[16,8,256]{2,1,0:T(8,128)S(1)} all-to-all(f32[16,8,256]{2,1,0:T(8,128)S(1)} %broadcast_in_dim.15), channel_id=1, replica_groups=mesh['groups'=2,'dp'=4,'tensor'=4] {'dp','tensor'}, dimensions={0} | all-to-all | bytes 262144 | tf_op jit(solution)/shard_map/all_to_all | solution.py:23
  77.9 2.0 %cg_step.4 = (f32[8,256]{1,0:T(8,128)S(1)}, f32[8,128]{1,0:T(8,128)S(1)}, f32[8,4096]{1,0:T(8,128)S(1)}, f32[8,4096]{1,0:T(8,128)S(1)}, f32[8,4096]{1,0:T(8,128)S(1)}) custom-call(f32[16,8,256]{2,1,0:T(8,128)S(1)} %all_to_all.37.refs_0_, bf16[256,4096]{1,0:T(8,128)(2,1)S(1)} %get-tuple-element.24.upper_ref.refs_1_, bf16[256,4096]{1,0:T(8,128)(2,1)S(1)} %copy-done.2, ...), custom_call_target="tpu_custom_call" | custom-call | tf_op jit(solution)/shard_map/cg_step/pallas_call | solution.py:176
  79.9 10.4 %all_to_all.38.refs_0_ = f32[16,8,256]{2,1,0:T(8,128)S(1)} all-to-all(f32[16,8,256]{2,1,0:T(8,128)S(1)} %broadcast_in_dim.16), channel_id=1, replica_groups=mesh['groups'=2,'dp'=4,'tensor'=4] {'dp','tensor'}, dimensions={0} | all-to-all | bytes 262144 | tf_op jit(solution)/shard_map/all_to_all | solution.py:23
  90.3 2.8 %cg_step.5 = (f32[8,128]{1,0:T(8,128)S(1)}, f32[8,128]{1,0:T(8,128)S(1)}, f32[8,32]{1,0:T(8,128)S(1)}, f32[8,32]{1,0:T(8,128)S(1)}) custom-call(f32[16,8,256]{2,1,0:T(8,128)S(1)} %all_to_all.38.refs_0_, bf16[256,4096]{1,0:T(8,128)(2,1)S(1)} %get-tuple-element.24.upper_ref.refs_1_, bf16[256,4096]{1,0:T(8,128)(2,1)S(1)} %copy-done.2, ...), custom_call_target="tpu_custom_call" | custom-call | tf_op jit(solution)/shard_map/cg_step/pallas_call | solution.py:176
  93.1 9.7 %all_to_all.39 = f32[16,8,128]{2,1,0:T(8,128)S(1)} all-to-all(f32[16,8,128]{2,1,0:T(8,128)S(1)} %broadcast_in_dim.17), channel_id=1, replica_groups=mesh['groups'=2,'dp'=4,'tensor'=4] {'dp','tensor'}, dimensions={0} | all-to-all | bytes 131072 | tf_op jit(solution)/shard_map/all_to_all | solution.py:23
  103.0 0.7 multiply_add_fusion
  (18 shorter events, 0.4 us)
Async XLA Ops:
  0.0 1.2 %copy-start = (bf16[64,8192]{1,0:T(8,128)(2,1)S(1)}, bf16[64,8192]{1,0:T(8,128)(2,1)}, u32[]{:S(2)}) copy-start(bf16[64,8192]{1,0:T(8,128)(2,1)} %param.7) | copy-start | bytes 3145732
  0.0 14.4 %copy-start.5 = (bf16[64,7168]{1,0:T(8,128)(2,1)S(1)}, bf16[64,7168]{1,0:T(8,128)(2,1)}, u32[]{:S(2)}) copy-start(bf16[64,7168]{1,0:T(8,128)(2,1)} %param.9) | copy-start | bytes 2752516
  8.1 20.8 %all-to-all-start = ((f32[4,64,512]{2,1,0:T(8,128)}), f32[4,64,512]{2,1,0:T(8,128)S(1)}, u32[]{:S(2)}, u32[]{:S(2)}) async-start(f32[4,64,512]{2,1,0:T(8,128)} %broadcast_in_dim.12), calls=%async_computation | async-start | bytes 1048576 | tf_op jit(solution)/shard_map/all_to_all | solution.py:23
  40.7 10.8 %all-to-all-start.2 = ((f32[16,2,1024]{2,1,0:T(2,128)}), f32[16,2,1024]{2,1,0:T(2,128)S(1)}, u32[]{:S(2)}, u32[]{:S(2)}) async-start(f32[16,2,1024]{2,1,0:T(2,128)} %broadcast_in_dim.13), calls=%async_computation.2 | async-start | bytes 262144 | tf_op jit(solution)/shard_map/all_to_all | solution.py:23
  44.3 2.2 %copy-start.3 = (f32[256,4096]{1,0:T(8,128)S(1)}, f32[256,4096]{1,0:T(8,128)}, u32[]{:S(2)}) copy-start(f32[256,4096]{1,0:T(8,128)} %prior_ref.1) | copy-start | bytes 12582916
  46.4 43.9 %copy-start.4 = (bf16[32,4096]{1,0:T(8,128)(2,1)S(1)}, bf16[32,4096]{1,0:T(8,128)(2,1)}, u32[]{:S(2)}) copy-start(bf16[32,4096]{1,0:T(8,128)(2,1)} %refs_8_.1) | copy-start | bytes 786436
  47.8 1.4 %copy-start.1 = (bf16[256,4096]{1,0:T(8,128)(2,1)}, bf16[256,4096]{1,0:T(8,128)(2,1)S(1)}, u32[]{:S(2)}) copy-start(bf16[256,4096]{1,0:T(8,128)(2,1)S(1)} %get-tuple-element.25.lower_ref.refs_2_) | copy-start | bytes 6291460
  51.6 1.6 %copy-start.2 = (bf16[256,4096]{1,0:T(8,128)(2,1)S(1)}, bf16[256,4096]{1,0:T(8,128)(2,1)}, u32[]{:S(2)}) copy-start(bf16[256,4096]{1,0:T(8,128)(2,1)} %copy-done.1) | copy-start | bytes 6291460

commit v4 on v3

--- a/solution.py
+++ b/solution.py
@@ -19,8 +19,34 @@
 F32 = functools.partial(jax.ShapeDtypeStruct, dtype=jnp.float32)
 
 
+def swap(value, axis, size, bit):
+    return lax.ppermute(value, axis, [(i, i ^ bit) for i in range(size)])
+
+
+def bits(size):
+    return [1 << b for b in reversed(range(size.bit_length() - 1))]
+
+
 def gather(value, axes, size):
     return lax.all_to_all(jnp.broadcast_to(value[None], (size,) + value.shape), axes, 0, 0)
+
+
+def sum_over(value, axis, size):
+    for bit in bits(size):
+        value = value + swap(value, axis, size, bit)
+    return value
+
+
+def doubled(value, axis, size):
+    held, order = value[None], [0]
+    for bit in bits(size):
+        held = jnp.concatenate([held, swap(held, axis, size, bit)], axis=0)
+        order = order + [k ^ bit for k in order]
+    return held, tuple(order)
+
+
+def direct(value, axis, size):
+    return [value] + [swap(value, axis, size, k) for k in reversed(range(1, size))][::-1]
 
 
 def dot_nt(a, b):
@@ -99,32 +125,48 @@
     return lax.axis_index("dp") * tensor_size + lax.axis_index("tensor")
 
 
-def start_kernel(tensor_size, pieces_ref, upper_ref, lower_ref, vectors_ref, applied_ref, norm_ref):
-    count, seqs, columns = pieces_ref.shape
-    for i in range(count):
-        dp, tensor = i // tensor_size, i % tensor_size
-        vectors_ref[dp * seqs : (dp + 1) * seqs, tensor * columns : (tensor + 1) * columns] = pieces_ref[i]
-    vectors = vectors_ref[...]
+def start_kernel(size, tensor_size, *refs):
+    pieces, (upper_ref, lower_ref, vectors_ref, applied_ref, norm_ref, held) = refs[:size], refs[size:]
+    dp = lax.axis_index("dp")
+    for k, piece in enumerate(pieces):
+        held[dp ^ k] = piece[...]
+    vectors = jnp.concatenate([held[k] for k in range(size)], axis=0)
+    vectors_ref[...] = vectors
     norm_ref[...] = jnp.broadcast_to(row_sum(vectors * vectors), norm_ref.shape)
     applied_ref[...] = apply_fisher(vectors, vectors_ref, upper_ref, lower_ref, flat_index(tensor_size))
 
 
 def start_cg(pieces, prior_pieces, tensor_size):
-    seqs = pieces.shape[0] // tensor_size * pieces.shape[1]
+    size, seqs = len(pieces), len(pieces) * pieces[0].shape[0]
     rows, width = prior_pieces[0].shape
     return pl.pallas_call(
-        functools.partial(start_kernel, tensor_size),
+        functools.partial(start_kernel, size, tensor_size),
         out_shape=(F32((seqs, width)), F32((seqs, rows)), F32((seqs, LANES))),
-        in_specs=[VMEM_SPEC] * 3,
+        in_specs=[VMEM_SPEC] * (size + 2),
         out_specs=(VMEM_SPEC,) * 3,
+        scratch_shapes=[pltpu.VMEM((size,) + pieces[0].shape, jnp.float32)],
         compiler_params=PARAMS,
         name="cg_start",
-    )(pieces, *prior_pieces)
-
-
-def step_kernel(tensor_size, first, last, *refs):
-    blocks_ref, upper_ref, lower_ref, vectors_ref, norm_ref = refs[:5]
-    refs = refs[5:]
+    )(*pieces, *prior_pieces)
+
+
+def place_blocks(blocks, order, tensor_size, held):
+    rows = blocks[0].shape[2]
+    if rows % LANES:
+        for i in range(blocks[0].shape[0]):
+            held[:, i * rows : (i + 1) * rows] = blocks[0][i]
+        return
+    dp, tensor = lax.axis_index("dp"), lax.axis_index("tensor")
+    for k, block in enumerate(blocks):
+        for i, j in enumerate(order):
+            start = ((dp ^ k) * tensor_size + (tensor ^ j)) * rows
+            held[:, pl.ds(pl.multiple_of(start, LANES), rows)] = block[i]
+
+
+def step_kernel(size, order, tensor_size, first, last, *refs):
+    blocks, refs = refs[:size], refs[size:]
+    upper_ref, lower_ref, vectors_ref, norm_ref = refs[:4]
+    refs = refs[4:]
     if not first:
         direction_ref, residual_ref, solution_ref = refs[:3]
         refs = refs[3:]
@@ -133,9 +175,7 @@
     else:
         applied_out, norm_out, direction_out, residual_out, solution_out, held = refs
     me = flat_index(tensor_size)
-    count, _, rows = blocks_ref.shape
-    for i in range(count):
-        held[:, i * rows : (i + 1) * rows] = blocks_ref[i]
+    place_blocks(blocks, order, tensor_size, held)
     applied = held[...]
     direction = vectors_ref[...] if first else direction_ref[...]
     residual = direction if first else residual_ref[...]
@@ -151,7 +191,7 @@
     applied_rows = apply_fisher(direction, vectors_ref, upper_ref, lower_ref, me)
     if last:
         held[...] = direction
-        own = own_columns(held, me, rows)
+        own = own_columns(held, me, applied_rows.shape[1])
         curvature_out[...] = jnp.broadcast_to(row_sum(own * applied_rows), curvature_out.shape)
         queries = queries_ref[...].astype(jnp.float32)
         solved_out[...] = dot_nt(solution, queries)
@@ -163,18 +203,19 @@
         solution_out[...] = solution
 
 
-def step_cg(blocks, prior_pieces, vectors, norm, state, queries, tensor_size):
+def step_cg(gathered, prior_pieces, vectors, norm, state, queries, tensor_size):
     first, last = state is None, queries is not None
+    blocks, order = gathered
     whole, column = F32(vectors.shape), F32(norm.shape)
     seqs = vectors.shape[0]
-    operands = [blocks, *prior_pieces, vectors, norm, *(state or ())] + ([queries] if last else [])
+    operands = [*blocks, *prior_pieces, vectors, norm, *(state or ())] + ([queries] if last else [])
     if last:
         scores = F32((seqs, queries.shape[0]))
         out_shape = (column, column, scores, scores)
     else:
-        out_shape = (F32((seqs, blocks.shape[2])), column, whole, whole, whole)
-    return pl.pallas_call(
-        functools.partial(step_kernel, tensor_size, first, last),
+        out_shape = (F32((seqs, prior_pieces[0].shape[0])), column, whole, whole, whole)
+    return pl.pallas_call(
+        functools.partial(step_kernel, len(blocks), order, tensor_size, first, last),
         out_shape=out_shape,
         in_specs=[VMEM_SPEC] * len(operands),
         out_specs=(VMEM_SPEC,) * len(out_shape),
@@ -190,18 +231,24 @@
     in_local = lax.dot_general(in_proj, inputs, NT, preferred_element_type=jnp.float32)
     in_all = gather(in_local, "tensor", tensor_size)
     out_local = lax.dot_general(out_proj, out_grads, NT, preferred_element_type=jnp.float32)
-    partial = partial_vectors(in_all, out_local).reshape(-1, tensor_size, width // tensor_size)
-    partial = lax.all_to_all(partial.transpose(1, 0, 2), "tensor", 0, 0)
-    pieces = gather(jnp.sum(partial, axis=0), both, devices)
+    partial = partial_vectors(in_all, out_local).reshape(-1, width)
+    pieces = direct(sum_over(partial, "tensor", tensor_size), "dp", dp_size)
     prior_pieces = split_prior(prior)
+
+    def gather_rows(values):
+        if values.shape[1] % LANES:
+            return [gather(values, both, devices)], None
+        held, order = doubled(values, "tensor", tensor_size)
+        return direct(held, "dp", dp_size), order
+
     vectors, applied_rows, norm = start_cg(pieces, prior_pieces, tensor_size)
     state = None
     for iteration in range(1, ITERS - 1):
-        blocks = gather(applied_rows, both, devices)
-        applied_rows, norm, *state = step_cg(blocks, prior_pieces, vectors, norm, state, None, tensor_size)
-    blocks = gather(applied_rows, both, devices)
-    curvature, norm, solved, along = step_cg(blocks, prior_pieces, vectors, norm, state, queries, tensor_size)
-    curvature = jnp.sum(gather(curvature, both, devices), axis=0)
+        gathered = gather_rows(applied_rows)
+        applied_rows, norm, *state = step_cg(gathered, prior_pieces, vectors, norm, state, None, tensor_size)
+    gathered = gather_rows(applied_rows)
+    curvature, norm, solved, along = step_cg(gathered, prior_pieces, vectors, norm, state, queries, tensor_size)
+    curvature = sum_over(sum_over(curvature, "tensor", tensor_size), "dp", dp_size)
     return solved + (norm / curvature)[:, :1] * along
 
 

time: 104 us -> 104 us (level)
  blocking collectives: 51.6 us -> 0 us
  starting transfers between devices: 9.83 us -> 38.8 us
  waiting for transfers between devices: 2.53 us -> 28.5 us
  local copies, waits for them, and re-layouts: 8.24 us -> 4.5 us
    all_to_all x5 -> x0, blocking collectives: 51.6 us -> none  [the longest x4 41.2 us: gather(): lax.all_to_all(jnp.broadcast_to(value[None], (size,) + value.shape), axes...]
    ppermute x0 -> x24, starting transfers between devices: none -> 32.5 us  [swap(): return lax.ppermute(value, axis, [(i, i ^ bit) for i in range(size)])]
    ppermute x0 -> x24, waiting for transfers between devices: none -> 28.3 us  [swap(): return lax.ppermute(value, axis, [(i, i ^ bit) for i in range(size)])]
    all_to_all x2 -> x1, starting transfers between devices: 9.83 us -> 6.32 us  [gather(): lax.all_to_all(jnp.broadcast_to(value[None], (size,) + value.shape), axes...]
    unnamed x12 -> x8, local copies, waits for them, and re-layouts: 6.35 us -> 3.42 us
    all_to_all x2 -> x1, waiting for transfers between devices: 2.53 us -> 0.17 us  [gather(): lax.all_to_all(jnp.broadcast_to(value[None], (size,) + value.shape), axes...]
  transfers between devices with their start and end apart: 2 -> 25, of which waited for: 2 -> 19; matrix products, arithmetic and copies ran while one was open for 14% -> 14% of each run, Pallas kernels for 1% -> 1%
where the time goes in v4:
time: 104 us; the launch traced here: 103 us
  starting transfers between devices  38.8 us (37%)
  waiting for transfers between devices  28.5 us (27%)
  matrix products  20.3 us (20%)
  Pallas kernels  10.4 us (10%)
  local copies, waits for them, and re-layouts  4.5 us (4%)
    ppermute x24, starting transfers between devices, swap(): return lax.ppermute(value, axis, [(i, i ^ bit) for i in range(size)])  32.5 us
    ppermute x24, waiting for transfers between devices, swap(): return lax.ppermute(value, axis, [(i, i ^ bit) for i in range(size)])  28.3 us
    dot_general x1, matrix products, on_device(): lax.dot_general(out_proj, out_grads, NT, preferred_element_type=jnp.float32)  14.3 us
    pallas_call x3, Pallas kernels, step_cg(): pl.pallas_call(functools.partial(step_kernel, len(blocks), order, tensor_...  6.82 us
    all_to_all x1, starting transfers between devices, gather(): lax.all_to_all(jnp.broadcast_to(value[None], (size,) + value.shape), axes...  6.32 us
    dot_general x1, matrix products, on_device(): lax.dot_general(in_proj, inputs, NT, preferred_element_type=jnp.float32)  6.04 us
    unnamed x8, local copies, waits for them, and re-layouts  3.42 us
  transfers between devices with their start and end apart: 25, of which 19 were waited for; matrix products, arithmetic and copies ran while one was open for 14% of the time, Pallas kernels for 1%

profile of v4, /device:TPU:0, one launch (start us, length us, event | category | flops | bytes accessed | tf_op | source)
XLA Modules:
  0.0 103.4 jit_solution(9567625402425045197)
XLA Ops:
  1.2 6.0 %fusion = f32[64,512]{1,0:T(8,128)S(1)} fusion(bf16[64,8192]{1,0:T(8,128)(2,1)S(1)} %copy-done, bf16[512,8192]{1,0:T(8,128)(2,1)} %param.6), kind=kOutput, calls=%fused_computation.9 | convolution fusion | flops 536870912 | bytes 9568256 | tf_op jit(solution)/shard_map/dot_general | solution.py:231
  8.1 6.3 %all-to-all-start = ((f32[4,64,512]{2,1,0:T(8,128)}), f32[4,64,512]{2,1,0:T(8,128)S(1)}, u32[]{:S(2)}, u32[]{:S(2)}) async-start(f32[4,64,512]{2,1,0:T(8,128)} %broadcast_in_dim.15), calls=%async_computation | async-start | bytes 1048576 | tf_op jit(solution)/shard_map/all_to_all | solution.py:31
  14.5 14.3 %fusion.1.out_ref = f32[64,2048]{1,0:T(8,128)S(1)} fusion(bf16[64,7168]{1,0:T(8,128)(2,1)S(1)} %copy-done.3, bf16[2048,7168]{1,0:T(8,128)(2,1)} %param.8), kind=kOutput, calls=%fused_computation.10 | convolution fusion | flops 1879048192 | bytes 30801920 | tf_op jit(solution)/shard_map/dot_general | solution.py:233
  29.6 2.8 %collective-permute-start = (f32[2,4096]{1,0:T(2,128)S(1)}, f32[2,4096]{1,0:T(2,128)S(1)}, u32[]{:S(2)}, u32[]{:S(2)}) collective-permute-start(f32[2,4096]{1,0:T(2,128)S(1)} %reshape.4), channel_id=1, source_target_pairs={{0,2},{1,3},{2,0},{3,1},{4,6},{5,7},{6,4},{7,5},{8,10},{9,11},{10,... | collective-permute-start | bytes 98312 | tf_op jit(solution)/shard_map/ppermute | solution.py:23
  32.4 2.1 %collective-permute-done = f32[2,4096]{1,0:T(2,128)S(1)} collective-permute-done((f32[2,4096]{1,0:T(2,128)S(1)}, f32[2,4096]{1,0:T(2,128)S(1)}, u32[]{:S(2)}, u32[]{:S(2)}) %collective-permute-start) | collective-permute-done | bytes 32800 | tf_op jit(solution)/shard_map/ppermute | solution.py:23
  34.5 1.9 %collective-permute-start.1 = (f32[2,4096]{1,0:T(2,128)S(1)}, f32[2,4096]{1,0:T(2,128)S(1)}, u32[]{:S(2)}, u32[]{:S(2)}) collective-permute-start(f32[2,4096]{1,0:T(2,128)S(1)} %add.21), channel_id=1, source_target_pairs={{0,1},{1,0},{2,3},{3,2},{4,5},{5,4},{6,7},{7,6},{8,9},{9,8},{10,11... | collective-permute-start | bytes 98312 | tf_op jit(solution)/shard_map/ppermute | solution.py:23
  36.5 2.1 %collective-permute-done.1 = f32[2,4096]{1,0:T(2,128)S(1)} collective-permute-done((f32[2,4096]{1,0:T(2,128)S(1)}, f32[2,4096]{1,0:T(2,128)S(1)}, u32[]{:S(2)}, u32[]{:S(2)}) %collective-permute-start.1) | collective-permute-done | bytes 32800 | tf_op jit(solution)/shard_map/ppermute | solution.py:23
  40.5 2.2 %copy-done.1 = f32[256,4096]{1,0:T(8,128)S(1)} copy-done((f32[256,4096]{1,0:T(8,128)S(1)}, f32[256,4096]{1,0:T(8,128)}, u32[]{:S(2)}) %copy-start.1) | copy-done | bytes 4194328
  45.7 2.8 %collective-permute-start.5 = (f32[1,8,256]{2,1,0:T(8,128)S(1)}, f32[1,8,256]{2,1,0:T(8,128)S(1)}, u32[]{:S(2)}, u32[]{:S(2)}) collective-permute-start(f32[1,8,256]{2,1,0:T(8,128)S(1)} %bitcast.13), channel_id=1, source_target_pairs={{0,2},{1,3},{2,0},{3,1},{4,6},{5,7},{6,4},{7,5},{8,10},{9,11},{10,... | collective-permute-start | bytes 24584 | tf_op jit(solution)/shard_map/ppermute | solution.py:23
  50.3 1.9 %collective-permute-start.6 = (f32[2,8,256]{2,1,0:T(8,128)S(1)}, f32[2,8,256]{2,1,0:T(8,128)S(1)}, u32[]{:S(2)}, u32[]{:S(2)}) collective-permute-start(f32[2,8,256]{2,1,0:T(8,128)S(1)} %pad_maximum_fusion.3), channel_id=1, source_target_pairs={{0,1},{1,0},{2,3},{3,2},{4,5},{5,4},{6,7},{7,6},{8,9},{9,8},{10,11... | collective-permute-start | bytes 49160 | tf_op jit(solution)/shard_map/ppermute | solution.py:23
  52.1 1.9 %collective-permute-done.6 = f32[2,8,256]{2,1,0:T(8,128)S(1)} collective-permute-done((f32[2,8,256]{2,1,0:T(8,128)S(1)}, f32[2,8,256]{2,1,0:T(8,128)S(1)}, u32[]{:S(2)}, u32[]{:S(2)}) %collective-permute-start.6) | collective-permute-done | bytes 16416 | tf_op jit(solution)/shard_map/ppermute | solution.py:23
  55.9 1.8 %collective-permute-done.9.refs_3_ = f32[4,8,256]{2,1,0:T(8,128)S(1)} collective-permute-done((f32[4,8,256]{2,1,0:T(8,128)S(1)}, f32[4,8,256]{2,1,0:T(8,128)S(1)}, u32[]{:S(2)}, u32[]{:S(2)}) %collective-permute-start.9) | collective-permute-done | bytes 32800 | tf_op jit(solution)/shard_map/ppermute | solution.py:23
  58.1 2.0 %cg_step.3 = (f32[8,256]{1,0:T(8,128)S(1)}, f32[8,128]{1,0:T(8,128)S(1)}, f32[8,4096]{1,0:T(8,128)S(1)}, f32[8,4096]{1,0:T(8,128)S(1)}, f32[8,4096]{1,0:T(8,128)S(1)}) custom-call(f32[4,8,256]{2,1,0:T(8,128)S(1)} %pad_maximum_fusion.refs_0_, f32[4,8,256]{2,1,0:T(8,128)S(1)} %collective-permute-done.7.refs_1_, ...), custom_call_target="tpu_custom_call" | custom-call | tf_op jit(solution)/shard_map/cg_step/pallas_call | solution.py:217
  60.1 2.8 %collective-permute-start.10 = (f32[1,8,256]{2,1,0:T(8,128)S(1)}, f32[1,8,256]{2,1,0:T(8,128)S(1)}, u32[]{:S(2)}, u32[]{:S(2)}) collective-permute-start(f32[1,8,256]{2,1,0:T(8,128)S(1)} %bitcast.10), channel_id=1, source_target_pairs={{0,2},{1,3},{2,0},{3,1},{4,6},{5,7},{6,4},{7,5},{8,10},{9,11},{10,... | collective-permute-start | bytes 24584 | tf_op jit(solution)/shard_map/ppermute | solution.py:23
  64.6 1.9 %collective-permute-start.11 = (f32[2,8,256]{2,1,0:T(8,128)S(1)}, f32[2,8,256]{2,1,0:T(8,128)S(1)}, u32[]{:S(2)}, u32[]{:S(2)}) collective-permute-start(f32[2,8,256]{2,1,0:T(8,128)S(1)} %pad_maximum_fusion.4), channel_id=1, source_target_pairs={{0,1},{1,0},{2,3},{3,2},{4,5},{5,4},{6,7},{7,6},{8,9},{9,8},{10,11... | collective-permute-start | bytes 49160 | tf_op jit(solution)/shard_map/ppermute | solution.py:23
  66.5 1.9 %collective-permute-done.11 = f32[2,8,256]{2,1,0:T(8,128)S(1)} collective-permute-done((f32[2,8,256]{2,1,0:T(8,128)S(1)}, f32[2,8,256]{2,1,0:T(8,128)S(1)}, u32[]{:S(2)}, u32[]{:S(2)}) %collective-permute-start.11) | collective-permute-done | bytes 16416 | tf_op jit(solution)/shard_map/ppermute | solution.py:23
  72.4 2.0 %cg_step.4 = (f32[8,256]{1,0:T(8,128)S(1)}, f32[8,128]{1,0:T(8,128)S(1)}, f32[8,4096]{1,0:T(8,128)S(1)}, f32[8,4096]{1,0:T(8,128)S(1)}, f32[8,4096]{1,0:T(8,128)S(1)}) custom-call(f32[4,8,256]{2,1,0:T(8,128)S(1)} %pad_maximum_fusion.1.refs_0_, f32[4,8,256]{2,1,0:T(8,128)S(1)} %collective-permute-done.12.refs_1_, ...), custom_call_target="tpu_custom_call" | custom-call | tf_op jit(solution)/shard_map/cg_step/pallas_call | solution.py:217
  74.4 2.8 %collective-permute-start.15 = (f32[1,8,256]{2,1,0:T(8,128)S(1)}, f32[1,8,256]{2,1,0:T(8,128)S(1)}, u32[]{:S(2)}, u32[]{:S(2)}) collective-permute-start(f32[1,8,256]{2,1,0:T(8,128)S(1)} %bitcast.7), channel_id=1, source_target_pairs={{0,2},{1,3},{2,0},{3,1},{4,6},{5,7},{6,4},{7,5},{8,10},{9,11},{10,... | collective-permute-start | bytes 24584 | tf_op jit(solution)/shard_map/ppermute | solution.py:23
  79.0 1.9 %collective-permute-start.16 = (f32[2,8,256]{2,1,0:T(8,128)S(1)}, f32[2,8,256]{2,1,0:T(8,128)S(1)}, u32[]{:S(2)}, u32[]{:S(2)}) collective-permute-start(f32[2,8,256]{2,1,0:T(8,128)S(1)} %pad_maximum_fusion.5), channel_id=1, source_target_pairs={{0,1},{1,0},{2,3},{3,2},{4,5},{5,4},{6,7},{7,6},{8,9},{9,8},{10,11... | collective-permute-start | bytes 49160 | tf_op jit(solution)/shard_map/ppermute | solution.py:23
  80.9 1.9 %collective-permute-done.16 = f32[2,8,256]{2,1,0:T(8,128)S(1)} collective-permute-done((f32[2,8,256]{2,1,0:T(8,128)S(1)}, f32[2,8,256]{2,1,0:T(8,128)S(1)}, u32[]{:S(2)}, u32[]{:S(2)}) %collective-permute-start.16) | collective-permute-done | bytes 16416 | tf_op jit(solution)/shard_map/ppermute | solution.py:23
  86.8 2.8 %cg_step.5 = (f32[8,128]{1,0:T(8,128)S(1)}, f32[8,128]{1,0:T(8,128)S(1)}, f32[8,32]{1,0:T(8,128)S(1)}, f32[8,32]{1,0:T(8,128)S(1)}) custom-call(f32[4,8,256]{2,1,0:T(8,128)S(1)} %pad_maximum_fusion.2.refs_0_, f32[4,8,256]{2,1,0:T(8,128)S(1)} %collective-permute-done.17.refs_1_, f32[4,8,256]{2,1,0:T(8,128)S(1)} %collective-permute-done.18.refs_2_, ...), custom_call_target="tpu_custom_call" | custom-call | tf_op jit(solution)/shard_map/cg_step/pallas_call | solution.py:217
  89.6 2.8 %collective-permute-start.20 = (f32[8,128]{1,0:T(8,128)S(1)}, f32[8,128]{1,0:T(8,128)S(1)}, u32[]{:S(2)}, u32[]{:S(2)}) collective-permute-start(f32[8,128]{1,0:T(8,128)S(1)} %get-tuple-element.41), channel_id=1, source_target_pairs={{0,2},{1,3},{2,0},{3,1},{4,6},{5,7},{6,4},{7,5},{8,10},{9,11},{10,... | collective-permute-start | bytes 12296 | tf_op jit(solution)/shard_map/ppermute | solution.py:23
  94.2 1.9 %collective-permute-start.21 = (f32[8,128]{1,0:T(8,128)S(1)}, f32[8,128]{1,0:T(8,128)S(1)}, u32[]{:S(2)}, u32[]{:S(2)}) collective-permute-start(f32[8,128]{1,0:T(8,128)S(1)} %add.23), channel_id=1, source_target_pairs={{0,1},{1,0},{2,3},{3,2},{4,5},{5,4},{6,7},{7,6},{8,9},{9,8},{10,11... | collective-permute-start | bytes 12296 | tf_op jit(solution)/shard_map/ppermute | solution.py:23
  99.3 2.1 %collective-permute-done.22 = f32[8,128]{1,0:T(8,128)S(1)} collective-permute-done((f32[8,128]{1,0:T(8,128)S(1)}, f32[8,128]{1,0:T(8,128)S(1)}, u32[]{:S(2)}, u32[]{:S(2)}) %collective-permute-start.22) | collective-permute-done | bytes 4128 | tf_op jit(solution)/shard_map/ppermute | solution.py:23
  (58 shorter events, 30.5 us)
Async XLA Ops:
  8.1 20.8 %all-to-all-start = ((f32[4,64,512]{2,1,0:T(8,128)}), f32[4,64,512]{2,1,0:T(8,128)S(1)}, u32[]{:S(2)}, u32[]{:S(2)}) async-start(f32[4,64,512]{2,1,0:T(8,128)} %broadcast_in_dim.15), calls=%async_computation | async-start | bytes 1048576 | tf_op jit(solution)/shard_map/all_to_all | solution.py:31
  29.6 4.9 %collective-permute-start = (f32[2,4096]{1,0:T(2,128)S(1)}, f32[2,4096]{1,0:T(2,128)S(1)}, u32[]{:S(2)}, u32[]{:S(2)}) collective-permute-start(f32[2,4096]{1,0:T(2,128)S(1)} %reshape.4), channel_id=1, source_target_pairs={{0,2},{1,3},{2,0},{3,1},{4,6},{5,7},{6,4},{7,5},{8,10},{9,11},{10,... | collective-permute-start | bytes 98312 | tf_op jit(solution)/shard_map/ppermute | solution.py:23
  34.5 4.0 %collective-permute-start.1 = (f32[2,4096]{1,0:T(2,128)S(1)}, f32[2,4096]{1,0:T(2,128)S(1)}, u32[]{:S(2)}, u32[]{:S(2)}) collective-permute-start(f32[2,4096]{1,0:T(2,128)S(1)} %add.21), channel_id=1, source_target_pairs={{0,1},{1,0},{2,3},{3,2},{4,5},{5,4},{6,7},{7,6},{8,9},{9,8},{10,11... | collective-permute-start | bytes 98312 | tf_op jit(solution)/shard_map/ppermute | solution.py:23
  38.5 5.5 %collective-permute-start.4 = (f32[2,4096]{1,0:T(2,128)S(1)}, f32[2,4096]{1,0:T(2,128)S(1)}, u32[]{:S(2)}, u32[]{:S(2)}) collective-permute-start(f32[2,4096]{1,0:T(2,128)S(1)} %add.22.refs_0_), channel_id=1, source_target_pairs={{0,12},{4,8},{8,4},{12,0},{1,13},{5,9},{9,5},{13,1},{2,14},{6,10},... | collective-permute-start | bytes 98312 | tf_op jit(solution)/shard_map/ppermute | solution.py:23
  38.6 5.5 %collective-permute-start.3 = (f32[2,4096]{1,0:T(2,128)S(1)}, f32[2,4096]{1,0:T(2,128)S(1)}, u32[]{:S(2)}, u32[]{:S(2)}) collective-permute-start(f32[2,4096]{1,0:T(2,128)S(1)} %add.22.refs_0_), channel_id=1, source_target_pairs={{0,8},{4,12},{8,0},{12,4},{1,9},{5,13},{9,1},{13,5},{2,10},{6,14},... | collective-permute-start | bytes 98312 | tf_op jit(solution)/shard_map/ppermute | solution.py:23
  40.2 3.9 %collective-permute-start.2 = (f32[2,4096]{1,0:T(2,128)S(1)}, f32[2,4096]{1,0:T(2,128)S(1)}, u32[]{:S(2)}, u32[]{:S(2)}) collective-permute-start(f32[2,4096]{1,0:T(2,128)S(1)} %add.22.refs_0_), channel_id=1, source_target_pairs={{0,4},{4,0},{8,12},{12,8},{1,5},{5,1},{9,13},{13,9},{2,6},{6,2},{1... | collective-permute-start | bytes 98312 | tf_op jit(solution)/shard_map/ppermute | solution.py:23
  45.7 4.6 %collective-permute-start.5 = (f32[1,8,256]{2,1,0:T(8,128)S(1)}, f32[1,8,256]{2,1,0:T(8,128)S(1)}, u32[]{:S(2)}, u32[]{:S(2)}) collective-permute-start(f32[1,8,256]{2,1,0:T(8,128)S(1)} %bitcast.13), channel_id=1, source_target_pairs={{0,2},{1,3},{2,0},{3,1},{4,6},{5,7},{6,4},{7,5},{8,10},{9,11},{10,... | collective-permute-start | bytes 24584 | tf_op jit(solution)/shard_map/ppermute | solution.py:23
  50.3 3.7 %collective-permute-start.6 = (f32[2,8,256]{2,1,0:T(8,128)S(1)}, f32[2,8,256]{2,1,0:T(8,128)S(1)}, u32[]{:S(2)}, u32[]{:S(2)}) collective-permute-start(f32[2,8,256]{2,1,0:T(8,128)S(1)} %pad_maximum_fusion.3), channel_id=1, source_target_pairs={{0,1},{1,0},{2,3},{3,2},{4,5},{5,4},{6,7},{7,6},{8,9},{9,8},{10,11... | collective-permute-start | bytes 49160 | tf_op jit(solution)/shard_map/ppermute | solution.py:23
  54.0 3.6 %collective-permute-start.9 = (f32[4,8,256]{2,1,0:T(8,128)S(1)}, f32[4,8,256]{2,1,0:T(8,128)S(1)}, u32[]{:S(2)}, u32[]{:S(2)}) collective-permute-start(f32[4,8,256]{2,1,0:T(8,128)S(1)} %pad_maximum_fusion.refs_0_), channel_id=1, source_target_pairs={{0,12},{4,8},{8,4},{12,0},{1,13},{5,9},{9,5},{13,1},{2,14},{6,10},... | collective-permute-start | bytes 98312 | tf_op jit(solution)/shard_map/ppermute | solution.py:23
  54.0 4.0 %collective-permute-start.8 = (f32[4,8,256]{2,1,0:T(8,128)S(1)}, f32[4,8,256]{2,1,0:T(8,128)S(1)}, u32[]{:S(2)}, u32[]{:S(2)}) collective-permute-start(f32[4,8,256]{2,1,0:T(8,128)S(1)} %pad_maximum_fusion.refs_0_), channel_id=1, source_target_pairs={{0,8},{4,12},{8,0},{12,4},{1,9},{5,13},{9,1},{13,5},{2,10},{6,14},... | collective-permute-start | bytes 98312 | tf_op jit(solution)/shard_map/ppermute | solution.py:23
  55.5 2.5 %collective-permute-start.7 = (f32[4,8,256]{2,1,0:T(8,128)S(1)}, f32[4,8,256]{2,1,0:T(8,128)S(1)}, u32[]{:S(2)}, u32[]{:S(2)}) collective-permute-start(f32[4,8,256]{2,1,0:T(8,128)S(1)} %pad_maximum_fusion.refs_0_), channel_id=1, source_target_pairs={{0,4},{4,0},{8,12},{12,8},{1,5},{5,1},{9,13},{13,9},{2,6},{6,2},{1... | collective-permute-start | bytes 98312 | tf_op jit(solution)/shard_map/ppermute | solution.py:23
  60.1 4.6 %collective-permute-start.10 = (f32[1,8,256]{2,1,0:T(8,128)S(1)}, f32[1,8,256]{2,1,0:T(8,128)S(1)}, u32[]{:S(2)}, u32[]{:S(2)}) collective-permute-start(f32[1,8,256]{2,1,0:T(8,128)S(1)} %bitcast.10), channel_id=1, source_target_pairs={{0,2},{1,3},{2,0},{3,1},{4,6},{5,7},{6,4},{7,5},{8,10},{9,11},{10,... | collective-permute-start | bytes 24584 | tf_op jit(solution)/shard_map/ppermute | solution.py:23
  64.6 3.7 %collective-permute-start.11 = (f32[2,8,256]{2,1,0:T(8,128)S(1)}, f32[2,8,256]{2,1,0:T(8,128)S(1)}, u32[]{:S(2)}, u32[]{:S(2)}) collective-permute-start(f32[2,8,256]{2,1,0:T(8,128)S(1)} %pad_maximum_fusion.4), channel_id=1, source_target_pairs={{0,1},{1,0},{2,3},{3,2},{4,5},{5,4},{6,7},{7,6},{8,9},{9,8},{10,11... | collective-permute-start | bytes 49160 | tf_op jit(solution)/shard_map/ppermute | solution.py:23
  68.4 3.6 %collective-permute-start.14 = (f32[4,8,256]{2,1,0:T(8,128)S(1)}, f32[4,8,256]{2,1,0:T(8,128)S(1)}, u32[]{:S(2)}, u32[]{:S(2)}) collective-permute-start(f32[4,8,256]{2,1,0:T(8,128)S(1)} %pad_maximum_fusion.1.refs_0_), channel_id=1, source_target_pairs={{0,12},{4,8},{8,4},{12,0},{1,13},{5,9},{9,5},{13,1},{2,14},{6,10},... | collective-permute-start | bytes 98312 | tf_op jit(solution)/shard_map/ppermute | solution.py:23
  68.4 4.0 %collective-permute-start.13 = (f32[4,8,256]{2,1,0:T(8,128)S(1)}, f32[4,8,256]{2,1,0:T(8,128)S(1)}, u32[]{:S(2)}, u32[]{:S(2)}) collective-permute-start(f32[4,8,256]{2,1,0:T(8,128)S(1)} %pad_maximum_fusion.1.refs_0_), channel_id=1, source_target_pairs={{0,8},{4,12},{8,0},{12,4},{1,9},{5,13},{9,1},{13,5},{2,10},{6,14},... | collective-permute-start | bytes 98312 | tf_op jit(solution)/shard_map/ppermute | solution.py:23
  69.9 2.5 %collective-permute-start.12 = (f32[4,8,256]{2,1,0:T(8,128)S(1)}, f32[4,8,256]{2,1,0:T(8,128)S(1)}, u32[]{:S(2)}, u32[]{:S(2)}) collective-permute-start(f32[4,8,256]{2,1,0:T(8,128)S(1)} %pad_maximum_fusion.1.refs_0_), channel_id=1, source_target_pairs={{0,4},{4,0},{8,12},{12,8},{1,5},{5,1},{9,13},{13,9},{2,6},{6,2},{1... | collective-permute-start | bytes 98312 | tf_op jit(solution)/shard_map/ppermute | solution.py:23
  74.4 4.6 %collective-permute-start.15 = (f32[1,8,256]{2,1,0:T(8,128)S(1)}, f32[1,8,256]{2,1,0:T(8,128)S(1)}, u32[]{:S(2)}, u32[]{:S(2)}) collective-permute-start(f32[1,8,256]{2,1,0:T(8,128)S(1)} %bitcast.7), channel_id=1, source_target_pairs={{0,2},{1,3},{2,0},{3,1},{4,6},{5,7},{6,4},{7,5},{8,10},{9,11},{10,... | collective-permute-start | bytes 24584 | tf_op jit(solution)/shard_map/ppermute | solution.py:23
  79.0 3.7 %collective-permute-start.16 = (f32[2,8,256]{2,1,0:T(8,128)S(1)}, f32[2,8,256]{2,1,0:T(8,128)S(1)}, u32[]{:S(2)}, u32[]{:S(2)}) collective-permute-start(f32[2,8,256]{2,1,0:T(8,128)S(1)} %pad_maximum_fusion.5), channel_id=1, source_target_pairs={{0,1},{1,0},{2,3},{3,2},{4,5},{5,4},{6,7},{7,6},{8,9},{9,8},{10,11... | collective-permute-start | bytes 49160 | tf_op jit(solution)/shard_map/ppermute | solution.py:23
  82.7 3.6 %collective-permute-start.19 = (f32[4,8,256]{2,1,0:T(8,128)S(1)}, f32[4,8,256]{2,1,0:T(8,128)S(1)}, u32[]{:S(2)}, u32[]{:S(2)}) collective-permute-start(f32[4,8,256]{2,1,0:T(8,128)S(1)} %pad_maximum_fusion.2.refs_0_), channel_id=1, source_target_pairs={{0,12},{4,8},{8,4},{12,0},{1,13},{5,9},{9,5},{13,1},{2,14},{6,10},... | collective-permute-start | bytes 98312 | tf_op jit(solution)/shard_map/ppermute | solution.py:23
  82.7 4.0 %collective-permute-start.18 = (f32[4,8,256]{2,1,0:T(8,128)S(1)}, f32[4,8,256]{2,1,0:T(8,128)S(1)}, u32[]{:S(2)}, u32[]{:S(2)}) collective-permute-start(f32[4,8,256]{2,1,0:T(8,128)S(1)} %pad_maximum_fusion.2.refs_0_), channel_id=1, source_target_pairs={{0,8},{4,12},{8,0},{12,4},{1,9},{5,13},{9,1},{13,5},{2,10},{6,14},... | collective-permute-start | bytes 98312 | tf_op jit(solution)/shard_map/ppermute | solution.py:23
  84.3 2.5 %collective-permute-start.17 = (f32[4,8,256]{2,1,0:T(8,128)S(1)}, f32[4,8,256]{2,1,0:T(8,128)S(1)}, u32[]{:S(2)}, u32[]{:S(2)}) collective-permute-start(f32[4,8,256]{2,1,0:T(8,128)S(1)} %pad_maximum_fusion.2.refs_0_), channel_id=1, source_target_pairs={{0,4},{4,0},{8,12},{12,8},{1,5},{5,1},{9,13},{13,9},{2,6},{6,2},{1... | collective-permute-start | bytes 98312 | tf_op jit(solution)/shard_map/ppermute | solution.py:23
  89.6 4.5 %collective-permute-start.20 = (f32[8,128]{1,0:T(8,128)S(1)}, f32[8,128]{1,0:T(8,128)S(1)}, u32[]{:S(2)}, u32[]{:S(2)}) collective-permute-start(f32[8,128]{1,0:T(8,128)S(1)} %get-tuple-element.41), channel_id=1, source_target_pairs={{0,2},{1,3},{2,0},{3,1},{4,6},{5,7},{6,4},{7,5},{8,10},{9,11},{10,... | collective-permute-start | bytes 12296 | tf_op jit(solution)/shard_map/ppermute | solution.py:23
  94.2 3.6 %collective-permute-start.21 = (f32[8,128]{1,0:T(8,128)S(1)}, f32[8,128]{1,0:T(8,128)S(1)}, u32[]{:S(2)}, u32[]{:S(2)}) collective-permute-start(f32[8,128]{1,0:T(8,128)S(1)} %add.23), channel_id=1, source_target_pairs={{0,1},{1,0},{2,3},{3,2},{4,5},{5,4},{6,7},{7,6},{8,9},{9,8},{10,11... | collective-permute-start | bytes 12296 | tf_op jit(solution)/shard_map/ppermute | solution.py:23
  97.8 3.6 %collective-permute-start.22 = (f32[8,128]{1,0:T(8,128)S(1)}, f32[8,128]{1,0:T(8,128)S(1)}, u32[]{:S(2)}, u32[]{:S(2)}) collective-permute-start(f32[8,128]{1,0:T(8,128)S(1)} %add.24), channel_id=1, source_target_pairs={{0,8},{4,12},{8,0},{12,4},{1,9},{5,13},{9,1},{13,5},{2,10},{6,14},... | collective-permute-start | bytes 12296 | tf_op jit(solution)/shard_map/ppermute | solution.py:23
  (5 other events, 63.2 us)

commit v5 on v3

--- a/solution.py
+++ b/solution.py
@@ -19,10 +19,28 @@
 F32 = functools.partial(jax.ShapeDtypeStruct, dtype=jnp.float32)
 
 
+def swap(value, axis, size, bit):
+    return lax.ppermute(value, axis, [(i, i ^ bit) for i in range(size)])
+
+
+def bits(size):
+    return [1 << b for b in reversed(range(size.bit_length() - 1))]
+
+
 def gather(value, axes, size):
     return lax.all_to_all(jnp.broadcast_to(value[None], (size,) + value.shape), axes, 0, 0)
 
 
+def sum_over(value, axis, size):
+    for bit in bits(size):
+        value = value + swap(value, axis, size, bit)
+    return value
+
+
+def direct(value, axis, size):
+    return [value] + [swap(value, axis, size, k) for k in reversed(range(1, size))][::-1]
+
+
 def dot_nt(a, b):
     return lax.dot_general(a, b, NT, precision=HIGHEST, preferred_element_type=jnp.float32)
 
@@ -31,47 +49,92 @@
     return jnp.sum(values, axis=1, keepdims=True)
 
 
-def partial_kernel(in_ref, out_ref, part_ref, held):
-    count, _, tokens = in_ref.shape
-    for k in range(count):
-        held[:, k * tokens : (k + 1) * tokens] = in_ref[k]
-    for s in range(part_ref.shape[0]):
-        span = slice(s * SEQ, (s + 1) * SEQ)
-        part_ref[s] = dot_nt(held[:, span], out_ref[:, span]) * (1.0 / SEQ)
-
-
-def partial_vectors(in_all, out_local):
-    seq_count = out_local.shape[1] // SEQ
-    return pl.pallas_call(
-        partial_kernel,
-        out_shape=F32((seq_count, R_IN, R_OUT)),
-        in_specs=[VMEM_SPEC] * 2,
-        out_specs=VMEM_SPEC,
-        scratch_shapes=[pltpu.VMEM(out_local.shape, jnp.float32)],
-        compiler_params=PARAMS,
-        name="partial_vectors",
-    )(in_all, out_local)
-
-
-def split_kernel(prior_ref, upper_ref, lower_ref):
+def in_kernel(in_ref, proj_ref, feats_ref, total):
+    step = pl.program_id(0)
+
+    @pl.when(step == 0)
+    def _():
+        total[...] = jnp.zeros_like(total)
+
+    total[...] += lax.dot_general(in_ref[...], proj_ref[...], NT, preferred_element_type=jnp.float32)
+
+    @pl.when(step == pl.num_programs(0) - 1)
+    def _():
+        feats_ref[...] = total[...].T
+
+
+def in_features(inputs, in_proj):
+    tokens, width = inputs.shape
+    chunk = 1024
+    return pl.pallas_call(
+        in_kernel,
+        grid=(width // chunk,),
+        out_shape=F32((R_IN, tokens)),
+        in_specs=[
+            pl.BlockSpec((tokens, chunk), lambda i: (0, i)),
+            pl.BlockSpec((R_IN, chunk), lambda i: (0, i)),
+        ],
+        out_specs=pl.BlockSpec((R_IN, tokens), lambda i: (0, 0)),
+        scratch_shapes=[pltpu.VMEM((tokens, R_IN), jnp.float32)],
+        compiler_params=PARAMS,
+        name="in_features",
+    )(inputs, in_proj)
+
+
+def out_kernel(grads_ref, proj_ref, prior_ref, feats_ref, upper_ref, lower_ref):
+    feats = lax.dot_general(grads_ref[...], proj_ref[...], NT, preferred_element_type=jnp.float32)
+    feats_ref[...] = feats.T
     block = prior_ref[...]
     upper = block.astype(jnp.bfloat16)
     upper_ref[...] = upper
     lower_ref[...] = (block - upper.astype(jnp.float32)).astype(jnp.bfloat16)
 
 
-def split_prior(prior):
+def out_features(out_grads, out_proj, prior):
+    tokens, hidden = out_grads.shape
     rows, width = prior.shape
-    spec = pl.BlockSpec((rows, width // 8), lambda i: (0, i))
-    return pl.pallas_call(
-        split_kernel,
-        grid=(8,),
-        out_shape=(jax.ShapeDtypeStruct(prior.shape, jnp.bfloat16),) * 2,
-        in_specs=[spec],
-        out_specs=(spec, spec),
-        compiler_params=PARAMS,
-        name="split_prior",
-    )(prior)
+    steps = tokens // LANES
+    prior_spec = pl.BlockSpec((rows, width // steps), lambda i: (0, i))
+    piece = jax.ShapeDtypeStruct(prior.shape, jnp.bfloat16)
+    feats, *pieces = pl.pallas_call(
+        out_kernel,
+        grid=(steps,),
+        out_shape=(F32((R_OUT, tokens)), piece, piece),
+        in_specs=[
+            pl.BlockSpec((LANES, hidden), lambda i: (i, 0)),
+            pl.BlockSpec((R_OUT, hidden), lambda i: (0, 0)),
+            prior_spec,
+        ],
+        out_specs=(pl.BlockSpec((R_OUT, LANES), lambda i: (0, i)), prior_spec, prior_spec),
+        compiler_params=PARAMS,
+        name="out_features",
+    )(out_grads, out_proj, prior)
+    return feats, pieces
+
+
+def partial_kernel(size, *refs):
+    blocks, (out_ref, part_ref, held) = refs[:size], refs[size:]
+    me = lax.axis_index("tensor")
+    tokens = blocks[0].shape[1]
+    for k, block in enumerate(blocks):
+        start = pl.multiple_of((me ^ k) * tokens, LANES)
+        held[:, pl.ds(start, tokens)] = block[...]
+    for s in range(part_ref.shape[0]):
+        span = slice(s * SEQ, (s + 1) * SEQ)
+        part_ref[s] = dot_nt(held[:, span], out_ref[:, span]) * (1.0 / SEQ)
+
+
+def partial_vectors(blocks, out_local):
+    seq_count = out_local.shape[1] // SEQ
+    return pl.pallas_call(
+        functools.partial(partial_kernel, len(blocks)),
+        out_shape=F32((seq_count, R_IN, R_OUT)),
+        in_specs=[VMEM_SPEC] * (len(blocks) + 1),
+        out_specs=VMEM_SPEC,
+        scratch_shapes=[pltpu.VMEM(out_local.shape, jnp.float32)],
+        compiler_params=PARAMS,
+        name="partial_vectors",
+    )(*blocks, out_local)
 
 
 def own_columns(ref, me, count):
@@ -99,27 +162,36 @@
     return lax.axis_index("dp") * tensor_size + lax.axis_index("tensor")
 
 
-def start_kernel(tensor_size, pieces_ref, upper_ref, lower_ref, vectors_ref, applied_ref, norm_ref):
-    count, seqs, columns = pieces_ref.shape
-    for i in range(count):
-        dp, tensor = i // tensor_size, i % tensor_size
-        vectors_ref[dp * seqs : (dp + 1) * seqs, tensor * columns : (tensor + 1) * columns] = pieces_ref[i]
-    vectors = vectors_ref[...]
+def start_kernel(size, tensor_size, *refs):
+    pieces, (upper_ref, lower_ref, vectors_ref, applied_ref, norm_ref, held) = refs[:size], refs[size:]
+    dp = lax.axis_index("dp")
+    for k, piece in enumerate(pieces):
+        held[dp ^ k] = piece[...]
+    vectors = jnp.concatenate([held[k] for k in range(size)], axis=0)
+    vectors_ref[...] = vectors
     norm_ref[...] = jnp.broadcast_to(row_sum(vectors * vectors), norm_ref.shape)
     applied_ref[...] = apply_fisher(vectors, vectors_ref, upper_ref, lower_ref, flat_index(tensor_size))
 
 
 def start_cg(pieces, prior_pieces, tensor_size):
-    seqs = pieces.shape[0] // tensor_size * pieces.shape[1]
+    size, seqs = len(pieces), len(pieces) * pieces[0].shape[0]
     rows, width = prior_pieces[0].shape
     return pl.pallas_call(
-        functools.partial(start_kernel, tensor_size),
+        functools.partial(start_kernel, size, tensor_size),
         out_shape=(F32((seqs, width)), F32((seqs, rows)), F32((seqs, LANES))),
-        in_specs=[VMEM_SPEC] * 3,
+        in_specs=[VMEM_SPEC] * (size + 2),
         out_specs=(VMEM_SPEC,) * 3,
+        scratch_shapes=[pltpu.VMEM((size,) + pieces[0].shape, jnp.float32)],
         compiler_params=PARAMS,
         name="cg_start",
-    )(pieces, *prior_pieces)
+    )(*pieces, *prior_pieces)
+
+
+def on_lanes(column):
+    seqs = column.shape[0]
+    row = lax.broadcasted_iota(jnp.int32, (seqs, LANES), 0)
+    lane = lax.broadcasted_iota(jnp.int32, (seqs, LANES), 1)
+    return jnp.sum(jnp.where(row == lane, column, 0.0), axis=0, keepdims=True)
 
 
 def step_kernel(tensor_size, first, last, *refs):
@@ -147,12 +219,12 @@
     residual = residual - step * applied
     norm_next = row_sum(residual * residual)
     direction = residual + (norm_next / norm) * direction
-    norm_out[...] = jnp.broadcast_to(norm_next, norm_out.shape)
+    norm_out[...] = on_lanes(norm_next) if last else jnp.broadcast_to(norm_next, norm_out.shape)
     applied_rows = apply_fisher(direction, vectors_ref, upper_ref, lower_ref, me)
     if last:
         held[...] = direction
         own = own_columns(held, me, rows)
-        curvature_out[...] = jnp.broadcast_to(row_sum(own * applied_rows), curvature_out.shape)
+        curvature_out[...] = on_lanes(row_sum(own * applied_rows))
         queries = queries_ref[...].astype(jnp.float32)
         solved_out[...] = dot_nt(solution, queries)
         along_out[...] = dot_nt(direction, queries)
@@ -170,9 +242,9 @@
     operands = [blocks, *prior_pieces, vectors, norm, *(state or ())] + ([queries] if last else [])
     if last:
         scores = F32((seqs, queries.shape[0]))
-        out_shape = (column, column, scores, scores)
+        out_shape = (F32((1, LANES)), F32((1, LANES)), scores, scores)
     else:
-        out_shape = (F32((seqs, blocks.shape[2])), column, whole, whole, whole)
+        out_shape = (F32((seqs, prior_pieces[0].shape[0])), column, whole, whole, whole)
     return pl.pallas_call(
         functools.partial(step_kernel, tensor_size, first, last),
         out_shape=out_shape,
@@ -187,13 +259,10 @@
 def on_device(dp_size, tensor_size, inputs, in_proj, out_grads, out_proj, prior, queries):
     width = R_IN * R_OUT
     both, devices = ("dp", "tensor"), dp_size * tensor_size
-    in_local = lax.dot_general(in_proj, inputs, NT, preferred_element_type=jnp.float32)
-    in_all = gather(in_local, "tensor", tensor_size)
-    out_local = lax.dot_general(out_proj, out_grads, NT, preferred_element_type=jnp.float32)
-    partial = partial_vectors(in_all, out_local).reshape(-1, tensor_size, width // tensor_size)
-    partial = lax.all_to_all(partial.transpose(1, 0, 2), "tensor", 0, 0)
-    pieces = gather(jnp.sum(partial, axis=0), both, devices)
-    prior_pieces = split_prior(prior)
+    in_blocks = direct(in_features(inputs, in_proj), "tensor", tensor_size)
+    out_local, prior_pieces = out_features(out_grads, out_proj, prior)
+    partial = partial_vectors(in_blocks, out_local).reshape(-1, width)
+    pieces = direct(sum_over(partial, "tensor", tensor_size), "dp", dp_size)
     vectors, applied_rows, norm = start_cg(pieces, prior_pieces, tensor_size)
     state = None
     for iteration in range(1, ITERS - 1):
@@ -202,7 +271,8 @@
     blocks = gather(applied_rows, both, devices)
     curvature, norm, solved, along = step_cg(blocks, prior_pieces, vectors, norm, state, queries, tensor_size)
     curvature = jnp.sum(gather(curvature, both, devices), axis=0)
-    return solved + (norm / curvature)[:, :1] * along
+    step = (norm / curvature)[0, : solved.shape[0]]
+    return solved + step[:, None] * along
 
 
 def solution(mesh):

time: 104 us -> 106 us (1.019)
  matrix products: 20.3 us -> 0 us
  Pallas kernels: 10.3 us -> 25.1 us
  local copies, waits for them, and re-layouts: 8.24 us -> 17.1 us
  blocking collectives: 51.6 us -> 43.4 us
  waiting for transfers between devices: 2.53 us -> 7.23 us
  starting transfers between devices: 9.83 us -> 11.5 us
    dot_general x2 -> x0, matrix products: 20.3 us -> none  [the longest x1 14.3 us: on_device(): lax.dot_general(out_proj, out_grads, NT, preferred_element_type=jnp.float32)]
    pallas_call x3 -> x4, Pallas kernels: 3.57 us -> 18.4 us  [the longest x1 12 us: out_features(): pl.pallas_call(out_kernel, grid=(steps,), out_shape=(F32((R_OUT, tokens))...]
    ppermute x0 -> x8, starting transfers between devices: none -> 11.5 us  [swap(): return lax.ppermute(value, axis, [(i, i ^ bit) for i in range(size)])]
    unnamed x12 -> x16, local copies, waits for them, and re-layouts: 6.35 us -> 16.9 us
    all_to_all x1 -> x0, blocking collectives: 10.4 us -> none  [on_device(): partial = lax.all_to_all(partial.transpose(1, 0, 2), 'tensor', 0, 0)]
    all_to_all x2 -> x0, starting transfers between devices: 9.83 us -> none  [gather(): lax.all_to_all(jnp.broadcast_to(value[None], (size,) + value.shape), axes...]
    ppermute x0 -> x8, waiting for transfers between devices: none -> 7.23 us  [swap(): return lax.ppermute(value, axis, [(i, i ^ bit) for i in range(size)])]
    all_to_all x2 -> x0, waiting for transfers between devices: 2.53 us -> none  [gather(): lax.all_to_all(jnp.broadcast_to(value[None], (size,) + value.shape), axes...]
  transfers between devices with their start and end apart: 2 -> 8, of which waited for: 2 -> 4; matrix products, arithmetic and copies ran while one was open for 14% -> 0% of each run, Pallas kernels for 1% -> 11%
where the time goes in v5:
time: 106 us; the launch traced here: 105 us
  blocking collectives  43.4 us (41%)
  Pallas kernels  25.1 us (24%)
  local copies, waits for them, and re-layouts  17.1 us (16%)
  starting transfers between devices  11.5 us (11%)
  waiting for transfers between devices  7.23 us (7%)
    all_to_all x4, blocking collectives, gather(): lax.all_to_all(jnp.broadcast_to(value[None], (size,) + value.shape), axes...  43.4 us
    unnamed x16, local copies, waits for them, and re-layouts  16.9 us
    pallas_call x1, Pallas kernels, out_features(): pl.pallas_call(out_kernel, grid=(steps,), out_shape=(F32((R_OUT, tokens))...  12 us
    ppermute x8, starting transfers between devices, swap(): return lax.ppermute(value, axis, [(i, i ^ bit) for i in range(size)])  11.5 us
    ppermute x8, waiting for transfers between devices, swap(): return lax.ppermute(value, axis, [(i, i ^ bit) for i in range(size)])  7.23 us
    pallas_call x3, Pallas kernels, step_cg(): pl.pallas_call(functools.partial(step_kernel, tensor_size, first, last),...  6.74 us
    pallas_call x1, Pallas kernels, in_features(): pl.pallas_call(in_kernel, grid=(width // chunk,), out_shape=F32((R_IN, to...  4.19 us
  transfers between devices with their start and end apart: 8, of which 4 were waited for; matrix products, arithmetic and copies ran while one was open for 0% of the time, Pallas kernels for 11%

profile of v5, /device:TPU:0, one launch (start us, length us, event | category | flops | bytes accessed | tf_op | source)
XLA Modules:
  0.0 105.2 jit_solution(226788123538822168)
XLA Ops:
  0.0 3.4 %copy-done.3 = bf16[512,8192]{1,0:T(8,128)(2,1)S(1)} copy-done((bf16[512,8192]{1,0:T(8,128)(2,1)S(1)}, bf16[512,8192]{1,0:T(8,128)(2,1)}, u32[]{:S(2)}) %copy-start.3) | copy-done | bytes 8388632
  3.4 1.2 %copy-done.5 = bf16[64,8192]{1,0:T(8,128)(2,1)S(1)} copy-done((bf16[64,8192]{1,0:T(8,128)(2,1)S(1)}, bf16[64,8192]{1,0:T(8,128)(2,1)}, u32[]{:S(2)}) %copy-start.5) | copy-done | bytes 1048600
  4.6 4.2 %in_features.1.refs_0_ = f32[64,512]{1,0:T(8,128)S(1)} custom-call(bf16[512,8192]{1,0:T(8,128)(2,1)S(1)} %copy-done.3, bf16[64,8192]{1,0:T(8,128)(2,1)S(1)} %copy-done.5), custom_call_target="tpu_custom_call" | custom-call | tf_op jit(solution)/shard_map/in_features/pallas_call | solution.py:69
  8.8 5.1 %collective-permute-start.2 = (f32[64,512]{1,0:T(8,128)S(1)}, f32[64,512]{1,0:T(8,128)S(1)}, u32[]{:S(2)}, u32[]{:S(2)}) collective-permute-start(f32[64,512]{1,0:T(8,128)S(1)} %in_features.1.refs_0_), channel_id=1, source_target_pairs={{0,3},{1,2},{2,1},{3,0},{4,7},{5,6},{6,5},{7,4},{8,11},{9,10},{10,... | collective-permute-start | bytes 393224 | tf_op jit(solution)/shard_map/ppermute | solution.py:23
  13.9 0.6 collective-permute-start
  14.6 9.3 %copy-done.2 = bf16[2048,7168]{1,0:T(8,128)(2,1)S(1)} copy-done((bf16[2048,7168]{1,0:T(8,128)(2,1)S(1)}, bf16[2048,7168]{1,0:T(8,128)(2,1)}, u32[]{:S(2)}) %copy-start.2) | copy-done | bytes 29360152
  23.9 12.0 %out_features.1 = (f32[64,2048]{1,0:T(8,128)S(1)}, bf16[256,4096]{1,0:T(8,128)(2,1)S(1)}, bf16[256,4096]{1,0:T(8,128)(2,1)S(1)}) custom-call(bf16[2048,7168]{1,0:T(8,128)(2,1)S(1)} %copy-done.2, bf16[64,7168]{1,0:T(8,128)(2,1)S(1)} %copy-done.6, f32[256,4096]{1,0:T(8,128)S(1)} %copy-done.4), custom_call_target="tpu_custom_call" | custom-call | tf_op jit(solution)/shard_map/out_features/pallas_call | solution.py:99
  35.9 1.3 %copy-done = bf16[256,4096]{1,0:T(8,128)(2,1)} copy-done((bf16[256,4096]{1,0:T(8,128)(2,1)}, bf16[256,4096]{1,0:T(8,128)(2,1)S(1)}, u32[]{:S(2)}) %copy-start) | copy-done | bytes 2097176
  38.0 2.4 %collective-permute-start.3 = (f32[2,4096]{1,0:T(2,128)S(1)}, f32[2,4096]{1,0:T(2,128)S(1)}, u32[]{:S(2)}, u32[]{:S(2)}) collective-permute-start(f32[2,4096]{1,0:T(2,128)S(1)} %reshape.11), channel_id=1, source_target_pairs={{0,2},{1,3},{2,0},{3,1},{4,6},{5,7},{6,4},{7,5},{8,10},{9,11},{10,... | collective-permute-start | bytes 98312 | tf_op jit(solution)/shard_map/ppermute | solution.py:23
  40.4 2.5 %collective-permute-done.3 = f32[2,4096]{1,0:T(2,128)S(1)} collective-permute-done((f32[2,4096]{1,0:T(2,128)S(1)}, f32[2,4096]{1,0:T(2,128)S(1)}, u32[]{:S(2)}, u32[]{:S(2)}) %collective-permute-start.3) | collective-permute-done | bytes 32800 | tf_op jit(solution)/shard_map/ppermute | solution.py:23
  42.9 1.5 %collective-permute-start.4 = (f32[2,4096]{1,0:T(2,128)S(1)}, f32[2,4096]{1,0:T(2,128)S(1)}, u32[]{:S(2)}, u32[]{:S(2)}) collective-permute-start(f32[2,4096]{1,0:T(2,128)S(1)} %add.9), channel_id=1, source_target_pairs={{0,1},{1,0},{2,3},{3,2},{4,5},{5,4},{6,7},{7,6},{8,9},{9,8},{10,11... | collective-permute-start | bytes 98312 | tf_op jit(solution)/shard_map/ppermute | solution.py:23
  44.4 2.5 %collective-permute-done.4 = f32[2,4096]{1,0:T(2,128)S(1)} collective-permute-done((f32[2,4096]{1,0:T(2,128)S(1)}, f32[2,4096]{1,0:T(2,128)S(1)}, u32[]{:S(2)}, u32[]{:S(2)}) %collective-permute-start.4) | collective-permute-done | bytes 32800 | tf_op jit(solution)/shard_map/ppermute | solution.py:23
  47.0 1.8 %collective-permute-start.6 = (f32[2,4096]{1,0:T(2,128)S(1)}, f32[2,4096]{1,0:T(2,128)S(1)}, u32[]{:S(2)}, u32[]{:S(2)}) collective-permute-start(f32[2,4096]{1,0:T(2,128)S(1)} %add.10.refs_0_), channel_id=1, source_target_pairs={{0,8},{4,12},{8,0},{12,4},{1,9},{5,13},{9,1},{13,5},{2,10},{6,14},... | collective-permute-start | bytes 98312 | tf_op jit(solution)/shard_map/ppermute | solution.py:23
  48.8 1.6 %collective-permute-done.7.refs_3_ = f32[2,4096]{1,0:T(2,128)S(1)} collective-permute-done((f32[2,4096]{1,0:T(2,128)S(1)}, f32[2,4096]{1,0:T(2,128)S(1)}, u32[]{:S(2)}, u32[]{:S(2)}) %collective-permute-start.7) | collective-permute-done | bytes 32800 | tf_op jit(solution)/shard_map/ppermute | solution.py:23
  51.0 1.6 %copy-done.1 = bf16[256,4096]{1,0:T(8,128)(2,1)S(1)} copy-done((bf16[256,4096]{1,0:T(8,128)(2,1)S(1)}, bf16[256,4096]{1,0:T(8,128)(2,1)}, u32[]{:S(2)}) %copy-start.1) | copy-done | bytes 2097176
  52.6 1.6 %cg_start.1 = (f32[8,4096]{1,0:T(8,128)S(1)}, f32[8,256]{1,0:T(8,128)S(1)}, f32[8,128]{1,0:T(8,128)S(1)}) custom-call(f32[2,4096]{1,0:T(2,128)S(1)} %add.10.refs_0_, f32[2,4096]{1,0:T(2,128)S(1)} %collective-permute-done.5.refs_1_, f32[2,4096]{1,0:T(2,128)S(1)} %collective-permute-done.6.refs_2_, f32[2,4096]{1,0:T(2,128)S(1)} %collective-permute-done.7.refs_3_, ...), custom_call_target="tpu_custom_call" | custom-call | tf_op jit(solution)/shard_map/cg_start/pallas_call | solution.py:179
  54.3 13.2 %all_to_all.20.refs_0_ = f32[16,8,256]{2,1,0:T(8,128)S(1)} all-to-all(f32[16,8,256]{2,1,0:T(8,128)S(1)} %broadcast_in_dim.10), channel_id=1, replica_groups=mesh['groups'=2,'dp'=4,'tensor'=4] {'dp','tensor'}, dimensions={0} | all-to-all | bytes 262144 | tf_op jit(solution)/shard_map/all_to_all | solution.py:31
  67.4 2.0 %cg_step.3 = (f32[8,256]{1,0:T(8,128)S(1)}, f32[8,128]{1,0:T(8,128)S(1)}, f32[8,4096]{1,0:T(8,128)S(1)}, f32[8,4096]{1,0:T(8,128)S(1)}, f32[8,4096]{1,0:T(8,128)S(1)}) custom-call(f32[16,8,256]{2,1,0:T(8,128)S(1)} %all_to_all.20.refs_0_, bf16[256,4096]{1,0:T(8,128)(2,1)S(1)} %get-tuple-element.26.refs_4_.refs_1_, bf16[256,4096]{1,0:T(8,128)(2,1)S(1)} %copy-done.1, ...), custom_call_target="tpu_custom_call" | custom-call | tf_op jit(solution)/shard_map/cg_step/pallas_call | solution.py:248
  69.4 10.4 %all_to_all.21.refs_0_ = f32[16,8,256]{2,1,0:T(8,128)S(1)} all-to-all(f32[16,8,256]{2,1,0:T(8,128)S(1)} %broadcast_in_dim.11), channel_id=1, replica_groups=mesh['groups'=2,'dp'=4,'tensor'=4] {'dp','tensor'}, dimensions={0} | all-to-all | bytes 262144 | tf_op jit(solution)/shard_map/all_to_all | solution.py:31
  79.8 2.0 %cg_step.4 = (f32[8,256]{1,0:T(8,128)S(1)}, f32[8,128]{1,0:T(8,128)S(1)}, f32[8,4096]{1,0:T(8,128)S(1)}, f32[8,4096]{1,0:T(8,128)S(1)}, f32[8,4096]{1,0:T(8,128)S(1)}) custom-call(f32[16,8,256]{2,1,0:T(8,128)S(1)} %all_to_all.21.refs_0_, bf16[256,4096]{1,0:T(8,128)(2,1)S(1)} %get-tuple-element.26.refs_4_.refs_1_, bf16[256,4096]{1,0:T(8,128)(2,1)S(1)} %copy-done.1, ...), custom_call_target="tpu_custom_call" | custom-call | tf_op jit(solution)/shard_map/cg_step/pallas_call | solution.py:248
  81.8 10.4 %all_to_all.22.refs_0_ = f32[16,8,256]{2,1,0:T(8,128)S(1)} all-to-all(f32[16,8,256]{2,1,0:T(8,128)S(1)} %broadcast_in_dim.12), channel_id=1, replica_groups=mesh['groups'=2,'dp'=4,'tensor'=4] {'dp','tensor'}, dimensions={0} | all-to-all | bytes 262144 | tf_op jit(solution)/shard_map/all_to_all | solution.py:31
  92.2 2.8 %cg_step.5 = (f32[1,128]{1,0:T(1,128)S(1)}, f32[1,128]{1,0:T(1,128)S(1)}, f32[8,32]{1,0:T(8,128)S(1)}, f32[8,32]{1,0:T(8,128)S(1)}) custom-call(f32[16,8,256]{2,1,0:T(8,128)S(1)} %all_to_all.22.refs_0_, bf16[256,4096]{1,0:T(8,128)(2,1)S(1)} %get-tuple-element.26.refs_4_.refs_1_, bf16[256,4096]{1,0:T(8,128)(2,1)S(1)} %copy-done.1, ...), custom_call_target="tpu_custom_call" | custom-call | tf_op jit(solution)/shard_map/cg_step/pallas_call | solution.py:248
  95.0 9.4 %all_to_all.23 = f32[16,1,128]{2,1,0:T(1,128)S(1)} all-to-all(f32[16,1,128]{2,1,0:T(1,128)S(1)} %broadcast_in_dim.14), channel_id=1, replica_groups=mesh['groups'=2,'dp'=4,'tensor'=4] {'dp','tensor'}, dimensions={0} | all-to-all | bytes 16384 | tf_op jit(solution)/shard_map/all_to_all | solution.py:31
  104.5 0.7 multiply_add_fusion
  (30 shorter events, 1.7 us)
Async XLA Ops:
  0.0 3.4 %copy-start.3 = (bf16[512,8192]{1,0:T(8,128)(2,1)S(1)}, bf16[512,8192]{1,0:T(8,128)(2,1)}, u32[]{:S(2)}) copy-start(bf16[512,8192]{1,0:T(8,128)(2,1)} %in_ref.1) | copy-start | bytes 25165828
  3.4 1.2 %copy-start.5 = (bf16[64,8192]{1,0:T(8,128)(2,1)S(1)}, bf16[64,8192]{1,0:T(8,128)(2,1)}, u32[]{:S(2)}) copy-start(bf16[64,8192]{1,0:T(8,128)(2,1)} %proj_ref.2) | copy-start | bytes 3145732
  4.6 10.0 %copy-start.4 = (f32[256,4096]{1,0:T(8,128)S(1)}, f32[256,4096]{1,0:T(8,128)}, u32[]{:S(2)}) copy-start(f32[256,4096]{1,0:T(8,128)} %prior_ref.1) | copy-start | bytes 12582916
  4.6 10.0 %copy-start.6 = (bf16[64,7168]{1,0:T(8,128)(2,1)S(1)}, bf16[64,7168]{1,0:T(8,128)(2,1)}, u32[]{:S(2)}) copy-start(bf16[64,7168]{1,0:T(8,128)(2,1)} %proj_ref.3) | copy-start | bytes 2752516
  8.8 28.5 %collective-permute-start.2 = (f32[64,512]{1,0:T(8,128)S(1)}, f32[64,512]{1,0:T(8,128)S(1)}, u32[]{:S(2)}, u32[]{:S(2)}) collective-permute-start(f32[64,512]{1,0:T(8,128)S(1)} %in_features.1.refs_0_), channel_id=1, source_target_pairs={{0,3},{1,2},{2,1},{3,0},{4,7},{5,6},{6,5},{7,4},{8,11},{9,10},{10,... | collective-permute-start | bytes 393224 | tf_op jit(solution)/shard_map/ppermute | solution.py:23
  13.9 23.3 %collective-permute-start.1 = (f32[64,512]{1,0:T(8,128)S(1)}, f32[64,512]{1,0:T(8,128)S(1)}, u32[]{:S(2)}, u32[]{:S(2)}) collective-permute-start(f32[64,512]{1,0:T(8,128)S(1)} %in_features.1.refs_0_), channel_id=1, source_target_pairs={{0,2},{1,3},{2,0},{3,1},{4,6},{5,7},{6,4},{7,5},{8,10},{9,11},{10,... | collective-permute-start | bytes 393224 | tf_op jit(solution)/shard_map/ppermute | solution.py:23
  13.9 23.3 %collective-permute-start = (f32[64,512]{1,0:T(8,128)S(1)}, f32[64,512]{1,0:T(8,128)S(1)}, u32[]{:S(2)}, u32[]{:S(2)}) collective-permute-start(f32[64,512]{1,0:T(8,128)S(1)} %in_features.1.refs_0_), channel_id=1, source_target_pairs={{0,1},{1,0},{2,3},{3,2},{4,5},{5,4},{6,7},{7,6},{8,9},{9,8},{10,11... | collective-permute-start | bytes 393224 | tf_op jit(solution)/shard_map/ppermute | solution.py:23
  14.6 9.4 %copy-start.2 = (bf16[2048,7168]{1,0:T(8,128)(2,1)S(1)}, bf16[2048,7168]{1,0:T(8,128)(2,1)}, u32[]{:S(2)}) copy-start(bf16[2048,7168]{1,0:T(8,128)(2,1)} %grads_ref.1) | copy-start | bytes 88080384
  35.9 1.3 %copy-start = (bf16[256,4096]{1,0:T(8,128)(2,1)}, bf16[256,4096]{1,0:T(8,128)(2,1)S(1)}, u32[]{:S(2)}) copy-start(bf16[256,4096]{1,0:T(8,128)(2,1)S(1)} %get-tuple-element.27.refs_5_.refs_2_) | copy-start | bytes 6291460
  38.0 4.9 %collective-permute-start.3 = (f32[2,4096]{1,0:T(2,128)S(1)}, f32[2,4096]{1,0:T(2,128)S(1)}, u32[]{:S(2)}, u32[]{:S(2)}) collective-permute-start(f32[2,4096]{1,0:T(2,128)S(1)} %reshape.11), channel_id=1, source_target_pairs={{0,2},{1,3},{2,0},{3,1},{4,6},{5,7},{6,4},{7,5},{8,10},{9,11},{10,... | collective-permute-start | bytes 98312 | tf_op jit(solution)/shard_map/ppermute | solution.py:23
  42.9 4.0 %collective-permute-start.4 = (f32[2,4096]{1,0:T(2,128)S(1)}, f32[2,4096]{1,0:T(2,128)S(1)}, u32[]{:S(2)}, u32[]{:S(2)}) collective-permute-start(f32[2,4096]{1,0:T(2,128)S(1)} %add.9), channel_id=1, source_target_pairs={{0,1},{1,0},{2,3},{3,2},{4,5},{5,4},{6,7},{7,6},{8,9},{9,8},{10,11... | collective-permute-start | bytes 98312 | tf_op jit(solution)/shard_map/ppermute | solution.py:23
  46.9 3.5 %collective-permute-start.7 = (f32[2,4096]{1,0:T(2,128)S(1)}, f32[2,4096]{1,0:T(2,128)S(1)}, u32[]{:S(2)}, u32[]{:S(2)}) collective-permute-start(f32[2,4096]{1,0:T(2,128)S(1)} %add.10.refs_0_), channel_id=1, source_target_pairs={{0,12},{4,8},{8,4},{12,0},{1,13},{5,9},{9,5},{13,1},{2,14},{6,10},... | collective-permute-start | bytes 98312 | tf_op jit(solution)/shard_map/ppermute | solution.py:23
  47.0 4.0 %collective-permute-start.6 = (f32[2,4096]{1,0:T(2,128)S(1)}, f32[2,4096]{1,0:T(2,128)S(1)}, u32[]{:S(2)}, u32[]{:S(2)}) collective-permute-start(f32[2,4096]{1,0:T(2,128)S(1)} %add.10.refs_0_), channel_id=1, source_target_pairs={{0,8},{4,12},{8,0},{12,4},{1,9},{5,13},{9,1},{13,5},{2,10},{6,14},... | collective-permute-start | bytes 98312 | tf_op jit(solution)/shard_map/ppermute | solution.py:23
  48.8 2.3 %collective-permute-start.5 = (f32[2,4096]{1,0:T(2,128)S(1)}, f32[2,4096]{1,0:T(2,128)S(1)}, u32[]{:S(2)}, u32[]{:S(2)}) collective-permute-start(f32[2,4096]{1,0:T(2,128)S(1)} %add.10.refs_0_), channel_id=1, source_target_pairs={{0,4},{4,0},{8,12},{12,8},{1,5},{5,1},{9,13},{13,9},{2,6},{6,2},{1... | collective-permute-start | bytes 98312 | tf_op jit(solution)/shard_map/ppermute | solution.py:23
  51.0 1.6 %copy-start.1 = (bf16[256,4096]{1,0:T(8,128)(2,1)S(1)}, bf16[256,4096]{1,0:T(8,128)(2,1)}, u32[]{:S(2)}) copy-start(bf16[256,4096]{1,0:T(8,128)(2,1)} %copy-done) | copy-start | bytes 6291460
  67.4 24.8 %copy-start.7 = (bf16[32,4096]{1,0:T(8,128)(2,1)S(1)}, bf16[32,4096]{1,0:T(8,128)(2,1)}, u32[]{:S(2)}) copy-start(bf16[32,4096]{1,0:T(8,128)(2,1)} %refs_8_.1) | copy-start | bytes 786436

commit v6 on v5

--- a/solution.py
+++ b/solution.py
@@ -76,40 +76,57 @@
         ],
         out_specs=pl.BlockSpec((R_IN, tokens), lambda i: (0, 0)),
         scratch_shapes=[pltpu.VMEM((tokens, R_IN), jnp.float32)],
-        compiler_params=PARAMS,
+        compiler_params=pltpu.CompilerParams(vmem_limit_bytes=60 * 2**20),
         name="in_features",
     )(inputs, in_proj)
 
 
-def out_kernel(grads_ref, proj_ref, prior_ref, feats_ref, upper_ref, lower_ref):
-    feats = lax.dot_general(grads_ref[...], proj_ref[...], NT, preferred_element_type=jnp.float32)
+def out_kernel(grads_ref, proj_ref, feats_ref, turned):
+    @pl.when(pl.program_id(0) == 0)
+    def _():
+        turned[...] = proj_ref[...].T
+
+    feats = jnp.dot(grads_ref[...], turned[...], preferred_element_type=jnp.float32)
     feats_ref[...] = feats.T
+
+
+def out_features(out_grads, out_proj):
+    tokens, hidden = out_grads.shape
+    block = 256
+    return pl.pallas_call(
+        out_kernel,
+        grid=(tokens // block,),
+        out_shape=F32((R_OUT, tokens)),
+        in_specs=[
+            pl.BlockSpec((block, hidden), lambda i: (i, 0)),
+            pl.BlockSpec((R_OUT, hidden), lambda i: (0, 0)),
+        ],
+        out_specs=pl.BlockSpec((R_OUT, block), lambda i: (0, i)),
+        scratch_shapes=[pltpu.VMEM((hidden, R_OUT), jnp.bfloat16)],
+        compiler_params=pltpu.CompilerParams(vmem_limit_bytes=60 * 2**20),
+        name="out_features",
+    )(out_grads, out_proj)
+
+
+def split_kernel(prior_ref, upper_ref, lower_ref):
     block = prior_ref[...]
     upper = block.astype(jnp.bfloat16)
     upper_ref[...] = upper
     lower_ref[...] = (block - upper.astype(jnp.float32)).astype(jnp.bfloat16)
 
 
-def out_features(out_grads, out_proj, prior):
-    tokens, hidden = out_grads.shape
+def split_prior(prior):
     rows, width = prior.shape
-    steps = tokens // LANES
-    prior_spec = pl.BlockSpec((rows, width // steps), lambda i: (0, i))
-    piece = jax.ShapeDtypeStruct(prior.shape, jnp.bfloat16)
-    feats, *pieces = pl.pallas_call(
-        out_kernel,
-        grid=(steps,),
-        out_shape=(F32((R_OUT, tokens)), piece, piece),
-        in_specs=[
-            pl.BlockSpec((LANES, hidden), lambda i: (i, 0)),
-            pl.BlockSpec((R_OUT, hidden), lambda i: (0, 0)),
-            prior_spec,
-        ],
-        out_specs=(pl.BlockSpec((R_OUT, LANES), lambda i: (0, i)), prior_spec, prior_spec),
-        compiler_params=PARAMS,
-        name="out_features",
-    )(out_grads, out_proj, prior)
-    return feats, pieces
+    spec = pl.BlockSpec((rows, width // 8), lambda i: (0, i))
+    return pl.pallas_call(
+        split_kernel,
+        grid=(8,),
+        out_shape=(jax.ShapeDtypeStruct(prior.shape, jnp.bfloat16),) * 2,
+        in_specs=[spec],
+        out_specs=(spec, spec),
+        compiler_params=pltpu.CompilerParams(vmem_limit_bytes=56 * 2**20),
+        name="split_prior",
+    )(prior)
 
 
 def partial_kernel(size, *refs):
@@ -260,9 +277,10 @@
     width = R_IN * R_OUT
     both, devices = ("dp", "tensor"), dp_size * tensor_size
     in_blocks = direct(in_features(inputs, in_proj), "tensor", tensor_size)
-    out_local, prior_pieces = out_features(out_grads, out_proj, prior)
+    out_local = out_features(out_grads, out_proj)
     partial = partial_vectors(in_blocks, out_local).reshape(-1, width)
     pieces = direct(sum_over(partial, "tensor", tensor_size), "dp", dp_size)
+    prior_pieces = split_prior(prior)
     vectors, applied_rows, norm = start_cg(pieces, prior_pieces, tensor_size)
     state = None
     for iteration in range(1, ITERS - 1):

time: 106 us -> 106 us (level)
  Pallas kernels: 25.1 us -> 39.8 us
  local copies, waits for them, and re-layouts: 17.1 us -> 4.42 us
  waiting for transfers between devices: 7.23 us -> 4.91 us
    unnamed x16 -> x10, local copies, waits for them, and re-layouts: 16.9 us -> 4.22 us
    pallas_call x1 -> x2, Pallas kernels: 12 us -> 22.8 us  [the longest x1 16 us: out_features(): pl.pallas_call(out_kernel, grid=(tokens // block,), out_shape=F32((R_OUT,...]
    pallas_call x1, Pallas kernels: 4.19 us -> 8.09 us  [in_features(): pl.pallas_call(in_kernel, grid=(width // chunk,), out_shape=F32((R_IN, to...]
    ppermute x8, waiting for transfers between devices: 7.23 us -> 4.91 us  [swap(): return lax.ppermute(value, axis, [(i, i ^ bit) for i in range(size)])]
  transfers between devices with their start and end apart: 8 -> 8, of which waited for: 4 -> 2; matrix products, arithmetic and copies ran while one was open for 0% -> 0% of each run, Pallas kernels for 11% -> 22%
where the time goes in v6:
time: 106 us; the launch traced here: 105 us
  blocking collectives  43.5 us (41%)
  Pallas kernels  39.8 us (38%)
  starting transfers between devices  11.5 us (11%)
  waiting for transfers between devices  4.91 us (5%)
  local copies, waits for them, and re-layouts  4.42 us (4%)
    all_to_all x4, blocking collectives, gather(): lax.all_to_all(jnp.broadcast_to(value[None], (size,) + value.shape), axes...  43.5 us
    pallas_call x1, Pallas kernels, out_features(): pl.pallas_call(out_kernel, grid=(tokens // block,), out_shape=F32((R_OUT,...  16 us
    ppermute x8, starting transfers between devices, swap(): return lax.ppermute(value, axis, [(i, i ^ bit) for i in range(size)])  11.5 us
    pallas_call x1, Pallas kernels, in_features(): pl.pallas_call(in_kernel, grid=(width // chunk,), out_shape=F32((R_IN, to...  8.09 us
    pallas_call x1, Pallas kernels, split_prior(): pl.pallas_call(split_kernel, grid=(8,), out_shape=(jax.ShapeDtypeStruct(p...  6.77 us
    pallas_call x3, Pallas kernels, step_cg(): pl.pallas_call(functools.partial(step_kernel, tensor_size, first, last),...  6.74 us
    ppermute x8, waiting for transfers between devices, swap(): return lax.ppermute(value, axis, [(i, i ^ bit) for i in range(size)])  4.91 us
    unnamed x10, local copies, waits for them, and re-layouts  4.22 us
  transfers between devices with their start and end apart: 8, of which 2 were waited for; matrix products, arithmetic and copies ran while one was open for 0% of the time, Pallas kernels for 22%

profile of v6, /device:TPU:0, one launch (start us, length us, event | category | flops | bytes accessed | tf_op | source)
XLA Modules:
  0.0 105.0 jit_solution(15572953481908297945)
XLA Ops:
  0.0 8.1 %in_features.1.refs_0_ = f32[64,512]{1,0:T(8,128)} custom-call(bf16[512,8192]{1,0:T(8,128)(2,1)} %in_ref.1, bf16[64,8192]{1,0:T(8,128)(2,1)} %proj_ref.2), custom_call_target="tpu_custom_call" | custom-call | tf_op jit(solution)/shard_map/in_features/pallas_call | solution.py:69
  8.1 5.1 %collective-permute-start.2 = (f32[64,512]{1,0:T(8,128)}, f32[64,512]{1,0:T(8,128)S(1)}, u32[]{:S(2)}, u32[]{:S(2)}) collective-permute-start(f32[64,512]{1,0:T(8,128)} %in_features.1.refs_0_), channel_id=1, source_target_pairs={{0,3},{1,2},{2,1},{3,0},{4,7},{5,6},{6,5},{7,4},{8,11},{9,10},{10,... | collective-permute-start | bytes 393224 | tf_op jit(solution)/shard_map/ppermute | solution.py:23
  13.1 0.6 collective-permute-start
  13.7 16.0 %out_features.1.refs_4_ = f32[64,2048]{1,0:T(8,128)} custom-call(bf16[2048,7168]{1,0:T(8,128)(2,1)} %grads_ref.1, bf16[64,7168]{1,0:T(8,128)(2,1)} %proj_ref.3), custom_call_target="tpu_custom_call" | custom-call | tf_op jit(solution)/shard_map/out_features/pallas_call | solution.py:96
  29.8 1.0 copy-done.2
  30.8 0.6 partial_vectors.1
  31.4 0.1 reshape.11
  31.5 2.4 %collective-permute-start.3 = (f32[2,4096]{1,0:T(2,128)S(1)}, f32[2,4096]{1,0:T(2,128)S(1)}, u32[]{:S(2)}, u32[]{:S(2)}) collective-permute-start(f32[2,4096]{1,0:T(2,128)S(1)} %reshape.11), channel_id=1, source_target_pairs={{0,2},{1,3},{2,0},{3,1},{4,6},{5,7},{6,4},{7,5},{8,10},{9,11},{10,... | collective-permute-start | bytes 98312 | tf_op jit(solution)/shard_map/ppermute | solution.py:23
  34.0 2.4 %collective-permute-done.3 = f32[2,4096]{1,0:T(2,128)S(1)} collective-permute-done((f32[2,4096]{1,0:T(2,128)S(1)}, f32[2,4096]{1,0:T(2,128)S(1)}, u32[]{:S(2)}, u32[]{:S(2)}) %collective-permute-start.3) | collective-permute-done | bytes 32800 | tf_op jit(solution)/shard_map/ppermute | solution.py:23
  36.4 1.5 %collective-permute-start.4 = (f32[2,4096]{1,0:T(2,128)S(1)}, f32[2,4096]{1,0:T(2,128)S(1)}, u32[]{:S(2)}, u32[]{:S(2)}) collective-permute-start(f32[2,4096]{1,0:T(2,128)S(1)} %add.9), channel_id=1, source_target_pairs={{0,1},{1,0},{2,3},{3,2},{4,5},{5,4},{6,7},{7,6},{8,9},{9,8},{10,11... | collective-permute-start | bytes 98312 | tf_op jit(solution)/shard_map/ppermute | solution.py:23
  38.0 2.4 %collective-permute-done.4 = f32[2,4096]{1,0:T(2,128)S(1)} collective-permute-done((f32[2,4096]{1,0:T(2,128)S(1)}, f32[2,4096]{1,0:T(2,128)S(1)}, u32[]{:S(2)}, u32[]{:S(2)}) %collective-permute-start.4) | collective-permute-done | bytes 32800 | tf_op jit(solution)/shard_map/ppermute | solution.py:23
  40.5 1.8 %collective-permute-start.6 = (f32[2,4096]{1,0:T(2,128)S(1)}, f32[2,4096]{1,0:T(2,128)S(1)}, u32[]{:S(2)}, u32[]{:S(2)}) collective-permute-start(f32[2,4096]{1,0:T(2,128)S(1)} %add.10.refs_0_), channel_id=1, source_target_pairs={{0,8},{4,12},{8,0},{12,4},{1,9},{5,13},{9,1},{13,5},{2,10},{6,14},... | collective-permute-start | bytes 98312 | tf_op jit(solution)/shard_map/ppermute | solution.py:23
  42.4 6.8 %split_prior.1 = (bf16[256,4096]{1,0:T(8,128)(2,1)}, bf16[256,4096]{1,0:T(8,128)(2,1)}) custom-call(f32[256,4096]{1,0:T(8,128)} %prior_ref.1), custom_call_target="tpu_custom_call" | custom-call | tf_op jit(solution)/shard_map/split_prior/pallas_call | solution.py:121
  49.2 1.6 %copy-done = bf16[256,4096]{1,0:T(8,128)(2,1)S(1)} copy-done((bf16[256,4096]{1,0:T(8,128)(2,1)S(1)}, bf16[256,4096]{1,0:T(8,128)(2,1)}, u32[]{:S(2)}) %copy-start) | copy-done | bytes 2097176
  50.8 1.6 %copy-done.1 = bf16[256,4096]{1,0:T(8,128)(2,1)S(1)} copy-done((bf16[256,4096]{1,0:T(8,128)(2,1)S(1)}, bf16[256,4096]{1,0:T(8,128)(2,1)}, u32[]{:S(2)}) %copy-start.1) | copy-done | bytes 2097176
  52.3 1.6 %cg_start.1 = (f32[8,4096]{1,0:T(8,128)S(1)}, f32[8,256]{1,0:T(8,128)S(1)}, f32[8,128]{1,0:T(8,128)S(1)}) custom-call(f32[2,4096]{1,0:T(2,128)S(1)} %add.10.refs_0_, f32[2,4096]{1,0:T(2,128)S(1)} %collective-permute-done.5.refs_1_, f32[2,4096]{1,0:T(2,128)S(1)} %collective-permute-done.6.refs_2_, f32[2,4096]{1,0:T(2,128)S(1)} %collective-permute-done.7.refs_3_, ...), custom_call_target="tpu_custom_call" | custom-call | tf_op jit(solution)/shard_map/cg_start/pallas_call | solution.py:196
  54.0 13.3 %all_to_all.20.refs_0_ = f32[16,8,256]{2,1,0:T(8,128)S(1)} all-to-all(f32[16,8,256]{2,1,0:T(8,128)S(1)} %broadcast_in_dim.10), channel_id=1, replica_groups=mesh['groups'=2,'dp'=4,'tensor'=4] {'dp','tensor'}, dimensions={0} | all-to-all | bytes 262144 | tf_op jit(solution)/shard_map/all_to_all | solution.py:31
  67.3 2.0 %cg_step.3 = (f32[8,256]{1,0:T(8,128)S(1)}, f32[8,128]{1,0:T(8,128)S(1)}, f32[8,4096]{1,0:T(8,128)S(1)}, f32[8,4096]{1,0:T(8,128)S(1)}, f32[8,4096]{1,0:T(8,128)S(1)}) custom-call(f32[16,8,256]{2,1,0:T(8,128)S(1)} %all_to_all.20.refs_0_, bf16[256,4096]{1,0:T(8,128)(2,1)S(1)} %copy-done, bf16[256,4096]{1,0:T(8,128)(2,1)S(1)} %copy-done.1, ...), custom_call_target="tpu_custom_call" | custom-call | tf_op jit(solution)/shard_map/cg_step/pallas_call | solution.py:265
  69.3 10.4 %all_to_all.21.refs_0_ = f32[16,8,256]{2,1,0:T(8,128)S(1)} all-to-all(f32[16,8,256]{2,1,0:T(8,128)S(1)} %broadcast_in_dim.11), channel_id=1, replica_groups=mesh['groups'=2,'dp'=4,'tensor'=4] {'dp','tensor'}, dimensions={0} | all-to-all | bytes 262144 | tf_op jit(solution)/shard_map/all_to_all | solution.py:31
  79.7 2.0 %cg_step.4 = (f32[8,256]{1,0:T(8,128)S(1)}, f32[8,128]{1,0:T(8,128)S(1)}, f32[8,4096]{1,0:T(8,128)S(1)}, f32[8,4096]{1,0:T(8,128)S(1)}, f32[8,4096]{1,0:T(8,128)S(1)}) custom-call(f32[16,8,256]{2,1,0:T(8,128)S(1)} %all_to_all.21.refs_0_, bf16[256,4096]{1,0:T(8,128)(2,1)S(1)} %copy-done, bf16[256,4096]{1,0:T(8,128)(2,1)S(1)} %copy-done.1, ...), custom_call_target="tpu_custom_call" | custom-call | tf_op jit(solution)/shard_map/cg_step/pallas_call | solution.py:265
  81.7 10.4 %all_to_all.22.refs_0_ = f32[16,8,256]{2,1,0:T(8,128)S(1)} all-to-all(f32[16,8,256]{2,1,0:T(8,128)S(1)} %broadcast_in_dim.12), channel_id=1, replica_groups=mesh['groups'=2,'dp'=4,'tensor'=4] {'dp','tensor'}, dimensions={0} | all-to-all | bytes 262144 | tf_op jit(solution)/shard_map/all_to_all | solution.py:31
  92.1 2.8 %cg_step.5 = (f32[1,128]{1,0:T(1,128)S(1)}, f32[1,128]{1,0:T(1,128)S(1)}, f32[8,32]{1,0:T(8,128)S(1)}, f32[8,32]{1,0:T(8,128)S(1)}) custom-call(f32[16,8,256]{2,1,0:T(8,128)S(1)} %all_to_all.22.refs_0_, bf16[256,4096]{1,0:T(8,128)(2,1)S(1)} %copy-done, bf16[256,4096]{1,0:T(8,128)(2,1)S(1)} %copy-done.1, f32[8,4096]{1,0:T(8,128)S(1)} %get-tuple-element.27.refs_3_, ...), custom_call_target="tpu_custom_call" | custom-call | tf_op jit(solution)/shard_map/cg_step/pallas_call | solution.py:265
  94.9 9.4 %all_to_all.23 = f32[16,1,128]{2,1,0:T(1,128)S(1)} all-to-all(f32[16,1,128]{2,1,0:T(1,128)S(1)} %broadcast_in_dim.14), channel_id=1, replica_groups=mesh['groups'=2,'dp'=4,'tensor'=4] {'dp','tensor'}, dimensions={0} | all-to-all | bytes 16384 | tf_op jit(solution)/shard_map/all_to_all | solution.py:31
  104.3 0.7 multiply_add_fusion
  (25 shorter events, 0.4 us)
Async XLA Ops:
  8.1 21.7 %copy-start.3 = (f32[64,512]{1,0:T(8,128)S(1)}, f32[64,512]{1,0:T(8,128)}, u32[]{:S(2)}) copy-start(f32[64,512]{1,0:T(8,128)} %in_features.1.refs_0_) | copy-start | bytes 393220
  8.1 21.6 %collective-permute-start.2 = (f32[64,512]{1,0:T(8,128)}, f32[64,512]{1,0:T(8,128)S(1)}, u32[]{:S(2)}, u32[]{:S(2)}) collective-permute-start(f32[64,512]{1,0:T(8,128)} %in_features.1.refs_0_), channel_id=1, source_target_pairs={{0,3},{1,2},{2,1},{3,0},{4,7},{5,6},{6,5},{7,4},{8,11},{9,10},{10,... | collective-permute-start | bytes 393224 | tf_op jit(solution)/shard_map/ppermute | solution.py:23
  13.1 16.6 %collective-permute-start.1 = (f32[64,512]{1,0:T(8,128)}, f32[64,512]{1,0:T(8,128)S(1)}, u32[]{:S(2)}, u32[]{:S(2)}) collective-permute-start(f32[64,512]{1,0:T(8,128)} %in_features.1.refs_0_), channel_id=1, source_target_pairs={{0,2},{1,3},{2,0},{3,1},{4,6},{5,7},{6,4},{7,5},{8,10},{9,11},{10,... | collective-permute-start | bytes 393224 | tf_op jit(solution)/shard_map/ppermute | solution.py:23
  13.1 16.6 %collective-permute-start = (f32[64,512]{1,0:T(8,128)}, f32[64,512]{1,0:T(8,128)S(1)}, u32[]{:S(2)}, u32[]{:S(2)}) collective-permute-start(f32[64,512]{1,0:T(8,128)} %in_features.1.refs_0_), channel_id=1, source_target_pairs={{0,1},{1,0},{2,3},{3,2},{4,5},{5,4},{6,7},{7,6},{8,9},{9,8},{10,11... | collective-permute-start | bytes 393224 | tf_op jit(solution)/shard_map/ppermute | solution.py:23
  29.8 1.0 copy-start.2
  31.5 4.9 %collective-permute-start.3 = (f32[2,4096]{1,0:T(2,128)S(1)}, f32[2,4096]{1,0:T(2,128)S(1)}, u32[]{:S(2)}, u32[]{:S(2)}) collective-permute-start(f32[2,4096]{1,0:T(2,128)S(1)} %reshape.11), channel_id=1, source_target_pairs={{0,2},{1,3},{2,0},{3,1},{4,6},{5,7},{6,4},{7,5},{8,10},{9,11},{10,... | collective-permute-start | bytes 98312 | tf_op jit(solution)/shard_map/ppermute | solution.py:23
  36.4 4.0 %collective-permute-start.4 = (f32[2,4096]{1,0:T(2,128)S(1)}, f32[2,4096]{1,0:T(2,128)S(1)}, u32[]{:S(2)}, u32[]{:S(2)}) collective-permute-start(f32[2,4096]{1,0:T(2,128)S(1)} %add.9), channel_id=1, source_target_pairs={{0,1},{1,0},{2,3},{3,2},{4,5},{5,4},{6,7},{7,6},{8,9},{9,8},{10,11... | collective-permute-start | bytes 98312 | tf_op jit(solution)/shard_map/ppermute | solution.py:23
  40.4 8.7 %collective-permute-start.7 = (f32[2,4096]{1,0:T(2,128)S(1)}, f32[2,4096]{1,0:T(2,128)S(1)}, u32[]{:S(2)}, u32[]{:S(2)}) collective-permute-start(f32[2,4096]{1,0:T(2,128)S(1)} %add.10.refs_0_), channel_id=1, source_target_pairs={{0,12},{4,8},{8,4},{12,0},{1,13},{5,9},{9,5},{13,1},{2,14},{6,10},... | collective-permute-start | bytes 98312 | tf_op jit(solution)/shard_map/ppermute | solution.py:23
  40.5 8.6 %collective-permute-start.6 = (f32[2,4096]{1,0:T(2,128)S(1)}, f32[2,4096]{1,0:T(2,128)S(1)}, u32[]{:S(2)}, u32[]{:S(2)}) collective-permute-start(f32[2,4096]{1,0:T(2,128)S(1)} %add.10.refs_0_), channel_id=1, source_target_pairs={{0,8},{4,12},{8,0},{12,4},{1,9},{5,13},{9,1},{13,5},{2,10},{6,14},... | collective-permute-start | bytes 98312 | tf_op jit(solution)/shard_map/ppermute | solution.py:23
  42.3 6.9 %collective-permute-start.5 = (f32[2,4096]{1,0:T(2,128)S(1)}, f32[2,4096]{1,0:T(2,128)S(1)}, u32[]{:S(2)}, u32[]{:S(2)}) collective-permute-start(f32[2,4096]{1,0:T(2,128)S(1)} %add.10.refs_0_), channel_id=1, source_target_pairs={{0,4},{4,0},{8,12},{12,8},{1,5},{5,1},{9,13},{13,9},{2,6},{6,2},{1... | collective-permute-start | bytes 98312 | tf_op jit(solution)/shard_map/ppermute | solution.py:23
  49.2 1.6 %copy-start = (bf16[256,4096]{1,0:T(8,128)(2,1)S(1)}, bf16[256,4096]{1,0:T(8,128)(2,1)}, u32[]{:S(2)}) copy-start(bf16[256,4096]{1,0:T(8,128)(2,1)} %get-tuple-element.24.refs_4_.refs_1_) | copy-start | bytes 6291460
  50.8 1.6 %copy-start.1 = (bf16[256,4096]{1,0:T(8,128)(2,1)S(1)}, bf16[256,4096]{1,0:T(8,128)(2,1)}, u32[]{:S(2)}) copy-start(bf16[256,4096]{1,0:T(8,128)(2,1)} %get-tuple-element.25.refs_5_.refs_2_) | copy-start | bytes 6291460
  67.3 24.8 %copy-start.4 = (bf16[32,4096]{1,0:T(8,128)(2,1)S(1)}, bf16[32,4096]{1,0:T(8,128)(2,1)}, u32[]{:S(2)}) copy-start(bf16[32,4096]{1,0:T(8,128)(2,1)} %refs_8_.1) | copy-start | bytes 786436

commit v7 on v6

--- a/solution.py
+++ b/solution.py
@@ -14,6 +14,7 @@
 LANES = 128
 NT = (((1,), (1,)), ((), ()))
 HIGHEST = lax.Precision.HIGHEST
+ANY_SPEC = pl.BlockSpec(memory_space=pl.ANY)
 VMEM_SPEC = pl.BlockSpec(memory_space=pltpu.VMEM)
 PARAMS = pltpu.CompilerParams(vmem_limit_bytes=16 * 2**20)
 F32 = functools.partial(jax.ShapeDtypeStruct, dtype=jnp.float32)
@@ -41,6 +42,14 @@
     return [value] + [swap(value, axis, size, k) for k in reversed(range(1, size))][::-1]
 
 
+def in_hbm(value):
+    return pltpu.with_memory_space_constraint(value, pltpu.HBM)
+
+
+def in_vmem(value):
+    return pltpu.with_memory_space_constraint(value, pltpu.VMEM)
+
+
 def dot_nt(a, b):
     return lax.dot_general(a, b, NT, precision=HIGHEST, preferred_element_type=jnp.float32)
 
@@ -49,84 +58,109 @@
     return jnp.sum(values, axis=1, keepdims=True)
 
 
-def in_kernel(in_ref, proj_ref, feats_ref, total):
-    step = pl.program_id(0)
-
-    @pl.when(step == 0)
-    def _():
-        total[...] = jnp.zeros_like(total)
-
-    total[...] += lax.dot_general(in_ref[...], proj_ref[...], NT, preferred_element_type=jnp.float32)
-
-    @pl.when(step == pl.num_programs(0) - 1)
-    def _():
-        feats_ref[...] = total[...].T
+def in_kernel(in_ref, proj_ref, feats_ref, held, proj, sems):
+    chunk = held.shape[1] // (sems.shape[0] - 1)
+    spans = [pl.ds(c * chunk, chunk) for c in range(sems.shape[0] - 1)]
+    first = pltpu.make_async_copy(proj_ref, proj, sems.at[len(spans)])
+    copies = [
+        pltpu.make_async_copy(in_ref.at[:, span], held.at[:, span], sems.at[c])
+        for c, span in enumerate(spans)
+    ]
+    first.start()
+    for copy in copies:
+        copy.start()
+    first.wait()
+    feats = jnp.zeros((held.shape[0], proj.shape[0]), jnp.float32)
+    for copy, span in zip(copies, spans):
+        copy.wait()
+        feats += lax.dot_general(held[:, span], proj[:, span], NT, preferred_element_type=jnp.float32)
+    feats_ref[...] = feats.T
 
 
 def in_features(inputs, in_proj):
-    tokens, width = inputs.shape
-    chunk = 1024
     return pl.pallas_call(
         in_kernel,
-        grid=(width // chunk,),
-        out_shape=F32((R_IN, tokens)),
-        in_specs=[
-            pl.BlockSpec((tokens, chunk), lambda i: (0, i)),
-            pl.BlockSpec((R_IN, chunk), lambda i: (0, i)),
+        out_shape=pltpu.VMEM((R_IN, inputs.shape[0]), jnp.float32),
+        in_specs=[ANY_SPEC] * 2,
+        out_specs=VMEM_SPEC,
+        scratch_shapes=[
+            pltpu.VMEM(inputs.shape, jnp.bfloat16),
+            pltpu.VMEM(in_proj.shape, jnp.bfloat16),
+            pltpu.SemaphoreType.DMA((9,)),
         ],
-        out_specs=pl.BlockSpec((R_IN, tokens), lambda i: (0, 0)),
-        scratch_shapes=[pltpu.VMEM((tokens, R_IN), jnp.float32)],
-        compiler_params=pltpu.CompilerParams(vmem_limit_bytes=60 * 2**20),
+        compiler_params=pltpu.CompilerParams(vmem_limit_bytes=16 * 2**20),
         name="in_features",
-    )(inputs, in_proj)
-
-
-def out_kernel(grads_ref, proj_ref, feats_ref, turned):
-    @pl.when(pl.program_id(0) == 0)
-    def _():
-        turned[...] = proj_ref[...].T
-
-    feats = jnp.dot(grads_ref[...], turned[...], preferred_element_type=jnp.float32)
-    feats_ref[...] = feats.T
+    )(in_hbm(inputs), in_hbm(in_proj))
+
+
+def out_kernel(grads_ref, proj_ref, feats_ref, held, proj, turned, sems):
+    tokens = held.shape[0]
+    spans, start = [], 0
+    while start < tokens:
+        rows = 2 * LANES if tokens - start > 2 * LANES else LANES
+        spans.append(pl.ds(start, rows))
+        start += rows
+    first = pltpu.make_async_copy(proj_ref, proj, sems.at[len(spans)])
+    copies = [
+        pltpu.make_async_copy(grads_ref.at[span], held.at[span], sems.at[c])
+        for c, span in enumerate(spans)
+    ]
+    first.start()
+    for copy in copies:
+        copy.start()
+    first.wait()
+    turned[...] = proj[...].T
+    for copy, span in zip(copies, spans):
+        copy.wait()
+        feats = jnp.dot(held[span], turned[...], preferred_element_type=jnp.float32)
+        feats_ref[:, span] = feats.T
 
 
 def out_features(out_grads, out_proj):
     tokens, hidden = out_grads.shape
-    block = 256
     return pl.pallas_call(
         out_kernel,
-        grid=(tokens // block,),
-        out_shape=F32((R_OUT, tokens)),
-        in_specs=[
-            pl.BlockSpec((block, hidden), lambda i: (i, 0)),
-            pl.BlockSpec((R_OUT, hidden), lambda i: (0, 0)),
+        out_shape=pltpu.VMEM((R_OUT, tokens), jnp.float32),
+        in_specs=[ANY_SPEC] * 2,
+        out_specs=VMEM_SPEC,
+        scratch_shapes=[
+            pltpu.VMEM(out_grads.shape, jnp.bfloat16),
+            pltpu.VMEM(out_proj.shape, jnp.bfloat16),
+            pltpu.VMEM((hidden, R_OUT), jnp.bfloat16),
+            pltpu.SemaphoreType.DMA((tokens // LANES + 1,)),
         ],
-        out_specs=pl.BlockSpec((R_OUT, block), lambda i: (0, i)),
-        scratch_shapes=[pltpu.VMEM((hidden, R_OUT), jnp.bfloat16)],
-        compiler_params=pltpu.CompilerParams(vmem_limit_bytes=60 * 2**20),
+        compiler_params=pltpu.CompilerParams(vmem_limit_bytes=40 * 2**20),
         name="out_features",
-    )(out_grads, out_proj)
-
-
-def split_kernel(prior_ref, upper_ref, lower_ref):
-    block = prior_ref[...]
-    upper = block.astype(jnp.bfloat16)
-    upper_ref[...] = upper
-    lower_ref[...] = (block - upper.astype(jnp.float32)).astype(jnp.bfloat16)
+    )(in_hbm(out_grads), in_hbm(out_proj))
+
+
+def split_kernel(prior_ref, upper_ref, lower_ref, held, sems):
+    chunk = held.shape[1] // sems.shape[0]
+    spans = [pl.ds(c * chunk, chunk) for c in range(sems.shape[0])]
+    copies = [
+        pltpu.make_async_copy(prior_ref.at[:, span], held.at[:, span], sems.at[c])
+        for c, span in enumerate(spans)
+    ]
+    for copy in copies:
+        copy.start()
+    for copy, span in zip(copies, spans):
+        copy.wait()
+        block = held[:, span]
+        upper = block.astype(jnp.bfloat16)
+        upper_ref[:, span] = upper
+        lower_ref[:, span] = (block - upper.astype(jnp.float32)).astype(jnp.bfloat16)
 
 
 def split_prior(prior):
-    rows, width = prior.shape
-    spec = pl.BlockSpec((rows, width // 8), lambda i: (0, i))
     return pl.pallas_call(
         split_kernel,
-        grid=(8,),
-        out_shape=(jax.ShapeDtypeStruct(prior.shape, jnp.bfloat16),) * 2,
-        in_specs=[spec],
-        out_specs=(spec, spec),
-        compiler_params=pltpu.CompilerParams(vmem_limit_bytes=56 * 2**20),
+        out_shape=(pltpu.VMEM(prior.shape, jnp.bfloat16),) * 2,
+        in_specs=[ANY_SPEC],
+        out_specs=(VMEM_SPEC,) * 2,
+        scratch_shapes=[pltpu.VMEM(prior.shape, jnp.float32), pltpu.SemaphoreType.DMA((8,))],
+        compiler_params=PARAMS,
         name="split_prior",
-    )(prior)
+    )(in_hbm(prior))
 
 
 def partial_kernel(size, *refs):
@@ -280,7 +314,7 @@
     out_local = out_features(out_grads, out_proj)
     partial = partial_vectors(in_blocks, out_local).reshape(-1, width)
     pieces = direct(sum_over(partial, "tensor", tensor_size), "dp", dp_size)
-    prior_pieces = split_prior(prior)
+    prior_pieces = [in_vmem(piece) for piece in split_prior(prior)]
     vectors, applied_rows, norm = start_cg(pieces, prior_pieces, tensor_size)
     state = None
     for iteration in range(1, ITERS - 1):

time: 106 us -> 91.3 us (0.86)
  Pallas kernels: 39.8 us -> 29.9 us
  local copies, waits for them, and re-layouts: 4.42 us -> 0.21 us
    pallas_call x3, Pallas kernels: 30.9 us -> 20.9 us  [the longest x1 11.9 us: out_features(): pl.pallas_call(out_kernel, out_shape=pltpu.VMEM((R_OUT, tokens), jnp.floa...]
    unnamed x10 -> x2, local copies, waits for them, and re-layouts: 4.22 us -> 0.01 us
  transfers between devices with their start and end apart: 8 -> 8, of which waited for: 2 -> 2; matrix products, arithmetic and copies ran while one was open for 0% -> 0% of each run, Pallas kernels for 22% -> 16%
where the time goes in v7:
time: 91.3 us; the launch traced here: 91.1 us
  blocking collectives  43.4 us (48%)
  Pallas kernels  29.9 us (33%)
  starting transfers between devices  11.7 us (13%)
  waiting for transfers between devices  5.07 us (6%)
    all_to_all x4, blocking collectives, gather(): lax.all_to_all(jnp.broadcast_to(value[None], (size,) + value.shape), axes...  43.4 us
    pallas_call x1, Pallas kernels, out_features(): pl.pallas_call(out_kernel, out_shape=pltpu.VMEM((R_OUT, tokens), jnp.floa...  11.9 us
    ppermute x8, starting transfers between devices, swap(): return lax.ppermute(value, axis, [(i, i ^ bit) for i in range(size)])  11.7 us
    pallas_call x3, Pallas kernels, step_cg(): pl.pallas_call(functools.partial(step_kernel, tensor_size, first, last),...  6.74 us
    pallas_call x1, Pallas kernels, in_features(): pl.pallas_call(in_kernel, out_shape=pltpu.VMEM((R_IN, inputs.shape[0]), j...  6.66 us
    ppermute x8, waiting for transfers between devices, swap(): return lax.ppermute(value, axis, [(i, i ^ bit) for i in range(size)])  5.07 us
    pallas_call x1, Pallas kernels, split_prior(): pl.pallas_call(split_kernel, out_shape=(pltpu.VMEM(prior.shape, jnp.bfloa...  2.32 us
  transfers between devices with their start and end apart: 8, of which 2 were waited for; matrix products, arithmetic and copies ran while one was open for 0% of the time, Pallas kernels for 16%

profile of v7, /device:TPU:0, one launch (start us, length us, event | category | flops | bytes accessed | tf_op | source)
XLA Modules:
  0.0 91.1 jit_solution(4258718108882834750)
XLA Ops:
  0.0 6.7 %in_features.1.refs_0_ = f32[64,512]{1,0:T(8,128)S(1)} custom-call(bf16[512,8192]{1,0:T(8,128)(2,1)} %in_ref.1, bf16[64,8192]{1,0:T(8,128)(2,1)} %proj_ref.2), custom_call_target="tpu_custom_call" | custom-call | tf_op jit(solution)/shard_map/in_features/pallas_call | solution.py:81
  6.7 5.1 %collective-permute-start.2 = (f32[64,512]{1,0:T(8,128)S(1)}, f32[64,512]{1,0:T(8,128)S(1)}, u32[]{:S(2)}, u32[]{:S(2)}) collective-permute-start(f32[64,512]{1,0:T(8,128)S(1)} %in_features.1.refs_0_), channel_id=1, source_target_pairs={{0,3},{1,2},{2,1},{3,0},{4,7},{5,6},{6,5},{7,4},{8,11},{9,10},{10,... | collective-permute-start | bytes 393224 | tf_op jit(solution)/shard_map/ppermute | solution.py:24
  11.8 0.6 collective-permute-start
  12.4 11.9 %out_features.1.refs_4_ = f32[64,2048]{1,0:T(8,128)S(1)} custom-call(bf16[2048,7168]{1,0:T(8,128)(2,1)} %grads_ref.1, bf16[64,7168]{1,0:T(8,128)(2,1)} %proj_ref.3), custom_call_target="tpu_custom_call" | custom-call | tf_op jit(solution)/shard_map/out_features/pallas_call | solution.py:121
  24.4 0.0 collective-permute-done.1.refs_2_
  24.4 0.6 partial_vectors.1
  25.0 0.1 reshape.11
  25.1 2.5 %collective-permute-start.3 = (f32[2,4096]{1,0:T(2,128)S(1)}, f32[2,4096]{1,0:T(2,128)S(1)}, u32[]{:S(2)}, u32[]{:S(2)}) collective-permute-start(f32[2,4096]{1,0:T(2,128)S(1)} %reshape.11), channel_id=1, source_target_pairs={{0,2},{1,3},{2,0},{3,1},{4,6},{5,7},{6,4},{7,5},{8,10},{9,11},{10,... | collective-permute-start | bytes 98312 | tf_op jit(solution)/shard_map/ppermute | solution.py:24
  27.7 2.5 %collective-permute-done.3 = f32[2,4096]{1,0:T(2,128)S(1)} collective-permute-done((f32[2,4096]{1,0:T(2,128)S(1)}, f32[2,4096]{1,0:T(2,128)S(1)}, u32[]{:S(2)}, u32[]{:S(2)}) %collective-permute-start.3) | collective-permute-done | bytes 32800 | tf_op jit(solution)/shard_map/ppermute | solution.py:24
  30.2 1.5 %collective-permute-start.4 = (f32[2,4096]{1,0:T(2,128)S(1)}, f32[2,4096]{1,0:T(2,128)S(1)}, u32[]{:S(2)}, u32[]{:S(2)}) collective-permute-start(f32[2,4096]{1,0:T(2,128)S(1)} %add.9), channel_id=1, source_target_pairs={{0,1},{1,0},{2,3},{3,2},{4,5},{5,4},{6,7},{7,6},{8,9},{9,8},{10,11... | collective-permute-start | bytes 98312 | tf_op jit(solution)/shard_map/ppermute | solution.py:24
  31.7 2.5 %collective-permute-done.4 = f32[2,4096]{1,0:T(2,128)S(1)} collective-permute-done((f32[2,4096]{1,0:T(2,128)S(1)}, f32[2,4096]{1,0:T(2,128)S(1)}, u32[]{:S(2)}, u32[]{:S(2)}) %collective-permute-start.4) | collective-permute-done | bytes 32800 | tf_op jit(solution)/shard_map/ppermute | solution.py:24
  34.2 0.1 collective-permute-start.7
  34.3 1.7 %collective-permute-start.6 = (f32[2,4096]{1,0:T(2,128)S(1)}, f32[2,4096]{1,0:T(2,128)S(1)}, u32[]{:S(2)}, u32[]{:S(2)}) collective-permute-start(f32[2,4096]{1,0:T(2,128)S(1)} %add.10.refs_0_), channel_id=1, source_target_pairs={{0,8},{4,12},{8,0},{12,4},{1,9},{5,13},{9,1},{13,5},{2,10},{6,14},... | collective-permute-start | bytes 98312 | tf_op jit(solution)/shard_map/ppermute | solution.py:24
  36.0 0.2 collective-permute-start.5
  36.1 2.3 %split_prior.1 = (bf16[256,4096]{1,0:T(8,128)(2,1)S(1)}, bf16[256,4096]{1,0:T(8,128)(2,1)S(1)}) custom-call(f32[256,4096]{1,0:T(8,128)} %prior_ref.1), custom_call_target="tpu_custom_call" | custom-call | tf_op jit(solution)/shard_map/split_prior/pallas_call | solution.py:155
  38.5 1.6 %cg_start.1 = (f32[8,4096]{1,0:T(8,128)S(1)}, f32[8,256]{1,0:T(8,128)S(1)}, f32[8,128]{1,0:T(8,128)S(1)}) custom-call(f32[2,4096]{1,0:T(2,128)S(1)} %add.10.refs_0_, f32[2,4096]{1,0:T(2,128)S(1)} %collective-permute-done.5.refs_1_, f32[2,4096]{1,0:T(2,128)S(1)} %collective-permute-done.6.refs_2_, f32[2,4096]{1,0:T(2,128)S(1)} %collective-permute-done.7.refs_3_, ...), custom_call_target="tpu_custom_call" | custom-call | tf_op jit(solution)/shard_map/cg_start/pallas_call | solution.py:230
  40.2 13.2 %all_to_all.20.refs_0_ = f32[16,8,256]{2,1,0:T(8,128)S(1)} all-to-all(f32[16,8,256]{2,1,0:T(8,128)S(1)} %broadcast_in_dim.10), channel_id=1, replica_groups=mesh['groups'=2,'dp'=4,'tensor'=4] {'dp','tensor'}, dimensions={0} | all-to-all | bytes 262144 | tf_op jit(solution)/shard_map/all_to_all | solution.py:32
  53.4 2.0 %cg_step.3 = (f32[8,256]{1,0:T(8,128)S(1)}, f32[8,128]{1,0:T(8,128)S(1)}, f32[8,4096]{1,0:T(8,128)S(1)}, f32[8,4096]{1,0:T(8,128)S(1)}, f32[8,4096]{1,0:T(8,128)S(1)}) custom-call(f32[16,8,256]{2,1,0:T(8,128)S(1)} %all_to_all.20.refs_0_, bf16[256,4096]{1,0:T(8,128)(2,1)S(1)} %get-tuple-element.24.refs_4_.refs_1_, ...), custom_call_target="tpu_custom_call" | custom-call | tf_op jit(solution)/shard_map/cg_step/pallas_call | solution.py:299
  55.4 10.4 %all_to_all.21.refs_0_ = f32[16,8,256]{2,1,0:T(8,128)S(1)} all-to-all(f32[16,8,256]{2,1,0:T(8,128)S(1)} %broadcast_in_dim.11), channel_id=1, replica_groups=mesh['groups'=2,'dp'=4,'tensor'=4] {'dp','tensor'}, dimensions={0} | all-to-all | bytes 262144 | tf_op jit(solution)/shard_map/all_to_all | solution.py:32
  65.8 2.0 %cg_step.4 = (f32[8,256]{1,0:T(8,128)S(1)}, f32[8,128]{1,0:T(8,128)S(1)}, f32[8,4096]{1,0:T(8,128)S(1)}, f32[8,4096]{1,0:T(8,128)S(1)}, f32[8,4096]{1,0:T(8,128)S(1)}) custom-call(f32[16,8,256]{2,1,0:T(8,128)S(1)} %all_to_all.21.refs_0_, bf16[256,4096]{1,0:T(8,128)(2,1)S(1)} %get-tuple-element.24.refs_4_.refs_1_, ...), custom_call_target="tpu_custom_call" | custom-call | tf_op jit(solution)/shard_map/cg_step/pallas_call | solution.py:299
  67.8 10.4 %all_to_all.22.refs_0_ = f32[16,8,256]{2,1,0:T(8,128)S(1)} all-to-all(f32[16,8,256]{2,1,0:T(8,128)S(1)} %broadcast_in_dim.12), channel_id=1, replica_groups=mesh['groups'=2,'dp'=4,'tensor'=4] {'dp','tensor'}, dimensions={0} | all-to-all | bytes 262144 | tf_op jit(solution)/shard_map/all_to_all | solution.py:32
  78.1 2.8 %cg_step.5 = (f32[1,128]{1,0:T(1,128)S(1)}, f32[1,128]{1,0:T(1,128)S(1)}, f32[8,32]{1,0:T(8,128)S(1)}, f32[8,32]{1,0:T(8,128)S(1)}) custom-call(f32[16,8,256]{2,1,0:T(8,128)S(1)} %all_to_all.22.refs_0_, bf16[256,4096]{1,0:T(8,128)(2,1)S(1)} %get-tuple-element.24.refs_4_.refs_1_, bf16[256,4096]{1,0:T(8,128)(2,1)S(1)} %get-tuple-element.25.refs_5_.refs_2_, ...), custom_call_target="tpu_custom_call" | custom-call | tf_op jit(solution)/shard_map/cg_step/pallas_call | solution.py:299
  81.0 9.4 %all_to_all.23 = f32[16,1,128]{2,1,0:T(1,128)S(1)} all-to-all(f32[16,1,128]{2,1,0:T(1,128)S(1)} %broadcast_in_dim.14), channel_id=1, replica_groups=mesh['groups'=2,'dp'=4,'tensor'=4] {'dp','tensor'}, dimensions={0} | all-to-all | bytes 16384 | tf_op jit(solution)/shard_map/all_to_all | solution.py:32
  90.4 0.7 multiply_add_fusion
  (17 shorter events, 0.2 us)
Async XLA Ops:
  6.7 17.7 %collective-permute-start.2 = (f32[64,512]{1,0:T(8,128)S(1)}, f32[64,512]{1,0:T(8,128)S(1)}, u32[]{:S(2)}, u32[]{:S(2)}) collective-permute-start(f32[64,512]{1,0:T(8,128)S(1)} %in_features.1.refs_0_), channel_id=1, source_target_pairs={{0,3},{1,2},{2,1},{3,0},{4,7},{5,6},{6,5},{7,4},{8,11},{9,10},{10,... | collective-permute-start | bytes 393224 | tf_op jit(solution)/shard_map/ppermute | solution.py:24
  11.8 12.6 %collective-permute-start.1 = (f32[64,512]{1,0:T(8,128)S(1)}, f32[64,512]{1,0:T(8,128)S(1)}, u32[]{:S(2)}, u32[]{:S(2)}) collective-permute-start(f32[64,512]{1,0:T(8,128)S(1)} %in_features.1.refs_0_), channel_id=1, source_target_pairs={{0,2},{1,3},{2,0},{3,1},{4,6},{5,7},{6,4},{7,5},{8,10},{9,11},{10,... | collective-permute-start | bytes 393224 | tf_op jit(solution)/shard_map/ppermute | solution.py:24
  11.8 12.6 %collective-permute-start = (f32[64,512]{1,0:T(8,128)S(1)}, f32[64,512]{1,0:T(8,128)S(1)}, u32[]{:S(2)}, u32[]{:S(2)}) collective-permute-start(f32[64,512]{1,0:T(8,128)S(1)} %in_features.1.refs_0_), channel_id=1, source_target_pairs={{0,1},{1,0},{2,3},{3,2},{4,5},{5,4},{6,7},{7,6},{8,9},{9,8},{10,11... | collective-permute-start | bytes 393224 | tf_op jit(solution)/shard_map/ppermute | solution.py:24
  25.1 5.1 %collective-permute-start.3 = (f32[2,4096]{1,0:T(2,128)S(1)}, f32[2,4096]{1,0:T(2,128)S(1)}, u32[]{:S(2)}, u32[]{:S(2)}) collective-permute-start(f32[2,4096]{1,0:T(2,128)S(1)} %reshape.11), channel_id=1, source_target_pairs={{0,2},{1,3},{2,0},{3,1},{4,6},{5,7},{6,4},{7,5},{8,10},{9,11},{10,... | collective-permute-start | bytes 98312 | tf_op jit(solution)/shard_map/ppermute | solution.py:24
  30.2 4.0 %collective-permute-start.4 = (f32[2,4096]{1,0:T(2,128)S(1)}, f32[2,4096]{1,0:T(2,128)S(1)}, u32[]{:S(2)}, u32[]{:S(2)}) collective-permute-start(f32[2,4096]{1,0:T(2,128)S(1)} %add.9), channel_id=1, source_target_pairs={{0,1},{1,0},{2,3},{3,2},{4,5},{5,4},{6,7},{7,6},{8,9},{9,8},{10,11... | collective-permute-start | bytes 98312 | tf_op jit(solution)/shard_map/ppermute | solution.py:24
  34.2 4.3 %collective-permute-start.7 = (f32[2,4096]{1,0:T(2,128)S(1)}, f32[2,4096]{1,0:T(2,128)S(1)}, u32[]{:S(2)}, u32[]{:S(2)}) collective-permute-start(f32[2,4096]{1,0:T(2,128)S(1)} %add.10.refs_0_), channel_id=1, source_target_pairs={{0,12},{4,8},{8,4},{12,0},{1,13},{5,9},{9,5},{13,1},{2,14},{6,10},... | collective-permute-start | bytes 98312 | tf_op jit(solution)/shard_map/ppermute | solution.py:24
  34.3 4.2 %collective-permute-start.6 = (f32[2,4096]{1,0:T(2,128)S(1)}, f32[2,4096]{1,0:T(2,128)S(1)}, u32[]{:S(2)}, u32[]{:S(2)}) collective-permute-start(f32[2,4096]{1,0:T(2,128)S(1)} %add.10.refs_0_), channel_id=1, source_target_pairs={{0,8},{4,12},{8,0},{12,4},{1,9},{5,13},{9,1},{13,5},{2,10},{6,14},... | collective-permute-start | bytes 98312 | tf_op jit(solution)/shard_map/ppermute | solution.py:24
  36.0 2.5 %collective-permute-start.5 = (f32[2,4096]{1,0:T(2,128)S(1)}, f32[2,4096]{1,0:T(2,128)S(1)}, u32[]{:S(2)}, u32[]{:S(2)}) collective-permute-start(f32[2,4096]{1,0:T(2,128)S(1)} %add.10.refs_0_), channel_id=1, source_target_pairs={{0,4},{4,0},{8,12},{12,8},{1,5},{5,1},{9,13},{13,9},{2,6},{6,2},{1... | collective-permute-start | bytes 98312 | tf_op jit(solution)/shard_map/ppermute | solution.py:24
  53.4 24.8 %copy-start = (bf16[32,4096]{1,0:T(8,128)(2,1)S(1)}, bf16[32,4096]{1,0:T(8,128)(2,1)}, u32[]{:S(2)}) copy-start(bf16[32,4096]{1,0:T(8,128)(2,1)} %refs_8_.1) | copy-start | bytes 786436

commit v8 on v7

v8 whole, which is shorter than its diff:
```python
import functools

import jax
import jax.numpy as jnp
from jax import lax
from jax.experimental import pallas as pl
from jax.experimental.pallas import tpu as pltpu
from jax.sharding import PartitionSpec as P

R_IN = 64
R_OUT = 64
SEQ = 1024
ITERS = 4
LANES = 128
NT = (((1,), (1,)), ((), ()))
HIGHEST = lax.Precision.HIGHEST
ANY_SPEC = pl.BlockSpec(memory_space=pl.ANY)
VMEM_SPEC = pl.BlockSpec(memory_space=pltpu.VMEM)
PARAMS = pltpu.CompilerParams(vmem_limit_bytes=16 * 2**20)
F32 = functools.partial(jax.ShapeDtypeStruct, dtype=jnp.float32)


def swap(value, axis, size, bit):
    return lax.ppermute(value, axis, [(i, i ^ bit) for i in range(size)])


def bits(size):
    return [1 << b for b in reversed(range(size.bit_length() - 1))]


def gather(value, axes, size):
    return lax.all_to_all(jnp.broadcast_to(value[None], (size,) + value.shape), axes, 0, 0)


def sum_over(value, axis, size):
    for bit in bits(size):
        value = value + swap(value, axis, size, bit)
    return value


def direct(value, axis, size):
    return [value] + [swap(value, axis, size, k) for k in reversed(range(1, size))][::-1]


def in_hbm(value):
    return pltpu.with_memory_space_constraint(value, pltpu.HBM)


def in_vmem(value):
    return pltpu.with_memory_space_constraint(value, pltpu.VMEM)


def dot_nt(a, b):
    return lax.dot_general(a, b, NT, precision=HIGHEST, preferred_element_type=jnp.float32)


def row_sum(values):
    return jnp.sum(values, axis=1, keepdims=True)


def row_spans(rows, sizes):
    spans, start = [], 0
    while start < rows:
        while len(sizes) > 1 and start + sizes[0] + sizes[-1] > rows:
            sizes = sizes[1:]
        spans.append(pl.ds(start, sizes[0]))
        start += sizes[0]
        sizes = sizes[1:] or sizes
    return spans


def stream_kernel(spans, rows_ref, proj_ref, feats_ref, held, proj, sems):
    first = pltpu.make_async_copy(proj_ref, proj, sems.at[len(spans)])
    copies = [
        pltpu.make_async_copy(rows_ref.at[span], held.at[span], sems.at[c])
        for c, span in enumerate(spans)
    ]
    first.start()
    for copy in copies:
        copy.start()
    first.wait()
    for copy, span in zip(copies, spans):
        copy.wait()
        feats = lax.dot_general(held[span], proj[...], NT, preferred_element_type=jnp.float32)
        feats_ref[:, span] = feats.T


def features(rows, proj, sizes, limit, name):
    spans = row_spans(rows.shape[0], sizes)
    return pl.pallas_call(
        functools.partial(stream_kernel, spans),
        out_shape=pltpu.VMEM((proj.shape[0], rows.shape[0]), jnp.float32),
        in_specs=[ANY_SPEC] * 2,
        out_specs=VMEM_SPEC,
        scratch_shapes=[
            pltpu.VMEM(rows.shape, jnp.bfloat16),
            pltpu.VMEM(proj.shape, jnp.bfloat16),
            pltpu.SemaphoreType.DMA((len(spans) + 1,)),
        ],
        compiler_params=pltpu.CompilerParams(vmem_limit_bytes=limit * 2**20),
        name=name,
    )(in_hbm(rows), in_hbm(proj))


def split_kernel(prior_ref, upper_ref, lower_ref, held, sems):
    chunk = held.shape[1] // sems.shape[0]
    spans = [pl.ds(c * chunk, chunk) for c in range(sems.shape[0])]
    copies = [
        pltpu.make_async_copy(prior_ref.at[:, span], held.at[:, span], sems.at[c])
        for c, span in enumerate(spans)
    ]
    for copy in copies:
        copy.start()
    for copy, span in zip(copies, spans):
        copy.wait()
        block = held[:, span]
        upper = block.astype(jnp.bfloat16)
        upper_ref[:, span] = upper
        lower_ref[:, span] = (block - upper.astype(jnp.float32)).astype(jnp.bfloat16)


def split_prior(prior):
    return pl.pallas_call(
        split_kernel,
        out_shape=(pltpu.VMEM(prior.shape, jnp.bfloat16),) * 2,
        in_specs=[ANY_SPEC],
        out_specs=(VMEM_SPEC,) * 2,
        scratch_shapes=[pltpu.VMEM(prior.shape, jnp.float32), pltpu.SemaphoreType.DMA((8,))],
        compiler_params=PARAMS,
        name="split_prior",
    )(in_hbm(prior))


def partial_kernel(size, *refs):
    blocks, (out_ref, part_ref, held) = refs[:size], refs[size:]
    me = lax.axis_index("tensor")
    tokens = blocks[0].shape[1]
    for k, block in enumerate(blocks):
        start = pl.multiple_of((me ^ k) * tokens, LANES)
        held[:, pl.ds(start, tokens)] = block[...]
    for s in range(part_ref.shape[0]):
        span = slice(s * SEQ, (s + 1) * SEQ)
        part_ref[s] = dot_nt(held[:, span], out_ref[:, span]) * (1.0 / SEQ)


def partial_vectors(blocks, out_local):
    seq_count = out_local.shape[1] // SEQ
    return pl.pallas_call(
        functools.partial(partial_kernel, len(blocks)),
        out_shape=F32((seq_count, R_IN, R_OUT)),
        in_specs=[VMEM_SPEC] * (len(blocks) + 1),
        out_specs=VMEM_SPEC,
        scratch_shapes=[pltpu.VMEM(out_local.shape, jnp.float32)],
        compiler_params=PARAMS,
        name="partial_vectors",
    )(*blocks, out_local)


def own_columns(ref, me, count):
    if count % LANES == 0:
        return ref[:, pl.ds(pl.multiple_of(me * count, LANES), count)]
    per = LANES // count
    held = ref[:, pl.ds(pl.multiple_of((me // per) * LANES, LANES), LANES)]
    return pltpu.roll(held, LANES - (me % per) * count, 1)[:, :count]


def pieces_of(values, count):
    held = []
    for _ in range(count):
        piece = values.astype(jnp.bfloat16)
        held.append(piece)
        values = values - piece.astype(jnp.float32)
    return jnp.concatenate(held, axis=0)


def dot_pieces(a, b, seqs):
    held = lax.dot_general(a, b, NT, preferred_element_type=jnp.float32)
    total = held[:seqs]
    for start in range(seqs, held.shape[0], seqs):
        total = total + held[start : start + seqs]
    return total


def apply_fisher(pieces, vectors_ref, vector_pieces, upper_ref, lower_ref, me):
    seqs = vectors_ref.shape[0]
    applied = dot_pieces(pieces, upper_ref[...], seqs)
    applied = applied + dot_pieces(pieces[: 2 * seqs], lower_ref[...], seqs)
    weights = dot_pieces(pieces, vector_pieces, seqs)
    weights = (weights[:, :seqs] + weights[:, seqs:]) * (1.0 / seqs)
    own = own_columns(vectors_ref, me, upper_ref.shape[0])
    return applied + jnp.dot(weights, own, precision=HIGHEST, preferred_element_type=jnp.float32)


def flat_index(tensor_size):
    return lax.axis_index("dp") * tensor_size + lax.axis_index("tensor")


def start_kernel(size, tensor_size, *refs):
    pieces, refs = refs[:size], refs[size:]
    upper_ref, lower_ref, vectors_ref, vector_pieces_ref, scale_ref, applied_ref, norm_ref, held = refs
    dp = lax.axis_index("dp")
    for k, piece in enumerate(pieces):
        held[dp ^ k] = piece[...]
    vectors = jnp.concatenate([held[k] for k in range(size)], axis=0)
    vectors_ref[...] = vectors
    split = pieces_of(vectors, 3)
    vector_pieces = split[: 2 * vectors.shape[0]]
    vector_pieces_ref[...] = vector_pieces
    norm = jnp.broadcast_to(row_sum(vectors * vectors), norm_ref.shape)
    norm_ref[...] = norm
    spread = jnp.sum(norm, axis=0, keepdims=True) * (1.0 / vectors.shape[0])
    scale_ref[...] = jnp.broadcast_to(1.0 / (1.0 + spread), scale_ref.shape)
    me = flat_index(tensor_size)
    applied_ref[...] = apply_fisher(split, vectors_ref, vector_pieces, upper_ref, lower_ref, me)


def start_cg(pieces, prior_pieces, tensor_size):
    size, seqs = len(pieces), len(pieces) * pieces[0].shape[0]
    rows, width = prior_pieces[0].shape
    vector_pieces = jax.ShapeDtypeStruct((2 * seqs, width), jnp.bfloat16)
    column = F32((seqs, LANES))
    return pl.pallas_call(
        functools.partial(start_kernel, size, tensor_size),
        out_shape=(F32((seqs, width)), vector_pieces, column, F32((seqs, rows)), column),
        in_specs=[VMEM_SPEC] * (size + 2),
        out_specs=(VMEM_SPEC,) * 5,
        scratch_shapes=[pltpu.VMEM((size,) + pieces[0].shape, jnp.float32)],
        compiler_params=PARAMS,
        name="cg_start",
    )(*pieces, *prior_pieces)


def on_lanes(column):
    seqs = column.shape[0]
    row = lax.broadcasted_iota(jnp.int32, (seqs, LANES), 0)
    lane = lax.broadcasted_iota(jnp.int32, (seqs, LANES), 1)
    return jnp.sum(jnp.where(row == lane, column, 0.0), axis=0, keepdims=True)


def step_kernel(tensor_size, first, last, *refs):
    blocks_ref, upper_ref, lower_ref, vectors_ref, vector_pieces_ref, scale_ref = refs[:6]
    norm_ref, fisher_direction_ref = refs[6:8]
    refs = refs[8:]
    if not first:
        fisher_residual_ref, direction_ref, residual_ref, solution_ref = refs[:4]
        refs = refs[4:]
    if last:
        curvature_out, norm_out, direction_out, solution_out, held = refs
    else:
        fisher_direction_out, norm_out, fisher_residual_out, direction_out, residual_out, solution_out, held = refs
    me = flat_index(tensor_size)
    count, _, rows = blocks_ref.shape
    for i in range(count):
        held[:, i * rows : (i + 1) * rows] = blocks_ref[i]
    applied = held[...]
    scale = scale_ref[...][:, :1]
    twice = apply_fisher(
        pieces_of(scale * applied, 3), vectors_ref, vector_pieces_ref[...], upper_ref, lower_ref, me
    )
    direction = vectors_ref[...] if first else direction_ref[...]
    residual = direction if first else residual_ref[...]
    norm = norm_ref[...][:, :1]
    step = norm / row_sum(direction * applied)
    solution = step * direction
    if not first:
        solution = solution_ref[...] + solution
    residual = residual - step * applied
    norm_next = row_sum(residual * residual)
    share = norm_next / norm
    direction = residual + share * direction
    fisher_direction = fisher_direction_ref[...]
    fisher_residual = (fisher_direction if first else fisher_residual_ref[...]) - (step / scale) * twice
    fisher_direction = fisher_residual + share * fisher_direction
    direction_out[...] = direction
    solution_out[...] = solution
    if last:
        own = own_columns(direction_out, me, rows)
        curvature_out[...] = on_lanes(row_sum(own * fisher_direction))
        norm_out[...] = on_lanes(norm_next)
    else:
        fisher_direction_out[...] = fisher_direction
        fisher_residual_out[...] = fisher_residual
        residual_out[...] = residual
        norm_out[...] = jnp.broadcast_to(norm_next, norm_out.shape)


def step_cg(blocks, fixed, norm, state, last, tensor_size):
    first = len(state) == 1
    whole, rows = F32(fixed[2].shape), F32(state[0].shape)
    row = F32((1, LANES))
    operands = [blocks, *fixed, norm, *state]
    out_shape = (row, row, whole, whole) if last else (rows, F32(norm.shape), rows, whole, whole, whole)
    return pl.pallas_call(
        functools.partial(step_kernel, tensor_size, first, last),
        out_shape=out_shape,
        in_specs=[VMEM_SPEC] * len(operands),
        out_specs=(VMEM_SPEC,) * len(out_shape),
        scratch_shapes=[pltpu.VMEM(whole.shape, jnp.float32)],
        compiler_params=PARAMS,
        name="cg_step",
    )(*operands)


def score_kernel(solution_ref, direction_ref, queries_ref, solved_ref, along_ref):
    seqs = solution_ref.shape[0]
    both = jnp.concatenate([solution_ref[...], direction_ref[...]], axis=0)
    scores = dot_pieces(pieces_of(both, 3), queries_ref[...], 2 * seqs)
    solved_ref[...] = scores[:seqs]
    along_ref[...] = scores[seqs:]


def score(solution, direction, queries):
    scores = F32((solution.shape[0], queries.shape[0]))
    return pl.pallas_call(
        score_kernel,
        out_shape=(scores, scores),
        in_specs=[VMEM_SPEC] * 3,
        out_specs=(VMEM_SPEC,) * 2,
        compiler_params=PARAMS,
        name="scores",
    )(solution, direction, queries)


def on_device(dp_size, tensor_size, inputs, in_proj, out_grads, out_proj, prior, queries):
    width = R_IN * R_OUT
    both, devices = ("dp", "tensor"), dp_size * tensor_size
    in_blocks = direct(features(inputs, in_proj, (256, 128), 16, "in_features"), "tensor", tensor_size)
    out_local = features(out_grads, out_proj, (512, 512, 512, 256, 128), 40, "out_features")
    partial = partial_vectors(in_blocks, out_local).reshape(-1, width)
    pieces = direct(sum_over(partial, "tensor", tensor_size), "dp", dp_size)
    prior_pieces = [in_vmem(piece) for piece in split_prior(prior)]
    vectors, vector_pieces, scale, applied_rows, norm = start_cg(pieces, prior_pieces, tensor_size)
    fixed = (*prior_pieces, vectors, vector_pieces, scale)
    state = [applied_rows]
    for iteration in range(1, ITERS - 1):
        blocks = gather(state[0], both, devices)
        applied_rows, norm, *others = step_cg(blocks, fixed, norm, state, False, tensor_size)
        state = [applied_rows, *others]
    blocks = gather(state[0], both, devices)
    curvature, norm, direction, solved = step_cg(blocks, fixed, norm, state, True, tensor_size)
    curvature = jnp.sum(gather(curvature, both, devices), axis=0)
    solved, along = score(solved, direction, queries)
    step = (norm / curvature)[0, : solved.shape[0]]
    return solved + step[:, None] * along


def solution(mesh):
    return jax.shard_map(
        functools.partial(on_device, mesh.shape["dp"], mesh.shape["tensor"]),
        mesh=mesh,
        in_specs=(
            P(("groups", "dp", "tensor"), None),
            P(),
            P(("groups", "dp"), "tensor"),
            P(None, "tensor"),
            P(("groups", "dp", "tensor"), None),
            P(("groups", "dp", "tensor"), None),
        ),
        out_specs=P("groups", ("dp", "tensor")),
        check_vma=False,
    )
```

time: 91.3 us -> 98.5 us (1.079)
  blocking collectives: 43.4 us -> 34 us
  Pallas kernels: 29.9 us -> 36.6 us
  waiting for transfers between devices: 5.07 us -> 11.1 us
  starting transfers between devices: 11.7 us -> 14.9 us
    all_to_all x4 -> x3, blocking collectives: 43.4 us -> 34 us  [gather(): lax.all_to_all(jnp.broadcast_to(value[None], (size,) + value.shape), axes...]
    pallas_call x2 -> x3, Pallas kernels: 18.6 us -> 27.3 us  [the longest x2 27 us: features(): pl.pallas_call(functools.partial(stream_kernel, spans), out_shape=pltpu.V...]
    all_to_all x0 -> x1, waiting for transfers between devices: none -> 6.03 us  [gather(): lax.all_to_all(jnp.broadcast_to(value[None], (size,) + value.shape), axes...]
    all_to_all x0 -> x1, starting transfers between devices: none -> 3.45 us  [gather(): lax.all_to_all(jnp.broadcast_to(value[None], (size,) + value.shape), axes...]
    pallas_call x3, Pallas kernels: 6.74 us -> 4.85 us  [step_cg(): pl.pallas_call(functools.partial(step_kernel, tensor_size, first, last),...]
  transfers between devices with their start and end apart: 8 -> 9, of which waited for: 2 -> 3; matrix products, arithmetic and copies ran while one was open for 0% -> 0% of each run, Pallas kernels for 16% -> 23%
where the time goes in v8:
time: 98.5 us; the launch traced here: 98.2 us
  Pallas kernels  36.6 us (37%)
  blocking collectives  34 us (35%)
  starting transfers between devices  14.9 us (15%)
  waiting for transfers between devices  11.1 us (11%)
    all_to_all x3, blocking collectives, gather(): lax.all_to_all(jnp.broadcast_to(value[None], (size,) + value.shape), axes...  34 us
    pallas_call x2, Pallas kernels, features(): pl.pallas_call(functools.partial(stream_kernel, spans), out_shape=pltpu.V...  27 us
    ppermute x8, starting transfers between devices, swap(): return lax.ppermute(value, axis, [(i, i ^ bit) for i in range(size)])  11.5 us
    all_to_all x1, waiting for transfers between devices, gather(): lax.all_to_all(jnp.broadcast_to(value[None], (size,) + value.shape), axes...  6.03 us
    ppermute x8, waiting for transfers between devices, swap(): return lax.ppermute(value, axis, [(i, i ^ bit) for i in range(size)])  5.06 us
    pallas_call x3, Pallas kernels, step_cg(): pl.pallas_call(functools.partial(step_kernel, tensor_size, first, last),...  4.85 us
    all_to_all x1, starting transfers between devices, gather(): lax.all_to_all(jnp.broadcast_to(value[None], (size,) + value.shape), axes...  3.45 us
    pallas_call x1, Pallas kernels, split_prior(): pl.pallas_call(split_kernel, out_shape=(pltpu.VMEM(prior.shape, jnp.bfloa...  2.32 us
  transfers between devices with their start and end apart: 9, of which 3 were waited for; matrix products, arithmetic and copies ran while one was open for 0% of the time, Pallas kernels for 23%

profile of v8, /device:TPU:0, one launch (start us, length us, event | category | flops | bytes accessed | tf_op | source)
XLA Modules:
  0.0 98.2 jit_solution(3289244794024299923)
XLA Ops:
  0.0 7.4 %in_features.1.refs_0_ = f32[64,512]{1,0:T(8,128)S(1)} custom-call(bf16[512,8192]{1,0:T(8,128)(2,1)} %rows_ref.2, bf16[64,8192]{1,0:T(8,128)(2,1)} %proj_ref.2), custom_call_target="tpu_custom_call" | custom-call | tf_op jit(solution)/shard_map/in_features/pallas_call | solution.py:90
  7.4 5.1 %collective-permute-start.2 = (f32[64,512]{1,0:T(8,128)S(1)}, f32[64,512]{1,0:T(8,128)S(1)}, u32[]{:S(2)}, u32[]{:S(2)}) collective-permute-start(f32[64,512]{1,0:T(8,128)S(1)} %in_features.1.refs_0_), channel_id=1, source_target_pairs={{0,3},{1,2},{2,1},{3,0},{4,7},{5,6},{6,5},{7,4},{8,11},{9,10},{10,... | collective-permute-start | bytes 393224 | tf_op jit(solution)/shard_map/ppermute | solution.py:24
  12.5 0.6 collective-permute-start
  13.2 19.6 %out_features.1.refs_4_ = f32[64,2048]{1,0:T(8,128)S(1)} custom-call(bf16[2048,7168]{1,0:T(8,128)(2,1)} %rows_ref.3, bf16[64,7168]{1,0:T(8,128)(2,1)} %proj_ref.3), custom_call_target="tpu_custom_call" | custom-call | tf_op jit(solution)/shard_map/out_features/pallas_call | solution.py:90
  32.9 0.6 partial_vectors.1
  33.6 2.4 %collective-permute-start.3 = (f32[2,4096]{1,0:T(2,128)S(1)}, f32[2,4096]{1,0:T(2,128)S(1)}, u32[]{:S(2)}, u32[]{:S(2)}) collective-permute-start(f32[2,4096]{1,0:T(2,128)S(1)} %reshape.11), channel_id=1, source_target_pairs={{0,2},{1,3},{2,0},{3,1},{4,6},{5,7},{6,4},{7,5},{8,10},{9,11},{10,... | collective-permute-start | bytes 98312 | tf_op jit(solution)/shard_map/ppermute | solution.py:24
  35.9 2.5 %collective-permute-done.3 = f32[2,4096]{1,0:T(2,128)S(1)} collective-permute-done((f32[2,4096]{1,0:T(2,128)S(1)}, f32[2,4096]{1,0:T(2,128)S(1)}, u32[]{:S(2)}, u32[]{:S(2)}) %collective-permute-start.3) | collective-permute-done | bytes 32800 | tf_op jit(solution)/shard_map/ppermute | solution.py:24
  38.5 1.5 %collective-permute-start.4 = (f32[2,4096]{1,0:T(2,128)S(1)}, f32[2,4096]{1,0:T(2,128)S(1)}, u32[]{:S(2)}, u32[]{:S(2)}) collective-permute-start(f32[2,4096]{1,0:T(2,128)S(1)} %add.9), channel_id=1, source_target_pairs={{0,1},{1,0},{2,3},{3,2},{4,5},{5,4},{6,7},{7,6},{8,9},{9,8},{10,11... | collective-permute-start | bytes 98312 | tf_op jit(solution)/shard_map/ppermute | solution.py:24
  39.9 2.5 %collective-permute-done.4 = f32[2,4096]{1,0:T(2,128)S(1)} collective-permute-done((f32[2,4096]{1,0:T(2,128)S(1)}, f32[2,4096]{1,0:T(2,128)S(1)}, u32[]{:S(2)}, u32[]{:S(2)}) %collective-permute-start.4) | collective-permute-done | bytes 32800 | tf_op jit(solution)/shard_map/ppermute | solution.py:24
  42.6 1.7 %collective-permute-start.6 = (f32[2,4096]{1,0:T(2,128)S(1)}, f32[2,4096]{1,0:T(2,128)S(1)}, u32[]{:S(2)}, u32[]{:S(2)}) collective-permute-start(f32[2,4096]{1,0:T(2,128)S(1)} %add.10.refs_0_), channel_id=1, source_target_pairs={{0,8},{4,12},{8,0},{12,4},{1,9},{5,13},{9,1},{13,5},{2,10},{6,14},... | collective-permute-start | bytes 98312 | tf_op jit(solution)/shard_map/ppermute | solution.py:24
  44.3 0.2 collective-permute-start.5
  44.4 2.3 %split_prior.1 = (bf16[256,4096]{1,0:T(8,128)(2,1)S(1)}, bf16[256,4096]{1,0:T(8,128)(2,1)S(1)}) custom-call(f32[256,4096]{1,0:T(8,128)} %prior_ref.1), custom_call_target="tpu_custom_call" | custom-call | tf_op jit(solution)/shard_map/split_prior/pallas_call | solution.py:123
  46.8 1.5 %cg_start.1 = (f32[8,4096]{1,0:T(8,128)S(1)}, bf16[16,4096]{1,0:T(8,128)(2,1)S(1)}, f32[8,128]{1,0:T(8,128)S(1)}, f32[8,256]{1,0:T(8,128)S(1)}, f32[8,128]{1,0:T(8,128)S(1)}) custom-call(f32[2,4096]{1,0:T(2,128)S(1)} %add.10.refs_0_, f32[2,4096]{1,0:T(2,128)S(1)} %collective-permute-done.5.refs_1_, f32[2,4096]{1,0:T(2,128)S(1)} %collective-permute-done.6.refs_2_, ...), custom_call_target="tpu_custom_call" | custom-call | tf_op jit(solution)/shard_map/cg_start/pallas_call | solution.py:222
  48.3 13.2 %all_to_all.20.refs_0_ = f32[16,8,256]{2,1,0:T(8,128)S(1)} all-to-all(f32[16,8,256]{2,1,0:T(8,128)S(1)} %broadcast_in_dim.10), channel_id=1, replica_groups=mesh['groups'=2,'dp'=4,'tensor'=4] {'dp','tensor'}, dimensions={0} | all-to-all | bytes 262144 | tf_op jit(solution)/shard_map/all_to_all | solution.py:32
  61.5 1.6 %cg_step.3 = (f32[8,256]{1,0:T(8,128)S(1)}, f32[8,128]{1,0:T(8,128)S(1)}, f32[8,256]{1,0:T(8,128)S(1)}, f32[8,4096]{1,0:T(8,128)S(1)}, f32[8,4096]{1,0:T(8,128)S(1)}, /*index=5*/f32[8,4096]{1,0:T(8,128)S(1)}) custom-call(f32[16,8,256]{2,1,0:T(8,128)S(1)} %all_to_all.20.refs_0_, bf16[256,4096]{1,0:T(8,128)(2,1)S(1)} %get-tuple-element.30.refs_4_.refs_1_, ...), custom_call_target="tpu_custom_call" | custom-call | tf_op jit(solution)/shard_map/cg_step/pallas_call | solution.py:293
  63.1 10.4 %all_to_all.21.refs_0_ = f32[16,8,256]{2,1,0:T(8,128)S(1)} all-to-all(f32[16,8,256]{2,1,0:T(8,128)S(1)} %broadcast_in_dim.11), channel_id=1, replica_groups=mesh['groups'=2,'dp'=4,'tensor'=4] {'dp','tensor'}, dimensions={0} | all-to-all | bytes 262144 | tf_op jit(solution)/shard_map/all_to_all | solution.py:32
  73.5 1.6 %cg_step.4 = (f32[8,256]{1,0:T(8,128)S(1)}, f32[8,128]{1,0:T(8,128)S(1)}, f32[8,256]{1,0:T(8,128)S(1)}, f32[8,4096]{1,0:T(8,128)S(1)}, f32[8,4096]{1,0:T(8,128)S(1)}, /*index=5*/f32[8,4096]{1,0:T(8,128)S(1)}) custom-call(f32[16,8,256]{2,1,0:T(8,128)S(1)} %all_to_all.21.refs_0_, bf16[256,4096]{1,0:T(8,128)(2,1)S(1)} %get-tuple-element.30.refs_4_.refs_1_, ...), custom_call_target="tpu_custom_call" | custom-call | tf_op jit(solution)/shard_map/cg_step/pallas_call | solution.py:293
  75.1 10.4 %all_to_all.22.refs_0_ = f32[16,8,256]{2,1,0:T(8,128)S(1)} all-to-all(f32[16,8,256]{2,1,0:T(8,128)S(1)} %broadcast_in_dim.12), channel_id=1, replica_groups=mesh['groups'=2,'dp'=4,'tensor'=4] {'dp','tensor'}, dimensions={0} | all-to-all | bytes 262144 | tf_op jit(solution)/shard_map/all_to_all | solution.py:32
  85.5 1.7 %cg_step.5 = (f32[1,128]{1,0:T(1,128)S(1)}, f32[1,128]{1,0:T(1,128)S(1)}, f32[8,4096]{1,0:T(8,128)S(1)}, f32[8,4096]{1,0:T(8,128)S(1)}) custom-call(f32[16,8,256]{2,1,0:T(8,128)S(1)} %all_to_all.22.refs_0_, bf16[256,4096]{1,0:T(8,128)(2,1)S(1)} %get-tuple-element.30.refs_4_.refs_1_, bf16[256,4096]{1,0:T(8,128)(2,1)S(1)} %get-tuple-element.31.refs_5_.refs_2_, ...), custom_call_target="tpu_custom_call" | custom-call | tf_op jit(solution)/shard_map/cg_step/pallas_call | solution.py:293
  87.2 0.6 broadcast_in_dim.14
  87.8 3.5 %all-to-all-start.3 = ((f32[16,1,128]{2,1,0:T(1,128)}), f32[16,1,128]{2,1,0:T(1,128)S(1)}, u32[]{:S(2)}, u32[]{:S(2)}) async-start(f32[16,1,128]{2,1,0:T(1,128)} %broadcast_in_dim.14), calls=%async_computation.3 | async-start | bytes 16384 | tf_op jit(solution)/shard_map/all_to_all | solution.py:32
  91.2 0.3 scores.1
  91.5 6.0 %all-to-all-done.3 = f32[16,1,128]{2,1,0:T(1,128)S(1)} async-done(((f32[16,1,128]{2,1,0:T(1,128)}), f32[16,1,128]{2,1,0:T(1,128)S(1)}, u32[]{:S(2)}, u32[]{:S(2)}) %all-to-all-start.3) | async-done | bytes 8224 | tf_op jit(solution)/shard_map/all_to_all | solution.py:32
  97.6 0.7 multiply_add_fusion
  (19 shorter events, 0.3 us)
Async XLA Ops:
  7.4 25.4 %collective-permute-start.2 = (f32[64,512]{1,0:T(8,128)S(1)}, f32[64,512]{1,0:T(8,128)S(1)}, u32[]{:S(2)}, u32[]{:S(2)}) collective-permute-start(f32[64,512]{1,0:T(8,128)S(1)} %in_features.1.refs_0_), channel_id=1, source_target_pairs={{0,3},{1,2},{2,1},{3,0},{4,7},{5,6},{6,5},{7,4},{8,11},{9,10},{10,... | collective-permute-start | bytes 393224 | tf_op jit(solution)/shard_map/ppermute | solution.py:24
  12.5 20.3 %collective-permute-start.1 = (f32[64,512]{1,0:T(8,128)S(1)}, f32[64,512]{1,0:T(8,128)S(1)}, u32[]{:S(2)}, u32[]{:S(2)}) collective-permute-start(f32[64,512]{1,0:T(8,128)S(1)} %in_features.1.refs_0_), channel_id=1, source_target_pairs={{0,2},{1,3},{2,0},{3,1},{4,6},{5,7},{6,4},{7,5},{8,10},{9,11},{10,... | collective-permute-start | bytes 393224 | tf_op jit(solution)/shard_map/ppermute | solution.py:24
  12.5 20.3 %collective-permute-start = (f32[64,512]{1,0:T(8,128)S(1)}, f32[64,512]{1,0:T(8,128)S(1)}, u32[]{:S(2)}, u32[]{:S(2)}) collective-permute-start(f32[64,512]{1,0:T(8,128)S(1)} %in_features.1.refs_0_), channel_id=1, source_target_pairs={{0,1},{1,0},{2,3},{3,2},{4,5},{5,4},{6,7},{7,6},{8,9},{9,8},{10,11... | collective-permute-start | bytes 393224 | tf_op jit(solution)/shard_map/ppermute | solution.py:24
  33.6 4.9 %collective-permute-start.3 = (f32[2,4096]{1,0:T(2,128)S(1)}, f32[2,4096]{1,0:T(2,128)S(1)}, u32[]{:S(2)}, u32[]{:S(2)}) collective-permute-start(f32[2,4096]{1,0:T(2,128)S(1)} %reshape.11), channel_id=1, source_target_pairs={{0,2},{1,3},{2,0},{3,1},{4,6},{5,7},{6,4},{7,5},{8,10},{9,11},{10,... | collective-permute-start | bytes 98312 | tf_op jit(solution)/shard_map/ppermute | solution.py:24
  38.5 4.0 %collective-permute-start.4 = (f32[2,4096]{1,0:T(2,128)S(1)}, f32[2,4096]{1,0:T(2,128)S(1)}, u32[]{:S(2)}, u32[]{:S(2)}) collective-permute-start(f32[2,4096]{1,0:T(2,128)S(1)} %add.9), channel_id=1, source_target_pairs={{0,1},{1,0},{2,3},{3,2},{4,5},{5,4},{6,7},{7,6},{8,9},{9,8},{10,11... | collective-permute-start | bytes 98312 | tf_op jit(solution)/shard_map/ppermute | solution.py:24
  42.5 4.3 %collective-permute-start.7 = (f32[2,4096]{1,0:T(2,128)S(1)}, f32[2,4096]{1,0:T(2,128)S(1)}, u32[]{:S(2)}, u32[]{:S(2)}) collective-permute-start(f32[2,4096]{1,0:T(2,128)S(1)} %add.10.refs_0_), channel_id=1, source_target_pairs={{0,12},{4,8},{8,4},{12,0},{1,13},{5,9},{9,5},{13,1},{2,14},{6,10},... | collective-permute-start | bytes 98312 | tf_op jit(solution)/shard_map/ppermute | solution.py:24
  42.6 4.2 %collective-permute-start.6 = (f32[2,4096]{1,0:T(2,128)S(1)}, f32[2,4096]{1,0:T(2,128)S(1)}, u32[]{:S(2)}, u32[]{:S(2)}) collective-permute-start(f32[2,4096]{1,0:T(2,128)S(1)} %add.10.refs_0_), channel_id=1, source_target_pairs={{0,8},{4,12},{8,0},{12,4},{1,9},{5,13},{9,1},{13,5},{2,10},{6,14},... | collective-permute-start | bytes 98312 | tf_op jit(solution)/shard_map/ppermute | solution.py:24
  44.3 2.5 %collective-permute-start.5 = (f32[2,4096]{1,0:T(2,128)S(1)}, f32[2,4096]{1,0:T(2,128)S(1)}, u32[]{:S(2)}, u32[]{:S(2)}) collective-permute-start(f32[2,4096]{1,0:T(2,128)S(1)} %add.10.refs_0_), channel_id=1, source_target_pairs={{0,4},{4,0},{8,12},{12,8},{1,5},{5,1},{9,13},{13,9},{2,6},{6,2},{1... | collective-permute-start | bytes 98312 | tf_op jit(solution)/shard_map/ppermute | solution.py:24
  73.5 17.7 %copy-start = (bf16[32,4096]{1,0:T(8,128)(2,1)S(1)}, bf16[32,4096]{1,0:T(8,128)(2,1)}, u32[]{:S(2)}) copy-start(bf16[32,4096]{1,0:T(8,128)(2,1)} %queries_ref.1) | copy-start | bytes 786436
  87.8 9.8 %all-to-all-start.3 = ((f32[16,1,128]{2,1,0:T(1,128)}), f32[16,1,128]{2,1,0:T(1,128)S(1)}, u32[]{:S(2)}, u32[]{:S(2)}) async-start(f32[16,1,128]{2,1,0:T(1,128)} %broadcast_in_dim.14), calls=%async_computation.3 | async-start | bytes 16384 | tf_op jit(solution)/shard_map/all_to_all | solution.py:32

commit v9 on v8

--- a/solution.py
+++ b/solution.py
@@ -69,37 +69,67 @@
     return spans
 
 
-def stream_kernel(spans, rows_ref, proj_ref, feats_ref, held, proj, sems):
-    first = pltpu.make_async_copy(proj_ref, proj, sems.at[len(spans)])
+def fetch(rows_ref, held, proj_ref, proj, sems, places):
+    count = proj_ref.shape[0]
+    first = pltpu.make_async_copy(proj_ref, proj.at[:count], sems.at[len(places)])
     copies = [
-        pltpu.make_async_copy(rows_ref.at[span], held.at[span], sems.at[c])
-        for c, span in enumerate(spans)
+        pltpu.make_async_copy(rows_ref.at[place], held.at[place], sems.at[c])
+        for c, place in enumerate(places)
     ]
     first.start()
     for copy in copies:
         copy.start()
+    proj[count:] = jnp.zeros((proj.shape[0] - count, proj.shape[1]), proj.dtype)
     first.wait()
+    return copies
+
+
+def in_kernel(rows_ref, proj_ref, feats_ref, held, proj, sems):
+    count = sems.shape[0] - 1
+    chunk = held.shape[1] // count
+    spans = [pl.ds(c * chunk, chunk) for c in range(count)]
+    copies = fetch(rows_ref, held, proj_ref, proj, sems, [(slice(None), span) for span in spans])
+    feats = None
+    for copy, span in zip(copies, spans):
+        copy.wait()
+        part = lax.dot_general(held[:, span], proj[:, span], NT, preferred_element_type=jnp.float32)
+        part = part[:, :LANES]
+        feats = part if feats is None else feats + part
+    feats_ref[...] = feats.T[: feats_ref.shape[0]]
+
+
+def out_kernel(spans, rows_ref, proj_ref, feats_ref, held, proj, sems):
+    copies = fetch(rows_ref, held, proj_ref, proj, sems, spans)
     for copy, span in zip(copies, spans):
         copy.wait()
         feats = lax.dot_general(held[span], proj[...], NT, preferred_element_type=jnp.float32)
-        feats_ref[:, span] = feats.T
-
-
-def features(rows, proj, sizes, limit, name):
-    spans = row_spans(rows.shape[0], sizes)
-    return pl.pallas_call(
-        functools.partial(stream_kernel, spans),
+        feats_ref[:, span] = feats[:, :LANES].T[: feats_ref.shape[0]]
+
+
+def features(rows, proj, kernel, copies, limit, name):
+    return pl.pallas_call(
+        kernel,
         out_shape=pltpu.VMEM((proj.shape[0], rows.shape[0]), jnp.float32),
         in_specs=[ANY_SPEC] * 2,
         out_specs=VMEM_SPEC,
         scratch_shapes=[
             pltpu.VMEM(rows.shape, jnp.bfloat16),
-            pltpu.VMEM(proj.shape, jnp.bfloat16),
-            pltpu.SemaphoreType.DMA((len(spans) + 1,)),
+            pltpu.VMEM((2 * LANES, proj.shape[1]), jnp.bfloat16),
+            pltpu.SemaphoreType.DMA((copies + 1,)),
         ],
         compiler_params=pltpu.CompilerParams(vmem_limit_bytes=limit * 2**20),
         name=name,
     )(in_hbm(rows), in_hbm(proj))
+
+
+def in_features(inputs, in_proj):
+    return features(inputs, in_proj, in_kernel, 8, 20, "in_features")
+
+
+def out_features(out_grads, out_proj):
+    spans = row_spans(out_grads.shape[0], (512, 512, 512, 256, 128))
+    kernel = functools.partial(out_kernel, spans)
+    return features(out_grads, out_proj, kernel, len(spans), 44, "out_features")
 
 
 def split_kernel(prior_ref, upper_ref, lower_ref, held, sems):
@@ -275,7 +305,7 @@
     solution_out[...] = solution
     if last:
         own = own_columns(direction_out, me, rows)
-        curvature_out[...] = on_lanes(row_sum(own * fisher_direction))
+        curvature_out[...] = jnp.broadcast_to(on_lanes(row_sum(own * fisher_direction))[None], curvature_out.shape)
         norm_out[...] = on_lanes(norm_next)
     else:
         fisher_direction_out[...] = fisher_direction
@@ -287,9 +317,9 @@
 def step_cg(blocks, fixed, norm, state, last, tensor_size):
     first = len(state) == 1
     whole, rows = F32(fixed[2].shape), F32(state[0].shape)
-    row = F32((1, LANES))
+    row, repeated = F32((1, LANES)), F32((blocks.shape[0], 1, LANES))
     operands = [blocks, *fixed, norm, *state]
-    out_shape = (row, row, whole, whole) if last else (rows, F32(norm.shape), rows, whole, whole, whole)
+    out_shape = (repeated, row, whole, whole) if last else (rows, F32(norm.shape), rows, whole, whole, whole)
     return pl.pallas_call(
         functools.partial(step_kernel, tensor_size, first, last),
         out_shape=out_shape,
@@ -324,8 +354,8 @@
 def on_device(dp_size, tensor_size, inputs, in_proj, out_grads, out_proj, prior, queries):
     width = R_IN * R_OUT
     both, devices = ("dp", "tensor"), dp_size * tensor_size
-    in_blocks = direct(features(inputs, in_proj, (256, 128), 16, "in_features"), "tensor", tensor_size)
-    out_local = features(out_grads, out_proj, (512, 512, 512, 256, 128), 40, "out_features")
+    in_blocks = direct(in_features(inputs, in_proj), "tensor", tensor_size)
+    out_local = out_features(out_grads, out_proj)
     partial = partial_vectors(in_blocks, out_local).reshape(-1, width)
     pieces = direct(sum_over(partial, "tensor", tensor_size), "dp", dp_size)
     prior_pieces = [in_vmem(piece) for piece in split_prior(prior)]
@@ -338,7 +368,7 @@
         state = [applied_rows, *others]
     blocks = gather(state[0], both, devices)
     curvature, norm, direction, solved = step_cg(blocks, fixed, norm, state, True, tensor_size)
-    curvature = jnp.sum(gather(curvature, both, devices), axis=0)
+    curvature = jnp.sum(lax.all_to_all(curvature, both, 0, 0), axis=0)
     solved, along = score(solved, direction, queries)
     step = (norm / curvature)[0, : solved.shape[0]]
     return solved + step[:, None] * along

time: 98.5 us -> 99.2 us (level)
  Pallas kernels: 36.6 us -> 37.8 us
  transfers between devices with their start and end apart: 9 -> 9, of which waited for: 3 -> 3; matrix products, arithmetic and copies ran while one was open for 0% -> 0% of each run, Pallas kernels for 23% -> 24%
where the time goes in v9:
time: 99.2 us; the launch traced here: 98.9 us
  Pallas kernels  37.8 us (38%)
  blocking collectives  34 us (34%)
  starting transfers between devices  15 us (15%)
  waiting for transfers between devices  11.1 us (11%)
    all_to_all x3, blocking collectives, gather(): lax.all_to_all(jnp.broadcast_to(value[None], (size,) + value.shape), axes...  34 us
    pallas_call x2, Pallas kernels, features(): pl.pallas_call(kernel, out_shape=pltpu.VMEM((proj.shape[0], rows.shape[0]...  27.7 us
    ppermute x8, starting transfers between devices, swap(): return lax.ppermute(value, axis, [(i, i ^ bit) for i in range(size)])  11.5 us
    all_to_all x1, waiting for transfers between devices, on_device(): curvature = jnp.sum(lax.all_to_all(curvature, both, 0, 0), axis=0)  6.04 us
    pallas_call x3, Pallas kernels, step_cg(): pl.pallas_call(functools.partial(step_kernel, tensor_size, first, last),...  5.45 us
    ppermute x8, waiting for transfers between devices, swap(): return lax.ppermute(value, axis, [(i, i ^ bit) for i in range(size)])  5.06 us
    all_to_all x1, starting transfers between devices, on_device(): curvature = jnp.sum(lax.all_to_all(curvature, both, 0, 0), axis=0)  3.45 us
    pallas_call x1, Pallas kernels, split_prior(): pl.pallas_call(split_kernel, out_shape=(pltpu.VMEM(prior.shape, jnp.bfloa...  2.32 us
  transfers between devices with their start and end apart: 9, of which 3 were waited for; matrix products, arithmetic and copies ran while one was open for 0% of the time, Pallas kernels for 24%

profile of v9, /device:TPU:0, one launch (start us, length us, event | category | flops | bytes accessed | tf_op | source)
XLA Modules:
  0.0 98.9 jit_solution(11039144797727180746)
XLA Ops:
  0.0 6.8 %in_features.1.refs_0_ = f32[64,512]{1,0:T(8,128)S(1)} custom-call(bf16[512,8192]{1,0:T(8,128)(2,1)} %rows_ref.2, bf16[64,8192]{1,0:T(8,128)(2,1)} %proj_ref.2), custom_call_target="tpu_custom_call" | custom-call | tf_op jit(solution)/shard_map/in_features/pallas_call | solution.py:110
  6.8 5.1 %collective-permute-start.2 = (f32[64,512]{1,0:T(8,128)S(1)}, f32[64,512]{1,0:T(8,128)S(1)}, u32[]{:S(2)}, u32[]{:S(2)}) collective-permute-start(f32[64,512]{1,0:T(8,128)S(1)} %in_features.1.refs_0_), channel_id=1, source_target_pairs={{0,3},{1,2},{2,1},{3,0},{4,7},{5,6},{6,5},{7,4},{8,11},{9,10},{10,... | collective-permute-start | bytes 393224 | tf_op jit(solution)/shard_map/ppermute | solution.py:24
  11.9 0.6 collective-permute-start
  12.5 21.0 %out_features.1.refs_4_ = f32[64,2048]{1,0:T(8,128)S(1)} custom-call(bf16[2048,7168]{1,0:T(8,128)(2,1)} %rows_ref.3, bf16[64,7168]{1,0:T(8,128)(2,1)} %proj_ref.3), custom_call_target="tpu_custom_call" | custom-call | tf_op jit(solution)/shard_map/out_features/pallas_call | solution.py:110
  33.5 0.6 partial_vectors.1
  34.1 0.1 reshape.8
  34.2 2.4 %collective-permute-start.3 = (f32[2,4096]{1,0:T(2,128)S(1)}, f32[2,4096]{1,0:T(2,128)S(1)}, u32[]{:S(2)}, u32[]{:S(2)}) collective-permute-start(f32[2,4096]{1,0:T(2,128)S(1)} %reshape.8), channel_id=1, source_target_pairs={{0,2},{1,3},{2,0},{3,1},{4,6},{5,7},{6,4},{7,5},{8,10},{9,11},{10,... | collective-permute-start | bytes 98312 | tf_op jit(solution)/shard_map/ppermute | solution.py:24
  36.6 2.5 %collective-permute-done.3 = f32[2,4096]{1,0:T(2,128)S(1)} collective-permute-done((f32[2,4096]{1,0:T(2,128)S(1)}, f32[2,4096]{1,0:T(2,128)S(1)}, u32[]{:S(2)}, u32[]{:S(2)}) %collective-permute-start.3) | collective-permute-done | bytes 32800 | tf_op jit(solution)/shard_map/ppermute | solution.py:24
  39.1 1.5 %collective-permute-start.4 = (f32[2,4096]{1,0:T(2,128)S(1)}, f32[2,4096]{1,0:T(2,128)S(1)}, u32[]{:S(2)}, u32[]{:S(2)}) collective-permute-start(f32[2,4096]{1,0:T(2,128)S(1)} %add.9), channel_id=1, source_target_pairs={{0,1},{1,0},{2,3},{3,2},{4,5},{5,4},{6,7},{7,6},{8,9},{9,8},{10,11... | collective-permute-start | bytes 98312 | tf_op jit(solution)/shard_map/ppermute | solution.py:24
  40.6 2.5 %collective-permute-done.4 = f32[2,4096]{1,0:T(2,128)S(1)} collective-permute-done((f32[2,4096]{1,0:T(2,128)S(1)}, f32[2,4096]{1,0:T(2,128)S(1)}, u32[]{:S(2)}, u32[]{:S(2)}) %collective-permute-start.4) | collective-permute-done | bytes 32800 | tf_op jit(solution)/shard_map/ppermute | solution.py:24
  43.2 1.7 %collective-permute-start.6 = (f32[2,4096]{1,0:T(2,128)S(1)}, f32[2,4096]{1,0:T(2,128)S(1)}, u32[]{:S(2)}, u32[]{:S(2)}) collective-permute-start(f32[2,4096]{1,0:T(2,128)S(1)} %add.10.refs_0_), channel_id=1, source_target_pairs={{0,8},{4,12},{8,0},{12,4},{1,9},{5,13},{9,1},{13,5},{2,10},{6,14},... | collective-permute-start | bytes 98312 | tf_op jit(solution)/shard_map/ppermute | solution.py:24
  44.9 0.2 collective-permute-start.5
  45.1 2.3 %split_prior.1 = (bf16[256,4096]{1,0:T(8,128)(2,1)S(1)}, bf16[256,4096]{1,0:T(8,128)(2,1)S(1)}) custom-call(f32[256,4096]{1,0:T(8,128)} %prior_ref.1), custom_call_target="tpu_custom_call" | custom-call | tf_op jit(solution)/shard_map/split_prior/pallas_call | solution.py:153
  47.4 1.5 %cg_start.1 = (f32[8,4096]{1,0:T(8,128)S(1)}, bf16[16,4096]{1,0:T(8,128)(2,1)S(1)}, f32[8,128]{1,0:T(8,128)S(1)}, f32[8,256]{1,0:T(8,128)S(1)}, f32[8,128]{1,0:T(8,128)S(1)}) custom-call(f32[2,4096]{1,0:T(2,128)S(1)} %add.10.refs_0_, f32[2,4096]{1,0:T(2,128)S(1)} %collective-permute-done.5.refs_1_, f32[2,4096]{1,0:T(2,128)S(1)} %collective-permute-done.6.refs_2_, ...), custom_call_target="tpu_custom_call" | custom-call | tf_op jit(solution)/shard_map/cg_start/pallas_call | solution.py:252
  49.0 13.2 %all_to_all.20.refs_0_ = f32[16,8,256]{2,1,0:T(8,128)S(1)} all-to-all(f32[16,8,256]{2,1,0:T(8,128)S(1)} %broadcast_in_dim.6), channel_id=1, replica_groups=mesh['groups'=2,'dp'=4,'tensor'=4] {'dp','tensor'}, dimensions={0} | all-to-all | bytes 262144 | tf_op jit(solution)/shard_map/all_to_all | solution.py:32
  62.1 1.6 %cg_step.3 = (f32[8,256]{1,0:T(8,128)S(1)}, f32[8,128]{1,0:T(8,128)S(1)}, f32[8,256]{1,0:T(8,128)S(1)}, f32[8,4096]{1,0:T(8,128)S(1)}, f32[8,4096]{1,0:T(8,128)S(1)}, /*index=5*/f32[8,4096]{1,0:T(8,128)S(1)}) custom-call(f32[16,8,256]{2,1,0:T(8,128)S(1)} %all_to_all.20.refs_0_, bf16[256,4096]{1,0:T(8,128)(2,1)S(1)} %get-tuple-element.30.refs_4_.refs_1_, ...), custom_call_target="tpu_custom_call" | custom-call | tf_op jit(solution)/shard_map/cg_step/pallas_call | solution.py:323
  63.8 10.4 %all_to_all.21.refs_0_ = f32[16,8,256]{2,1,0:T(8,128)S(1)} all-to-all(f32[16,8,256]{2,1,0:T(8,128)S(1)} %broadcast_in_dim.7), channel_id=1, replica_groups=mesh['groups'=2,'dp'=4,'tensor'=4] {'dp','tensor'}, dimensions={0} | all-to-all | bytes 262144 | tf_op jit(solution)/shard_map/all_to_all | solution.py:32
  74.1 1.6 %cg_step.4 = (f32[8,256]{1,0:T(8,128)S(1)}, f32[8,128]{1,0:T(8,128)S(1)}, f32[8,256]{1,0:T(8,128)S(1)}, f32[8,4096]{1,0:T(8,128)S(1)}, f32[8,4096]{1,0:T(8,128)S(1)}, /*index=5*/f32[8,4096]{1,0:T(8,128)S(1)}) custom-call(f32[16,8,256]{2,1,0:T(8,128)S(1)} %all_to_all.21.refs_0_, bf16[256,4096]{1,0:T(8,128)(2,1)S(1)} %get-tuple-element.30.refs_4_.refs_1_, ...), custom_call_target="tpu_custom_call" | custom-call | tf_op jit(solution)/shard_map/cg_step/pallas_call | solution.py:323
  75.8 10.4 %all_to_all.22.refs_0_ = f32[16,8,256]{2,1,0:T(8,128)S(1)} all-to-all(f32[16,8,256]{2,1,0:T(8,128)S(1)} %broadcast_in_dim.8), channel_id=1, replica_groups=mesh['groups'=2,'dp'=4,'tensor'=4] {'dp','tensor'}, dimensions={0} | all-to-all | bytes 262144 | tf_op jit(solution)/shard_map/all_to_all | solution.py:32
  86.2 2.3 %cg_step.5 = (f32[16,1,128]{2,1,0:T(1,128)}, f32[1,128]{1,0:T(1,128)S(1)}, f32[8,4096]{1,0:T(8,128)S(1)}, f32[8,4096]{1,0:T(8,128)S(1)}) custom-call(f32[16,8,256]{2,1,0:T(8,128)S(1)} %all_to_all.22.refs_0_, bf16[256,4096]{1,0:T(8,128)(2,1)S(1)} %get-tuple-element.30.refs_4_.refs_1_, bf16[256,4096]{1,0:T(8,128)(2,1)S(1)} %get-tuple-element.31.refs_5_.refs_2_, ...), custom_call_target="tpu_custom_call" | custom-call | tf_op jit(solution)/shard_map/cg_step/pallas_call | solution.py:323
  88.4 3.5 %all-to-all-start.3 = ((f32[16,1,128]{2,1,0:T(1,128)}), f32[16,1,128]{2,1,0:T(1,128)S(1)}, u32[]{:S(2)}, u32[]{:S(2)}) async-start(f32[16,1,128]{2,1,0:T(1,128)} %get-tuple-element.53), calls=%async_computation.3 | async-start | bytes 16384 | tf_op jit(solution)/shard_map/all_to_all | solution.py:371
  91.9 0.3 scores.1
  92.2 6.0 %all-to-all-done.3 = f32[16,1,128]{2,1,0:T(1,128)S(1)} async-done(((f32[16,1,128]{2,1,0:T(1,128)}), f32[16,1,128]{2,1,0:T(1,128)S(1)}, u32[]{:S(2)}, u32[]{:S(2)}) %all-to-all-start.3) | async-done | bytes 8224 | tf_op jit(solution)/shard_map/all_to_all | solution.py:371
  98.3 0.7 multiply_add_fusion
  (18 shorter events, 0.2 us)
Async XLA Ops:
  6.8 26.7 %collective-permute-start.2 = (f32[64,512]{1,0:T(8,128)S(1)}, f32[64,512]{1,0:T(8,128)S(1)}, u32[]{:S(2)}, u32[]{:S(2)}) collective-permute-start(f32[64,512]{1,0:T(8,128)S(1)} %in_features.1.refs_0_), channel_id=1, source_target_pairs={{0,3},{1,2},{2,1},{3,0},{4,7},{5,6},{6,5},{7,4},{8,11},{9,10},{10,... | collective-permute-start | bytes 393224 | tf_op jit(solution)/shard_map/ppermute | solution.py:24
  11.9 21.6 %collective-permute-start.1 = (f32[64,512]{1,0:T(8,128)S(1)}, f32[64,512]{1,0:T(8,128)S(1)}, u32[]{:S(2)}, u32[]{:S(2)}) collective-permute-start(f32[64,512]{1,0:T(8,128)S(1)} %in_features.1.refs_0_), channel_id=1, source_target_pairs={{0,2},{1,3},{2,0},{3,1},{4,6},{5,7},{6,4},{7,5},{8,10},{9,11},{10,... | collective-permute-start | bytes 393224 | tf_op jit(solution)/shard_map/ppermute | solution.py:24
  11.9 21.6 %collective-permute-start = (f32[64,512]{1,0:T(8,128)S(1)}, f32[64,512]{1,0:T(8,128)S(1)}, u32[]{:S(2)}, u32[]{:S(2)}) collective-permute-start(f32[64,512]{1,0:T(8,128)S(1)} %in_features.1.refs_0_), channel_id=1, source_target_pairs={{0,1},{1,0},{2,3},{3,2},{4,5},{5,4},{6,7},{7,6},{8,9},{9,8},{10,11... | collective-permute-start | bytes 393224 | tf_op jit(solution)/shard_map/ppermute | solution.py:24
  34.2 4.9 %collective-permute-start.3 = (f32[2,4096]{1,0:T(2,128)S(1)}, f32[2,4096]{1,0:T(2,128)S(1)}, u32[]{:S(2)}, u32[]{:S(2)}) collective-permute-start(f32[2,4096]{1,0:T(2,128)S(1)} %reshape.8), channel_id=1, source_target_pairs={{0,2},{1,3},{2,0},{3,1},{4,6},{5,7},{6,4},{7,5},{8,10},{9,11},{10,... | collective-permute-start | bytes 98312 | tf_op jit(solution)/shard_map/ppermute | solution.py:24
  39.1 4.0 %collective-permute-start.4 = (f32[2,4096]{1,0:T(2,128)S(1)}, f32[2,4096]{1,0:T(2,128)S(1)}, u32[]{:S(2)}, u32[]{:S(2)}) collective-permute-start(f32[2,4096]{1,0:T(2,128)S(1)} %add.9), channel_id=1, source_target_pairs={{0,1},{1,0},{2,3},{3,2},{4,5},{5,4},{6,7},{7,6},{8,9},{9,8},{10,11... | collective-permute-start | bytes 98312 | tf_op jit(solution)/shard_map/ppermute | solution.py:24
  43.1 4.3 %collective-permute-start.7 = (f32[2,4096]{1,0:T(2,128)S(1)}, f32[2,4096]{1,0:T(2,128)S(1)}, u32[]{:S(2)}, u32[]{:S(2)}) collective-permute-start(f32[2,4096]{1,0:T(2,128)S(1)} %add.10.refs_0_), channel_id=1, source_target_pairs={{0,12},{4,8},{8,4},{12,0},{1,13},{5,9},{9,5},{13,1},{2,14},{6,10},... | collective-permute-start | bytes 98312 | tf_op jit(solution)/shard_map/ppermute | solution.py:24
  43.2 4.2 %collective-permute-start.6 = (f32[2,4096]{1,0:T(2,128)S(1)}, f32[2,4096]{1,0:T(2,128)S(1)}, u32[]{:S(2)}, u32[]{:S(2)}) collective-permute-start(f32[2,4096]{1,0:T(2,128)S(1)} %add.10.refs_0_), channel_id=1, source_target_pairs={{0,8},{4,12},{8,0},{12,4},{1,9},{5,13},{9,1},{13,5},{2,10},{6,14},... | collective-permute-start | bytes 98312 | tf_op jit(solution)/shard_map/ppermute | solution.py:24
  44.9 2.5 %collective-permute-start.5 = (f32[2,4096]{1,0:T(2,128)S(1)}, f32[2,4096]{1,0:T(2,128)S(1)}, u32[]{:S(2)}, u32[]{:S(2)}) collective-permute-start(f32[2,4096]{1,0:T(2,128)S(1)} %add.10.refs_0_), channel_id=1, source_target_pairs={{0,4},{4,0},{8,12},{12,8},{1,5},{5,1},{9,13},{13,9},{2,6},{6,2},{1... | collective-permute-start | bytes 98312 | tf_op jit(solution)/shard_map/ppermute | solution.py:24
  74.1 17.8 %copy-start = (bf16[32,4096]{1,0:T(8,128)(2,1)S(1)}, bf16[32,4096]{1,0:T(8,128)(2,1)}, u32[]{:S(2)}) copy-start(bf16[32,4096]{1,0:T(8,128)(2,1)} %queries_ref.1) | copy-start | bytes 786436
  88.4 9.8 %all-to-all-start.3 = ((f32[16,1,128]{2,1,0:T(1,128)}), f32[16,1,128]{2,1,0:T(1,128)S(1)}, u32[]{:S(2)}, u32[]{:S(2)}) async-start(f32[16,1,128]{2,1,0:T(1,128)} %get-tuple-element.53), calls=%async_computation.3 | async-start | bytes 16384 | tf_op jit(solution)/shard_map/all_to_all | solution.py:371

commit v10 on v8

--- a/solution.py
+++ b/solution.py
@@ -81,8 +81,7 @@
     first.wait()
     for copy, span in zip(copies, spans):
         copy.wait()
-        feats = lax.dot_general(held[span], proj[...], NT, preferred_element_type=jnp.float32)
-        feats_ref[:, span] = feats.T
+        feats_ref[:, span] = lax.dot_general(proj[...], held[span], NT, preferred_element_type=jnp.float32)
 
 
 def features(rows, proj, sizes, limit, name):
@@ -325,7 +324,7 @@
     width = R_IN * R_OUT
     both, devices = ("dp", "tensor"), dp_size * tensor_size
     in_blocks = direct(features(inputs, in_proj, (256, 128), 16, "in_features"), "tensor", tensor_size)
-    out_local = features(out_grads, out_proj, (512, 512, 512, 256, 128), 40, "out_features")
+    out_local = features(out_grads, out_proj, (256,) * 7 + (128,), 40, "out_features")
     partial = partial_vectors(in_blocks, out_local).reshape(-1, width)
     pieces = direct(sum_over(partial, "tensor", tensor_size), "dp", dp_size)
     prior_pieces = [in_vmem(piece) for piece in split_prior(prior)]

time: 98.5 us -> 97.4 us (0.989)
  Pallas kernels: 36.6 us -> 35.5 us
    pallas_call x2, Pallas kernels: 27 us -> 26 us  [features(): pl.pallas_call(functools.partial(stream_kernel, spans), out_shape=pltpu.V...]
  transfers between devices with their start and end apart: 9 -> 9, of which waited for: 3 -> 3; matrix products, arithmetic and copies ran while one was open for 0% -> 0% of each run, Pallas kernels for 23% -> 22%
where the time goes in v10:
time: 97.4 us; the launch traced here: 97.1 us
  Pallas kernels  35.5 us (36%)
  blocking collectives  33.9 us (35%)
  starting transfers between devices  14.9 us (15%)
  waiting for transfers between devices  11.1 us (11%)
    all_to_all x3, blocking collectives, gather(): lax.all_to_all(jnp.broadcast_to(value[None], (size,) + value.shape), axes...  33.9 us
    pallas_call x2, Pallas kernels, features(): pl.pallas_call(functools.partial(stream_kernel, spans), out_shape=pltpu.V...  26 us
    ppermute x8, starting transfers between devices, swap(): return lax.ppermute(value, axis, [(i, i ^ bit) for i in range(size)])  11.5 us
    all_to_all x1, waiting for transfers between devices, gather(): lax.all_to_all(jnp.broadcast_to(value[None], (size,) + value.shape), axes...  6.04 us
    ppermute x8, waiting for transfers between devices, swap(): return lax.ppermute(value, axis, [(i, i ^ bit) for i in range(size)])  5.07 us
    pallas_call x3, Pallas kernels, step_cg(): pl.pallas_call(functools.partial(step_kernel, tensor_size, first, last),...  4.86 us
    all_to_all x1, starting transfers between devices, gather(): lax.all_to_all(jnp.broadcast_to(value[None], (size,) + value.shape), axes...  3.45 us
    pallas_call x1, Pallas kernels, split_prior(): pl.pallas_call(split_kernel, out_shape=(pltpu.VMEM(prior.shape, jnp.bfloa...  2.32 us
  transfers between devices with their start and end apart: 9, of which 3 were waited for; matrix products, arithmetic and copies ran while one was open for 0% of the time, Pallas kernels for 22%

profile of v10, /device:TPU:0, one launch (start us, length us, event | category | flops | bytes accessed | tf_op | source)
XLA Modules:
  0.0 97.1 jit_solution(9158958018157068136)
XLA Ops:
  0.0 7.3 %in_features.1.refs_0_ = f32[64,512]{1,0:T(8,128)S(1)} custom-call(bf16[512,8192]{1,0:T(8,128)(2,1)} %rows_ref.2, bf16[64,8192]{1,0:T(8,128)(2,1)} %proj_ref.2), custom_call_target="tpu_custom_call" | custom-call | tf_op jit(solution)/shard_map/in_features/pallas_call | solution.py:89
  7.3 5.1 %collective-permute-start.2 = (f32[64,512]{1,0:T(8,128)S(1)}, f32[64,512]{1,0:T(8,128)S(1)}, u32[]{:S(2)}, u32[]{:S(2)}) collective-permute-start(f32[64,512]{1,0:T(8,128)S(1)} %in_features.1.refs_0_), channel_id=1, source_target_pairs={{0,3},{1,2},{2,1},{3,0},{4,7},{5,6},{6,5},{7,4},{8,11},{9,10},{10,... | collective-permute-start | bytes 393224 | tf_op jit(solution)/shard_map/ppermute | solution.py:24
  12.4 0.6 collective-permute-start
  13.0 18.7 %out_features.1.refs_4_ = f32[64,2048]{1,0:T(8,128)S(1)} custom-call(bf16[2048,7168]{1,0:T(8,128)(2,1)} %rows_ref.3, bf16[64,7168]{1,0:T(8,128)(2,1)} %proj_ref.3), custom_call_target="tpu_custom_call" | custom-call | tf_op jit(solution)/shard_map/out_features/pallas_call | solution.py:89
  31.8 0.6 partial_vectors.1
  32.5 2.4 %collective-permute-start.3 = (f32[2,4096]{1,0:T(2,128)S(1)}, f32[2,4096]{1,0:T(2,128)S(1)}, u32[]{:S(2)}, u32[]{:S(2)}) collective-permute-start(f32[2,4096]{1,0:T(2,128)S(1)} %reshape.11), channel_id=1, source_target_pairs={{0,2},{1,3},{2,0},{3,1},{4,6},{5,7},{6,4},{7,5},{8,10},{9,11},{10,... | collective-permute-start | bytes 98312 | tf_op jit(solution)/shard_map/ppermute | solution.py:24
  34.9 2.5 %collective-permute-done.3 = f32[2,4096]{1,0:T(2,128)S(1)} collective-permute-done((f32[2,4096]{1,0:T(2,128)S(1)}, f32[2,4096]{1,0:T(2,128)S(1)}, u32[]{:S(2)}, u32[]{:S(2)}) %collective-permute-start.3) | collective-permute-done | bytes 32800 | tf_op jit(solution)/shard_map/ppermute | solution.py:24
  37.4 1.4 %collective-permute-start.4 = (f32[2,4096]{1,0:T(2,128)S(1)}, f32[2,4096]{1,0:T(2,128)S(1)}, u32[]{:S(2)}, u32[]{:S(2)}) collective-permute-start(f32[2,4096]{1,0:T(2,128)S(1)} %add.9), channel_id=1, source_target_pairs={{0,1},{1,0},{2,3},{3,2},{4,5},{5,4},{6,7},{7,6},{8,9},{9,8},{10,11... | collective-permute-start | bytes 98312 | tf_op jit(solution)/shard_map/ppermute | solution.py:24
  38.9 2.5 %collective-permute-done.4 = f32[2,4096]{1,0:T(2,128)S(1)} collective-permute-done((f32[2,4096]{1,0:T(2,128)S(1)}, f32[2,4096]{1,0:T(2,128)S(1)}, u32[]{:S(2)}, u32[]{:S(2)}) %collective-permute-start.4) | collective-permute-done | bytes 32800 | tf_op jit(solution)/shard_map/ppermute | solution.py:24
  41.5 1.7 %collective-permute-start.6 = (f32[2,4096]{1,0:T(2,128)S(1)}, f32[2,4096]{1,0:T(2,128)S(1)}, u32[]{:S(2)}, u32[]{:S(2)}) collective-permute-start(f32[2,4096]{1,0:T(2,128)S(1)} %add.10.refs_0_), channel_id=1, source_target_pairs={{0,8},{4,12},{8,0},{12,4},{1,9},{5,13},{9,1},{13,5},{2,10},{6,14},... | collective-permute-start | bytes 98312 | tf_op jit(solution)/shard_map/ppermute | solution.py:24
  43.2 0.2 collective-permute-start.5
  43.3 2.3 %split_prior.1 = (bf16[256,4096]{1,0:T(8,128)(2,1)S(1)}, bf16[256,4096]{1,0:T(8,128)(2,1)S(1)}) custom-call(f32[256,4096]{1,0:T(8,128)} %prior_ref.1), custom_call_target="tpu_custom_call" | custom-call | tf_op jit(solution)/shard_map/split_prior/pallas_call | solution.py:122
  45.7 1.5 %cg_start.1 = (f32[8,4096]{1,0:T(8,128)S(1)}, bf16[16,4096]{1,0:T(8,128)(2,1)S(1)}, f32[8,128]{1,0:T(8,128)S(1)}, f32[8,256]{1,0:T(8,128)S(1)}, f32[8,128]{1,0:T(8,128)S(1)}) custom-call(f32[2,4096]{1,0:T(2,128)S(1)} %add.10.refs_0_, f32[2,4096]{1,0:T(2,128)S(1)} %collective-permute-done.5.refs_1_, f32[2,4096]{1,0:T(2,128)S(1)} %collective-permute-done.6.refs_2_, ...), custom_call_target="tpu_custom_call" | custom-call | tf_op jit(solution)/shard_map/cg_start/pallas_call | solution.py:221
  47.2 13.2 %all_to_all.20.refs_0_ = f32[16,8,256]{2,1,0:T(8,128)S(1)} all-to-all(f32[16,8,256]{2,1,0:T(8,128)S(1)} %broadcast_in_dim.10), channel_id=1, replica_groups=mesh['groups'=2,'dp'=4,'tensor'=4] {'dp','tensor'}, dimensions={0} | all-to-all | bytes 262144 | tf_op jit(solution)/shard_map/all_to_all | solution.py:32
  60.4 1.6 %cg_step.3 = (f32[8,256]{1,0:T(8,128)S(1)}, f32[8,128]{1,0:T(8,128)S(1)}, f32[8,256]{1,0:T(8,128)S(1)}, f32[8,4096]{1,0:T(8,128)S(1)}, f32[8,4096]{1,0:T(8,128)S(1)}, /*index=5*/f32[8,4096]{1,0:T(8,128)S(1)}) custom-call(f32[16,8,256]{2,1,0:T(8,128)S(1)} %all_to_all.20.refs_0_, bf16[256,4096]{1,0:T(8,128)(2,1)S(1)} %get-tuple-element.30.refs_4_.refs_1_, ...), custom_call_target="tpu_custom_call" | custom-call | tf_op jit(solution)/shard_map/cg_step/pallas_call | solution.py:292
  62.0 10.4 %all_to_all.21.refs_0_ = f32[16,8,256]{2,1,0:T(8,128)S(1)} all-to-all(f32[16,8,256]{2,1,0:T(8,128)S(1)} %broadcast_in_dim.11), channel_id=1, replica_groups=mesh['groups'=2,'dp'=4,'tensor'=4] {'dp','tensor'}, dimensions={0} | all-to-all | bytes 262144 | tf_op jit(solution)/shard_map/all_to_all | solution.py:32
  72.4 1.6 %cg_step.4 = (f32[8,256]{1,0:T(8,128)S(1)}, f32[8,128]{1,0:T(8,128)S(1)}, f32[8,256]{1,0:T(8,128)S(1)}, f32[8,4096]{1,0:T(8,128)S(1)}, f32[8,4096]{1,0:T(8,128)S(1)}, /*index=5*/f32[8,4096]{1,0:T(8,128)S(1)}) custom-call(f32[16,8,256]{2,1,0:T(8,128)S(1)} %all_to_all.21.refs_0_, bf16[256,4096]{1,0:T(8,128)(2,1)S(1)} %get-tuple-element.30.refs_4_.refs_1_, ...), custom_call_target="tpu_custom_call" | custom-call | tf_op jit(solution)/shard_map/cg_step/pallas_call | solution.py:292
  74.0 10.4 %all_to_all.22.refs_0_ = f32[16,8,256]{2,1,0:T(8,128)S(1)} all-to-all(f32[16,8,256]{2,1,0:T(8,128)S(1)} %broadcast_in_dim.12), channel_id=1, replica_groups=mesh['groups'=2,'dp'=4,'tensor'=4] {'dp','tensor'}, dimensions={0} | all-to-all | bytes 262144 | tf_op jit(solution)/shard_map/all_to_all | solution.py:32
  84.4 1.7 %cg_step.5 = (f32[1,128]{1,0:T(1,128)S(1)}, f32[1,128]{1,0:T(1,128)S(1)}, f32[8,4096]{1,0:T(8,128)S(1)}, f32[8,4096]{1,0:T(8,128)S(1)}) custom-call(f32[16,8,256]{2,1,0:T(8,128)S(1)} %all_to_all.22.refs_0_, bf16[256,4096]{1,0:T(8,128)(2,1)S(1)} %get-tuple-element.30.refs_4_.refs_1_, bf16[256,4096]{1,0:T(8,128)(2,1)S(1)} %get-tuple-element.31.refs_5_.refs_2_, ...), custom_call_target="tpu_custom_call" | custom-call | tf_op jit(solution)/shard_map/cg_step/pallas_call | solution.py:292
  86.1 0.6 broadcast_in_dim.14
  86.7 3.5 %all-to-all-start.3 = ((f32[16,1,128]{2,1,0:T(1,128)}), f32[16,1,128]{2,1,0:T(1,128)S(1)}, u32[]{:S(2)}, u32[]{:S(2)}) async-start(f32[16,1,128]{2,1,0:T(1,128)} %broadcast_in_dim.14), calls=%async_computation.3 | async-start | bytes 16384 | tf_op jit(solution)/shard_map/all_to_all | solution.py:32
  90.1 0.3 scores.1
  90.4 6.0 %all-to-all-done.3 = f32[16,1,128]{2,1,0:T(1,128)S(1)} async-done(((f32[16,1,128]{2,1,0:T(1,128)}), f32[16,1,128]{2,1,0:T(1,128)S(1)}, u32[]{:S(2)}, u32[]{:S(2)}) %all-to-all-start.3) | async-done | bytes 8224 | tf_op jit(solution)/shard_map/all_to_all | solution.py:32
  96.5 0.7 multiply_add_fusion
  (19 shorter events, 0.3 us)
Async XLA Ops:
  7.3 24.5 %collective-permute-start.2 = (f32[64,512]{1,0:T(8,128)S(1)}, f32[64,512]{1,0:T(8,128)S(1)}, u32[]{:S(2)}, u32[]{:S(2)}) collective-permute-start(f32[64,512]{1,0:T(8,128)S(1)} %in_features.1.refs_0_), channel_id=1, source_target_pairs={{0,3},{1,2},{2,1},{3,0},{4,7},{5,6},{6,5},{7,4},{8,11},{9,10},{10,... | collective-permute-start | bytes 393224 | tf_op jit(solution)/shard_map/ppermute | solution.py:24
  12.4 19.4 %collective-permute-start.1 = (f32[64,512]{1,0:T(8,128)S(1)}, f32[64,512]{1,0:T(8,128)S(1)}, u32[]{:S(2)}, u32[]{:S(2)}) collective-permute-start(f32[64,512]{1,0:T(8,128)S(1)} %in_features.1.refs_0_), channel_id=1, source_target_pairs={{0,2},{1,3},{2,0},{3,1},{4,6},{5,7},{6,4},{7,5},{8,10},{9,11},{10,... | collective-permute-start | bytes 393224 | tf_op jit(solution)/shard_map/ppermute | solution.py:24
  12.4 19.4 %collective-permute-start = (f32[64,512]{1,0:T(8,128)S(1)}, f32[64,512]{1,0:T(8,128)S(1)}, u32[]{:S(2)}, u32[]{:S(2)}) collective-permute-start(f32[64,512]{1,0:T(8,128)S(1)} %in_features.1.refs_0_), channel_id=1, source_target_pairs={{0,1},{1,0},{2,3},{3,2},{4,5},{5,4},{6,7},{7,6},{8,9},{9,8},{10,11... | collective-permute-start | bytes 393224 | tf_op jit(solution)/shard_map/ppermute | solution.py:24
  32.5 4.9 %collective-permute-start.3 = (f32[2,4096]{1,0:T(2,128)S(1)}, f32[2,4096]{1,0:T(2,128)S(1)}, u32[]{:S(2)}, u32[]{:S(2)}) collective-permute-start(f32[2,4096]{1,0:T(2,128)S(1)} %reshape.11), channel_id=1, source_target_pairs={{0,2},{1,3},{2,0},{3,1},{4,6},{5,7},{6,4},{7,5},{8,10},{9,11},{10,... | collective-permute-start | bytes 98312 | tf_op jit(solution)/shard_map/ppermute | solution.py:24
  37.4 4.0 %collective-permute-start.4 = (f32[2,4096]{1,0:T(2,128)S(1)}, f32[2,4096]{1,0:T(2,128)S(1)}, u32[]{:S(2)}, u32[]{:S(2)}) collective-permute-start(f32[2,4096]{1,0:T(2,128)S(1)} %add.9), channel_id=1, source_target_pairs={{0,1},{1,0},{2,3},{3,2},{4,5},{5,4},{6,7},{7,6},{8,9},{9,8},{10,11... | collective-permute-start | bytes 98312 | tf_op jit(solution)/shard_map/ppermute | solution.py:24
  41.4 4.3 %collective-permute-start.7 = (f32[2,4096]{1,0:T(2,128)S(1)}, f32[2,4096]{1,0:T(2,128)S(1)}, u32[]{:S(2)}, u32[]{:S(2)}) collective-permute-start(f32[2,4096]{1,0:T(2,128)S(1)} %add.10.refs_0_), channel_id=1, source_target_pairs={{0,12},{4,8},{8,4},{12,0},{1,13},{5,9},{9,5},{13,1},{2,14},{6,10},... | collective-permute-start | bytes 98312 | tf_op jit(solution)/shard_map/ppermute | solution.py:24
  41.5 4.2 %collective-permute-start.6 = (f32[2,4096]{1,0:T(2,128)S(1)}, f32[2,4096]{1,0:T(2,128)S(1)}, u32[]{:S(2)}, u32[]{:S(2)}) collective-permute-start(f32[2,4096]{1,0:T(2,128)S(1)} %add.10.refs_0_), channel_id=1, source_target_pairs={{0,8},{4,12},{8,0},{12,4},{1,9},{5,13},{9,1},{13,5},{2,10},{6,14},... | collective-permute-start | bytes 98312 | tf_op jit(solution)/shard_map/ppermute | solution.py:24
  43.2 2.5 %collective-permute-start.5 = (f32[2,4096]{1,0:T(2,128)S(1)}, f32[2,4096]{1,0:T(2,128)S(1)}, u32[]{:S(2)}, u32[]{:S(2)}) collective-permute-start(f32[2,4096]{1,0:T(2,128)S(1)} %add.10.refs_0_), channel_id=1, source_target_pairs={{0,4},{4,0},{8,12},{12,8},{1,5},{5,1},{9,13},{13,9},{2,6},{6,2},{1... | collective-permute-start | bytes 98312 | tf_op jit(solution)/shard_map/ppermute | solution.py:24
  72.4 17.7 %copy-start = (bf16[32,4096]{1,0:T(8,128)(2,1)S(1)}, bf16[32,4096]{1,0:T(8,128)(2,1)}, u32[]{:S(2)}) copy-start(bf16[32,4096]{1,0:T(8,128)(2,1)} %queries_ref.1) | copy-start | bytes 786436
  86.7 9.8 %all-to-all-start.3 = ((f32[16,1,128]{2,1,0:T(1,128)}), f32[16,1,128]{2,1,0:T(1,128)S(1)}, u32[]{:S(2)}, u32[]{:S(2)}) async-start(f32[16,1,128]{2,1,0:T(1,128)} %broadcast_in_dim.14), calls=%async_computation.3 | async-start | bytes 16384 | tf_op jit(solution)/shard_map/all_to_all | solution.py:32

commit v11 on v8

--- a/solution.py
+++ b/solution.py
@@ -12,6 +12,7 @@
 SEQ = 1024
 ITERS = 4
 LANES = 128
+FEW = 4
 NT = (((1,), (1,)), ((), ()))
 HIGHEST = lax.Precision.HIGHEST
 ANY_SPEC = pl.BlockSpec(memory_space=pl.ANY)
@@ -32,14 +33,23 @@
     return lax.all_to_all(jnp.broadcast_to(value[None], (size,) + value.shape), axes, 0, 0)
 
 
+def order_of(size):
+    return (0, 2, 3, 1) if size == 4 else tuple(range(size))
+
+
+def direct(value, axis, size):
+    return [value] + [swap(value, axis, size, k) for k in order_of(size)[1:]]
+
+
 def sum_over(value, axis, size):
-    for bit in bits(size):
-        value = value + swap(value, axis, size, bit)
-    return value
-
-
-def direct(value, axis, size):
-    return [value] + [swap(value, axis, size, k) for k in reversed(range(1, size))][::-1]
+    if size > FEW:
+        for bit in bits(size):
+            value = value + swap(value, axis, size, bit)
+        return value
+    blocks = direct(value, axis, size)
+    while len(blocks) > 1:
+        blocks = [a + b for a, b in zip(blocks[::2], blocks[1::2])]
+    return blocks[0]
 
 
 def in_hbm(value):
@@ -69,7 +79,7 @@
     return spans
 
 
-def stream_kernel(spans, rows_ref, proj_ref, feats_ref, held, proj, sems):
+def stream_kernel(spans, rows_ref, proj_ref, feats_ref, held, proj, turned, sems):
     first = pltpu.make_async_copy(proj_ref, proj, sems.at[len(spans)])
     copies = [
         pltpu.make_async_copy(rows_ref.at[span], held.at[span], sems.at[c])
@@ -79,9 +89,10 @@
     for copy in copies:
         copy.start()
     first.wait()
+    turned[...] = proj[...].T
     for copy, span in zip(copies, spans):
         copy.wait()
-        feats = lax.dot_general(held[span], proj[...], NT, preferred_element_type=jnp.float32)
+        feats = jnp.dot(held[span], turned[...], preferred_element_type=jnp.float32)
         feats_ref[:, span] = feats.T
 
 
@@ -95,6 +106,7 @@
         scratch_shapes=[
             pltpu.VMEM(rows.shape, jnp.bfloat16),
             pltpu.VMEM(proj.shape, jnp.bfloat16),
+            pltpu.VMEM(proj.shape[::-1], jnp.bfloat16),
             pltpu.SemaphoreType.DMA((len(spans) + 1,)),
         ],
         compiler_params=pltpu.CompilerParams(vmem_limit_bytes=limit * 2**20),
@@ -135,7 +147,7 @@
     blocks, (out_ref, part_ref, held) = refs[:size], refs[size:]
     me = lax.axis_index("tensor")
     tokens = blocks[0].shape[1]
-    for k, block in enumerate(blocks):
+    for k, block in zip(order_of(size), blocks):
         start = pl.multiple_of((me ^ k) * tokens, LANES)
         held[:, pl.ds(start, tokens)] = block[...]
     for s in range(part_ref.shape[0]):
@@ -199,7 +211,7 @@
     pieces, refs = refs[:size], refs[size:]
     upper_ref, lower_ref, vectors_ref, vector_pieces_ref, scale_ref, applied_ref, norm_ref, held = refs
     dp = lax.axis_index("dp")
-    for k, piece in enumerate(pieces):
+    for k, piece in zip(order_of(size), pieces):
         held[dp ^ k] = piece[...]
     vectors = jnp.concatenate([held[k] for k in range(size)], axis=0)
     vectors_ref[...] = vectors
@@ -230,17 +242,25 @@
     )(*pieces, *prior_pieces)
 
 
-def on_lanes(column):
-    seqs = column.shape[0]
-    row = lax.broadcasted_iota(jnp.int32, (seqs, LANES), 0)
-    lane = lax.broadcasted_iota(jnp.int32, (seqs, LANES), 1)
-    return jnp.sum(jnp.where(row == lane, column, 0.0), axis=0, keepdims=True)
-
-
-def step_kernel(tensor_size, first, last, *refs):
-    blocks_ref, upper_ref, lower_ref, vectors_ref, vector_pieces_ref, scale_ref = refs[:6]
-    norm_ref, fisher_direction_ref = refs[6:8]
-    refs = refs[8:]
+def place_blocks(blocks, sizes, held):
+    if len(blocks) == 1:
+        count, _, rows = blocks[0].shape
+        for i in range(count):
+            held[:, i * rows : (i + 1) * rows] = blocks[0][i]
+        return
+    dp, tensor = lax.axis_index("dp"), lax.axis_index("tensor")
+    rows = blocks[0].shape[2]
+    for k, block in zip(order_of(sizes[0]), blocks):
+        for i, j in enumerate(order_of(sizes[1])):
+            start = ((dp ^ k) * sizes[1] + (tensor ^ j)) * rows
+            held[:, pl.ds(pl.multiple_of(start, LANES), rows)] = block[i]
+
+
+def step_kernel(count, sizes, first, last, *refs):
+    blocks, refs = refs[:count], refs[count:]
+    upper_ref, lower_ref, vectors_ref, vector_pieces_ref, scale_ref = refs[:5]
+    norm_ref, fisher_direction_ref = refs[5:7]
+    refs = refs[7:]
     if not first:
         fisher_residual_ref, direction_ref, residual_ref, solution_ref = refs[:4]
         refs = refs[4:]
@@ -248,10 +268,8 @@
         curvature_out, norm_out, direction_out, solution_out, held = refs
     else:
         fisher_direction_out, norm_out, fisher_residual_out, direction_out, residual_out, solution_out, held = refs
-    me = flat_index(tensor_size)
-    count, _, rows = blocks_ref.shape
-    for i in range(count):
-        held[:, i * rows : (i + 1) * rows] = blocks_ref[i]
+    me = flat_index(sizes[1])
+    place_blocks(blocks, sizes, held)
     applied = held[...]
     scale = scale_ref[...][:, :1]
     twice = apply_fisher(
@@ -273,25 +291,24 @@
     fisher_direction = fisher_residual + share * fisher_direction
     direction_out[...] = direction
     solution_out[...] = solution
+    norm_out[...] = jnp.broadcast_to(norm_next, norm_out.shape)
     if last:
-        own = own_columns(direction_out, me, rows)
-        curvature_out[...] = on_lanes(row_sum(own * fisher_direction))
-        norm_out[...] = on_lanes(norm_next)
+        own = own_columns(direction_out, me, fisher_direction.shape[1])
+        curvature_out[...] = jnp.broadcast_to(row_sum(own * fisher_direction), curvature_out.shape)
     else:
         fisher_direction_out[...] = fisher_direction
         fisher_residual_out[...] = fisher_residual
         residual_out[...] = residual
-        norm_out[...] = jnp.broadcast_to(norm_next, norm_out.shape)
-
-
-def step_cg(blocks, fixed, norm, state, last, tensor_size):
+
+
+def step_cg(blocks, fixed, norm, state, last, sizes):
     first = len(state) == 1
     whole, rows = F32(fixed[2].shape), F32(state[0].shape)
-    row = F32((1, LANES))
-    operands = [blocks, *fixed, norm, *state]
-    out_shape = (row, row, whole, whole) if last else (rows, F32(norm.shape), rows, whole, whole, whole)
-    return pl.pallas_call(
-        functools.partial(step_kernel, tensor_size, first, last),
+    column = F32(norm.shape)
+    operands = [*blocks, *fixed, norm, *state]
+    out_shape = (column, column, whole, whole) if last else (rows, column, rows, whole, whole, whole)
+    return pl.pallas_call(
+        functools.partial(step_kernel, len(blocks), sizes, first, last),
         out_shape=out_shape,
         in_specs=[VMEM_SPEC] * len(operands),
         out_specs=(VMEM_SPEC,) * len(out_shape),
@@ -323,25 +340,34 @@
 
 def on_device(dp_size, tensor_size, inputs, in_proj, out_grads, out_proj, prior, queries):
     width = R_IN * R_OUT
-    both, devices = ("dp", "tensor"), dp_size * tensor_size
-    in_blocks = direct(features(inputs, in_proj, (256, 128), 16, "in_features"), "tensor", tensor_size)
-    out_local = features(out_grads, out_proj, (512, 512, 512, 256, 128), 40, "out_features")
+    both, devices, sizes = ("dp", "tensor"), dp_size * tensor_size, (dp_size, tensor_size)
+    in_blocks = direct(features(inputs, in_proj, (256, 128), 20, "in_features"), "tensor", tensor_size)
+    out_local = features(out_grads, out_proj, (256,) * 7 + (128,), 44, "out_features")
     partial = partial_vectors(in_blocks, out_local).reshape(-1, width)
     pieces = direct(sum_over(partial, "tensor", tensor_size), "dp", dp_size)
     prior_pieces = [in_vmem(piece) for piece in split_prior(prior)]
+    few = max(sizes) <= FEW and prior.shape[0] % LANES == 0
+
+    def gather_rows(values):
+        if not few:
+            return [gather(values, both, devices)]
+        return direct(jnp.stack(direct(values, "tensor", tensor_size)), "dp", dp_size)
+
     vectors, vector_pieces, scale, applied_rows, norm = start_cg(pieces, prior_pieces, tensor_size)
     fixed = (*prior_pieces, vectors, vector_pieces, scale)
     state = [applied_rows]
     for iteration in range(1, ITERS - 1):
-        blocks = gather(state[0], both, devices)
-        applied_rows, norm, *others = step_cg(blocks, fixed, norm, state, False, tensor_size)
+        blocks = gather_rows(state[0])
+        applied_rows, norm, *others = step_cg(blocks, fixed, norm, state, False, sizes)
         state = [applied_rows, *others]
-    blocks = gather(state[0], both, devices)
-    curvature, norm, direction, solved = step_cg(blocks, fixed, norm, state, True, tensor_size)
-    curvature = jnp.sum(gather(curvature, both, devices), axis=0)
+    blocks = gather_rows(state[0])
+    curvature, norm, direction, solved = step_cg(blocks, fixed, norm, state, True, sizes)
+    if few:
+        curvature = sum_over(sum_over(curvature, "tensor", tensor_size), "dp", dp_size)
+    else:
+        curvature = jnp.sum(gather(curvature, both, devices), axis=0)
     solved, along = score(solved, direction, queries)
-    step = (norm / curvature)[0, : solved.shape[0]]
-    return solved + step[:, None] * along
+    return solved + (norm / curvature)[:, :1] * along
 
 
 def solution(mesh):

time: 98.5 us -> 94 us (0.954)
  blocking collectives: 34 us -> 0 us
  starting transfers between devices: 14.9 us -> 34.9 us
  waiting for transfers between devices: 11.1 us -> 31 us
  Pallas kernels: 36.6 us -> 26.9 us
    all_to_all x3 -> x0, blocking collectives: 34 us -> none  [gather(): lax.all_to_all(jnp.broadcast_to(value[None], (size,) + value.shape), axes...]
    ppermute x8 -> x33, waiting for transfers between devices: 5.06 us -> 31 us  [swap(): return lax.ppermute(value, axis, [(i, i ^ bit) for i in range(size)])]
    ppermute x8 -> x33, starting transfers between devices: 11.5 us -> 34.9 us  [swap(): return lax.ppermute(value, axis, [(i, i ^ bit) for i in range(size)])]
    pallas_call x2, Pallas kernels: 27 us -> 17.4 us  [features(): pl.pallas_call(functools.partial(stream_kernel, spans), out_shape=pltpu.V...]
    all_to_all x1 -> x0, waiting for transfers between devices: 6.03 us -> none  [gather(): lax.all_to_all(jnp.broadcast_to(value[None], (size,) + value.shape), axes...]
    all_to_all x1 -> x0, starting transfers between devices: 3.45 us -> none  [gather(): lax.all_to_all(jnp.broadcast_to(value[None], (size,) + value.shape), axes...]
  transfers between devices with their start and end apart: 9 -> 33, of which waited for: 3 -> 23; matrix products, arithmetic and copies ran while one was open for 0% -> 0% of each run, Pallas kernels for 23% -> 16%
where the time goes in v11:
time: 94 us; the launch traced here: 93.9 us
  starting transfers between devices  34.9 us (37%)
  waiting for transfers between devices  31 us (33%)
  Pallas kernels  26.9 us (29%)
    ppermute x33, starting transfers between devices, swap(): return lax.ppermute(value, axis, [(i, i ^ bit) for i in range(size)])  34.9 us
    ppermute x33, waiting for transfers between devices, swap(): return lax.ppermute(value, axis, [(i, i ^ bit) for i in range(size)])  31 us
    pallas_call x2, Pallas kernels, features(): pl.pallas_call(functools.partial(stream_kernel, spans), out_shape=pltpu.V...  17.4 us
    pallas_call x3, Pallas kernels, step_cg(): pl.pallas_call(functools.partial(step_kernel, len(blocks), sizes, first,...  4.84 us
    pallas_call x1, Pallas kernels, split_prior(): pl.pallas_call(split_kernel, out_shape=(pltpu.VMEM(prior.shape, jnp.bfloa...  2.32 us
  transfers between devices with their start and end apart: 33, of which 23 were waited for; matrix products, arithmetic and copies ran while one was open for 0% of the time, Pallas kernels for 16%

profile of v11, /device:TPU:0, one launch (start us, length us, event | category | flops | bytes accessed | tf_op | source)
XLA Modules:
  0.0 93.9 jit_solution(10298760862672268227)
XLA Ops:
  0.0 5.3 %in_features.1.refs_0_ = f32[64,512]{1,0:T(8,128)S(1)} custom-call(bf16[512,8192]{1,0:T(8,128)(2,1)} %rows_ref.2, bf16[64,8192]{1,0:T(8,128)(2,1)} %proj_ref.2), custom_call_target="tpu_custom_call" | custom-call | tf_op jit(solution)/shard_map/in_features/pallas_call | solution.py:101
  5.3 3.1 %collective-permute-start.2 = (f32[64,512]{1,0:T(8,128)S(1)}, f32[64,512]{1,0:T(8,128)S(1)}, u32[]{:S(2)}, u32[]{:S(2)}) collective-permute-start(f32[64,512]{1,0:T(8,128)S(1)} %in_features.1.refs_0_), channel_id=1, source_target_pairs={{0,1},{1,0},{2,3},{3,2},{4,5},{5,4},{6,7},{7,6},{8,9},{9,8},{10,11... | collective-permute-start | bytes 393224 | tf_op jit(solution)/shard_map/ppermute | solution.py:25
  8.4 2.5 %collective-permute-start.1 = (f32[64,512]{1,0:T(8,128)S(1)}, f32[64,512]{1,0:T(8,128)S(1)}, u32[]{:S(2)}, u32[]{:S(2)}) collective-permute-start(f32[64,512]{1,0:T(8,128)S(1)} %in_features.1.refs_0_), channel_id=1, source_target_pairs={{0,3},{1,2},{2,1},{3,0},{4,7},{5,6},{6,5},{7,4},{8,11},{9,10},{10,... | collective-permute-start | bytes 393224 | tf_op jit(solution)/shard_map/ppermute | solution.py:25
  11.0 12.1 %out_features.1.refs_4_ = f32[64,2048]{1,0:T(8,128)S(1)} custom-call(bf16[2048,7168]{1,0:T(8,128)(2,1)} %rows_ref.3, bf16[64,7168]{1,0:T(8,128)(2,1)} %proj_ref.3), custom_call_target="tpu_custom_call" | custom-call | tf_op jit(solution)/shard_map/out_features/pallas_call | solution.py:101
  23.9 1.9 %collective-permute-start.5 = (f32[2,4096]{1,0:T(2,128)S(1)}, f32[2,4096]{1,0:T(2,128)S(1)}, u32[]{:S(2)}, u32[]{:S(2)}) collective-permute-start(f32[2,4096]{1,0:T(2,128)S(1)} %reshape.3), channel_id=1, source_target_pairs={{0,1},{1,0},{2,3},{3,2},{4,5},{5,4},{6,7},{7,6},{8,9},{9,8},{10,11... | collective-permute-start | bytes 98312 | tf_op jit(solution)/shard_map/ppermute | solution.py:25
  25.7 2.5 %collective-permute-start.4 = (f32[2,4096]{1,0:T(2,128)S(1)}, f32[2,4096]{1,0:T(2,128)S(1)}, u32[]{:S(2)}, u32[]{:S(2)}) collective-permute-start(f32[2,4096]{1,0:T(2,128)S(1)} %reshape.3), channel_id=1, source_target_pairs={{0,3},{1,2},{2,1},{3,0},{4,7},{5,6},{6,5},{7,4},{8,11},{9,10},{10,... | collective-permute-start | bytes 98312 | tf_op jit(solution)/shard_map/ppermute | solution.py:25
  28.2 3.2 %collective-permute-done.4 = f32[2,4096]{1,0:T(2,128)S(1)} collective-permute-done((f32[2,4096]{1,0:T(2,128)S(1)}, f32[2,4096]{1,0:T(2,128)S(1)}, u32[]{:S(2)}, u32[]{:S(2)}) %collective-permute-start.4) | collective-permute-done | bytes 32800 | tf_op jit(solution)/shard_map/ppermute | solution.py:25
  33.1 1.6 %collective-permute-start.7 = (f32[2,4096]{1,0:T(2,128)S(1)}, f32[2,4096]{1,0:T(2,128)S(1)}, u32[]{:S(2)}, u32[]{:S(2)}) collective-permute-start(f32[2,4096]{1,0:T(2,128)S(1)} %add_add_fusion.refs_0_), channel_id=1, source_target_pairs={{0,12},{4,8},{8,4},{12,0},{1,13},{5,9},{9,5},{13,1},{2,14},{6,10},... | collective-permute-start | bytes 98312 | tf_op jit(solution)/shard_map/ppermute | solution.py:25
  35.3 2.3 %split_prior.1 = (bf16[256,4096]{1,0:T(8,128)(2,1)S(1)}, bf16[256,4096]{1,0:T(8,128)(2,1)S(1)}) custom-call(f32[256,4096]{1,0:T(8,128)} %prior_ref.1), custom_call_target="tpu_custom_call" | custom-call | tf_op jit(solution)/shard_map/split_prior/pallas_call | solution.py:135
  40.1 1.9 %collective-permute-start.10 = (f32[8,256]{1,0:T(8,128)S(1)}, f32[8,256]{1,0:T(8,128)S(1)}, u32[]{:S(2)}, u32[]{:S(2)}) collective-permute-start(f32[8,256]{1,0:T(8,128)S(1)} %get-tuple-element.32.refs_10_), channel_id=1, source_target_pairs={{0,3},{1,2},{2,1},{3,0},{4,7},{5,6},{6,5},{7,4},{8,11},{9,10},{10,... | collective-permute-start | bytes 24584 | tf_op jit(solution)/shard_map/ppermute | solution.py:25
  42.0 1.7 %collective-permute-start.9 = (f32[8,256]{1,0:T(8,128)S(1)}, f32[8,256]{1,0:T(8,128)S(1)}, u32[]{:S(2)}, u32[]{:S(2)}) collective-permute-start(f32[8,256]{1,0:T(8,128)S(1)} %get-tuple-element.32.refs_10_), channel_id=1, source_target_pairs={{0,2},{1,3},{2,0},{3,1},{4,6},{5,7},{6,4},{7,5},{8,10},{9,11},{10,... | collective-permute-start | bytes 24584 | tf_op jit(solution)/shard_map/ppermute | solution.py:25
  43.8 1.8 %collective-permute-done.10 = f32[8,256]{1,0:T(8,128)S(1)} collective-permute-done((f32[8,256]{1,0:T(8,128)S(1)}, f32[8,256]{1,0:T(8,128)S(1)}, u32[]{:S(2)}, u32[]{:S(2)}) %collective-permute-start.10) | collective-permute-done | bytes 8224 | tf_op jit(solution)/shard_map/ppermute | solution.py:25
  53.7 2.2 %collective-permute-start.16 = (f32[8,256]{1,0:T(8,128)S(1)}, f32[8,256]{1,0:T(8,128)S(1)}, u32[]{:S(2)}, u32[]{:S(2)}) collective-permute-start(f32[8,256]{1,0:T(8,128)S(1)} %get-tuple-element.37.refs_10_), channel_id=1, source_target_pairs={{0,3},{1,2},{2,1},{3,0},{4,7},{5,6},{6,5},{7,4},{8,11},{9,10},{10,... | collective-permute-start | bytes 24584 | tf_op jit(solution)/shard_map/ppermute | solution.py:25
  56.4 2.7 %collective-permute-done.16 = f32[8,256]{1,0:T(8,128)S(1)} collective-permute-done((f32[8,256]{1,0:T(8,128)S(1)}, f32[8,256]{1,0:T(8,128)S(1)}, u32[]{:S(2)}, u32[]{:S(2)}) %collective-permute-start.16) | collective-permute-done | bytes 8224 | tf_op jit(solution)/shard_map/ppermute | solution.py:25
  60.4 1.6 %collective-permute-start.19 = (f32[4,8,256]{2,1,0:T(8,128)S(1)}, f32[4,8,256]{2,1,0:T(8,128)S(1)}, u32[]{:S(2)}, u32[]{:S(2)}) collective-permute-start(f32[4,8,256]{2,1,0:T(8,128)S(1)} %pad_maximum_fusion.1.refs_0_), channel_id=1, source_target_pairs={{0,12},{4,8},{8,4},{12,0},{1,13},{5,9},{9,5},{13,1},{2,14},{6,10},... | collective-permute-start | bytes 98312 | tf_op jit(solution)/shard_map/ppermute | solution.py:25
  63.8 2.2 %collective-permute-done.18.refs_1_ = f32[4,8,256]{2,1,0:T(8,128)S(1)} collective-permute-done((f32[4,8,256]{2,1,0:T(8,128)S(1)}, f32[4,8,256]{2,1,0:T(8,128)S(1)}, u32[]{:S(2)}, u32[]{:S(2)}) %collective-permute-start.18) | collective-permute-done | bytes 32800 | tf_op jit(solution)/shard_map/ppermute | solution.py:25
  67.7 1.8 %collective-permute-start.22 = (f32[8,256]{1,0:T(8,128)S(1)}, f32[8,256]{1,0:T(8,128)S(1)}, u32[]{:S(2)}, u32[]{:S(2)}) collective-permute-start(f32[8,256]{1,0:T(8,128)S(1)} %get-tuple-element.43.refs_10_), channel_id=1, source_target_pairs={{0,3},{1,2},{2,1},{3,0},{4,7},{5,6},{6,5},{7,4},{8,11},{9,10},{10,... | collective-permute-start | bytes 24584 | tf_op jit(solution)/shard_map/ppermute | solution.py:25
  69.5 1.6 %collective-permute-start.21 = (f32[8,256]{1,0:T(8,128)S(1)}, f32[8,256]{1,0:T(8,128)S(1)}, u32[]{:S(2)}, u32[]{:S(2)}) collective-permute-start(f32[8,256]{1,0:T(8,128)S(1)} %get-tuple-element.43.refs_10_), channel_id=1, source_target_pairs={{0,2},{1,3},{2,0},{3,1},{4,6},{5,7},{6,4},{7,5},{8,10},{9,11},{10,... | collective-permute-start | bytes 24584 | tf_op jit(solution)/shard_map/ppermute | solution.py:25
  71.3 1.9 %collective-permute-done.22 = f32[8,256]{1,0:T(8,128)S(1)} collective-permute-done((f32[8,256]{1,0:T(8,128)S(1)}, f32[8,256]{1,0:T(8,128)S(1)}, u32[]{:S(2)}, u32[]{:S(2)}) %collective-permute-start.22) | collective-permute-done | bytes 8224 | tf_op jit(solution)/shard_map/ppermute | solution.py:25
  78.6 1.7 %cg_step.5 = (f32[8,128]{1,0:T(8,128)S(1)}, f32[8,128]{1,0:T(8,128)S(1)}, f32[8,4096]{1,0:T(8,128)S(1)}, f32[8,4096]{1,0:T(8,128)S(1)}) custom-call(f32[4,8,256]{2,1,0:T(8,128)S(1)} %pad_maximum_fusion.2.refs_0_, f32[4,8,256]{2,1,0:T(8,128)S(1)} %collective-permute-done.24.refs_1_, f32[4,8,256]{2,1,0:T(8,128)S(1)} %collective-permute-done.25.refs_2_, ...), custom_call_target="tpu_custom_call" | custom-call | tf_op jit(solution)/shard_map/cg_step/pallas_call | solution.py:310
  81.1 2.2 %collective-permute-start.28 = (f32[8,128]{1,0:T(8,128)S(1)}, f32[8,128]{1,0:T(8,128)S(1)}, u32[]{:S(2)}, u32[]{:S(2)}) collective-permute-start(f32[8,128]{1,0:T(8,128)S(1)} %get-tuple-element.53), channel_id=1, source_target_pairs={{0,3},{1,2},{2,1},{3,0},{4,7},{5,6},{6,5},{7,4},{8,11},{9,10},{10,... | collective-permute-start | bytes 12296 | tf_op jit(solution)/shard_map/ppermute | solution.py:25
  83.8 2.7 %collective-permute-done.28 = f32[8,128]{1,0:T(8,128)S(1)} collective-permute-done((f32[8,128]{1,0:T(8,128)S(1)}, f32[8,128]{1,0:T(8,128)S(1)}, u32[]{:S(2)}, u32[]{:S(2)}) %collective-permute-start.28) | collective-permute-done | bytes 4128 | tf_op jit(solution)/shard_map/ppermute | solution.py:25
  87.9 1.6 %collective-permute-start.31 = (f32[8,128]{1,0:T(8,128)S(1)}, f32[8,128]{1,0:T(8,128)S(1)}, u32[]{:S(2)}, u32[]{:S(2)}) collective-permute-start(f32[8,128]{1,0:T(8,128)S(1)} %add_add_fusion.1), channel_id=1, source_target_pairs={{0,12},{4,8},{8,4},{12,0},{1,13},{5,9},{9,5},{13,1},{2,14},{6,10},... | collective-permute-start | bytes 12296 | tf_op jit(solution)/shard_map/ppermute | solution.py:25
  91.0 2.1 %collective-permute-done.30 = f32[8,128]{1,0:T(8,128)S(1)} collective-permute-done((f32[8,128]{1,0:T(8,128)S(1)}, f32[8,128]{1,0:T(8,128)S(1)}, u32[]{:S(2)}, u32[]{:S(2)}) %collective-permute-start.30) | collective-permute-done | bytes 4128 | tf_op jit(solution)/shard_map/ppermute | solution.py:25
  (62 shorter events, 29.6 us)
Async XLA Ops:
  5.3 17.8 %collective-permute-start.2 = (f32[64,512]{1,0:T(8,128)S(1)}, f32[64,512]{1,0:T(8,128)S(1)}, u32[]{:S(2)}, u32[]{:S(2)}) collective-permute-start(f32[64,512]{1,0:T(8,128)S(1)} %in_features.1.refs_0_), channel_id=1, source_target_pairs={{0,1},{1,0},{2,3},{3,2},{4,5},{5,4},{6,7},{7,6},{8,9},{9,8},{10,11... | collective-permute-start | bytes 393224 | tf_op jit(solution)/shard_map/ppermute | solution.py:25
  8.4 14.7 %collective-permute-start.1 = (f32[64,512]{1,0:T(8,128)S(1)}, f32[64,512]{1,0:T(8,128)S(1)}, u32[]{:S(2)}, u32[]{:S(2)}) collective-permute-start(f32[64,512]{1,0:T(8,128)S(1)} %in_features.1.refs_0_), channel_id=1, source_target_pairs={{0,3},{1,2},{2,1},{3,0},{4,7},{5,6},{6,5},{7,4},{8,11},{9,10},{10,... | collective-permute-start | bytes 393224 | tf_op jit(solution)/shard_map/ppermute | solution.py:25
  10.9 12.2 %collective-permute-start = (f32[64,512]{1,0:T(8,128)S(1)}, f32[64,512]{1,0:T(8,128)S(1)}, u32[]{:S(2)}, u32[]{:S(2)}) collective-permute-start(f32[64,512]{1,0:T(8,128)S(1)} %in_features.1.refs_0_), channel_id=1, source_target_pairs={{0,2},{1,3},{2,0},{3,1},{4,6},{5,7},{6,4},{7,5},{8,10},{9,11},{10,... | collective-permute-start | bytes 393224 | tf_op jit(solution)/shard_map/ppermute | solution.py:25
  23.9 4.3 %collective-permute-start.5 = (f32[2,4096]{1,0:T(2,128)S(1)}, f32[2,4096]{1,0:T(2,128)S(1)}, u32[]{:S(2)}, u32[]{:S(2)}) collective-permute-start(f32[2,4096]{1,0:T(2,128)S(1)} %reshape.3), channel_id=1, source_target_pairs={{0,1},{1,0},{2,3},{3,2},{4,5},{5,4},{6,7},{7,6},{8,9},{9,8},{10,11... | collective-permute-start | bytes 98312 | tf_op jit(solution)/shard_map/ppermute | solution.py:25
  25.7 5.7 %collective-permute-start.4 = (f32[2,4096]{1,0:T(2,128)S(1)}, f32[2,4096]{1,0:T(2,128)S(1)}, u32[]{:S(2)}, u32[]{:S(2)}) collective-permute-start(f32[2,4096]{1,0:T(2,128)S(1)} %reshape.3), channel_id=1, source_target_pairs={{0,3},{1,2},{2,1},{3,0},{4,7},{5,6},{6,5},{7,4},{8,11},{9,10},{10,... | collective-permute-start | bytes 98312 | tf_op jit(solution)/shard_map/ppermute | solution.py:25
  28.2 4.8 %collective-permute-start.3 = (f32[2,4096]{1,0:T(2,128)S(1)}, f32[2,4096]{1,0:T(2,128)S(1)}, u32[]{:S(2)}, u32[]{:S(2)}) collective-permute-start(f32[2,4096]{1,0:T(2,128)S(1)} %reshape.3), channel_id=1, source_target_pairs={{0,2},{1,3},{2,0},{3,1},{4,6},{5,7},{6,4},{7,5},{8,10},{9,11},{10,... | collective-permute-start | bytes 98312 | tf_op jit(solution)/shard_map/ppermute | solution.py:25
  33.1 4.6 %collective-permute-start.8 = (f32[2,4096]{1,0:T(2,128)S(1)}, f32[2,4096]{1,0:T(2,128)S(1)}, u32[]{:S(2)}, u32[]{:S(2)}) collective-permute-start(f32[2,4096]{1,0:T(2,128)S(1)} %add_add_fusion.refs_0_), channel_id=1, source_target_pairs={{0,4},{4,0},{8,12},{12,8},{1,5},{5,1},{9,13},{13,9},{2,6},{6,2},{1... | collective-permute-start | bytes 98312 | tf_op jit(solution)/shard_map/ppermute | solution.py:25
  33.1 4.5 %collective-permute-start.7 = (f32[2,4096]{1,0:T(2,128)S(1)}, f32[2,4096]{1,0:T(2,128)S(1)}, u32[]{:S(2)}, u32[]{:S(2)}) collective-permute-start(f32[2,4096]{1,0:T(2,128)S(1)} %add_add_fusion.refs_0_), channel_id=1, source_target_pairs={{0,12},{4,8},{8,4},{12,0},{1,13},{5,9},{9,5},{13,1},{2,14},{6,10},... | collective-permute-start | bytes 98312 | tf_op jit(solution)/shard_map/ppermute | solution.py:25
  34.7 3.9 %collective-permute-start.6 = (f32[2,4096]{1,0:T(2,128)S(1)}, f32[2,4096]{1,0:T(2,128)S(1)}, u32[]{:S(2)}, u32[]{:S(2)}) collective-permute-start(f32[2,4096]{1,0:T(2,128)S(1)} %add_add_fusion.refs_0_), channel_id=1, source_target_pairs={{0,8},{4,12},{8,0},{12,4},{1,9},{5,13},{9,1},{13,5},{2,10},{6,14},... | collective-permute-start | bytes 98312 | tf_op jit(solution)/shard_map/ppermute | solution.py:25
  40.1 3.7 %collective-permute-start.11 = (f32[8,256]{1,0:T(8,128)S(1)}, f32[8,256]{1,0:T(8,128)S(1)}, u32[]{:S(2)}, u32[]{:S(2)}) collective-permute-start(f32[8,256]{1,0:T(8,128)S(1)} %get-tuple-element.32.refs_10_), channel_id=1, source_target_pairs={{0,1},{1,0},{2,3},{3,2},{4,5},{5,4},{6,7},{7,6},{8,9},{9,8},{10,11... | collective-permute-start | bytes 24584 | tf_op jit(solution)/shard_map/ppermute | solution.py:25
  40.1 5.5 %collective-permute-start.10 = (f32[8,256]{1,0:T(8,128)S(1)}, f32[8,256]{1,0:T(8,128)S(1)}, u32[]{:S(2)}, u32[]{:S(2)}) collective-permute-start(f32[8,256]{1,0:T(8,128)S(1)} %get-tuple-element.32.refs_10_), channel_id=1, source_target_pairs={{0,3},{1,2},{2,1},{3,0},{4,7},{5,6},{6,5},{7,4},{8,11},{9,10},{10,... | collective-permute-start | bytes 24584 | tf_op jit(solution)/shard_map/ppermute | solution.py:25
  42.0 4.5 %collective-permute-start.9 = (f32[8,256]{1,0:T(8,128)S(1)}, f32[8,256]{1,0:T(8,128)S(1)}, u32[]{:S(2)}, u32[]{:S(2)}) collective-permute-start(f32[8,256]{1,0:T(8,128)S(1)} %get-tuple-element.32.refs_10_), channel_id=1, source_target_pairs={{0,2},{1,3},{2,0},{3,1},{4,6},{5,7},{6,4},{7,5},{8,10},{9,11},{10,... | collective-permute-start | bytes 24584 | tf_op jit(solution)/shard_map/ppermute | solution.py:25
  47.2 3.9 %collective-permute-start.12 = (f32[4,8,256]{2,1,0:T(8,128)S(1)}, f32[4,8,256]{2,1,0:T(8,128)S(1)}, u32[]{:S(2)}, u32[]{:S(2)}) collective-permute-start(f32[4,8,256]{2,1,0:T(8,128)S(1)} %pad_maximum_fusion.refs_0_), channel_id=1, source_target_pairs={{0,8},{4,12},{8,0},{12,4},{1,9},{5,13},{9,1},{13,5},{2,10},{6,14},... | collective-permute-start | bytes 98312 | tf_op jit(solution)/shard_map/ppermute | solution.py:25
  52.7 3.7 %collective-permute-start.17 = (f32[8,256]{1,0:T(8,128)S(1)}, f32[8,256]{1,0:T(8,128)S(1)}, u32[]{:S(2)}, u32[]{:S(2)}) collective-permute-start(f32[8,256]{1,0:T(8,128)S(1)} %get-tuple-element.37.refs_10_), channel_id=1, source_target_pairs={{0,1},{1,0},{2,3},{3,2},{4,5},{5,4},{6,7},{7,6},{8,9},{9,8},{10,11... | collective-permute-start | bytes 24584 | tf_op jit(solution)/shard_map/ppermute | solution.py:25
  53.7 5.4 %collective-permute-start.16 = (f32[8,256]{1,0:T(8,128)S(1)}, f32[8,256]{1,0:T(8,128)S(1)}, u32[]{:S(2)}, u32[]{:S(2)}) collective-permute-start(f32[8,256]{1,0:T(8,128)S(1)} %get-tuple-element.37.refs_10_), channel_id=1, source_target_pairs={{0,3},{1,2},{2,1},{3,0},{4,7},{5,6},{6,5},{7,4},{8,11},{9,10},{10,... | collective-permute-start | bytes 24584 | tf_op jit(solution)/shard_map/ppermute | solution.py:25
  55.9 4.5 %collective-permute-start.15 = (f32[8,256]{1,0:T(8,128)S(1)}, f32[8,256]{1,0:T(8,128)S(1)}, u32[]{:S(2)}, u32[]{:S(2)}) collective-permute-start(f32[8,256]{1,0:T(8,128)S(1)} %get-tuple-element.37.refs_10_), channel_id=1, source_target_pairs={{0,2},{1,3},{2,0},{3,1},{4,6},{5,7},{6,4},{7,5},{8,10},{9,11},{10,... | collective-permute-start | bytes 24584 | tf_op jit(solution)/shard_map/ppermute | solution.py:25
  62.0 3.9 %collective-permute-start.18 = (f32[4,8,256]{2,1,0:T(8,128)S(1)}, f32[4,8,256]{2,1,0:T(8,128)S(1)}, u32[]{:S(2)}, u32[]{:S(2)}) collective-permute-start(f32[4,8,256]{2,1,0:T(8,128)S(1)} %pad_maximum_fusion.1.refs_0_), channel_id=1, source_target_pairs={{0,8},{4,12},{8,0},{12,4},{1,9},{5,13},{9,1},{13,5},{2,10},{6,14},... | collective-permute-start | bytes 98312 | tf_op jit(solution)/shard_map/ppermute | solution.py:25
  67.6 3.7 %collective-permute-start.23 = (f32[8,256]{1,0:T(8,128)S(1)}, f32[8,256]{1,0:T(8,128)S(1)}, u32[]{:S(2)}, u32[]{:S(2)}) collective-permute-start(f32[8,256]{1,0:T(8,128)S(1)} %get-tuple-element.43.refs_10_), channel_id=1, source_target_pairs={{0,1},{1,0},{2,3},{3,2},{4,5},{5,4},{6,7},{7,6},{8,9},{9,8},{10,11... | collective-permute-start | bytes 24584 | tf_op jit(solution)/shard_map/ppermute | solution.py:25
  67.7 5.5 %collective-permute-start.22 = (f32[8,256]{1,0:T(8,128)S(1)}, f32[8,256]{1,0:T(8,128)S(1)}, u32[]{:S(2)}, u32[]{:S(2)}) collective-permute-start(f32[8,256]{1,0:T(8,128)S(1)} %get-tuple-element.43.refs_10_), channel_id=1, source_target_pairs={{0,3},{1,2},{2,1},{3,0},{4,7},{5,6},{6,5},{7,4},{8,11},{9,10},{10,... | collective-permute-start | bytes 24584 | tf_op jit(solution)/shard_map/ppermute | solution.py:25
  69.5 4.5 %collective-permute-start.21 = (f32[8,256]{1,0:T(8,128)S(1)}, f32[8,256]{1,0:T(8,128)S(1)}, u32[]{:S(2)}, u32[]{:S(2)}) collective-permute-start(f32[8,256]{1,0:T(8,128)S(1)} %get-tuple-element.43.refs_10_), channel_id=1, source_target_pairs={{0,2},{1,3},{2,0},{3,1},{4,6},{5,7},{6,4},{7,5},{8,10},{9,11},{10,... | collective-permute-start | bytes 24584 | tf_op jit(solution)/shard_map/ppermute | solution.py:25
  74.7 3.9 %collective-permute-start.24 = (f32[4,8,256]{2,1,0:T(8,128)S(1)}, f32[4,8,256]{2,1,0:T(8,128)S(1)}, u32[]{:S(2)}, u32[]{:S(2)}) collective-permute-start(f32[4,8,256]{2,1,0:T(8,128)S(1)} %pad_maximum_fusion.2.refs_0_), channel_id=1, source_target_pairs={{0,8},{4,12},{8,0},{12,4},{1,9},{5,13},{9,1},{13,5},{2,10},{6,14},... | collective-permute-start | bytes 98312 | tf_op jit(solution)/shard_map/ppermute | solution.py:25
  80.2 3.6 %collective-permute-start.29 = (f32[8,128]{1,0:T(8,128)S(1)}, f32[8,128]{1,0:T(8,128)S(1)}, u32[]{:S(2)}, u32[]{:S(2)}) collective-permute-start(f32[8,128]{1,0:T(8,128)S(1)} %get-tuple-element.53), channel_id=1, source_target_pairs={{0,1},{1,0},{2,3},{3,2},{4,5},{5,4},{6,7},{7,6},{8,9},{9,8},{10,11... | collective-permute-start | bytes 12296 | tf_op jit(solution)/shard_map/ppermute | solution.py:25
  81.1 5.4 %collective-permute-start.28 = (f32[8,128]{1,0:T(8,128)S(1)}, f32[8,128]{1,0:T(8,128)S(1)}, u32[]{:S(2)}, u32[]{:S(2)}) collective-permute-start(f32[8,128]{1,0:T(8,128)S(1)} %get-tuple-element.53), channel_id=1, source_target_pairs={{0,3},{1,2},{2,1},{3,0},{4,7},{5,6},{6,5},{7,4},{8,11},{9,10},{10,... | collective-permute-start | bytes 12296 | tf_op jit(solution)/shard_map/ppermute | solution.py:25
  83.4 4.5 %collective-permute-start.27 = (f32[8,128]{1,0:T(8,128)S(1)}, f32[8,128]{1,0:T(8,128)S(1)}, u32[]{:S(2)}, u32[]{:S(2)}) collective-permute-start(f32[8,128]{1,0:T(8,128)S(1)} %get-tuple-element.53), channel_id=1, source_target_pairs={{0,2},{1,3},{2,0},{3,1},{4,6},{5,7},{6,4},{7,5},{8,10},{9,11},{10,... | collective-permute-start | bytes 12296 | tf_op jit(solution)/shard_map/ppermute | solution.py:25
  (10 other events, 49.6 us)

commit v12 on v10

--- a/solution.py
+++ b/solution.py
@@ -32,14 +32,18 @@
     return lax.all_to_all(jnp.broadcast_to(value[None], (size,) + value.shape), axes, 0, 0)
 
 
+def order_of(size):
+    return (0, 2, 3, 1) if size == 4 else tuple(range(size))
+
+
+def direct(value, axis, size):
+    return [value] + [swap(value, axis, size, k) for k in order_of(size)[1:]]
+
+
 def sum_over(value, axis, size):
     for bit in bits(size):
         value = value + swap(value, axis, size, bit)
     return value
-
-
-def direct(value, axis, size):
-    return [value] + [swap(value, axis, size, k) for k in reversed(range(1, size))][::-1]
 
 
 def in_hbm(value):
@@ -69,19 +73,28 @@
     return spans
 
 
-def stream_kernel(spans, rows_ref, proj_ref, feats_ref, held, proj, sems):
-    first = pltpu.make_async_copy(proj_ref, proj, sems.at[len(spans)])
+def stream_kernel(spans, rows_ref, proj_ref, feats_ref, held, proj, turned, sems):
+    count, half = proj_ref.shape[0], proj.shape[1]
+    firsts = [
+        pltpu.make_async_copy(
+            proj_ref.at[:, pl.ds(h * half, half)], proj.at[pl.ds(h * count, count)], sems.at[len(spans) + h]
+        )
+        for h in range(2)
+    ]
     copies = [
         pltpu.make_async_copy(rows_ref.at[span], held.at[span], sems.at[c])
         for c, span in enumerate(spans)
     ]
-    first.start()
-    for copy in copies:
+    for copy in firsts + copies:
         copy.start()
-    first.wait()
+    for copy in firsts:
+        copy.wait()
+    turned[...] = proj[...].T
     for copy, span in zip(copies, spans):
         copy.wait()
-        feats_ref[:, span] = lax.dot_general(proj[...], held[span], NT, preferred_element_type=jnp.float32)
+        left = jnp.dot(held[span, :half], turned[...], preferred_element_type=jnp.float32)
+        right = jnp.dot(held[span, half:], turned[...], preferred_element_type=jnp.float32)
+        feats_ref[:, span] = left.T[:count] + right.T[count:]
 
 
 def features(rows, proj, sizes, limit, name):
@@ -93,8 +106,9 @@
         out_specs=VMEM_SPEC,
         scratch_shapes=[
             pltpu.VMEM(rows.shape, jnp.bfloat16),
-            pltpu.VMEM(proj.shape, jnp.bfloat16),
-            pltpu.SemaphoreType.DMA((len(spans) + 1,)),
+            pltpu.VMEM((2 * proj.shape[0], proj.shape[1] // 2), jnp.bfloat16),
+            pltpu.VMEM((proj.shape[1] // 2, 2 * proj.shape[0]), jnp.bfloat16),
+            pltpu.SemaphoreType.DMA((len(spans) + 2,)),
         ],
         compiler_params=pltpu.CompilerParams(vmem_limit_bytes=limit * 2**20),
         name=name,
@@ -134,7 +148,7 @@
     blocks, (out_ref, part_ref, held) = refs[:size], refs[size:]
     me = lax.axis_index("tensor")
     tokens = blocks[0].shape[1]
-    for k, block in enumerate(blocks):
+    for k, block in zip(order_of(size), blocks):
         start = pl.multiple_of((me ^ k) * tokens, LANES)
         held[:, pl.ds(start, tokens)] = block[...]
     for s in range(part_ref.shape[0]):
@@ -198,7 +212,7 @@
     pieces, refs = refs[:size], refs[size:]
     upper_ref, lower_ref, vectors_ref, vector_pieces_ref, scale_ref, applied_ref, norm_ref, held = refs
     dp = lax.axis_index("dp")
-    for k, piece in enumerate(pieces):
+    for k, piece in zip(order_of(size), pieces):
         held[dp ^ k] = piece[...]
     vectors = jnp.concatenate([held[k] for k in range(size)], axis=0)
     vectors_ref[...] = vectors
@@ -227,13 +241,6 @@
         compiler_params=PARAMS,
         name="cg_start",
     )(*pieces, *prior_pieces)
-
-
-def on_lanes(column):
-    seqs = column.shape[0]
-    row = lax.broadcasted_iota(jnp.int32, (seqs, LANES), 0)
-    lane = lax.broadcasted_iota(jnp.int32, (seqs, LANES), 1)
-    return jnp.sum(jnp.where(row == lane, column, 0.0), axis=0, keepdims=True)
 
 
 def step_kernel(tensor_size, first, last, *refs):
@@ -272,23 +279,22 @@
     fisher_direction = fisher_residual + share * fisher_direction
     direction_out[...] = direction
     solution_out[...] = solution
+    norm_out[...] = jnp.broadcast_to(norm_next, norm_out.shape)
     if last:
         own = own_columns(direction_out, me, rows)
-        curvature_out[...] = on_lanes(row_sum(own * fisher_direction))
-        norm_out[...] = on_lanes(norm_next)
+        curvature_out[...] = jnp.broadcast_to(row_sum(own * fisher_direction), curvature_out.shape)
     else:
         fisher_direction_out[...] = fisher_direction
         fisher_residual_out[...] = fisher_residual
         residual_out[...] = residual
-        norm_out[...] = jnp.broadcast_to(norm_next, norm_out.shape)
 
 
 def step_cg(blocks, fixed, norm, state, last, tensor_size):
     first = len(state) == 1
     whole, rows = F32(fixed[2].shape), F32(state[0].shape)
-    row = F32((1, LANES))
+    column = F32(norm.shape)
     operands = [blocks, *fixed, norm, *state]
-    out_shape = (row, row, whole, whole) if last else (rows, F32(norm.shape), rows, whole, whole, whole)
+    out_shape = (column, column, whole, whole) if last else (rows, column, rows, whole, whole, whole)
     return pl.pallas_call(
         functools.partial(step_kernel, tensor_size, first, last),
         out_shape=out_shape,
@@ -323,8 +329,8 @@
 def on_device(dp_size, tensor_size, inputs, in_proj, out_grads, out_proj, prior, queries):
     width = R_IN * R_OUT
     both, devices = ("dp", "tensor"), dp_size * tensor_size
-    in_blocks = direct(features(inputs, in_proj, (256, 128), 16, "in_features"), "tensor", tensor_size)
-    out_local = features(out_grads, out_proj, (256,) * 7 + (128,), 40, "out_features")
+    in_blocks = direct(features(inputs, in_proj, (128,), 20, "in_features"), "tensor", tensor_size)
+    out_local = features(out_grads, out_proj, (256,) * 7 + (128,), 44, "out_features")
     partial = partial_vectors(in_blocks, out_local).reshape(-1, width)
     pieces = direct(sum_over(partial, "tensor", tensor_size), "dp", dp_size)
     prior_pieces = [in_vmem(piece) for piece in split_prior(prior)]
@@ -339,8 +345,7 @@
     curvature, norm, direction, solved = step_cg(blocks, fixed, norm, state, True, tensor_size)
     curvature = jnp.sum(gather(curvature, both, devices), axis=0)
     solved, along = score(solved, direction, queries)
-    step = (norm / curvature)[0, : solved.shape[0]]
-    return solved + step[:, None] * along
+    return solved + (norm / curvature)[:, :1] * along
 
 
 def solution(mesh):

time: 97.4 us -> 88.7 us (0.911)
  Pallas kernels: 35.5 us -> 26.8 us
  blocking collectives: 33.9 us -> 32.2 us
  starting transfers between devices: 14.9 us -> 16.1 us
    pallas_call x2, Pallas kernels: 26 us -> 17.3 us  [features(): pl.pallas_call(functools.partial(stream_kernel, spans), out_shape=pltpu.V...]
    all_to_all x3, blocking collectives: 33.9 us -> 32.2 us  [gather(): lax.all_to_all(jnp.broadcast_to(value[None], (size,) + value.shape), axes...]
    ppermute x8, starting transfers between devices: 11.5 us -> 12.6 us  [swap(): return lax.ppermute(value, axis, [(i, i ^ bit) for i in range(size)])]
  transfers between devices with their start and end apart: 9 -> 9, of which waited for: 3 -> 4; matrix products, arithmetic and copies ran while one was open for 0% -> 0% of each run, Pallas kernels for 22% -> 17%
where the time goes in v12:
time: 88.7 us; the launch traced here: 88.4 us
  blocking collectives  32.2 us (36%)
  Pallas kernels  26.8 us (30%)
  starting transfers between devices  16.1 us (18%)
  waiting for transfers between devices  11.5 us (13%)
  local copies, waits for them, and re-layouts  0.9 us (1%)
    all_to_all x3, blocking collectives, gather(): lax.all_to_all(jnp.broadcast_to(value[None], (size,) + value.shape), axes...  32.2 us
    pallas_call x2, Pallas kernels, features(): pl.pallas_call(functools.partial(stream_kernel, spans), out_shape=pltpu.V...  17.3 us
    ppermute x8, starting transfers between devices, swap(): return lax.ppermute(value, axis, [(i, i ^ bit) for i in range(size)])  12.6 us
    all_to_all x1, waiting for transfers between devices, gather(): lax.all_to_all(jnp.broadcast_to(value[None], (size,) + value.shape), axes...  6.29 us
    ppermute x8, waiting for transfers between devices, swap(): return lax.ppermute(value, axis, [(i, i ^ bit) for i in range(size)])  5.16 us
    pallas_call x3, Pallas kernels, step_cg(): pl.pallas_call(functools.partial(step_kernel, tensor_size, first, last),...  4.84 us
    all_to_all x1, starting transfers between devices, gather(): lax.all_to_all(jnp.broadcast_to(value[None], (size,) + value.shape), axes...  3.49 us
    pallas_call x1, Pallas kernels, split_prior(): pl.pallas_call(split_kernel, out_shape=(pltpu.VMEM(prior.shape, jnp.bfloa...  2.32 us
  transfers between devices with their start and end apart: 9, of which 4 were waited for; matrix products, arithmetic and copies ran while one was open for 0% of the time, Pallas kernels for 17%

profile of v12, /device:TPU:0, one launch (start us, length us, event | category | flops | bytes accessed | tf_op | source)
XLA Modules:
  0.0 88.4 jit_solution(2786573017536565981)
XLA Ops:
  0.0 5.0 %in_features.1.refs_0_ = f32[64,512]{1,0:T(8,128)S(1)} custom-call(bf16[512,8192]{1,0:T(8,128)(2,1)} %rows_ref.2, bf16[64,8192]{1,0:T(8,128)(2,1)} %proj_ref.2), custom_call_target="tpu_custom_call" | custom-call | tf_op jit(solution)/shard_map/in_features/pallas_call | solution.py:102
  5.1 3.1 %collective-permute-start.2 = (f32[64,512]{1,0:T(8,128)S(1)}, f32[64,512]{1,0:T(8,128)S(1)}, u32[]{:S(2)}, u32[]{:S(2)}) collective-permute-start(f32[64,512]{1,0:T(8,128)S(1)} %in_features.1.refs_0_), channel_id=1, source_target_pairs={{0,1},{1,0},{2,3},{3,2},{4,5},{5,4},{6,7},{7,6},{8,9},{9,8},{10,11... | collective-permute-start | bytes 393224 | tf_op jit(solution)/shard_map/ppermute | solution.py:24
  8.1 2.5 %collective-permute-start.1 = (f32[64,512]{1,0:T(8,128)S(1)}, f32[64,512]{1,0:T(8,128)S(1)}, u32[]{:S(2)}, u32[]{:S(2)}) collective-permute-start(f32[64,512]{1,0:T(8,128)S(1)} %in_features.1.refs_0_), channel_id=1, source_target_pairs={{0,3},{1,2},{2,1},{3,0},{4,7},{5,6},{6,5},{7,4},{8,11},{9,10},{10,... | collective-permute-start | bytes 393224 | tf_op jit(solution)/shard_map/ppermute | solution.py:24
  10.7 12.3 %out_features.1.refs_4_ = f32[64,2048]{1,0:T(8,128)S(1)} custom-call(bf16[2048,7168]{1,0:T(8,128)(2,1)} %rows_ref.3, bf16[64,7168]{1,0:T(8,128)(2,1)} %proj_ref.3), custom_call_target="tpu_custom_call" | custom-call | tf_op jit(solution)/shard_map/out_features/pallas_call | solution.py:102
  23.1 0.6 partial_vectors.1
  23.8 2.9 %collective-permute-start.3 = (f32[2,4096]{1,0:T(2,128)S(1)}, f32[2,4096]{1,0:T(2,128)S(1)}, u32[]{:S(2)}, u32[]{:S(2)}) collective-permute-start(f32[2,4096]{1,0:T(2,128)S(1)} %reshape.7), channel_id=1, source_target_pairs={{0,2},{1,3},{2,0},{3,1},{4,6},{5,7},{6,4},{7,5},{8,10},{9,11},{10,... | collective-permute-start | bytes 98312 | tf_op jit(solution)/shard_map/ppermute | solution.py:24
  26.7 2.0 %collective-permute-done.3 = f32[2,4096]{1,0:T(2,128)S(1)} collective-permute-done((f32[2,4096]{1,0:T(2,128)S(1)}, f32[2,4096]{1,0:T(2,128)S(1)}, u32[]{:S(2)}, u32[]{:S(2)}) %collective-permute-start.3) | collective-permute-done | bytes 32800 | tf_op jit(solution)/shard_map/ppermute | solution.py:24
  28.7 1.9 %collective-permute-start.4 = (f32[2,4096]{1,0:T(2,128)S(1)}, f32[2,4096]{1,0:T(2,128)S(1)}, u32[]{:S(2)}, u32[]{:S(2)}) collective-permute-start(f32[2,4096]{1,0:T(2,128)S(1)} %add.9), channel_id=1, source_target_pairs={{0,1},{1,0},{2,3},{3,2},{4,5},{5,4},{6,7},{7,6},{8,9},{9,8},{10,11... | collective-permute-start | bytes 98312 | tf_op jit(solution)/shard_map/ppermute | solution.py:24
  30.5 2.1 %collective-permute-done.4 = f32[2,4096]{1,0:T(2,128)S(1)} collective-permute-done((f32[2,4096]{1,0:T(2,128)S(1)}, f32[2,4096]{1,0:T(2,128)S(1)}, u32[]{:S(2)}, u32[]{:S(2)}) %collective-permute-start.4) | collective-permute-done | bytes 32800 | tf_op jit(solution)/shard_map/ppermute | solution.py:24
  32.8 1.6 %collective-permute-start.6 = (f32[2,4096]{1,0:T(2,128)S(1)}, f32[2,4096]{1,0:T(2,128)S(1)}, u32[]{:S(2)}, u32[]{:S(2)}) collective-permute-start(f32[2,4096]{1,0:T(2,128)S(1)} %add.10.refs_0_), channel_id=1, source_target_pairs={{0,12},{4,8},{8,4},{12,0},{1,13},{5,9},{9,5},{13,1},{2,14},{6,10},... | collective-permute-start | bytes 98312 | tf_op jit(solution)/shard_map/ppermute | solution.py:24
  34.4 0.5 collective-permute-start.5
  34.9 2.3 %split_prior.1 = (bf16[256,4096]{1,0:T(8,128)(2,1)S(1)}, bf16[256,4096]{1,0:T(8,128)(2,1)S(1)}) custom-call(f32[256,4096]{1,0:T(8,128)} %prior_ref.1), custom_call_target="tpu_custom_call" | custom-call | tf_op jit(solution)/shard_map/split_prior/pallas_call | solution.py:136
  37.3 1.0 %collective-permute-done.5.refs_1_ = f32[2,4096]{1,0:T(2,128)S(1)} collective-permute-done((f32[2,4096]{1,0:T(2,128)S(1)}, f32[2,4096]{1,0:T(2,128)S(1)}, u32[]{:S(2)}, u32[]{:S(2)}) %collective-permute-start.5) | collective-permute-done | bytes 32800 | tf_op jit(solution)/shard_map/ppermute | solution.py:24
  38.3 1.5 %cg_start.1 = (f32[8,4096]{1,0:T(8,128)S(1)}, bf16[16,4096]{1,0:T(8,128)(2,1)S(1)}, f32[8,128]{1,0:T(8,128)S(1)}, f32[8,256]{1,0:T(8,128)S(1)}, f32[8,128]{1,0:T(8,128)S(1)}) custom-call(f32[2,4096]{1,0:T(2,128)S(1)} %add.10.refs_0_, f32[2,4096]{1,0:T(2,128)S(1)} %collective-permute-done.5.refs_1_, f32[2,4096]{1,0:T(2,128)S(1)} %collective-permute-done.6.refs_2_, ...), custom_call_target="tpu_custom_call" | custom-call | tf_op jit(solution)/shard_map/cg_start/pallas_call | solution.py:235
  39.8 11.5 %all_to_all.20.refs_0_ = f32[16,8,256]{2,1,0:T(8,128)S(1)} all-to-all(f32[16,8,256]{2,1,0:T(8,128)S(1)} %broadcast_in_dim.8), channel_id=1, replica_groups=mesh['groups'=2,'dp'=4,'tensor'=4] {'dp','tensor'}, dimensions={0} | all-to-all | bytes 262144 | tf_op jit(solution)/shard_map/all_to_all | solution.py:32
  51.2 1.6 %cg_step.3 = (f32[8,256]{1,0:T(8,128)S(1)}, f32[8,128]{1,0:T(8,128)S(1)}, f32[8,256]{1,0:T(8,128)S(1)}, f32[8,4096]{1,0:T(8,128)S(1)}, f32[8,4096]{1,0:T(8,128)S(1)}, /*index=5*/f32[8,4096]{1,0:T(8,128)S(1)}) custom-call(f32[16,8,256]{2,1,0:T(8,128)S(1)} %all_to_all.20.refs_0_, bf16[256,4096]{1,0:T(8,128)(2,1)S(1)} %get-tuple-element.30.refs_4_.refs_1_, ...), custom_call_target="tpu_custom_call" | custom-call | tf_op jit(solution)/shard_map/cg_step/pallas_call | solution.py:298
  52.9 10.4 %all_to_all.21.refs_0_ = f32[16,8,256]{2,1,0:T(8,128)S(1)} all-to-all(f32[16,8,256]{2,1,0:T(8,128)S(1)} %broadcast_in_dim.9), channel_id=1, replica_groups=mesh['groups'=2,'dp'=4,'tensor'=4] {'dp','tensor'}, dimensions={0} | all-to-all | bytes 262144 | tf_op jit(solution)/shard_map/all_to_all | solution.py:32
  63.2 1.6 %cg_step.4 = (f32[8,256]{1,0:T(8,128)S(1)}, f32[8,128]{1,0:T(8,128)S(1)}, f32[8,256]{1,0:T(8,128)S(1)}, f32[8,4096]{1,0:T(8,128)S(1)}, f32[8,4096]{1,0:T(8,128)S(1)}, /*index=5*/f32[8,4096]{1,0:T(8,128)S(1)}) custom-call(f32[16,8,256]{2,1,0:T(8,128)S(1)} %all_to_all.21.refs_0_, bf16[256,4096]{1,0:T(8,128)(2,1)S(1)} %get-tuple-element.30.refs_4_.refs_1_, ...), custom_call_target="tpu_custom_call" | custom-call | tf_op jit(solution)/shard_map/cg_step/pallas_call | solution.py:298
  64.9 10.4 %all_to_all.22.refs_0_ = f32[16,8,256]{2,1,0:T(8,128)S(1)} all-to-all(f32[16,8,256]{2,1,0:T(8,128)S(1)} %broadcast_in_dim.10), channel_id=1, replica_groups=mesh['groups'=2,'dp'=4,'tensor'=4] {'dp','tensor'}, dimensions={0} | all-to-all | bytes 262144 | tf_op jit(solution)/shard_map/all_to_all | solution.py:32
  75.2 1.7 %cg_step.5 = (f32[8,128]{1,0:T(8,128)S(1)}, f32[8,128]{1,0:T(8,128)S(1)}, f32[8,4096]{1,0:T(8,128)S(1)}, f32[8,4096]{1,0:T(8,128)S(1)}) custom-call(f32[16,8,256]{2,1,0:T(8,128)S(1)} %all_to_all.22.refs_0_, bf16[256,4096]{1,0:T(8,128)(2,1)S(1)} %get-tuple-element.30.refs_4_.refs_1_, bf16[256,4096]{1,0:T(8,128)(2,1)S(1)} %get-tuple-element.31.refs_5_.refs_2_, ...), custom_call_target="tpu_custom_call" | custom-call | tf_op jit(solution)/shard_map/cg_step/pallas_call | solution.py:298
  76.9 0.6 broadcast_in_dim.11
  77.5 3.5 %all-to-all-start.3 = ((f32[16,8,128]{2,1,0:T(8,128)}), f32[16,8,128]{2,1,0:T(8,128)S(1)}, u32[]{:S(2)}, u32[]{:S(2)}) async-start(f32[16,8,128]{2,1,0:T(8,128)} %broadcast_in_dim.11), calls=%async_computation.3 | async-start | bytes 131072 | tf_op jit(solution)/shard_map/all_to_all | solution.py:32
  81.3 6.3 %all-to-all-done.3 = f32[16,8,128]{2,1,0:T(8,128)S(1)} async-done(((f32[16,8,128]{2,1,0:T(8,128)}), f32[16,8,128]{2,1,0:T(8,128)S(1)}, u32[]{:S(2)}, u32[]{:S(2)}) %all-to-all-start.3) | async-done | bytes 65568 | tf_op jit(solution)/shard_map/all_to_all | solution.py:32
  87.7 0.7 multiply_add_fusion
  (19 shorter events, 0.8 us)
Async XLA Ops:
  5.1 18.0 %collective-permute-start.2 = (f32[64,512]{1,0:T(8,128)S(1)}, f32[64,512]{1,0:T(8,128)S(1)}, u32[]{:S(2)}, u32[]{:S(2)}) collective-permute-start(f32[64,512]{1,0:T(8,128)S(1)} %in_features.1.refs_0_), channel_id=1, source_target_pairs={{0,1},{1,0},{2,3},{3,2},{4,5},{5,4},{6,7},{7,6},{8,9},{9,8},{10,11... | collective-permute-start | bytes 393224 | tf_op jit(solution)/shard_map/ppermute | solution.py:24
  8.1 14.9 %collective-permute-start.1 = (f32[64,512]{1,0:T(8,128)S(1)}, f32[64,512]{1,0:T(8,128)S(1)}, u32[]{:S(2)}, u32[]{:S(2)}) collective-permute-start(f32[64,512]{1,0:T(8,128)S(1)} %in_features.1.refs_0_), channel_id=1, source_target_pairs={{0,3},{1,2},{2,1},{3,0},{4,7},{5,6},{6,5},{7,4},{8,11},{9,10},{10,... | collective-permute-start | bytes 393224 | tf_op jit(solution)/shard_map/ppermute | solution.py:24
  10.6 12.4 %collective-permute-start = (f32[64,512]{1,0:T(8,128)S(1)}, f32[64,512]{1,0:T(8,128)S(1)}, u32[]{:S(2)}, u32[]{:S(2)}) collective-permute-start(f32[64,512]{1,0:T(8,128)S(1)} %in_features.1.refs_0_), channel_id=1, source_target_pairs={{0,2},{1,3},{2,0},{3,1},{4,6},{5,7},{6,4},{7,5},{8,10},{9,11},{10,... | collective-permute-start | bytes 393224 | tf_op jit(solution)/shard_map/ppermute | solution.py:24
  23.8 4.9 %collective-permute-start.3 = (f32[2,4096]{1,0:T(2,128)S(1)}, f32[2,4096]{1,0:T(2,128)S(1)}, u32[]{:S(2)}, u32[]{:S(2)}) collective-permute-start(f32[2,4096]{1,0:T(2,128)S(1)} %reshape.7), channel_id=1, source_target_pairs={{0,2},{1,3},{2,0},{3,1},{4,6},{5,7},{6,4},{7,5},{8,10},{9,11},{10,... | collective-permute-start | bytes 98312 | tf_op jit(solution)/shard_map/ppermute | solution.py:24
  28.7 4.0 %collective-permute-start.4 = (f32[2,4096]{1,0:T(2,128)S(1)}, f32[2,4096]{1,0:T(2,128)S(1)}, u32[]{:S(2)}, u32[]{:S(2)}) collective-permute-start(f32[2,4096]{1,0:T(2,128)S(1)} %add.9), channel_id=1, source_target_pairs={{0,1},{1,0},{2,3},{3,2},{4,5},{5,4},{6,7},{7,6},{8,9},{9,8},{10,11... | collective-permute-start | bytes 98312 | tf_op jit(solution)/shard_map/ppermute | solution.py:24
  32.7 4.6 %collective-permute-start.7 = (f32[2,4096]{1,0:T(2,128)S(1)}, f32[2,4096]{1,0:T(2,128)S(1)}, u32[]{:S(2)}, u32[]{:S(2)}) collective-permute-start(f32[2,4096]{1,0:T(2,128)S(1)} %add.10.refs_0_), channel_id=1, source_target_pairs={{0,4},{4,0},{8,12},{12,8},{1,5},{5,1},{9,13},{13,9},{2,6},{6,2},{1... | collective-permute-start | bytes 98312 | tf_op jit(solution)/shard_map/ppermute | solution.py:24
  32.8 4.5 %collective-permute-start.6 = (f32[2,4096]{1,0:T(2,128)S(1)}, f32[2,4096]{1,0:T(2,128)S(1)}, u32[]{:S(2)}, u32[]{:S(2)}) collective-permute-start(f32[2,4096]{1,0:T(2,128)S(1)} %add.10.refs_0_), channel_id=1, source_target_pairs={{0,12},{4,8},{8,4},{12,0},{1,13},{5,9},{9,5},{13,1},{2,14},{6,10},... | collective-permute-start | bytes 98312 | tf_op jit(solution)/shard_map/ppermute | solution.py:24
  34.4 3.9 %collective-permute-start.5 = (f32[2,4096]{1,0:T(2,128)S(1)}, f32[2,4096]{1,0:T(2,128)S(1)}, u32[]{:S(2)}, u32[]{:S(2)}) collective-permute-start(f32[2,4096]{1,0:T(2,128)S(1)} %add.10.refs_0_), channel_id=1, source_target_pairs={{0,8},{4,12},{8,0},{12,4},{1,9},{5,13},{9,1},{13,5},{2,10},{6,14},... | collective-permute-start | bytes 98312 | tf_op jit(solution)/shard_map/ppermute | solution.py:24
  63.2 17.8 %copy-start = (bf16[32,4096]{1,0:T(8,128)(2,1)S(1)}, bf16[32,4096]{1,0:T(8,128)(2,1)}, u32[]{:S(2)}) copy-start(bf16[32,4096]{1,0:T(8,128)(2,1)} %queries_ref.1) | copy-start | bytes 786436
  77.5 10.1 %all-to-all-start.3 = ((f32[16,8,128]{2,1,0:T(8,128)}), f32[16,8,128]{2,1,0:T(8,128)S(1)}, u32[]{:S(2)}, u32[]{:S(2)}) async-start(f32[16,8,128]{2,1,0:T(8,128)} %broadcast_in_dim.11), calls=%async_computation.3 | async-start | bytes 131072 | tf_op jit(solution)/shard_map/all_to_all | solution.py:32

commit v13 on v12

--- a/solution.py
+++ b/solution.py
@@ -12,6 +12,7 @@
 SEQ = 1024
 ITERS = 4
 LANES = 128
+DEPTH = 4
 NT = (((1,), (1,)), ((), ()))
 HIGHEST = lax.Precision.HIGHEST
 ANY_SPEC = pl.BlockSpec(memory_space=pl.ANY)
@@ -38,12 +39,6 @@
 
 def direct(value, axis, size):
     return [value] + [swap(value, axis, size, k) for k in order_of(size)[1:]]
-
-
-def sum_over(value, axis, size):
-    for bit in bits(size):
-        value = value + swap(value, axis, size, bit)
-    return value
 
 
 def in_hbm(value):
@@ -85,13 +80,15 @@
         pltpu.make_async_copy(rows_ref.at[span], held.at[span], sems.at[c])
         for c, span in enumerate(spans)
     ]
-    for copy in firsts + copies:
+    for copy in firsts + copies[:DEPTH]:
         copy.start()
     for copy in firsts:
         copy.wait()
     turned[...] = proj[...].T
-    for copy, span in zip(copies, spans):
-        copy.wait()
+    for c, span in enumerate(spans):
+        copies[c].wait()
+        if c + DEPTH < len(spans):
+            copies[c + DEPTH].start()
         left = jnp.dot(held[span, :half], turned[...], preferred_element_type=jnp.float32)
         right = jnp.dot(held[span, half:], turned[...], preferred_element_type=jnp.float32)
         feats_ref[:, span] = left.T[:count] + right.T[count:]
@@ -251,7 +248,7 @@
         fisher_residual_ref, direction_ref, residual_ref, solution_ref = refs[:4]
         refs = refs[4:]
     if last:
-        curvature_out, norm_out, direction_out, solution_out, held = refs
+        queries_ref, curvature_out, norm_out, solved_out, along_out, held = refs
     else:
         fisher_direction_out, norm_out, fisher_residual_out, direction_out, residual_out, solution_out, held = refs
     me = flat_index(tensor_size)
@@ -277,24 +274,34 @@
     fisher_direction = fisher_direction_ref[...]
     fisher_residual = (fisher_direction if first else fisher_residual_ref[...]) - (step / scale) * twice
     fisher_direction = fisher_residual + share * fisher_direction
-    direction_out[...] = direction
-    solution_out[...] = solution
     norm_out[...] = jnp.broadcast_to(norm_next, norm_out.shape)
     if last:
-        own = own_columns(direction_out, me, rows)
+        held[...] = direction
+        own = own_columns(held, me, rows)
         curvature_out[...] = jnp.broadcast_to(row_sum(own * fisher_direction), curvature_out.shape)
+        seqs = direction.shape[0]
+        solved = jnp.concatenate([solution, direction], axis=0)
+        scores = dot_pieces(pieces_of(solved, 3), queries_ref[...], 2 * seqs)
+        solved_out[...] = scores[:seqs]
+        along_out[...] = scores[seqs:]
     else:
         fisher_direction_out[...] = fisher_direction
         fisher_residual_out[...] = fisher_residual
         residual_out[...] = residual
-
-
-def step_cg(blocks, fixed, norm, state, last, tensor_size):
-    first = len(state) == 1
+        direction_out[...] = direction
+        solution_out[...] = solution
+
+
+def step_cg(blocks, fixed, norm, state, queries, tensor_size):
+    first, last = len(state) == 1, queries is not None
     whole, rows = F32(fixed[2].shape), F32(state[0].shape)
     column = F32(norm.shape)
     operands = [blocks, *fixed, norm, *state]
-    out_shape = (column, column, whole, whole) if last else (rows, column, rows, whole, whole, whole)
+    out_shape = (rows, column, rows, whole, whole, whole)
+    if last:
+        operands.append(queries)
+        scores = F32((whole.shape[0], queries.shape[0]))
+        out_shape = (column, column, scores, scores)
     return pl.pallas_call(
         functools.partial(step_kernel, tensor_size, first, last),
         out_shape=out_shape,
@@ -306,45 +313,30 @@
     )(*operands)
 
 
-def score_kernel(solution_ref, direction_ref, queries_ref, solved_ref, along_ref):
-    seqs = solution_ref.shape[0]
-    both = jnp.concatenate([solution_ref[...], direction_ref[...]], axis=0)
-    scores = dot_pieces(pieces_of(both, 3), queries_ref[...], 2 * seqs)
-    solved_ref[...] = scores[:seqs]
-    along_ref[...] = scores[seqs:]
-
-
-def score(solution, direction, queries):
-    scores = F32((solution.shape[0], queries.shape[0]))
-    return pl.pallas_call(
-        score_kernel,
-        out_shape=(scores, scores),
-        in_specs=[VMEM_SPEC] * 3,
-        out_specs=(VMEM_SPEC,) * 2,
-        compiler_params=PARAMS,
-        name="scores",
-    )(solution, direction, queries)
-
-
 def on_device(dp_size, tensor_size, inputs, in_proj, out_grads, out_proj, prior, queries):
     width = R_IN * R_OUT
     both, devices = ("dp", "tensor"), dp_size * tensor_size
     in_blocks = direct(features(inputs, in_proj, (128,), 20, "in_features"), "tensor", tensor_size)
-    out_local = features(out_grads, out_proj, (256,) * 7 + (128,), 44, "out_features")
+    out_local = features(out_grads, out_proj, (128, 128) + (256,) * 6 + (128,), 44, "out_features")
     partial = partial_vectors(in_blocks, out_local).reshape(-1, width)
-    pieces = direct(sum_over(partial, "tensor", tensor_size), "dp", dp_size)
-    prior_pieces = [in_vmem(piece) for piece in split_prior(prior)]
+    first, *rest = bits(tensor_size)
+    prior, partial = lax.optimization_barrier((prior, partial))
+    partial = partial + swap(partial, "tensor", tensor_size, first)
+    partial, prior_pieces = lax.optimization_barrier((partial, split_prior(prior)))
+    for bit in rest:
+        partial = partial + swap(partial, "tensor", tensor_size, bit)
+    pieces = direct(partial, "dp", dp_size)
+    prior_pieces = [in_vmem(piece) for piece in prior_pieces]
     vectors, vector_pieces, scale, applied_rows, norm = start_cg(pieces, prior_pieces, tensor_size)
     fixed = (*prior_pieces, vectors, vector_pieces, scale)
     state = [applied_rows]
     for iteration in range(1, ITERS - 1):
         blocks = gather(state[0], both, devices)
-        applied_rows, norm, *others = step_cg(blocks, fixed, norm, state, False, tensor_size)
+        applied_rows, norm, *others = step_cg(blocks, fixed, norm, state, None, tensor_size)
         state = [applied_rows, *others]
     blocks = gather(state[0], both, devices)
-    curvature, norm, direction, solved = step_cg(blocks, fixed, norm, state, True, tensor_size)
+    curvature, norm, solved, along = step_cg(blocks, fixed, norm, state, queries, tensor_size)
     curvature = jnp.sum(gather(curvature, both, devices), axis=0)
-    solved, along = score(solved, direction, queries)
     return solved + (norm / curvature)[:, :1] * along
 
 

time: 88.7 us -> 87.9 us (level)
  blocking collectives: 32.2 us -> 41.6 us
  waiting for transfers between devices: 11.5 us -> 5.85 us
  starting transfers between devices: 16.1 us -> 12.3 us
    all_to_all x3 -> x4, blocking collectives: 32.2 us -> 41.6 us  [gather(): lax.all_to_all(jnp.broadcast_to(value[None], (size,) + value.shape), axes...]
    all_to_all x1 -> x0, waiting for transfers between devices: 6.29 us -> none  [gather(): lax.all_to_all(jnp.broadcast_to(value[None], (size,) + value.shape), axes...]
    all_to_all x1 -> x0, starting transfers between devices: 3.49 us -> none  [gather(): lax.all_to_all(jnp.broadcast_to(value[None], (size,) + value.shape), axes...]
  transfers between devices with their start and end apart: 9 -> 8, of which waited for: 4 -> 3; matrix products, arithmetic and copies ran while one was open for 0% -> 0% of each run, Pallas kernels for 17% -> 17%
where the time goes in v13:
time: 87.9 us; the launch traced here: 87.6 us
  blocking collectives  41.6 us (47%)
  Pallas kernels  26.8 us (30%)
  starting transfers between devices  12.3 us (14%)
  waiting for transfers between devices  5.85 us (7%)
    all_to_all x4, blocking collectives, gather(): lax.all_to_all(jnp.broadcast_to(value[None], (size,) + value.shape), axes...  41.6 us
    pallas_call x2, Pallas kernels, features(): pl.pallas_call(functools.partial(stream_kernel, spans), out_shape=pltpu.V...  17.2 us
    ppermute x8, starting transfers between devices, swap(): return lax.ppermute(value, axis, [(i, i ^ bit) for i in range(size)])  12.3 us
    ppermute x8, waiting for transfers between devices, swap(): return lax.ppermute(value, axis, [(i, i ^ bit) for i in range(size)])  5.85 us
    pallas_call x3, Pallas kernels, step_cg(): pl.pallas_call(functools.partial(step_kernel, tensor_size, first, last),...  5.12 us
    pallas_call x1, Pallas kernels, split_prior(): pl.pallas_call(split_kernel, out_shape=(pltpu.VMEM(prior.shape, jnp.bfloa...  2.32 us
  transfers between devices with their start and end apart: 8, of which 3 were waited for; matrix products, arithmetic and copies ran while one was open for 0% of the time, Pallas kernels for 17%

profile of v13, /device:TPU:0, one launch (start us, length us, event | category | flops | bytes accessed | tf_op | source)
XLA Modules:
  0.0 87.6 jit_solution(3251596563595458333)
XLA Ops:
  0.0 5.0 %in_features.1.refs_0_ = f32[64,512]{1,0:T(8,128)S(1)} custom-call(bf16[512,8192]{1,0:T(8,128)(2,1)} %rows_ref.2, bf16[64,8192]{1,0:T(8,128)(2,1)} %proj_ref.2), custom_call_target="tpu_custom_call" | custom-call | tf_op jit(solution)/shard_map/in_features/pallas_call | solution.py:99
  5.1 3.1 %collective-permute-start.2 = (f32[64,512]{1,0:T(8,128)S(1)}, f32[64,512]{1,0:T(8,128)S(1)}, u32[]{:S(2)}, u32[]{:S(2)}) collective-permute-start(f32[64,512]{1,0:T(8,128)S(1)} %in_features.1.refs_0_), channel_id=1, source_target_pairs={{0,1},{1,0},{2,3},{3,2},{4,5},{5,4},{6,7},{7,6},{8,9},{9,8},{10,11... | collective-permute-start | bytes 393224 | tf_op jit(solution)/shard_map/ppermute | solution.py:25
  8.1 2.5 %collective-permute-start.1 = (f32[64,512]{1,0:T(8,128)S(1)}, f32[64,512]{1,0:T(8,128)S(1)}, u32[]{:S(2)}, u32[]{:S(2)}) collective-permute-start(f32[64,512]{1,0:T(8,128)S(1)} %in_features.1.refs_0_), channel_id=1, source_target_pairs={{0,3},{1,2},{2,1},{3,0},{4,7},{5,6},{6,5},{7,4},{8,11},{9,10},{10,... | collective-permute-start | bytes 393224 | tf_op jit(solution)/shard_map/ppermute | solution.py:25
  10.6 0.1 collective-permute-start
  10.7 12.2 %out_features.1.refs_4_ = f32[64,2048]{1,0:T(8,128)S(1)} custom-call(bf16[2048,7168]{1,0:T(8,128)(2,1)} %rows_ref.3, bf16[64,7168]{1,0:T(8,128)(2,1)} %proj_ref.3), custom_call_target="tpu_custom_call" | custom-call | tf_op jit(solution)/shard_map/out_features/pallas_call | solution.py:99
  23.0 0.6 partial_vectors.1
  23.7 2.9 %collective-permute-start.3 = (f32[2,4096]{1,0:T(2,128)S(1)}, f32[2,4096]{1,0:T(2,128)S(1)}, u32[]{:S(2)}, u32[]{:S(2)}) collective-permute-start(f32[2,4096]{1,0:T(2,128)S(1)} %reshape.7), channel_id=1, source_target_pairs={{0,2},{1,3},{2,0},{3,1},{4,6},{5,7},{6,4},{7,5},{8,10},{9,11},{10,... | collective-permute-start | bytes 98312 | tf_op jit(solution)/shard_map/ppermute | solution.py:25
  26.6 2.3 %split_prior.1 = (bf16[256,4096]{1,0:T(8,128)(2,1)S(1)}, bf16[256,4096]{1,0:T(8,128)(2,1)S(1)}) custom-call(f32[256,4096]{1,0:T(8,128)} %prior_ref), custom_call_target="tpu_custom_call" | custom-call | tf_op jit(solution)/shard_map/split_prior/pallas_call | solution.py:133
  28.9 1.5 %collective-permute-start.4 = (f32[2,4096]{1,0:T(2,128)S(1)}, f32[2,4096]{1,0:T(2,128)S(1)}, u32[]{:S(2)}, u32[]{:S(2)}) collective-permute-start(f32[2,4096]{1,0:T(2,128)S(1)} %add.9), channel_id=1, source_target_pairs={{0,1},{1,0},{2,3},{3,2},{4,5},{5,4},{6,7},{7,6},{8,9},{9,8},{10,11... | collective-permute-start | bytes 98312 | tf_op jit(solution)/shard_map/ppermute | solution.py:25
  30.5 2.5 %collective-permute-done.4 = f32[2,4096]{1,0:T(2,128)S(1)} collective-permute-done((f32[2,4096]{1,0:T(2,128)S(1)}, f32[2,4096]{1,0:T(2,128)S(1)}, u32[]{:S(2)}, u32[]{:S(2)}) %collective-permute-start.4) | collective-permute-done | bytes 32800 | tf_op jit(solution)/shard_map/ppermute | solution.py:25
  33.0 1.6 %collective-permute-start.6 = (f32[2,4096]{1,0:T(2,128)S(1)}, f32[2,4096]{1,0:T(2,128)S(1)}, u32[]{:S(2)}, u32[]{:S(2)}) collective-permute-start(f32[2,4096]{1,0:T(2,128)S(1)} %add.10.refs_0_), channel_id=1, source_target_pairs={{0,12},{4,8},{8,4},{12,0},{1,13},{5,9},{9,5},{13,1},{2,14},{6,10},... | collective-permute-start | bytes 98312 | tf_op jit(solution)/shard_map/ppermute | solution.py:25
  34.6 0.5 collective-permute-start.5
  35.2 1.3 %collective-permute-done.6.refs_2_ = f32[2,4096]{1,0:T(2,128)S(1)} collective-permute-done((f32[2,4096]{1,0:T(2,128)S(1)}, f32[2,4096]{1,0:T(2,128)S(1)}, u32[]{:S(2)}, u32[]{:S(2)}) %collective-permute-start.6) | collective-permute-done | bytes 32800 | tf_op jit(solution)/shard_map/ppermute | solution.py:25
  36.4 2.1 %collective-permute-done.5.refs_1_ = f32[2,4096]{1,0:T(2,128)S(1)} collective-permute-done((f32[2,4096]{1,0:T(2,128)S(1)}, f32[2,4096]{1,0:T(2,128)S(1)}, u32[]{:S(2)}, u32[]{:S(2)}) %collective-permute-start.5) | collective-permute-done | bytes 32800 | tf_op jit(solution)/shard_map/ppermute | solution.py:25
  38.6 1.5 %cg_start.1 = (f32[8,4096]{1,0:T(8,128)S(1)}, bf16[16,4096]{1,0:T(8,128)(2,1)S(1)}, f32[8,128]{1,0:T(8,128)S(1)}, f32[8,256]{1,0:T(8,128)S(1)}, f32[8,128]{1,0:T(8,128)S(1)}) custom-call(f32[2,4096]{1,0:T(2,128)S(1)} %add.10.refs_0_, f32[2,4096]{1,0:T(2,128)S(1)} %collective-permute-done.5.refs_1_, f32[2,4096]{1,0:T(2,128)S(1)} %collective-permute-done.6.refs_2_, ...), custom_call_target="tpu_custom_call" | custom-call | tf_op jit(solution)/shard_map/cg_start/pallas_call | solution.py:232
  40.1 11.1 %all_to_all.20.refs_0_ = f32[16,8,256]{2,1,0:T(8,128)S(1)} all-to-all(f32[16,8,256]{2,1,0:T(8,128)S(1)} %broadcast_in_dim.8), channel_id=1, replica_groups=mesh['groups'=2,'dp'=4,'tensor'=4] {'dp','tensor'}, dimensions={0} | all-to-all | bytes 262144 | tf_op jit(solution)/shard_map/all_to_all | solution.py:33
  51.2 1.6 %cg_step.3 = (f32[8,256]{1,0:T(8,128)S(1)}, f32[8,128]{1,0:T(8,128)S(1)}, f32[8,256]{1,0:T(8,128)S(1)}, f32[8,4096]{1,0:T(8,128)S(1)}, f32[8,4096]{1,0:T(8,128)S(1)}, /*index=5*/f32[8,4096]{1,0:T(8,128)S(1)}) custom-call(f32[16,8,256]{2,1,0:T(8,128)S(1)} %all_to_all.20.refs_0_, bf16[256,4096]{1,0:T(8,128)(2,1)S(1)} %get-tuple-element.38.refs_4_.refs_1_, ...), custom_call_target="tpu_custom_call" | custom-call | tf_op jit(solution)/shard_map/cg_step/pallas_call | solution.py:305
  52.8 10.4 %all_to_all.21.refs_0_ = f32[16,8,256]{2,1,0:T(8,128)S(1)} all-to-all(f32[16,8,256]{2,1,0:T(8,128)S(1)} %broadcast_in_dim.9), channel_id=1, replica_groups=mesh['groups'=2,'dp'=4,'tensor'=4] {'dp','tensor'}, dimensions={0} | all-to-all | bytes 262144 | tf_op jit(solution)/shard_map/all_to_all | solution.py:33
  63.2 1.6 %cg_step.4 = (f32[8,256]{1,0:T(8,128)S(1)}, f32[8,128]{1,0:T(8,128)S(1)}, f32[8,256]{1,0:T(8,128)S(1)}, f32[8,4096]{1,0:T(8,128)S(1)}, f32[8,4096]{1,0:T(8,128)S(1)}, /*index=5*/f32[8,4096]{1,0:T(8,128)S(1)}) custom-call(f32[16,8,256]{2,1,0:T(8,128)S(1)} %all_to_all.21.refs_0_, bf16[256,4096]{1,0:T(8,128)(2,1)S(1)} %get-tuple-element.38.refs_4_.refs_1_, ...), custom_call_target="tpu_custom_call" | custom-call | tf_op jit(solution)/shard_map/cg_step/pallas_call | solution.py:305
  64.8 10.4 %all_to_all.22.refs_0_ = f32[16,8,256]{2,1,0:T(8,128)S(1)} all-to-all(f32[16,8,256]{2,1,0:T(8,128)S(1)} %broadcast_in_dim.10), channel_id=1, replica_groups=mesh['groups'=2,'dp'=4,'tensor'=4] {'dp','tensor'}, dimensions={0} | all-to-all | bytes 262144 | tf_op jit(solution)/shard_map/all_to_all | solution.py:33
  75.2 1.9 %cg_step.5 = (f32[8,128]{1,0:T(8,128)S(1)}, f32[8,128]{1,0:T(8,128)S(1)}, f32[8,32]{1,0:T(8,128)S(1)}, f32[8,32]{1,0:T(8,128)S(1)}) custom-call(f32[16,8,256]{2,1,0:T(8,128)S(1)} %all_to_all.22.refs_0_, bf16[256,4096]{1,0:T(8,128)(2,1)S(1)} %get-tuple-element.38.refs_4_.refs_1_, bf16[256,4096]{1,0:T(8,128)(2,1)S(1)} %get-tuple-element.39.refs_5_.refs_2_, ...), custom_call_target="tpu_custom_call" | custom-call | tf_op jit(solution)/shard_map/cg_step/pallas_call | solution.py:305
  77.1 9.7 %all_to_all.23 = f32[16,8,128]{2,1,0:T(8,128)S(1)} all-to-all(f32[16,8,128]{2,1,0:T(8,128)S(1)} %broadcast_in_dim.11), channel_id=1, replica_groups=mesh['groups'=2,'dp'=4,'tensor'=4] {'dp','tensor'}, dimensions={0} | all-to-all | bytes 131072 | tf_op jit(solution)/shard_map/all_to_all | solution.py:33
  86.8 0.1 slice_reduce_fusion
  86.9 0.7 multiply_add_fusion
  (17 shorter events, 0.3 us)
Async XLA Ops:
  5.1 17.9 %collective-permute-start.2 = (f32[64,512]{1,0:T(8,128)S(1)}, f32[64,512]{1,0:T(8,128)S(1)}, u32[]{:S(2)}, u32[]{:S(2)}) collective-permute-start(f32[64,512]{1,0:T(8,128)S(1)} %in_features.1.refs_0_), channel_id=1, source_target_pairs={{0,1},{1,0},{2,3},{3,2},{4,5},{5,4},{6,7},{7,6},{8,9},{9,8},{10,11... | collective-permute-start | bytes 393224 | tf_op jit(solution)/shard_map/ppermute | solution.py:25
  8.1 14.8 %collective-permute-start.1 = (f32[64,512]{1,0:T(8,128)S(1)}, f32[64,512]{1,0:T(8,128)S(1)}, u32[]{:S(2)}, u32[]{:S(2)}) collective-permute-start(f32[64,512]{1,0:T(8,128)S(1)} %in_features.1.refs_0_), channel_id=1, source_target_pairs={{0,3},{1,2},{2,1},{3,0},{4,7},{5,6},{6,5},{7,4},{8,11},{9,10},{10,... | collective-permute-start | bytes 393224 | tf_op jit(solution)/shard_map/ppermute | solution.py:25
  10.6 12.3 %collective-permute-start = (f32[64,512]{1,0:T(8,128)S(1)}, f32[64,512]{1,0:T(8,128)S(1)}, u32[]{:S(2)}, u32[]{:S(2)}) collective-permute-start(f32[64,512]{1,0:T(8,128)S(1)} %in_features.1.refs_0_), channel_id=1, source_target_pairs={{0,2},{1,3},{2,0},{3,1},{4,6},{5,7},{6,4},{7,5},{8,10},{9,11},{10,... | collective-permute-start | bytes 393224 | tf_op jit(solution)/shard_map/ppermute | solution.py:25
  23.7 5.2 %collective-permute-start.3 = (f32[2,4096]{1,0:T(2,128)S(1)}, f32[2,4096]{1,0:T(2,128)S(1)}, u32[]{:S(2)}, u32[]{:S(2)}) collective-permute-start(f32[2,4096]{1,0:T(2,128)S(1)} %reshape.7), channel_id=1, source_target_pairs={{0,2},{1,3},{2,0},{3,1},{4,6},{5,7},{6,4},{7,5},{8,10},{9,11},{10,... | collective-permute-start | bytes 98312 | tf_op jit(solution)/shard_map/ppermute | solution.py:25
  28.9 4.0 %collective-permute-start.4 = (f32[2,4096]{1,0:T(2,128)S(1)}, f32[2,4096]{1,0:T(2,128)S(1)}, u32[]{:S(2)}, u32[]{:S(2)}) collective-permute-start(f32[2,4096]{1,0:T(2,128)S(1)} %add.9), channel_id=1, source_target_pairs={{0,1},{1,0},{2,3},{3,2},{4,5},{5,4},{6,7},{7,6},{8,9},{9,8},{10,11... | collective-permute-start | bytes 98312 | tf_op jit(solution)/shard_map/ppermute | solution.py:25
  32.9 2.2 %collective-permute-start.7 = (f32[2,4096]{1,0:T(2,128)S(1)}, f32[2,4096]{1,0:T(2,128)S(1)}, u32[]{:S(2)}, u32[]{:S(2)}) collective-permute-start(f32[2,4096]{1,0:T(2,128)S(1)} %add.10.refs_0_), channel_id=1, source_target_pairs={{0,4},{4,0},{8,12},{12,8},{1,5},{5,1},{9,13},{13,9},{2,6},{6,2},{1... | collective-permute-start | bytes 98312 | tf_op jit(solution)/shard_map/ppermute | solution.py:25
  33.0 3.4 %collective-permute-start.6 = (f32[2,4096]{1,0:T(2,128)S(1)}, f32[2,4096]{1,0:T(2,128)S(1)}, u32[]{:S(2)}, u32[]{:S(2)}) collective-permute-start(f32[2,4096]{1,0:T(2,128)S(1)} %add.10.refs_0_), channel_id=1, source_target_pairs={{0,12},{4,8},{8,4},{12,0},{1,13},{5,9},{9,5},{13,1},{2,14},{6,10},... | collective-permute-start | bytes 98312 | tf_op jit(solution)/shard_map/ppermute | solution.py:25
  34.6 3.9 %collective-permute-start.5 = (f32[2,4096]{1,0:T(2,128)S(1)}, f32[2,4096]{1,0:T(2,128)S(1)}, u32[]{:S(2)}, u32[]{:S(2)}) collective-permute-start(f32[2,4096]{1,0:T(2,128)S(1)} %add.10.refs_0_), channel_id=1, source_target_pairs={{0,8},{4,12},{8,0},{12,4},{1,9},{5,13},{9,1},{13,5},{2,10},{6,14},... | collective-permute-start | bytes 98312 | tf_op jit(solution)/shard_map/ppermute | solution.py:25
  51.2 24.0 %copy-start = (bf16[32,4096]{1,0:T(8,128)(2,1)S(1)}, bf16[32,4096]{1,0:T(8,128)(2,1)}, u32[]{:S(2)}) copy-start(bf16[32,4096]{1,0:T(8,128)(2,1)} %refs_12_.1) | copy-start | bytes 786436

commit v14 on v13

--- a/solution.py
+++ b/solution.py
@@ -12,7 +12,6 @@
 SEQ = 1024
 ITERS = 4
 LANES = 128
-DEPTH = 4
 NT = (((1,), (1,)), ((), ()))
 HIGHEST = lax.Precision.HIGHEST
 ANY_SPEC = pl.BlockSpec(memory_space=pl.ANY)
@@ -37,8 +36,8 @@
     return (0, 2, 3, 1) if size == 4 else tuple(range(size))
 
 
-def direct(value, axis, size):
-    return [value] + [swap(value, axis, size, k) for k in order_of(size)[1:]]
+def direct(value, axis, size, order):
+    return [value] + [swap(value, axis, size, k) for k in order[1:]]
 
 
 def in_hbm(value):
@@ -57,55 +56,49 @@
     return jnp.sum(values, axis=1, keepdims=True)
 
 
-def row_spans(rows, sizes):
-    spans, start = [], 0
-    while start < rows:
-        while len(sizes) > 1 and start + sizes[0] + sizes[-1] > rows:
-            sizes = sizes[1:]
-        spans.append(pl.ds(start, sizes[0]))
-        start += sizes[0]
-        sizes = sizes[1:] or sizes
-    return spans
-
-
-def stream_kernel(spans, rows_ref, proj_ref, feats_ref, held, proj, turned, sems):
+def stream_kernel(block, rows_ref, proj_ref, feats_ref, held, proj, turned, sems):
     count, half = proj_ref.shape[0], proj.shape[1]
+    steps = held.shape[0] // block
     firsts = [
         pltpu.make_async_copy(
-            proj_ref.at[:, pl.ds(h * half, half)], proj.at[pl.ds(h * count, count)], sems.at[len(spans) + h]
+            proj_ref.at[:, pl.ds(h * half, half)], proj.at[pl.ds(h * count, count)], sems.at[steps + h]
         )
         for h in range(2)
     ]
-    copies = [
-        pltpu.make_async_copy(rows_ref.at[span], held.at[span], sems.at[c])
-        for c, span in enumerate(spans)
-    ]
-    for copy in firsts + copies[:DEPTH]:
+
+    def fetch(step):
+        span = pl.ds(pl.multiple_of(step * block, block), block)
+        return pltpu.make_async_copy(rows_ref.at[span], held.at[span], sems.at[step])
+
+    for copy in firsts:
         copy.start()
+    for step in range(steps):
+        fetch(step).start()
     for copy in firsts:
         copy.wait()
     turned[...] = proj[...].T
-    for c, span in enumerate(spans):
-        copies[c].wait()
-        if c + DEPTH < len(spans):
-            copies[c + DEPTH].start()
+
+    @pl.loop(0, steps)
+    def _(step):
+        fetch(step).wait()
+        span = pl.ds(pl.multiple_of(step * block, block), block)
         left = jnp.dot(held[span, :half], turned[...], preferred_element_type=jnp.float32)
         right = jnp.dot(held[span, half:], turned[...], preferred_element_type=jnp.float32)
         feats_ref[:, span] = left.T[:count] + right.T[count:]
 
 
-def features(rows, proj, sizes, limit, name):
-    spans = row_spans(rows.shape[0], sizes)
-    return pl.pallas_call(
-        functools.partial(stream_kernel, spans),
-        out_shape=pltpu.VMEM((proj.shape[0], rows.shape[0]), jnp.float32),
+def features(rows, proj, block, limit, name):
+    count, width = proj.shape
+    return pl.pallas_call(
+        functools.partial(stream_kernel, block),
+        out_shape=pltpu.VMEM((count, rows.shape[0]), jnp.float32),
         in_specs=[ANY_SPEC] * 2,
         out_specs=VMEM_SPEC,
         scratch_shapes=[
             pltpu.VMEM(rows.shape, jnp.bfloat16),
-            pltpu.VMEM((2 * proj.shape[0], proj.shape[1] // 2), jnp.bfloat16),
-            pltpu.VMEM((proj.shape[1] // 2, 2 * proj.shape[0]), jnp.bfloat16),
-            pltpu.SemaphoreType.DMA((len(spans) + 2,)),
+            pltpu.VMEM((2 * count, width // 2), jnp.bfloat16),
+            pltpu.VMEM((width // 2, 2 * count), jnp.bfloat16),
+            pltpu.SemaphoreType.DMA((rows.shape[0] // block + 2,)),
         ],
         compiler_params=pltpu.CompilerParams(vmem_limit_bytes=limit * 2**20),
         name=name,
@@ -209,7 +202,7 @@
     pieces, refs = refs[:size], refs[size:]
     upper_ref, lower_ref, vectors_ref, vector_pieces_ref, scale_ref, applied_ref, norm_ref, held = refs
     dp = lax.axis_index("dp")
-    for k, piece in zip(order_of(size), pieces):
+    for k, piece in enumerate(pieces):
         held[dp ^ k] = piece[...]
     vectors = jnp.concatenate([held[k] for k in range(size)], axis=0)
     vectors_ref[...] = vectors
@@ -316,8 +309,8 @@
 def on_device(dp_size, tensor_size, inputs, in_proj, out_grads, out_proj, prior, queries):
     width = R_IN * R_OUT
     both, devices = ("dp", "tensor"), dp_size * tensor_size
-    in_blocks = direct(features(inputs, in_proj, (128,), 20, "in_features"), "tensor", tensor_size)
-    out_local = features(out_grads, out_proj, (128, 128) + (256,) * 6 + (128,), 44, "out_features")
+    in_blocks = direct(features(inputs, in_proj, LANES, 20, "in_features"), "tensor", tensor_size, order_of(tensor_size))
+    out_local = features(out_grads, out_proj, 2 * LANES, 44, "out_features")
     partial = partial_vectors(in_blocks, out_local).reshape(-1, width)
     first, *rest = bits(tensor_size)
     prior, partial = lax.optimization_barrier((prior, partial))
@@ -325,7 +318,7 @@
     partial, prior_pieces = lax.optimization_barrier((partial, split_prior(prior)))
     for bit in rest:
         partial = partial + swap(partial, "tensor", tensor_size, bit)
-    pieces = direct(partial, "dp", dp_size)
+    pieces = direct(partial, "dp", dp_size, range(dp_size))
     prior_pieces = [in_vmem(piece) for piece in prior_pieces]
     vectors, vector_pieces, scale, applied_rows, norm = start_cg(pieces, prior_pieces, tensor_size)
     fixed = (*prior_pieces, vectors, vector_pieces, scale)

time: 87.9 us -> 87 us (0.990)
  waiting for transfers between devices: 5.85 us -> 4.65 us
  blocking collectives: 41.6 us -> 42.5 us
    ppermute x8, waiting for transfers between devices: 5.85 us -> 4.65 us  [swap(): return lax.ppermute(value, axis, [(i, i ^ bit) for i in range(size)])]
    all_to_all x4, blocking collectives: 41.6 us -> 42.5 us  [gather(): lax.all_to_all(jnp.broadcast_to(value[None], (size,) + value.shape), axes...]
  transfers between devices with their start and end apart: 8 -> 8, of which waited for: 3 -> 3; matrix products, arithmetic and copies ran while one was open for 0% -> 0% of each run, Pallas kernels for 17% -> 16%
where the time goes in v14:
time: 87 us; the launch traced here: 86.7 us
  blocking collectives  42.5 us (49%)
  Pallas kernels  26.4 us (30%)
  starting transfers between devices  12 us (14%)
  waiting for transfers between devices  4.65 us (5%)
    all_to_all x4, blocking collectives, gather(): lax.all_to_all(jnp.broadcast_to(value[None], (size,) + value.shape), axes...  42.5 us
    pallas_call x2, Pallas kernels, features(): pl.pallas_call(functools.partial(stream_kernel, block), out_shape=pltpu.V...  16.9 us
    ppermute x8, starting transfers between devices, swap(): return lax.ppermute(value, axis, [(i, i ^ bit) for i in range(size)])  12 us
    pallas_call x3, Pallas kernels, step_cg(): pl.pallas_call(functools.partial(step_kernel, tensor_size, first, last),...  5.12 us
    ppermute x8, waiting for transfers between devices, swap(): return lax.ppermute(value, axis, [(i, i ^ bit) for i in range(size)])  4.65 us
    pallas_call x1, Pallas kernels, split_prior(): pl.pallas_call(split_kernel, out_shape=(pltpu.VMEM(prior.shape, jnp.bfloa...  2.32 us
  transfers between devices with their start and end apart: 8, of which 3 were waited for; matrix products, arithmetic and copies ran while one was open for 0% of the time, Pallas kernels for 16%

profile of v14, /device:TPU:0, one launch (start us, length us, event | category | flops | bytes accessed | tf_op | source)
XLA Modules:
  0.0 86.7 jit_solution(3696599347793796921)
XLA Ops:
  0.0 5.1 %in_features.1.refs_0_ = f32[64,512]{1,0:T(8,128)S(1)} custom-call(bf16[512,8192]{1,0:T(8,128)(2,1)} %rows_ref.2, bf16[64,8192]{1,0:T(8,128)(2,1)} %proj_ref.2), custom_call_target="tpu_custom_call" | custom-call | tf_op jit(solution)/shard_map/in_features/pallas_call | solution.py:92
  5.1 3.1 %collective-permute-start.2 = (f32[64,512]{1,0:T(8,128)S(1)}, f32[64,512]{1,0:T(8,128)S(1)}, u32[]{:S(2)}, u32[]{:S(2)}) collective-permute-start(f32[64,512]{1,0:T(8,128)S(1)} %in_features.1.refs_0_), channel_id=1, source_target_pairs={{0,1},{1,0},{2,3},{3,2},{4,5},{5,4},{6,7},{7,6},{8,9},{9,8},{10,11... | collective-permute-start | bytes 393224 | tf_op jit(solution)/shard_map/ppermute | solution.py:24
  8.1 2.5 %collective-permute-start.1 = (f32[64,512]{1,0:T(8,128)S(1)}, f32[64,512]{1,0:T(8,128)S(1)}, u32[]{:S(2)}, u32[]{:S(2)}) collective-permute-start(f32[64,512]{1,0:T(8,128)S(1)} %in_features.1.refs_0_), channel_id=1, source_target_pairs={{0,3},{1,2},{2,1},{3,0},{4,7},{5,6},{6,5},{7,4},{8,11},{9,10},{10,... | collective-permute-start | bytes 393224 | tf_op jit(solution)/shard_map/ppermute | solution.py:24
  10.6 0.1 collective-permute-start
  10.7 11.8 %out_features.1.refs_4_ = f32[64,2048]{1,0:T(8,128)S(1)} custom-call(bf16[2048,7168]{1,0:T(8,128)(2,1)} %rows_ref.3, bf16[64,7168]{1,0:T(8,128)(2,1)} %proj_ref.3), custom_call_target="tpu_custom_call" | custom-call | tf_op jit(solution)/shard_map/out_features/pallas_call | solution.py:92
  22.6 0.6 partial_vectors.1
  23.3 2.9 %collective-permute-start.3 = (f32[2,4096]{1,0:T(2,128)S(1)}, f32[2,4096]{1,0:T(2,128)S(1)}, u32[]{:S(2)}, u32[]{:S(2)}) collective-permute-start(f32[2,4096]{1,0:T(2,128)S(1)} %reshape.7), channel_id=1, source_target_pairs={{0,2},{1,3},{2,0},{3,1},{4,6},{5,7},{6,4},{7,5},{8,10},{9,11},{10,... | collective-permute-start | bytes 98312 | tf_op jit(solution)/shard_map/ppermute | solution.py:24
  26.2 2.3 %split_prior.1 = (bf16[256,4096]{1,0:T(8,128)(2,1)S(1)}, bf16[256,4096]{1,0:T(8,128)(2,1)S(1)}) custom-call(f32[256,4096]{1,0:T(8,128)} %prior_ref), custom_call_target="tpu_custom_call" | custom-call | tf_op jit(solution)/shard_map/split_prior/pallas_call | solution.py:126
  28.6 1.5 %collective-permute-start.4 = (f32[2,4096]{1,0:T(2,128)S(1)}, f32[2,4096]{1,0:T(2,128)S(1)}, u32[]{:S(2)}, u32[]{:S(2)}) collective-permute-start(f32[2,4096]{1,0:T(2,128)S(1)} %add.9), channel_id=1, source_target_pairs={{0,1},{1,0},{2,3},{3,2},{4,5},{5,4},{6,7},{7,6},{8,9},{9,8},{10,11... | collective-permute-start | bytes 98312 | tf_op jit(solution)/shard_map/ppermute | solution.py:24
  30.1 2.5 %collective-permute-done.4 = f32[2,4096]{1,0:T(2,128)S(1)} collective-permute-done((f32[2,4096]{1,0:T(2,128)S(1)}, f32[2,4096]{1,0:T(2,128)S(1)}, u32[]{:S(2)}, u32[]{:S(2)}) %collective-permute-start.4) | collective-permute-done | bytes 32800 | tf_op jit(solution)/shard_map/ppermute | solution.py:24
  32.6 1.6 %collective-permute-start.6 = (f32[2,4096]{1,0:T(2,128)S(1)}, f32[2,4096]{1,0:T(2,128)S(1)}, u32[]{:S(2)}, u32[]{:S(2)}) collective-permute-start(f32[2,4096]{1,0:T(2,128)S(1)} %add.10.refs_0_), channel_id=1, source_target_pairs={{0,8},{4,12},{8,0},{12,4},{1,9},{5,13},{9,1},{13,5},{2,10},{6,14},... | collective-permute-start | bytes 98312 | tf_op jit(solution)/shard_map/ppermute | solution.py:24
  34.2 0.3 collective-permute-start.5
  34.5 1.8 %collective-permute-done.7.refs_3_ = f32[2,4096]{1,0:T(2,128)S(1)} collective-permute-done((f32[2,4096]{1,0:T(2,128)S(1)}, f32[2,4096]{1,0:T(2,128)S(1)}, u32[]{:S(2)}, u32[]{:S(2)}) %collective-permute-start.7) | collective-permute-done | bytes 32800 | tf_op jit(solution)/shard_map/ppermute | solution.py:24
  36.3 0.4 collective-permute-done.6.refs_2_
  36.7 1.5 %cg_start.1 = (f32[8,4096]{1,0:T(8,128)S(1)}, bf16[16,4096]{1,0:T(8,128)(2,1)S(1)}, f32[8,128]{1,0:T(8,128)S(1)}, f32[8,256]{1,0:T(8,128)S(1)}, f32[8,128]{1,0:T(8,128)S(1)}) custom-call(f32[2,4096]{1,0:T(2,128)S(1)} %add.10.refs_0_, f32[2,4096]{1,0:T(2,128)S(1)} %collective-permute-done.5.refs_1_, f32[2,4096]{1,0:T(2,128)S(1)} %collective-permute-done.6.refs_2_, ...), custom_call_target="tpu_custom_call" | custom-call | tf_op jit(solution)/shard_map/cg_start/pallas_call | solution.py:225
  38.2 12.1 %all_to_all.20.refs_0_ = f32[16,8,256]{2,1,0:T(8,128)S(1)} all-to-all(f32[16,8,256]{2,1,0:T(8,128)S(1)} %broadcast_in_dim.8), channel_id=1, replica_groups=mesh['groups'=2,'dp'=4,'tensor'=4] {'dp','tensor'}, dimensions={0} | all-to-all | bytes 262144 | tf_op jit(solution)/shard_map/all_to_all | solution.py:32
  50.2 1.6 %cg_step.3 = (f32[8,256]{1,0:T(8,128)S(1)}, f32[8,128]{1,0:T(8,128)S(1)}, f32[8,256]{1,0:T(8,128)S(1)}, f32[8,4096]{1,0:T(8,128)S(1)}, f32[8,4096]{1,0:T(8,128)S(1)}, /*index=5*/f32[8,4096]{1,0:T(8,128)S(1)}) custom-call(f32[16,8,256]{2,1,0:T(8,128)S(1)} %all_to_all.20.refs_0_, bf16[256,4096]{1,0:T(8,128)(2,1)S(1)} %get-tuple-element.38.refs_4_.refs_1_, ...), custom_call_target="tpu_custom_call" | custom-call | tf_op jit(solution)/shard_map/cg_step/pallas_call | solution.py:298
  51.9 10.4 %all_to_all.21.refs_0_ = f32[16,8,256]{2,1,0:T(8,128)S(1)} all-to-all(f32[16,8,256]{2,1,0:T(8,128)S(1)} %broadcast_in_dim.9), channel_id=1, replica_groups=mesh['groups'=2,'dp'=4,'tensor'=4] {'dp','tensor'}, dimensions={0} | all-to-all | bytes 262144 | tf_op jit(solution)/shard_map/all_to_all | solution.py:32
  62.2 1.6 %cg_step.4 = (f32[8,256]{1,0:T(8,128)S(1)}, f32[8,128]{1,0:T(8,128)S(1)}, f32[8,256]{1,0:T(8,128)S(1)}, f32[8,4096]{1,0:T(8,128)S(1)}, f32[8,4096]{1,0:T(8,128)S(1)}, /*index=5*/f32[8,4096]{1,0:T(8,128)S(1)}) custom-call(f32[16,8,256]{2,1,0:T(8,128)S(1)} %all_to_all.21.refs_0_, bf16[256,4096]{1,0:T(8,128)(2,1)S(1)} %get-tuple-element.38.refs_4_.refs_1_, ...), custom_call_target="tpu_custom_call" | custom-call | tf_op jit(solution)/shard_map/cg_step/pallas_call | solution.py:298
  63.9 10.4 %all_to_all.22.refs_0_ = f32[16,8,256]{2,1,0:T(8,128)S(1)} all-to-all(f32[16,8,256]{2,1,0:T(8,128)S(1)} %broadcast_in_dim.10), channel_id=1, replica_groups=mesh['groups'=2,'dp'=4,'tensor'=4] {'dp','tensor'}, dimensions={0} | all-to-all | bytes 262144 | tf_op jit(solution)/shard_map/all_to_all | solution.py:32
  74.3 1.9 %cg_step.5 = (f32[8,128]{1,0:T(8,128)S(1)}, f32[8,128]{1,0:T(8,128)S(1)}, f32[8,32]{1,0:T(8,128)S(1)}, f32[8,32]{1,0:T(8,128)S(1)}) custom-call(f32[16,8,256]{2,1,0:T(8,128)S(1)} %all_to_all.22.refs_0_, bf16[256,4096]{1,0:T(8,128)(2,1)S(1)} %get-tuple-element.38.refs_4_.refs_1_, bf16[256,4096]{1,0:T(8,128)(2,1)S(1)} %get-tuple-element.39.refs_5_.refs_2_, ...), custom_call_target="tpu_custom_call" | custom-call | tf_op jit(solution)/shard_map/cg_step/pallas_call | solution.py:298
  76.2 9.7 %all_to_all.23 = f32[16,8,128]{2,1,0:T(8,128)S(1)} all-to-all(f32[16,8,128]{2,1,0:T(8,128)S(1)} %broadcast_in_dim.11), channel_id=1, replica_groups=mesh['groups'=2,'dp'=4,'tensor'=4] {'dp','tensor'}, dimensions={0} | all-to-all | bytes 131072 | tf_op jit(solution)/shard_map/all_to_all | solution.py:32
  85.9 0.1 slice_reduce_fusion
  86.0 0.7 multiply_add_fusion
  (17 shorter events, 0.3 us)
Async XLA Ops:
  5.1 17.5 %collective-permute-start.2 = (f32[64,512]{1,0:T(8,128)S(1)}, f32[64,512]{1,0:T(8,128)S(1)}, u32[]{:S(2)}, u32[]{:S(2)}) collective-permute-start(f32[64,512]{1,0:T(8,128)S(1)} %in_features.1.refs_0_), channel_id=1, source_target_pairs={{0,1},{1,0},{2,3},{3,2},{4,5},{5,4},{6,7},{7,6},{8,9},{9,8},{10,11... | collective-permute-start | bytes 393224 | tf_op jit(solution)/shard_map/ppermute | solution.py:24
  8.1 14.4 %collective-permute-start.1 = (f32[64,512]{1,0:T(8,128)S(1)}, f32[64,512]{1,0:T(8,128)S(1)}, u32[]{:S(2)}, u32[]{:S(2)}) collective-permute-start(f32[64,512]{1,0:T(8,128)S(1)} %in_features.1.refs_0_), channel_id=1, source_target_pairs={{0,3},{1,2},{2,1},{3,0},{4,7},{5,6},{6,5},{7,4},{8,11},{9,10},{10,... | collective-permute-start | bytes 393224 | tf_op jit(solution)/shard_map/ppermute | solution.py:24
  10.6 12.0 %collective-permute-start = (f32[64,512]{1,0:T(8,128)S(1)}, f32[64,512]{1,0:T(8,128)S(1)}, u32[]{:S(2)}, u32[]{:S(2)}) collective-permute-start(f32[64,512]{1,0:T(8,128)S(1)} %in_features.1.refs_0_), channel_id=1, source_target_pairs={{0,2},{1,3},{2,0},{3,1},{4,6},{5,7},{6,4},{7,5},{8,10},{9,11},{10,... | collective-permute-start | bytes 393224 | tf_op jit(solution)/shard_map/ppermute | solution.py:24
  23.3 5.2 %collective-permute-start.3 = (f32[2,4096]{1,0:T(2,128)S(1)}, f32[2,4096]{1,0:T(2,128)S(1)}, u32[]{:S(2)}, u32[]{:S(2)}) collective-permute-start(f32[2,4096]{1,0:T(2,128)S(1)} %reshape.7), channel_id=1, source_target_pairs={{0,2},{1,3},{2,0},{3,1},{4,6},{5,7},{6,4},{7,5},{8,10},{9,11},{10,... | collective-permute-start | bytes 98312 | tf_op jit(solution)/shard_map/ppermute | solution.py:24
  28.6 4.0 %collective-permute-start.4 = (f32[2,4096]{1,0:T(2,128)S(1)}, f32[2,4096]{1,0:T(2,128)S(1)}, u32[]{:S(2)}, u32[]{:S(2)}) collective-permute-start(f32[2,4096]{1,0:T(2,128)S(1)} %add.9), channel_id=1, source_target_pairs={{0,1},{1,0},{2,3},{3,2},{4,5},{5,4},{6,7},{7,6},{8,9},{9,8},{10,11... | collective-permute-start | bytes 98312 | tf_op jit(solution)/shard_map/ppermute | solution.py:24
  32.6 3.7 %collective-permute-start.7 = (f32[2,4096]{1,0:T(2,128)S(1)}, f32[2,4096]{1,0:T(2,128)S(1)}, u32[]{:S(2)}, u32[]{:S(2)}) collective-permute-start(f32[2,4096]{1,0:T(2,128)S(1)} %add.10.refs_0_), channel_id=1, source_target_pairs={{0,12},{4,8},{8,4},{12,0},{1,13},{5,9},{9,5},{13,1},{2,14},{6,10},... | collective-permute-start | bytes 98312 | tf_op jit(solution)/shard_map/ppermute | solution.py:24
  32.6 4.0 %collective-permute-start.6 = (f32[2,4096]{1,0:T(2,128)S(1)}, f32[2,4096]{1,0:T(2,128)S(1)}, u32[]{:S(2)}, u32[]{:S(2)}) collective-permute-start(f32[2,4096]{1,0:T(2,128)S(1)} %add.10.refs_0_), channel_id=1, source_target_pairs={{0,8},{4,12},{8,0},{12,4},{1,9},{5,13},{9,1},{13,5},{2,10},{6,14},... | collective-permute-start | bytes 98312 | tf_op jit(solution)/shard_map/ppermute | solution.py:24
  34.2 2.5 %collective-permute-start.5 = (f32[2,4096]{1,0:T(2,128)S(1)}, f32[2,4096]{1,0:T(2,128)S(1)}, u32[]{:S(2)}, u32[]{:S(2)}) collective-permute-start(f32[2,4096]{1,0:T(2,128)S(1)} %add.10.refs_0_), channel_id=1, source_target_pairs={{0,4},{4,0},{8,12},{12,8},{1,5},{5,1},{9,13},{13,9},{2,6},{6,2},{1... | collective-permute-start | bytes 98312 | tf_op jit(solution)/shard_map/ppermute | solution.py:24
  50.2 24.0 %copy-start = (bf16[32,4096]{1,0:T(8,128)(2,1)S(1)}, bf16[32,4096]{1,0:T(8,128)(2,1)}, u32[]{:S(2)}) copy-start(bf16[32,4096]{1,0:T(8,128)(2,1)} %refs_12_.1) | copy-start | bytes 786436

commit v15 on v14

--- a/solution.py
+++ b/solution.py
@@ -28,8 +28,16 @@
     return [1 << b for b in reversed(range(size.bit_length() - 1))]
 
 
-def gather(value, axes, size):
-    return lax.all_to_all(jnp.broadcast_to(value[None], (size,) + value.shape), axes, 0, 0)
+def group_order(sizes):
+    dp_size, tensor_size = sizes
+    first = min(1, dp_size - 1) * tensor_size + (tensor_size - 1) // 2
+    return [first] + [i for i in range(dp_size * tensor_size) if i != first]
+
+
+def gather(value, sizes):
+    order = group_order(sizes)
+    value = jnp.broadcast_to(value[None], (len(order),) + value.shape)
+    return lax.all_to_all(value, ("dp", "tensor"), 0, 0, axis_index_groups=[order])
 
 
 def order_of(size):
@@ -233,7 +241,7 @@
     )(*pieces, *prior_pieces)
 
 
-def step_kernel(tensor_size, first, last, *refs):
+def step_kernel(sizes, first, last, *refs):
     blocks_ref, upper_ref, lower_ref, vectors_ref, vector_pieces_ref, scale_ref = refs[:6]
     norm_ref, fisher_direction_ref = refs[6:8]
     refs = refs[8:]
@@ -244,10 +252,10 @@
         queries_ref, curvature_out, norm_out, solved_out, along_out, held = refs
     else:
         fisher_direction_out, norm_out, fisher_residual_out, direction_out, residual_out, solution_out, held = refs
-    me = flat_index(tensor_size)
-    count, _, rows = blocks_ref.shape
-    for i in range(count):
-        held[:, i * rows : (i + 1) * rows] = blocks_ref[i]
+    me = flat_index(sizes[1])
+    rows = blocks_ref.shape[2]
+    for i, k in enumerate(group_order(sizes)):
+        held[:, k * rows : (k + 1) * rows] = blocks_ref[i]
     applied = held[...]
     scale = scale_ref[...][:, :1]
     twice = apply_fisher(
@@ -285,7 +293,7 @@
         solution_out[...] = solution
 
 
-def step_cg(blocks, fixed, norm, state, queries, tensor_size):
+def step_cg(blocks, fixed, norm, state, queries, sizes):
     first, last = len(state) == 1, queries is not None
     whole, rows = F32(fixed[2].shape), F32(state[0].shape)
     column = F32(norm.shape)
@@ -296,7 +304,7 @@
         scores = F32((whole.shape[0], queries.shape[0]))
         out_shape = (column, column, scores, scores)
     return pl.pallas_call(
-        functools.partial(step_kernel, tensor_size, first, last),
+        functools.partial(step_kernel, sizes, first, last),
         out_shape=out_shape,
         in_specs=[VMEM_SPEC] * len(operands),
         out_specs=(VMEM_SPEC,) * len(out_shape),
@@ -308,7 +316,7 @@
 
 def on_device(dp_size, tensor_size, inputs, in_proj, out_grads, out_proj, prior, queries):
     width = R_IN * R_OUT
-    both, devices = ("dp", "tensor"), dp_size * tensor_size
+    sizes = dp_size, tensor_size
     in_blocks = direct(features(inputs, in_proj, LANES, 20, "in_features"), "tensor", tensor_size, order_of(tensor_size))
     out_local = features(out_grads, out_proj, 2 * LANES, 44, "out_features")
     partial = partial_vectors(in_blocks, out_local).reshape(-1, width)
@@ -324,12 +332,12 @@
     fixed = (*prior_pieces, vectors, vector_pieces, scale)
     state = [applied_rows]
     for iteration in range(1, ITERS - 1):
-        blocks = gather(state[0], both, devices)
-        applied_rows, norm, *others = step_cg(blocks, fixed, norm, state, None, tensor_size)
+        blocks = gather(state[0], sizes)
+        applied_rows, norm, *others = step_cg(blocks, fixed, norm, state, None, sizes)
         state = [applied_rows, *others]
-    blocks = gather(state[0], both, devices)
-    curvature, norm, solved, along = step_cg(blocks, fixed, norm, state, queries, tensor_size)
-    curvature = jnp.sum(gather(curvature, both, devices), axis=0)
+    blocks = gather(state[0], sizes)
+    curvature, norm, solved, along = step_cg(blocks, fixed, norm, state, queries, sizes)
+    curvature = jnp.sum(gather(curvature, sizes), axis=0)
     return solved + (norm / curvature)[:, :1] * along
 
 

time: 87 us -> 82.1 us (0.944)
  blocking collectives: 42.5 us -> 37.6 us
    all_to_all x4, blocking collectives: 42.5 us -> 37.6 us  [gather(): lax.all_to_all(value, ('dp', 'tensor'), 0, 0, axis_index_groups=[order])]
  transfers between devices with their start and end apart: 8 -> 8, of which waited for: 3 -> 3; matrix products, arithmetic and copies ran while one was open for 0% -> 0% of each run, Pallas kernels for 16% -> 17%
where the time goes in v15:
time: 82.1 us; the launch traced here: 81.8 us
  blocking collectives  37.6 us (46%)
  Pallas kernels  26.4 us (32%)
  starting transfers between devices  12 us (15%)
  waiting for transfers between devices  4.65 us (6%)
    all_to_all x4, blocking collectives, gather(): lax.all_to_all(value, ('dp', 'tensor'), 0, 0, axis_index_groups=[order])  37.6 us
    pallas_call x2, Pallas kernels, features(): pl.pallas_call(functools.partial(stream_kernel, block), out_shape=pltpu.V...  16.9 us
    ppermute x8, starting transfers between devices, swap(): return lax.ppermute(value, axis, [(i, i ^ bit) for i in range(size)])  12 us
    pallas_call x3, Pallas kernels, step_cg(): pl.pallas_call(functools.partial(step_kernel, sizes, first, last), out_sh...  5.14 us
    ppermute x8, waiting for transfers between devices, swap(): return lax.ppermute(value, axis, [(i, i ^ bit) for i in range(size)])  4.65 us
    pallas_call x1, Pallas kernels, split_prior(): pl.pallas_call(split_kernel, out_shape=(pltpu.VMEM(prior.shape, jnp.bfloa...  2.32 us
  transfers between devices with their start and end apart: 8, of which 3 were waited for; matrix products, arithmetic and copies ran while one was open for 0% of the time, Pallas kernels for 17%

profile of v15, /device:TPU:0, one launch (start us, length us, event | category | flops | bytes accessed | tf_op | source)
XLA Modules:
  0.0 81.8 jit_solution(12662908870481421686)
XLA Ops:
  0.0 5.1 %in_features.1.refs_0_ = f32[64,512]{1,0:T(8,128)S(1)} custom-call(bf16[512,8192]{1,0:T(8,128)(2,1)} %rows_ref.2, bf16[64,8192]{1,0:T(8,128)(2,1)} %proj_ref.2), custom_call_target="tpu_custom_call" | custom-call | tf_op jit(solution)/shard_map/in_features/pallas_call | solution.py:100
  5.1 3.1 %collective-permute-start.2 = (f32[64,512]{1,0:T(8,128)S(1)}, f32[64,512]{1,0:T(8,128)S(1)}, u32[]{:S(2)}, u32[]{:S(2)}) collective-permute-start(f32[64,512]{1,0:T(8,128)S(1)} %in_features.1.refs_0_), channel_id=1, source_target_pairs={{0,1},{1,0},{2,3},{3,2},{4,5},{5,4},{6,7},{7,6},{8,9},{9,8},{10,11... | collective-permute-start | bytes 393224 | tf_op jit(solution)/shard_map/ppermute | solution.py:24
  8.1 2.5 %collective-permute-start.1 = (f32[64,512]{1,0:T(8,128)S(1)}, f32[64,512]{1,0:T(8,128)S(1)}, u32[]{:S(2)}, u32[]{:S(2)}) collective-permute-start(f32[64,512]{1,0:T(8,128)S(1)} %in_features.1.refs_0_), channel_id=1, source_target_pairs={{0,3},{1,2},{2,1},{3,0},{4,7},{5,6},{6,5},{7,4},{8,11},{9,10},{10,... | collective-permute-start | bytes 393224 | tf_op jit(solution)/shard_map/ppermute | solution.py:24
  10.6 0.1 collective-permute-start
  10.7 11.8 %out_features.1.refs_4_ = f32[64,2048]{1,0:T(8,128)S(1)} custom-call(bf16[2048,7168]{1,0:T(8,128)(2,1)} %rows_ref.3, bf16[64,7168]{1,0:T(8,128)(2,1)} %proj_ref.3), custom_call_target="tpu_custom_call" | custom-call | tf_op jit(solution)/shard_map/out_features/pallas_call | solution.py:100
  22.6 0.6 partial_vectors.1
  23.3 2.9 %collective-permute-start.3 = (f32[2,4096]{1,0:T(2,128)S(1)}, f32[2,4096]{1,0:T(2,128)S(1)}, u32[]{:S(2)}, u32[]{:S(2)}) collective-permute-start(f32[2,4096]{1,0:T(2,128)S(1)} %reshape.7), channel_id=1, source_target_pairs={{0,2},{1,3},{2,0},{3,1},{4,6},{5,7},{6,4},{7,5},{8,10},{9,11},{10,... | collective-permute-start | bytes 98312 | tf_op jit(solution)/shard_map/ppermute | solution.py:24
  26.2 2.3 %split_prior.1 = (bf16[256,4096]{1,0:T(8,128)(2,1)S(1)}, bf16[256,4096]{1,0:T(8,128)(2,1)S(1)}) custom-call(f32[256,4096]{1,0:T(8,128)} %prior_ref), custom_call_target="tpu_custom_call" | custom-call | tf_op jit(solution)/shard_map/split_prior/pallas_call | solution.py:134
  28.6 1.5 %collective-permute-start.4 = (f32[2,4096]{1,0:T(2,128)S(1)}, f32[2,4096]{1,0:T(2,128)S(1)}, u32[]{:S(2)}, u32[]{:S(2)}) collective-permute-start(f32[2,4096]{1,0:T(2,128)S(1)} %add.9), channel_id=1, source_target_pairs={{0,1},{1,0},{2,3},{3,2},{4,5},{5,4},{6,7},{7,6},{8,9},{9,8},{10,11... | collective-permute-start | bytes 98312 | tf_op jit(solution)/shard_map/ppermute | solution.py:24
  30.1 2.5 %collective-permute-done.4 = f32[2,4096]{1,0:T(2,128)S(1)} collective-permute-done((f32[2,4096]{1,0:T(2,128)S(1)}, f32[2,4096]{1,0:T(2,128)S(1)}, u32[]{:S(2)}, u32[]{:S(2)}) %collective-permute-start.4) | collective-permute-done | bytes 32800 | tf_op jit(solution)/shard_map/ppermute | solution.py:24
  32.6 1.6 %collective-permute-start.6 = (f32[2,4096]{1,0:T(2,128)S(1)}, f32[2,4096]{1,0:T(2,128)S(1)}, u32[]{:S(2)}, u32[]{:S(2)}) collective-permute-start(f32[2,4096]{1,0:T(2,128)S(1)} %add.10.refs_0_), channel_id=1, source_target_pairs={{0,8},{4,12},{8,0},{12,4},{1,9},{5,13},{9,1},{13,5},{2,10},{6,14},... | collective-permute-start | bytes 98312 | tf_op jit(solution)/shard_map/ppermute | solution.py:24
  34.2 0.3 collective-permute-start.5
  34.5 1.8 %collective-permute-done.7.refs_3_ = f32[2,4096]{1,0:T(2,128)S(1)} collective-permute-done((f32[2,4096]{1,0:T(2,128)S(1)}, f32[2,4096]{1,0:T(2,128)S(1)}, u32[]{:S(2)}, u32[]{:S(2)}) %collective-permute-start.7) | collective-permute-done | bytes 32800 | tf_op jit(solution)/shard_map/ppermute | solution.py:24
  36.3 0.4 collective-permute-done.6.refs_2_
  36.7 1.5 %cg_start.1 = (f32[8,4096]{1,0:T(8,128)S(1)}, bf16[16,4096]{1,0:T(8,128)(2,1)S(1)}, f32[8,128]{1,0:T(8,128)S(1)}, f32[8,256]{1,0:T(8,128)S(1)}, f32[8,128]{1,0:T(8,128)S(1)}) custom-call(f32[2,4096]{1,0:T(2,128)S(1)} %add.10.refs_0_, f32[2,4096]{1,0:T(2,128)S(1)} %collective-permute-done.5.refs_1_, f32[2,4096]{1,0:T(2,128)S(1)} %collective-permute-done.6.refs_2_, ...), custom_call_target="tpu_custom_call" | custom-call | tf_op jit(solution)/shard_map/cg_start/pallas_call | solution.py:233
  38.2 11.0 %all_to_all.20.refs_0_ = f32[16,8,256]{2,1,0:T(8,128)S(1)} all-to-all(f32[16,8,256]{2,1,0:T(8,128)S(1)} %broadcast_in_dim.8), channel_id=1, replica_groups={{5,0,1,2,3,4,6,7,8,9,10,11,12,13,14,15},{21,16,17,18,19,20,22,23,24,25,..., dimensions={0} | all-to-all | bytes 262144 | tf_op jit(solution)/shard_map/all_to_all | solution.py:40
  49.2 1.6 %cg_step.3 = (f32[8,256]{1,0:T(8,128)S(1)}, f32[8,128]{1,0:T(8,128)S(1)}, f32[8,256]{1,0:T(8,128)S(1)}, f32[8,4096]{1,0:T(8,128)S(1)}, f32[8,4096]{1,0:T(8,128)S(1)}, /*index=5*/f32[8,4096]{1,0:T(8,128)S(1)}) custom-call(f32[16,8,256]{2,1,0:T(8,128)S(1)} %all_to_all.20.refs_0_, bf16[256,4096]{1,0:T(8,128)(2,1)S(1)} %get-tuple-element.38.refs_4_.refs_1_, ...), custom_call_target="tpu_custom_call" | custom-call | tf_op jit(solution)/shard_map/cg_step/pallas_call | solution.py:306
  50.8 9.2 %all_to_all.21.refs_0_ = f32[16,8,256]{2,1,0:T(8,128)S(1)} all-to-all(f32[16,8,256]{2,1,0:T(8,128)S(1)} %broadcast_in_dim.9), channel_id=1, replica_groups={{5,0,1,2,3,4,6,7,8,9,10,11,12,13,14,15},{21,16,17,18,19,20,22,23,24,25,..., dimensions={0} | all-to-all | bytes 262144 | tf_op jit(solution)/shard_map/all_to_all | solution.py:40
  60.0 1.6 %cg_step.4 = (f32[8,256]{1,0:T(8,128)S(1)}, f32[8,128]{1,0:T(8,128)S(1)}, f32[8,256]{1,0:T(8,128)S(1)}, f32[8,4096]{1,0:T(8,128)S(1)}, f32[8,4096]{1,0:T(8,128)S(1)}, /*index=5*/f32[8,4096]{1,0:T(8,128)S(1)}) custom-call(f32[16,8,256]{2,1,0:T(8,128)S(1)} %all_to_all.21.refs_0_, bf16[256,4096]{1,0:T(8,128)(2,1)S(1)} %get-tuple-element.38.refs_4_.refs_1_, ...), custom_call_target="tpu_custom_call" | custom-call | tf_op jit(solution)/shard_map/cg_step/pallas_call | solution.py:306
  61.6 9.2 %all_to_all.22.refs_0_ = f32[16,8,256]{2,1,0:T(8,128)S(1)} all-to-all(f32[16,8,256]{2,1,0:T(8,128)S(1)} %broadcast_in_dim.10), channel_id=1, replica_groups={{5,0,1,2,3,4,6,7,8,9,10,11,12,13,14,15},{21,16,17,18,19,20,22,23,24,25,..., dimensions={0} | all-to-all | bytes 262144 | tf_op jit(solution)/shard_map/all_to_all | solution.py:40
  70.9 1.9 %cg_step.5 = (f32[8,128]{1,0:T(8,128)S(1)}, f32[8,128]{1,0:T(8,128)S(1)}, f32[8,32]{1,0:T(8,128)S(1)}, f32[8,32]{1,0:T(8,128)S(1)}) custom-call(f32[16,8,256]{2,1,0:T(8,128)S(1)} %all_to_all.22.refs_0_, bf16[256,4096]{1,0:T(8,128)(2,1)S(1)} %get-tuple-element.38.refs_4_.refs_1_, bf16[256,4096]{1,0:T(8,128)(2,1)S(1)} %get-tuple-element.39.refs_5_.refs_2_, ...), custom_call_target="tpu_custom_call" | custom-call | tf_op jit(solution)/shard_map/cg_step/pallas_call | solution.py:306
  72.8 8.2 %all_to_all.23 = f32[16,8,128]{2,1,0:T(8,128)S(1)} all-to-all(f32[16,8,128]{2,1,0:T(8,128)S(1)} %broadcast_in_dim.11), channel_id=1, replica_groups={{5,0,1,2,3,4,6,7,8,9,10,11,12,13,14,15},{21,16,17,18,19,20,22,23,24,25,..., dimensions={0} | all-to-all | bytes 131072 | tf_op jit(solution)/shard_map/all_to_all | solution.py:40
  81.1 0.1 slice_reduce_fusion
  81.2 0.7 multiply_add_fusion
  (17 shorter events, 0.3 us)
Async XLA Ops:
  5.1 17.5 %collective-permute-start.2 = (f32[64,512]{1,0:T(8,128)S(1)}, f32[64,512]{1,0:T(8,128)S(1)}, u32[]{:S(2)}, u32[]{:S(2)}) collective-permute-start(f32[64,512]{1,0:T(8,128)S(1)} %in_features.1.refs_0_), channel_id=1, source_target_pairs={{0,1},{1,0},{2,3},{3,2},{4,5},{5,4},{6,7},{7,6},{8,9},{9,8},{10,11... | collective-permute-start | bytes 393224 | tf_op jit(solution)/shard_map/ppermute | solution.py:24
  8.1 14.4 %collective-permute-start.1 = (f32[64,512]{1,0:T(8,128)S(1)}, f32[64,512]{1,0:T(8,128)S(1)}, u32[]{:S(2)}, u32[]{:S(2)}) collective-permute-start(f32[64,512]{1,0:T(8,128)S(1)} %in_features.1.refs_0_), channel_id=1, source_target_pairs={{0,3},{1,2},{2,1},{3,0},{4,7},{5,6},{6,5},{7,4},{8,11},{9,10},{10,... | collective-permute-start | bytes 393224 | tf_op jit(solution)/shard_map/ppermute | solution.py:24
  10.6 12.0 %collective-permute-start = (f32[64,512]{1,0:T(8,128)S(1)}, f32[64,512]{1,0:T(8,128)S(1)}, u32[]{:S(2)}, u32[]{:S(2)}) collective-permute-start(f32[64,512]{1,0:T(8,128)S(1)} %in_features.1.refs_0_), channel_id=1, source_target_pairs={{0,2},{1,3},{2,0},{3,1},{4,6},{5,7},{6,4},{7,5},{8,10},{9,11},{10,... | collective-permute-start | bytes 393224 | tf_op jit(solution)/shard_map/ppermute | solution.py:24
  23.3 5.2 %collective-permute-start.3 = (f32[2,4096]{1,0:T(2,128)S(1)}, f32[2,4096]{1,0:T(2,128)S(1)}, u32[]{:S(2)}, u32[]{:S(2)}) collective-permute-start(f32[2,4096]{1,0:T(2,128)S(1)} %reshape.7), channel_id=1, source_target_pairs={{0,2},{1,3},{2,0},{3,1},{4,6},{5,7},{6,4},{7,5},{8,10},{9,11},{10,... | collective-permute-start | bytes 98312 | tf_op jit(solution)/shard_map/ppermute | solution.py:24
  28.6 4.0 %collective-permute-start.4 = (f32[2,4096]{1,0:T(2,128)S(1)}, f32[2,4096]{1,0:T(2,128)S(1)}, u32[]{:S(2)}, u32[]{:S(2)}) collective-permute-start(f32[2,4096]{1,0:T(2,128)S(1)} %add.9), channel_id=1, source_target_pairs={{0,1},{1,0},{2,3},{3,2},{4,5},{5,4},{6,7},{7,6},{8,9},{9,8},{10,11... | collective-permute-start | bytes 98312 | tf_op jit(solution)/shard_map/ppermute | solution.py:24
  32.6 3.7 %collective-permute-start.7 = (f32[2,4096]{1,0:T(2,128)S(1)}, f32[2,4096]{1,0:T(2,128)S(1)}, u32[]{:S(2)}, u32[]{:S(2)}) collective-permute-start(f32[2,4096]{1,0:T(2,128)S(1)} %add.10.refs_0_), channel_id=1, source_target_pairs={{0,12},{4,8},{8,4},{12,0},{1,13},{5,9},{9,5},{13,1},{2,14},{6,10},... | collective-permute-start | bytes 98312 | tf_op jit(solution)/shard_map/ppermute | solution.py:24
  32.6 4.0 %collective-permute-start.6 = (f32[2,4096]{1,0:T(2,128)S(1)}, f32[2,4096]{1,0:T(2,128)S(1)}, u32[]{:S(2)}, u32[]{:S(2)}) collective-permute-start(f32[2,4096]{1,0:T(2,128)S(1)} %add.10.refs_0_), channel_id=1, source_target_pairs={{0,8},{4,12},{8,0},{12,4},{1,9},{5,13},{9,1},{13,5},{2,10},{6,14},... | collective-permute-start | bytes 98312 | tf_op jit(solution)/shard_map/ppermute | solution.py:24
  34.2 2.5 %collective-permute-start.5 = (f32[2,4096]{1,0:T(2,128)S(1)}, f32[2,4096]{1,0:T(2,128)S(1)}, u32[]{:S(2)}, u32[]{:S(2)}) collective-permute-start(f32[2,4096]{1,0:T(2,128)S(1)} %add.10.refs_0_), channel_id=1, source_target_pairs={{0,4},{4,0},{8,12},{12,8},{1,5},{5,1},{9,13},{13,9},{2,6},{6,2},{1... | collective-permute-start | bytes 98312 | tf_op jit(solution)/shard_map/ppermute | solution.py:24
  49.2 21.7 %copy-start = (bf16[32,4096]{1,0:T(8,128)(2,1)S(1)}, bf16[32,4096]{1,0:T(8,128)(2,1)}, u32[]{:S(2)}) copy-start(bf16[32,4096]{1,0:T(8,128)(2,1)} %refs_12_.1) | copy-start | bytes 786436

commit v16 on v15

--- a/solution.py
+++ b/solution.py
@@ -30,14 +30,17 @@
 
 def group_order(sizes):
     dp_size, tensor_size = sizes
-    first = min(1, dp_size - 1) * tensor_size + (tensor_size - 1) // 2
-    return [first] + [i for i in range(dp_size * tensor_size) if i != first]
-
-
-def gather(value, sizes):
-    order = group_order(sizes)
+    order = [min(1, dp_size - 1) * tensor_size + (tensor_size - 1) // 2]
+    for t in range((tensor_size + 1) // 2):
+        for dp in range(dp_size):
+            across = (dp + dp_size // 2) % dp_size
+            order += [dp * tensor_size + tensor_size - 1 - t, across * tensor_size + t]
+    return list(dict.fromkeys(order))
+
+
+def gather(value, axes, order):
     value = jnp.broadcast_to(value[None], (len(order),) + value.shape)
-    return lax.all_to_all(value, ("dp", "tensor"), 0, 0, axis_index_groups=[order])
+    return lax.all_to_all(value, axes, 0, 0, axis_index_groups=[order])
 
 
 def order_of(size):
@@ -206,13 +209,9 @@
     return lax.axis_index("dp") * tensor_size + lax.axis_index("tensor")
 
 
-def start_kernel(size, tensor_size, *refs):
-    pieces, refs = refs[:size], refs[size:]
-    upper_ref, lower_ref, vectors_ref, vector_pieces_ref, scale_ref, applied_ref, norm_ref, held = refs
-    dp = lax.axis_index("dp")
-    for k, piece in enumerate(pieces):
-        held[dp ^ k] = piece[...]
-    vectors = jnp.concatenate([held[k] for k in range(size)], axis=0)
+def start_kernel(order, tensor_size, *refs):
+    pieces_ref, upper_ref, lower_ref, vectors_ref, vector_pieces_ref, scale_ref, applied_ref, norm_ref = refs
+    vectors = jnp.concatenate([pieces_ref[order.index(k)] for k in range(len(order))], axis=0)
     vectors_ref[...] = vectors
     split = pieces_of(vectors, 3)
     vector_pieces = split[: 2 * vectors.shape[0]]
@@ -225,20 +224,19 @@
     applied_ref[...] = apply_fisher(split, vectors_ref, vector_pieces, upper_ref, lower_ref, me)
 
 
-def start_cg(pieces, prior_pieces, tensor_size):
-    size, seqs = len(pieces), len(pieces) * pieces[0].shape[0]
+def start_cg(pieces, prior_pieces, order, tensor_size):
+    seqs = len(order) * pieces.shape[1]
     rows, width = prior_pieces[0].shape
     vector_pieces = jax.ShapeDtypeStruct((2 * seqs, width), jnp.bfloat16)
     column = F32((seqs, LANES))
     return pl.pallas_call(
-        functools.partial(start_kernel, size, tensor_size),
+        functools.partial(start_kernel, order, tensor_size),
         out_shape=(F32((seqs, width)), vector_pieces, column, F32((seqs, rows)), column),
-        in_specs=[VMEM_SPEC] * (size + 2),
+        in_specs=[VMEM_SPEC] * 3,
         out_specs=(VMEM_SPEC,) * 5,
-        scratch_shapes=[pltpu.VMEM((size,) + pieces[0].shape, jnp.float32)],
         compiler_params=PARAMS,
         name="cg_start",
-    )(*pieces, *prior_pieces)
+    )(pieces, *prior_pieces)
 
 
 def step_kernel(sizes, first, last, *refs):
@@ -316,7 +314,8 @@
 
 def on_device(dp_size, tensor_size, inputs, in_proj, out_grads, out_proj, prior, queries):
     width = R_IN * R_OUT
-    sizes = dp_size, tensor_size
+    both, sizes = ("dp", "tensor"), (dp_size, tensor_size)
+    order, dp_order = group_order(sizes), group_order((dp_size, 1))
     in_blocks = direct(features(inputs, in_proj, LANES, 20, "in_features"), "tensor", tensor_size, order_of(tensor_size))
     out_local = features(out_grads, out_proj, 2 * LANES, 44, "out_features")
     partial = partial_vectors(in_blocks, out_local).reshape(-1, width)
@@ -326,18 +325,18 @@
     partial, prior_pieces = lax.optimization_barrier((partial, split_prior(prior)))
     for bit in rest:
         partial = partial + swap(partial, "tensor", tensor_size, bit)
-    pieces = direct(partial, "dp", dp_size, range(dp_size))
+    pieces = gather(partial, "dp", dp_order)
     prior_pieces = [in_vmem(piece) for piece in prior_pieces]
-    vectors, vector_pieces, scale, applied_rows, norm = start_cg(pieces, prior_pieces, tensor_size)
+    vectors, vector_pieces, scale, applied_rows, norm = start_cg(pieces, prior_pieces, dp_order, tensor_size)
     fixed = (*prior_pieces, vectors, vector_pieces, scale)
     state = [applied_rows]
     for iteration in range(1, ITERS - 1):
-        blocks = gather(state[0], sizes)
+        blocks = gather(state[0], both, order)
         applied_rows, norm, *others = step_cg(blocks, fixed, norm, state, None, sizes)
         state = [applied_rows, *others]
-    blocks = gather(state[0], sizes)
+    blocks = gather(state[0], both, order)
     curvature, norm, solved, along = step_cg(blocks, fixed, norm, state, queries, sizes)
-    curvature = jnp.sum(gather(curvature, sizes), axis=0)
+    curvature = jnp.sum(gather(curvature, both, order), axis=0)
     return solved + (norm / curvature)[:, :1] * along
 
 

time: 82.1 us -> 84.4 us (1.028)
  blocking collectives: 37.6 us -> 44 us
  waiting for transfers between devices: 4.65 us -> 2.47 us
  starting transfers between devices: 12 us -> 10.1 us
    all_to_all x4 -> x5, blocking collectives: 37.6 us -> 44 us  [gather(): return lax.all_to_all(value, axes, 0, 0, axis_index_groups=[order])]
    ppermute x8 -> x5, waiting for transfers between devices: 4.65 us -> 2.47 us  [swap(): return lax.ppermute(value, axis, [(i, i ^ bit) for i in range(size)])]
    ppermute x8 -> x5, starting transfers between devices: 12 us -> 10.1 us  [swap(): return lax.ppermute(value, axis, [(i, i ^ bit) for i in range(size)])]
  transfers between devices with their start and end apart: 8 -> 5, of which waited for: 3 -> 1; matrix products, arithmetic and copies ran while one was open for 0% -> 0% of each run, Pallas kernels for 17% -> 17%
where the time goes in v16:
time: 84.4 us; the launch traced here: 84.1 us
  blocking collectives  44 us (52%)
  Pallas kernels  26.4 us (31%)
  starting transfers between devices  10.1 us (12%)
  waiting for transfers between devices  2.47 us (3%)
    all_to_all x5, blocking collectives, gather(): return lax.all_to_all(value, axes, 0, 0, axis_index_groups=[order])  44 us
    pallas_call x2, Pallas kernels, features(): pl.pallas_call(functools.partial(stream_kernel, block), out_shape=pltpu.V...  16.9 us
    ppermute x5, starting transfers between devices, swap(): return lax.ppermute(value, axis, [(i, i ^ bit) for i in range(size)])  10.1 us
    pallas_call x3, Pallas kernels, step_cg(): pl.pallas_call(functools.partial(step_kernel, sizes, first, last), out_sh...  5.12 us
    ppermute x5, waiting for transfers between devices, swap(): return lax.ppermute(value, axis, [(i, i ^ bit) for i in range(size)])  2.47 us
    pallas_call x1, Pallas kernels, split_prior(): pl.pallas_call(split_kernel, out_shape=(pltpu.VMEM(prior.shape, jnp.bfloa...  2.32 us
  transfers between devices with their start and end apart: 5, of which 1 were waited for; matrix products, arithmetic and copies ran while one was open for 0% of the time, Pallas kernels for 17%

profile of v16, /device:TPU:0, one launch (start us, length us, event | category | flops | bytes accessed | tf_op | source)
XLA Modules:
  0.0 84.1 jit_solution(5437291558542506780)
XLA Ops:
  0.0 5.1 %in_features.1.refs_0_ = f32[64,512]{1,0:T(8,128)S(1)} custom-call(bf16[512,8192]{1,0:T(8,128)(2,1)} %rows_ref.2, bf16[64,8192]{1,0:T(8,128)(2,1)} %proj_ref.2), custom_call_target="tpu_custom_call" | custom-call | tf_op jit(solution)/shard_map/in_features/pallas_call | solution.py:103
  5.1 3.1 %collective-permute-start.2 = (f32[64,512]{1,0:T(8,128)S(1)}, f32[64,512]{1,0:T(8,128)S(1)}, u32[]{:S(2)}, u32[]{:S(2)}) collective-permute-start(f32[64,512]{1,0:T(8,128)S(1)} %in_features.1.refs_0_), channel_id=1, source_target_pairs={{0,1},{1,0},{2,3},{3,2},{4,5},{5,4},{6,7},{7,6},{8,9},{9,8},{10,11... | collective-permute-start | bytes 393224 | tf_op jit(solution)/shard_map/ppermute | solution.py:24
  8.1 2.5 %collective-permute-start.1 = (f32[64,512]{1,0:T(8,128)S(1)}, f32[64,512]{1,0:T(8,128)S(1)}, u32[]{:S(2)}, u32[]{:S(2)}) collective-permute-start(f32[64,512]{1,0:T(8,128)S(1)} %in_features.1.refs_0_), channel_id=1, source_target_pairs={{0,3},{1,2},{2,1},{3,0},{4,7},{5,6},{6,5},{7,4},{8,11},{9,10},{10,... | collective-permute-start | bytes 393224 | tf_op jit(solution)/shard_map/ppermute | solution.py:24
  10.6 0.1 collective-permute-start
  10.7 11.8 %out_features.1.refs_4_ = f32[64,2048]{1,0:T(8,128)S(1)} custom-call(bf16[2048,7168]{1,0:T(8,128)(2,1)} %rows_ref.3, bf16[64,7168]{1,0:T(8,128)(2,1)} %proj_ref.3), custom_call_target="tpu_custom_call" | custom-call | tf_op jit(solution)/shard_map/out_features/pallas_call | solution.py:103
  22.6 0.0 collective-permute-done.2.refs_3_
  22.6 0.0 collective-permute-done.refs_1_
  22.6 0.6 partial_vectors.1
  23.2 0.1 reshape.8
  23.3 2.9 %collective-permute-start.3 = (f32[2,4096]{1,0:T(2,128)S(1)}, f32[2,4096]{1,0:T(2,128)S(1)}, u32[]{:S(2)}, u32[]{:S(2)}) collective-permute-start(f32[2,4096]{1,0:T(2,128)S(1)} %reshape.8), channel_id=1, source_target_pairs={{0,2},{1,3},{2,0},{3,1},{4,6},{5,7},{6,4},{7,5},{8,10},{9,11},{10,... | collective-permute-start | bytes 98312 | tf_op jit(solution)/shard_map/ppermute | solution.py:24
  26.2 2.3 %split_prior.1 = (bf16[256,4096]{1,0:T(8,128)(2,1)S(1)}, bf16[256,4096]{1,0:T(8,128)(2,1)S(1)}) custom-call(f32[256,4096]{1,0:T(8,128)} %prior_ref), custom_call_target="tpu_custom_call" | custom-call | tf_op jit(solution)/shard_map/split_prior/pallas_call | solution.py:137
  28.6 1.5 %collective-permute-start.4 = (f32[2,4096]{1,0:T(2,128)S(1)}, f32[2,4096]{1,0:T(2,128)S(1)}, u32[]{:S(2)}, u32[]{:S(2)}) collective-permute-start(f32[2,4096]{1,0:T(2,128)S(1)} %add.9), channel_id=1, source_target_pairs={{0,1},{1,0},{2,3},{3,2},{4,5},{5,4},{6,7},{7,6},{8,9},{9,8},{10,11... | collective-permute-start | bytes 98312 | tf_op jit(solution)/shard_map/ppermute | solution.py:24
  30.1 2.5 %collective-permute-done.4 = f32[2,4096]{1,0:T(2,128)S(1)} collective-permute-done((f32[2,4096]{1,0:T(2,128)S(1)}, f32[2,4096]{1,0:T(2,128)S(1)}, u32[]{:S(2)}, u32[]{:S(2)}) %collective-permute-start.4) | collective-permute-done | bytes 32800 | tf_op jit(solution)/shard_map/ppermute | solution.py:24
  32.6 6.6 %all_to_all.25.refs_0_ = f32[4,2,4096]{2,1,0:T(2,128)S(1)} all-to-all(f32[4,2,4096]{2,1,0:T(2,128)S(1)} %broadcast_in_dim.10), channel_id=1, replica_groups={{4,0,8,12},{5,1,9,13},{6,2,10,14},{7,3,11,15},{20,16,24,28},{21,17,25,2..., dimensions={0} | all-to-all | bytes 262144 | tf_op jit(solution)/shard_map/all_to_all | solution.py:43
  39.2 1.5 %cg_start.1 = (f32[8,4096]{1,0:T(8,128)S(1)}, bf16[16,4096]{1,0:T(8,128)(2,1)S(1)}, f32[8,128]{1,0:T(8,128)S(1)}, f32[8,256]{1,0:T(8,128)S(1)}, f32[8,128]{1,0:T(8,128)S(1)}) custom-call(f32[4,2,4096]{2,1,0:T(2,128)S(1)} %all_to_all.25.refs_0_, bf16[256,4096]{1,0:T(8,128)(2,1)S(1)} %get-tuple-element.38.refs_1_, bf16[256,4096]{1,0:T(8,128)(2,1)S(1)} %get-tuple-element.39.refs_2_), custom_call_target="tpu_custom_call" | custom-call | tf_op jit(solution)/shard_map/cg_start/pallas_call | solution.py:232
  40.7 9.9 %all_to_all.26.refs_0_ = f32[16,8,256]{2,1,0:T(8,128)S(1)} all-to-all(f32[16,8,256]{2,1,0:T(8,128)S(1)} %broadcast_in_dim.11), channel_id=1, replica_groups={{5,3,8,7,12,11,0,15,4,2,9,6,13,10,1,14},{21,19,24,23,28,27,16,31,20,18,..., dimensions={0} | all-to-all | bytes 262144 | tf_op jit(solution)/shard_map/all_to_all | solution.py:43
  50.6 1.6 %cg_step.3 = (f32[8,256]{1,0:T(8,128)S(1)}, f32[8,128]{1,0:T(8,128)S(1)}, f32[8,256]{1,0:T(8,128)S(1)}, f32[8,4096]{1,0:T(8,128)S(1)}, f32[8,4096]{1,0:T(8,128)S(1)}, /*index=5*/f32[8,4096]{1,0:T(8,128)S(1)}) custom-call(f32[16,8,256]{2,1,0:T(8,128)S(1)} %all_to_all.26.refs_0_, bf16[256,4096]{1,0:T(8,128)(2,1)S(1)} %get-tuple-element.38.refs_1_, ...), custom_call_target="tpu_custom_call" | custom-call | tf_op jit(solution)/shard_map/cg_step/pallas_call | solution.py:304
  52.2 9.4 %all_to_all.27.refs_0_ = f32[16,8,256]{2,1,0:T(8,128)S(1)} all-to-all(f32[16,8,256]{2,1,0:T(8,128)S(1)} %broadcast_in_dim.12), channel_id=1, replica_groups={{5,3,8,7,12,11,0,15,4,2,9,6,13,10,1,14},{21,19,24,23,28,27,16,31,20,18,..., dimensions={0} | all-to-all | bytes 262144 | tf_op jit(solution)/shard_map/all_to_all | solution.py:43
  61.6 1.6 %cg_step.4 = (f32[8,256]{1,0:T(8,128)S(1)}, f32[8,128]{1,0:T(8,128)S(1)}, f32[8,256]{1,0:T(8,128)S(1)}, f32[8,4096]{1,0:T(8,128)S(1)}, f32[8,4096]{1,0:T(8,128)S(1)}, /*index=5*/f32[8,4096]{1,0:T(8,128)S(1)}) custom-call(f32[16,8,256]{2,1,0:T(8,128)S(1)} %all_to_all.27.refs_0_, bf16[256,4096]{1,0:T(8,128)(2,1)S(1)} %get-tuple-element.38.refs_1_, ...), custom_call_target="tpu_custom_call" | custom-call | tf_op jit(solution)/shard_map/cg_step/pallas_call | solution.py:304
  63.2 9.4 %all_to_all.28.refs_0_ = f32[16,8,256]{2,1,0:T(8,128)S(1)} all-to-all(f32[16,8,256]{2,1,0:T(8,128)S(1)} %broadcast_in_dim.13), channel_id=1, replica_groups={{5,3,8,7,12,11,0,15,4,2,9,6,13,10,1,14},{21,19,24,23,28,27,16,31,20,18,..., dimensions={0} | all-to-all | bytes 262144 | tf_op jit(solution)/shard_map/all_to_all | solution.py:43
  72.6 1.9 %cg_step.5 = (f32[8,128]{1,0:T(8,128)S(1)}, f32[8,128]{1,0:T(8,128)S(1)}, f32[8,32]{1,0:T(8,128)S(1)}, f32[8,32]{1,0:T(8,128)S(1)}) custom-call(f32[16,8,256]{2,1,0:T(8,128)S(1)} %all_to_all.28.refs_0_, bf16[256,4096]{1,0:T(8,128)(2,1)S(1)} %get-tuple-element.38.refs_1_, bf16[256,4096]{1,0:T(8,128)(2,1)S(1)} %get-tuple-element.39.refs_2_, ...), custom_call_target="tpu_custom_call" | custom-call | tf_op jit(solution)/shard_map/cg_step/pallas_call | solution.py:304
  74.5 8.7 %all_to_all.29 = f32[16,8,128]{2,1,0:T(8,128)S(1)} all-to-all(f32[16,8,128]{2,1,0:T(8,128)S(1)} %broadcast_in_dim.14), channel_id=1, replica_groups={{5,3,8,7,12,11,0,15,4,2,9,6,13,10,1,14},{21,19,24,23,28,27,16,31,20,18,..., dimensions={0} | all-to-all | bytes 131072 | tf_op jit(solution)/shard_map/all_to_all | solution.py:43
  83.3 0.1 slice_reduce_fusion
  83.4 0.7 multiply_add_fusion
  (13 shorter events, 0.2 us)
Async XLA Ops:
  5.1 17.5 %collective-permute-start.2 = (f32[64,512]{1,0:T(8,128)S(1)}, f32[64,512]{1,0:T(8,128)S(1)}, u32[]{:S(2)}, u32[]{:S(2)}) collective-permute-start(f32[64,512]{1,0:T(8,128)S(1)} %in_features.1.refs_0_), channel_id=1, source_target_pairs={{0,1},{1,0},{2,3},{3,2},{4,5},{5,4},{6,7},{7,6},{8,9},{9,8},{10,11... | collective-permute-start | bytes 393224 | tf_op jit(solution)/shard_map/ppermute | solution.py:24
  8.1 14.4 %collective-permute-start.1 = (f32[64,512]{1,0:T(8,128)S(1)}, f32[64,512]{1,0:T(8,128)S(1)}, u32[]{:S(2)}, u32[]{:S(2)}) collective-permute-start(f32[64,512]{1,0:T(8,128)S(1)} %in_features.1.refs_0_), channel_id=1, source_target_pairs={{0,3},{1,2},{2,1},{3,0},{4,7},{5,6},{6,5},{7,4},{8,11},{9,10},{10,... | collective-permute-start | bytes 393224 | tf_op jit(solution)/shard_map/ppermute | solution.py:24
  10.6 12.0 %collective-permute-start = (f32[64,512]{1,0:T(8,128)S(1)}, f32[64,512]{1,0:T(8,128)S(1)}, u32[]{:S(2)}, u32[]{:S(2)}) collective-permute-start(f32[64,512]{1,0:T(8,128)S(1)} %in_features.1.refs_0_), channel_id=1, source_target_pairs={{0,2},{1,3},{2,0},{3,1},{4,6},{5,7},{6,4},{7,5},{8,10},{9,11},{10,... | collective-permute-start | bytes 393224 | tf_op jit(solution)/shard_map/ppermute | solution.py:24
  23.3 5.2 %collective-permute-start.3 = (f32[2,4096]{1,0:T(2,128)S(1)}, f32[2,4096]{1,0:T(2,128)S(1)}, u32[]{:S(2)}, u32[]{:S(2)}) collective-permute-start(f32[2,4096]{1,0:T(2,128)S(1)} %reshape.8), channel_id=1, source_target_pairs={{0,2},{1,3},{2,0},{3,1},{4,6},{5,7},{6,4},{7,5},{8,10},{9,11},{10,... | collective-permute-start | bytes 98312 | tf_op jit(solution)/shard_map/ppermute | solution.py:24
  28.6 4.0 %collective-permute-start.4 = (f32[2,4096]{1,0:T(2,128)S(1)}, f32[2,4096]{1,0:T(2,128)S(1)}, u32[]{:S(2)}, u32[]{:S(2)}) collective-permute-start(f32[2,4096]{1,0:T(2,128)S(1)} %add.9), channel_id=1, source_target_pairs={{0,1},{1,0},{2,3},{3,2},{4,5},{5,4},{6,7},{7,6},{8,9},{9,8},{10,11... | collective-permute-start | bytes 98312 | tf_op jit(solution)/shard_map/ppermute | solution.py:24
  50.6 22.0 %copy-start = (bf16[32,4096]{1,0:T(8,128)(2,1)S(1)}, bf16[32,4096]{1,0:T(8,128)(2,1)}, u32[]{:S(2)}) copy-start(bf16[32,4096]{1,0:T(8,128)(2,1)} %refs_12_.1) | copy-start | bytes 786436

commit v17 on v15

--- a/solution.py
+++ b/solution.py
@@ -12,6 +12,7 @@
 SEQ = 1024
 ITERS = 4
 LANES = 128
+HEAD = 2 * LANES
 NT = (((1,), (1,)), ((), ()))
 HIGHEST = lax.Precision.HIGHEST
 ANY_SPEC = pl.BlockSpec(memory_space=pl.ANY)
@@ -64,53 +65,114 @@
     return jnp.sum(values, axis=1, keepdims=True)
 
 
-def stream_kernel(block, rows_ref, proj_ref, feats_ref, held, proj, turned, sems):
+def fetch(rows_ref, held, sems, step, block):
+    span = pl.ds(pl.multiple_of(step * block, block), block)
+    return pltpu.make_async_copy(rows_ref.at[span], held.at[span], sems.at[step])
+
+
+def fetch_halves(proj_ref, proj, sems):
     count, half = proj_ref.shape[0], proj.shape[1]
-    steps = held.shape[0] // block
-    firsts = [
+    return [
         pltpu.make_async_copy(
-            proj_ref.at[:, pl.ds(h * half, half)], proj.at[pl.ds(h * count, count)], sems.at[steps + h]
+            proj_ref.at[:, pl.ds(h * half, half)], proj.at[pl.ds(h * count, count)], sems.at[h]
         )
         for h in range(2)
     ]
 
-    def fetch(step):
-        span = pl.ds(pl.multiple_of(step * block, block), block)
-        return pltpu.make_async_copy(rows_ref.at[span], held.at[span], sems.at[step])
-
+
+def project(rows, turned, count):
+    half = turned.shape[0]
+    left = jnp.dot(rows[:, :half], turned[...], preferred_element_type=jnp.float32)
+    right = jnp.dot(rows[:, half:], turned[...], preferred_element_type=jnp.float32)
+    return left.T[:count] + right.T[count:]
+
+
+def in_kernel(rows_ref, proj_ref, grads_ref, next_proj_ref, feats_ref, head_ref, next_turned_ref, *scratch):
+    held, proj, turned, next_proj, row_sems, proj_sems, next_sems, head_sem = scratch
+    steps = held.shape[0] // LANES
+    firsts = fetch_halves(proj_ref, proj, proj_sems)
+    nexts = fetch_halves(next_proj_ref, next_proj, next_sems)
+    head = pltpu.make_async_copy(grads_ref.at[pl.ds(0, HEAD)], head_ref, head_sem)
     for copy in firsts:
         copy.start()
-    for step in range(steps):
-        fetch(step).start()
+    fetch(rows_ref, held, row_sems, 0, LANES).start()
+    for copy in nexts:
+        copy.start()
+    for step in range(1, steps):
+        fetch(rows_ref, held, row_sems, step, LANES).start()
+    head.start()
     for copy in firsts:
         copy.wait()
     turned[...] = proj[...].T
+    for copy in nexts:
+        copy.wait()
+    part = next_proj.shape[1] // steps
 
     @pl.loop(0, steps)
     def _(step):
-        fetch(step).wait()
-        span = pl.ds(pl.multiple_of(step * block, block), block)
-        left = jnp.dot(held[span, :half], turned[...], preferred_element_type=jnp.float32)
-        right = jnp.dot(held[span, half:], turned[...], preferred_element_type=jnp.float32)
-        feats_ref[:, span] = left.T[:count] + right.T[count:]
-
-
-def features(rows, proj, block, limit, name):
-    count, width = proj.shape
-    return pl.pallas_call(
-        functools.partial(stream_kernel, block),
-        out_shape=pltpu.VMEM((count, rows.shape[0]), jnp.float32),
-        in_specs=[ANY_SPEC] * 2,
+        fetch(rows_ref, held, row_sems, step, LANES).wait()
+        span = pl.ds(pl.multiple_of(step * LANES, LANES), LANES)
+        feats_ref[:, span] = project(held.at[span], turned, proj_ref.shape[0])
+        span = pl.ds(pl.multiple_of(step * part, LANES), part)
+        next_turned_ref[span, :] = next_proj[:, span].T
+
+    head.wait()
+
+
+def in_features(inputs, in_proj, out_grads, out_proj):
+    count, width = in_proj.shape
+    next_count, next_width = out_proj.shape
+    return pl.pallas_call(
+        in_kernel,
+        out_shape=(
+            pltpu.VMEM((count, inputs.shape[0]), jnp.float32),
+            pltpu.VMEM((HEAD, next_width), jnp.bfloat16),
+            pltpu.VMEM((next_width // 2, 2 * next_count), jnp.bfloat16),
+        ),
+        in_specs=[ANY_SPEC] * 4,
+        out_specs=(VMEM_SPEC,) * 3,
+        scratch_shapes=[
+            pltpu.VMEM(inputs.shape, jnp.bfloat16),
+            pltpu.VMEM((2 * count, width // 2), jnp.bfloat16),
+            pltpu.VMEM((width // 2, 2 * count), jnp.bfloat16),
+            pltpu.VMEM((2 * next_count, next_width // 2), jnp.bfloat16),
+            pltpu.SemaphoreType.DMA((inputs.shape[0] // LANES,)),
+            pltpu.SemaphoreType.DMA((2,)),
+            pltpu.SemaphoreType.DMA((2,)),
+            pltpu.SemaphoreType.DMA,
+        ],
+        compiler_params=pltpu.CompilerParams(vmem_limit_bytes=24 * 2**20),
+        name="in_features",
+    )(in_hbm(inputs), in_hbm(in_proj), in_hbm(out_grads), in_hbm(out_proj))
+
+
+def out_kernel(rows_ref, head_ref, turned_ref, feats_ref, held, sems):
+    count, steps = feats_ref.shape[0], held.shape[0] // HEAD
+    for step in range(1, steps):
+        fetch(rows_ref, held, sems, step, HEAD).start()
+    feats_ref[:, :HEAD] = project(head_ref, turned_ref, count)
+
+    @pl.loop(1, steps)
+    def _(step):
+        fetch(rows_ref, held, sems, step, HEAD).wait()
+        span = pl.ds(pl.multiple_of(step * HEAD, HEAD), HEAD)
+        feats_ref[:, span] = project(held.at[span], turned_ref, count)
+
+
+def out_features(out_grads, head, turned):
+    tokens = out_grads.shape[0]
+    return pl.pallas_call(
+        out_kernel,
+        out_shape=pltpu.VMEM((R_OUT, tokens), jnp.float32),
+        in_specs=[ANY_SPEC, VMEM_SPEC, VMEM_SPEC],
         out_specs=VMEM_SPEC,
         scratch_shapes=[
-            pltpu.VMEM(rows.shape, jnp.bfloat16),
-            pltpu.VMEM((2 * count, width // 2), jnp.bfloat16),
-            pltpu.VMEM((width // 2, 2 * count), jnp.bfloat16),
-            pltpu.SemaphoreType.DMA((rows.shape[0] // block + 2,)),
+            pltpu.VMEM(out_grads.shape, jnp.bfloat16),
+            pltpu.SemaphoreType.DMA((tokens // HEAD,)),
         ],
-        compiler_params=pltpu.CompilerParams(vmem_limit_bytes=limit * 2**20),
-        name=name,
-    )(in_hbm(rows), in_hbm(proj))
+        compiler_params=pltpu.CompilerParams(vmem_limit_bytes=40 * 2**20),
+        name="out_features",
+    )(in_hbm(out_grads), in_vmem(head), in_vmem(turned))
 
 
 def split_kernel(prior_ref, upper_ref, lower_ref, held, sems):
@@ -151,7 +213,9 @@
         held[:, pl.ds(start, tokens)] = block[...]
     for s in range(part_ref.shape[0]):
         span = slice(s * SEQ, (s + 1) * SEQ)
-        part_ref[s] = dot_nt(held[:, span], out_ref[:, span]) * (1.0 / SEQ)
+        outs = pieces_of(out_ref[:, span], 2)
+        sums = dot_pieces(pieces_of(held[:, span], 2), outs, R_IN)
+        part_ref[s] = (sums[:, :R_OUT] + sums[:, R_OUT:]) * (1.0 / SEQ)
 
 
 def partial_vectors(blocks, out_local):
@@ -314,11 +378,28 @@
     )(*operands)
 
 
+def combine_kernel(curvature_ref, norm_ref, solved_ref, along_ref, scores_ref):
+    step = norm_ref[...] / jnp.sum(curvature_ref[...], axis=0)
+    scores_ref[...] = solved_ref[...] + step[:, :1] * along_ref[...]
+
+
+def combine(curvature, norm, solved, along):
+    return pl.pallas_call(
+        combine_kernel,
+        out_shape=F32(solved.shape),
+        in_specs=[VMEM_SPEC] * 4,
+        out_specs=VMEM_SPEC,
+        compiler_params=PARAMS,
+        name="combine",
+    )(curvature, norm, solved, along)
+
+
 def on_device(dp_size, tensor_size, inputs, in_proj, out_grads, out_proj, prior, queries):
     width = R_IN * R_OUT
     sizes = dp_size, tensor_size
-    in_blocks = direct(features(inputs, in_proj, LANES, 20, "in_features"), "tensor", tensor_size, order_of(tensor_size))
-    out_local = features(out_grads, out_proj, 2 * LANES, 44, "out_features")
+    in_local, head, turned = in_features(inputs, in_proj, out_grads, out_proj)
+    in_blocks = direct(in_local, "tensor", tensor_size, order_of(tensor_size))
+    out_local = out_features(out_grads, head, turned)
     partial = partial_vectors(in_blocks, out_local).reshape(-1, width)
     first, *rest = bits(tensor_size)
     prior, partial = lax.optimization_barrier((prior, partial))
@@ -337,8 +418,7 @@
         state = [applied_rows, *others]
     blocks = gather(state[0], sizes)
     curvature, norm, solved, along = step_cg(blocks, fixed, norm, state, queries, sizes)
-    curvature = jnp.sum(gather(curvature, sizes), axis=0)
-    return solved + (norm / curvature)[:, :1] * along
+    return combine(gather(curvature, sizes), norm, solved, along)
 
 
 def solution(mesh):

time: 82.1 us -> 82.9 us (level)
  Pallas kernels: 26.4 us -> 28 us
    pallas_call x2 -> x3, Pallas kernels: 16.9 us -> 18.8 us  [the longest x1 11.3 us: out_features(): pl.pallas_call(out_kernel, out_shape=pltpu.VMEM((R_OUT, tokens), jnp.floa...]
  transfers between devices with their start and end apart: 8 -> 8, of which waited for: 3 -> 4; matrix products, arithmetic and copies ran while one was open for 0% -> 0% of each run, Pallas kernels for 17% -> 17%
where the time goes in v17:
time: 82.9 us; the launch traced here: 82.6 us
  blocking collectives  37.6 us (45%)
  Pallas kernels  28 us (34%)
  starting transfers between devices  11.7 us (14%)
  waiting for transfers between devices  4.94 us (6%)
    all_to_all x4, blocking collectives, gather(): lax.all_to_all(value, ('dp', 'tensor'), 0, 0, axis_index_groups=[order])  37.6 us
    ppermute x8, starting transfers between devices, swap(): return lax.ppermute(value, axis, [(i, i ^ bit) for i in range(size)])  11.7 us
    pallas_call x1, Pallas kernels, out_features(): pl.pallas_call(out_kernel, out_shape=pltpu.VMEM((R_OUT, tokens), jnp.floa...  11.3 us
    pallas_call x1, Pallas kernels, in_features(): pl.pallas_call(in_kernel, out_shape=(pltpu.VMEM((count, inputs.shape[0]),...  6.75 us
    pallas_call x3, Pallas kernels, step_cg(): pl.pallas_call(functools.partial(step_kernel, sizes, first, last), out_sh...  5.12 us
    ppermute x8, waiting for transfers between devices, swap(): return lax.ppermute(value, axis, [(i, i ^ bit) for i in range(size)])  4.94 us
    pallas_call x1, Pallas kernels, split_prior(): pl.pallas_call(split_kernel, out_shape=(pltpu.VMEM(prior.shape, jnp.bfloa...  2.32 us
  transfers between devices with their start and end apart: 8, of which 4 were waited for; matrix products, arithmetic and copies ran while one was open for 0% of the time, Pallas kernels for 17%

profile of v17, /device:TPU:0, one launch (start us, length us, event | category | flops | bytes accessed | tf_op | source)
XLA Modules:
  0.0 82.6 jit_solution(8599427606481298844)
XLA Ops:
  0.0 6.7 %in_features.1 = (f32[64,512]{1,0:T(8,128)S(1)}, bf16[256,7168]{1,0:T(8,128)(2,1)S(1)}, bf16[3584,128]{1,0:T(8,128)(2,1)S(1)}) custom-call(bf16[512,8192]{1,0:T(8,128)(2,1)} %rows_ref.2, bf16[64,8192]{1,0:T(8,128)(2,1)} %proj_ref.1, bf16[2048,7168]{1,0:T(8,128)(2,1)} %rows_ref.3, bf16[64,7168]{1,0:T(8,128)(2,1)} %next_proj_ref.1), custom_call_target="tpu_custom_call" | custom-call | tf_op jit(solution)/shard_map/in_features/pallas_call | solution.py:125
  6.8 3.1 %collective-permute-start.2 = (f32[64,512]{1,0:T(8,128)S(1)}, f32[64,512]{1,0:T(8,128)S(1)}, u32[]{:S(2)}, u32[]{:S(2)}) collective-permute-start(f32[64,512]{1,0:T(8,128)S(1)} %get-tuple-element.36.refs_0_), channel_id=1, source_target_pairs={{0,1},{1,0},{2,3},{3,2},{4,5},{5,4},{6,7},{7,6},{8,9},{9,8},{10,11... | collective-permute-start | bytes 393224 | tf_op jit(solution)/shard_map/ppermute | solution.py:25
  9.8 2.5 %collective-permute-start.1 = (f32[64,512]{1,0:T(8,128)S(1)}, f32[64,512]{1,0:T(8,128)S(1)}, u32[]{:S(2)}, u32[]{:S(2)}) collective-permute-start(f32[64,512]{1,0:T(8,128)S(1)} %get-tuple-element.36.refs_0_), channel_id=1, source_target_pairs={{0,3},{1,2},{2,1},{3,0},{4,7},{5,6},{6,5},{7,4},{8,11},{9,10},{10,... | collective-permute-start | bytes 393224 | tf_op jit(solution)/shard_map/ppermute | solution.py:25
  12.3 0.1 collective-permute-start
  12.4 11.3 %out_features.1.refs_4_ = f32[64,2048]{1,0:T(8,128)S(1)} custom-call(bf16[2048,7168]{1,0:T(8,128)(2,1)} %rows_ref.3, bf16[256,7168]{1,0:T(8,128)(2,1)S(1)} %get-tuple-element.37.head_ref, bf16[3584,128]{1,0:T(8,128)(2,1)S(1)} %get-tuple-element.38.turned_ref), custom_call_target="tpu_custom_call" | custom-call | tf_op jit(solution)/shard_map/out_features/pallas_call | solution.py:164
  23.8 0.3 collective-permute-done.refs_1_
  24.1 0.4 partial_vectors.1
  24.6 2.6 %collective-permute-start.3 = (f32[2,4096]{1,0:T(2,128)S(1)}, f32[2,4096]{1,0:T(2,128)S(1)}, u32[]{:S(2)}, u32[]{:S(2)}) collective-permute-start(f32[2,4096]{1,0:T(2,128)S(1)} %reshape.7), channel_id=1, source_target_pairs={{0,2},{1,3},{2,0},{3,1},{4,6},{5,7},{6,4},{7,5},{8,10},{9,11},{10,... | collective-permute-start | bytes 98312 | tf_op jit(solution)/shard_map/ppermute | solution.py:25
  27.2 2.3 %split_prior.1 = (bf16[256,4096]{1,0:T(8,128)(2,1)S(1)}, bf16[256,4096]{1,0:T(8,128)(2,1)S(1)}) custom-call(f32[256,4096]{1,0:T(8,128)} %prior_ref), custom_call_target="tpu_custom_call" | custom-call | tf_op jit(solution)/shard_map/split_prior/pallas_call | solution.py:196
  29.5 1.5 %collective-permute-start.4 = (f32[2,4096]{1,0:T(2,128)S(1)}, f32[2,4096]{1,0:T(2,128)S(1)}, u32[]{:S(2)}, u32[]{:S(2)}) collective-permute-start(f32[2,4096]{1,0:T(2,128)S(1)} %add.6), channel_id=1, source_target_pairs={{0,1},{1,0},{2,3},{3,2},{4,5},{5,4},{6,7},{7,6},{8,9},{9,8},{10,11... | collective-permute-start | bytes 98312 | tf_op jit(solution)/shard_map/ppermute | solution.py:25
  31.1 2.5 %collective-permute-done.4 = f32[2,4096]{1,0:T(2,128)S(1)} collective-permute-done((f32[2,4096]{1,0:T(2,128)S(1)}, f32[2,4096]{1,0:T(2,128)S(1)}, u32[]{:S(2)}, u32[]{:S(2)}) %collective-permute-start.4) | collective-permute-done | bytes 32800 | tf_op jit(solution)/shard_map/ppermute | solution.py:25
  33.6 1.6 %collective-permute-start.6 = (f32[2,4096]{1,0:T(2,128)S(1)}, f32[2,4096]{1,0:T(2,128)S(1)}, u32[]{:S(2)}, u32[]{:S(2)}) collective-permute-start(f32[2,4096]{1,0:T(2,128)S(1)} %add.7.refs_0_), channel_id=1, source_target_pairs={{0,8},{4,12},{8,0},{12,4},{1,9},{5,13},{9,1},{13,5},{2,10},{6,14},... | collective-permute-start | bytes 98312 | tf_op jit(solution)/shard_map/ppermute | solution.py:25
  35.2 0.3 collective-permute-start.5
  35.5 1.8 %collective-permute-done.7.refs_3_ = f32[2,4096]{1,0:T(2,128)S(1)} collective-permute-done((f32[2,4096]{1,0:T(2,128)S(1)}, f32[2,4096]{1,0:T(2,128)S(1)}, u32[]{:S(2)}, u32[]{:S(2)}) %collective-permute-start.7) | collective-permute-done | bytes 32800 | tf_op jit(solution)/shard_map/ppermute | solution.py:25
  37.3 0.4 collective-permute-done.6.refs_2_
  37.6 1.5 %cg_start.1 = (f32[8,4096]{1,0:T(8,128)S(1)}, bf16[16,4096]{1,0:T(8,128)(2,1)S(1)}, f32[8,128]{1,0:T(8,128)S(1)}, f32[8,256]{1,0:T(8,128)S(1)}, f32[8,128]{1,0:T(8,128)S(1)}) custom-call(f32[2,4096]{1,0:T(2,128)S(1)} %add.7.refs_0_, f32[2,4096]{1,0:T(2,128)S(1)} %collective-permute-done.5.refs_1_, f32[2,4096]{1,0:T(2,128)S(1)} %collective-permute-done.6.refs_2_, ...), custom_call_target="tpu_custom_call" | custom-call | tf_op jit(solution)/shard_map/cg_start/pallas_call | solution.py:297
  39.1 11.0 %all_to_all.20.refs_0_ = f32[16,8,256]{2,1,0:T(8,128)S(1)} all-to-all(f32[16,8,256]{2,1,0:T(8,128)S(1)} %broadcast_in_dim.8), channel_id=1, replica_groups={{5,0,1,2,3,4,6,7,8,9,10,11,12,13,14,15},{21,16,17,18,19,20,22,23,24,25,..., dimensions={0} | all-to-all | bytes 262144 | tf_op jit(solution)/shard_map/all_to_all | solution.py:41
  50.1 1.6 %cg_step.3 = (f32[8,256]{1,0:T(8,128)S(1)}, f32[8,128]{1,0:T(8,128)S(1)}, f32[8,256]{1,0:T(8,128)S(1)}, f32[8,4096]{1,0:T(8,128)S(1)}, f32[8,4096]{1,0:T(8,128)S(1)}, /*index=5*/f32[8,4096]{1,0:T(8,128)S(1)}) custom-call(f32[16,8,256]{2,1,0:T(8,128)S(1)} %all_to_all.20.refs_0_, bf16[256,4096]{1,0:T(8,128)(2,1)S(1)} %get-tuple-element.44.refs_4_.refs_1_, ...), custom_call_target="tpu_custom_call" | custom-call | tf_op jit(solution)/shard_map/cg_step/pallas_call | solution.py:370
  51.7 9.2 %all_to_all.21.refs_0_ = f32[16,8,256]{2,1,0:T(8,128)S(1)} all-to-all(f32[16,8,256]{2,1,0:T(8,128)S(1)} %broadcast_in_dim.9), channel_id=1, replica_groups={{5,0,1,2,3,4,6,7,8,9,10,11,12,13,14,15},{21,16,17,18,19,20,22,23,24,25,..., dimensions={0} | all-to-all | bytes 262144 | tf_op jit(solution)/shard_map/all_to_all | solution.py:41
  61.0 1.6 %cg_step.4 = (f32[8,256]{1,0:T(8,128)S(1)}, f32[8,128]{1,0:T(8,128)S(1)}, f32[8,256]{1,0:T(8,128)S(1)}, f32[8,4096]{1,0:T(8,128)S(1)}, f32[8,4096]{1,0:T(8,128)S(1)}, /*index=5*/f32[8,4096]{1,0:T(8,128)S(1)}) custom-call(f32[16,8,256]{2,1,0:T(8,128)S(1)} %all_to_all.21.refs_0_, bf16[256,4096]{1,0:T(8,128)(2,1)S(1)} %get-tuple-element.44.refs_4_.refs_1_, ...), custom_call_target="tpu_custom_call" | custom-call | tf_op jit(solution)/shard_map/cg_step/pallas_call | solution.py:370
  62.6 9.2 %all_to_all.22.refs_0_ = f32[16,8,256]{2,1,0:T(8,128)S(1)} all-to-all(f32[16,8,256]{2,1,0:T(8,128)S(1)} %broadcast_in_dim.10), channel_id=1, replica_groups={{5,0,1,2,3,4,6,7,8,9,10,11,12,13,14,15},{21,16,17,18,19,20,22,23,24,25,..., dimensions={0} | all-to-all | bytes 262144 | tf_op jit(solution)/shard_map/all_to_all | solution.py:41
  71.8 1.9 %cg_step.5 = (f32[8,128]{1,0:T(8,128)S(1)}, f32[8,128]{1,0:T(8,128)S(1)}, f32[8,32]{1,0:T(8,128)S(1)}, f32[8,32]{1,0:T(8,128)S(1)}) custom-call(f32[16,8,256]{2,1,0:T(8,128)S(1)} %all_to_all.22.refs_0_, bf16[256,4096]{1,0:T(8,128)(2,1)S(1)} %get-tuple-element.44.refs_4_.refs_1_, bf16[256,4096]{1,0:T(8,128)(2,1)S(1)} %get-tuple-element.45.refs_5_.refs_2_, ...), custom_call_target="tpu_custom_call" | custom-call | tf_op jit(solution)/shard_map/cg_step/pallas_call | solution.py:370
  73.7 8.2 %all_to_all.23.curvature_ref = f32[16,8,128]{2,1,0:T(8,128)S(1)} all-to-all(f32[16,8,128]{2,1,0:T(8,128)S(1)} %broadcast_in_dim.11), channel_id=1, replica_groups={{5,0,1,2,3,4,6,7,8,9,10,11,12,13,14,15},{21,16,17,18,19,20,22,23,24,25,..., dimensions={0} | all-to-all | bytes 131072 | tf_op jit(solution)/shard_map/all_to_all | solution.py:41
  82.0 0.7 combine.1
  (14 shorter events, 0.3 us)
Async XLA Ops:
  6.8 17.0 %collective-permute-start.2 = (f32[64,512]{1,0:T(8,128)S(1)}, f32[64,512]{1,0:T(8,128)S(1)}, u32[]{:S(2)}, u32[]{:S(2)}) collective-permute-start(f32[64,512]{1,0:T(8,128)S(1)} %get-tuple-element.36.refs_0_), channel_id=1, source_target_pairs={{0,1},{1,0},{2,3},{3,2},{4,5},{5,4},{6,7},{7,6},{8,9},{9,8},{10,11... | collective-permute-start | bytes 393224 | tf_op jit(solution)/shard_map/ppermute | solution.py:25
  9.8 13.9 %collective-permute-start.1 = (f32[64,512]{1,0:T(8,128)S(1)}, f32[64,512]{1,0:T(8,128)S(1)}, u32[]{:S(2)}, u32[]{:S(2)}) collective-permute-start(f32[64,512]{1,0:T(8,128)S(1)} %get-tuple-element.36.refs_0_), channel_id=1, source_target_pairs={{0,3},{1,2},{2,1},{3,0},{4,7},{5,6},{6,5},{7,4},{8,11},{9,10},{10,... | collective-permute-start | bytes 393224 | tf_op jit(solution)/shard_map/ppermute | solution.py:25
  12.3 11.8 %collective-permute-start = (f32[64,512]{1,0:T(8,128)S(1)}, f32[64,512]{1,0:T(8,128)S(1)}, u32[]{:S(2)}, u32[]{:S(2)}) collective-permute-start(f32[64,512]{1,0:T(8,128)S(1)} %get-tuple-element.36.refs_0_), channel_id=1, source_target_pairs={{0,2},{1,3},{2,0},{3,1},{4,6},{5,7},{6,4},{7,5},{8,10},{9,11},{10,... | collective-permute-start | bytes 393224 | tf_op jit(solution)/shard_map/ppermute | solution.py:25
  24.6 4.9 %collective-permute-start.3 = (f32[2,4096]{1,0:T(2,128)S(1)}, f32[2,4096]{1,0:T(2,128)S(1)}, u32[]{:S(2)}, u32[]{:S(2)}) collective-permute-start(f32[2,4096]{1,0:T(2,128)S(1)} %reshape.7), channel_id=1, source_target_pairs={{0,2},{1,3},{2,0},{3,1},{4,6},{5,7},{6,4},{7,5},{8,10},{9,11},{10,... | collective-permute-start | bytes 98312 | tf_op jit(solution)/shard_map/ppermute | solution.py:25
  29.5 4.0 %collective-permute-start.4 = (f32[2,4096]{1,0:T(2,128)S(1)}, f32[2,4096]{1,0:T(2,128)S(1)}, u32[]{:S(2)}, u32[]{:S(2)}) collective-permute-start(f32[2,4096]{1,0:T(2,128)S(1)} %add.6), channel_id=1, source_target_pairs={{0,1},{1,0},{2,3},{3,2},{4,5},{5,4},{6,7},{7,6},{8,9},{9,8},{10,11... | collective-permute-start | bytes 98312 | tf_op jit(solution)/shard_map/ppermute | solution.py:25
  33.5 3.7 %collective-permute-start.7 = (f32[2,4096]{1,0:T(2,128)S(1)}, f32[2,4096]{1,0:T(2,128)S(1)}, u32[]{:S(2)}, u32[]{:S(2)}) collective-permute-start(f32[2,4096]{1,0:T(2,128)S(1)} %add.7.refs_0_), channel_id=1, source_target_pairs={{0,12},{4,8},{8,4},{12,0},{1,13},{5,9},{9,5},{13,1},{2,14},{6,10},... | collective-permute-start | bytes 98312 | tf_op jit(solution)/shard_map/ppermute | solution.py:25
  33.6 4.0 %collective-permute-start.6 = (f32[2,4096]{1,0:T(2,128)S(1)}, f32[2,4096]{1,0:T(2,128)S(1)}, u32[]{:S(2)}, u32[]{:S(2)}) collective-permute-start(f32[2,4096]{1,0:T(2,128)S(1)} %add.7.refs_0_), channel_id=1, source_target_pairs={{0,8},{4,12},{8,0},{12,4},{1,9},{5,13},{9,1},{13,5},{2,10},{6,14},... | collective-permute-start | bytes 98312 | tf_op jit(solution)/shard_map/ppermute | solution.py:25
  35.2 2.5 %collective-permute-start.5 = (f32[2,4096]{1,0:T(2,128)S(1)}, f32[2,4096]{1,0:T(2,128)S(1)}, u32[]{:S(2)}, u32[]{:S(2)}) collective-permute-start(f32[2,4096]{1,0:T(2,128)S(1)} %add.7.refs_0_), channel_id=1, source_target_pairs={{0,4},{4,0},{8,12},{12,8},{1,5},{5,1},{9,13},{13,9},{2,6},{6,2},{1... | collective-permute-start | bytes 98312 | tf_op jit(solution)/shard_map/ppermute | solution.py:25
  50.1 21.7 %copy-start = (bf16[32,4096]{1,0:T(8,128)(2,1)S(1)}, bf16[32,4096]{1,0:T(8,128)(2,1)}, u32[]{:S(2)}) copy-start(bf16[32,4096]{1,0:T(8,128)(2,1)} %refs_12_.1) | copy-start | bytes 786436

commit v18 on v15

--- a/solution.py
+++ b/solution.py
@@ -41,7 +41,7 @@
 
 
 def order_of(size):
-    return (0, 2, 3, 1) if size == 4 else tuple(range(size))
+    return (0, 1, 3, 2) if size == 4 else tuple(range(size))
 
 
 def direct(value, axis, size, order):
@@ -66,33 +66,46 @@
 
 def stream_kernel(block, rows_ref, proj_ref, feats_ref, held, proj, turned, sems):
     count, half = proj_ref.shape[0], proj.shape[1]
-    steps = held.shape[0] // block
+    steps, tail = held.shape[0] // block, block // LANES
     firsts = [
         pltpu.make_async_copy(
-            proj_ref.at[:, pl.ds(h * half, half)], proj.at[pl.ds(h * count, count)], sems.at[steps + h]
+            proj_ref.at[:, pl.ds(h * half, half)], proj.at[pl.ds(h * count, count)], sems.at[h]
         )
         for h in range(2)
     ]
 
-    def fetch(step):
-        span = pl.ds(pl.multiple_of(step * block, block), block)
-        return pltpu.make_async_copy(rows_ref.at[span], held.at[span], sems.at[step])
+    def span_of(step, size):
+        return pl.ds(pl.multiple_of(step * size, size), size)
+
+    def fetch(step, size):
+        sem = step + 2 if size == block else step - (steps - 1) * tail + steps + 1
+        span = span_of(step, size)
+        return pltpu.make_async_copy(rows_ref.at[span], held.at[span], sems.at[sem])
+
+    def project(step, size):
+        fetch(step, size).wait()
+        span = span_of(step, size)
+        left = jnp.dot(held[span, :half], turned[...], preferred_element_type=jnp.float32)
+        right = jnp.dot(held[span, half:], turned[...], preferred_element_type=jnp.float32)
+        feats_ref[:, span] = left.T[:count] + right.T[count:]
 
     for copy in firsts:
         copy.start()
-    for step in range(steps):
-        fetch(step).start()
+    for step in range(steps - 1):
+        fetch(step, block).start()
+    for step in range((steps - 1) * tail, steps * tail):
+        fetch(step, LANES).start()
     for copy in firsts:
         copy.wait()
     turned[...] = proj[...].T
 
-    @pl.loop(0, steps)
+    @pl.loop(0, steps - 1)
     def _(step):
-        fetch(step).wait()
-        span = pl.ds(pl.multiple_of(step * block, block), block)
-        left = jnp.dot(held[span, :half], turned[...], preferred_element_type=jnp.float32)
-        right = jnp.dot(held[span, half:], turned[...], preferred_element_type=jnp.float32)
-        feats_ref[:, span] = left.T[:count] + right.T[count:]
+        project(step, block)
+
+    @pl.loop((steps - 1) * tail, steps * tail)
+    def _(step):
+        project(step, LANES)
 
 
 def features(rows, proj, block, limit, name):
@@ -106,7 +119,7 @@
             pltpu.VMEM(rows.shape, jnp.bfloat16),
             pltpu.VMEM((2 * count, width // 2), jnp.bfloat16),
             pltpu.VMEM((width // 2, 2 * count), jnp.bfloat16),
-            pltpu.SemaphoreType.DMA((rows.shape[0] // block + 2,)),
+            pltpu.SemaphoreType.DMA((rows.shape[0] // block + block // LANES + 1,)),
         ],
         compiler_params=pltpu.CompilerParams(vmem_limit_bytes=limit * 2**20),
         name=name,
@@ -151,7 +164,9 @@
         held[:, pl.ds(start, tokens)] = block[...]
     for s in range(part_ref.shape[0]):
         span = slice(s * SEQ, (s + 1) * SEQ)
-        part_ref[s] = dot_nt(held[:, span], out_ref[:, span]) * (1.0 / SEQ)
+        outs = pieces_of(out_ref[:, span], 2)
+        sums = dot_pieces(pieces_of(held[:, span], 2), outs, R_IN)
+        part_ref[s] = (sums[:, :R_OUT] + sums[:, R_OUT:]) * (1.0 / SEQ)
 
 
 def partial_vectors(blocks, out_local):
@@ -195,7 +210,7 @@
 def apply_fisher(pieces, vectors_ref, vector_pieces, upper_ref, lower_ref, me):
     seqs = vectors_ref.shape[0]
     applied = dot_pieces(pieces, upper_ref[...], seqs)
-    applied = applied + dot_pieces(pieces[: 2 * seqs], lower_ref[...], seqs)
+    applied = applied + dot_pieces(pieces, lower_ref[...], seqs)
     weights = dot_pieces(pieces, vector_pieces, seqs)
     weights = (weights[:, :seqs] + weights[:, seqs:]) * (1.0 / seqs)
     own = own_columns(vectors_ref, me, upper_ref.shape[0])
@@ -214,15 +229,14 @@
         held[dp ^ k] = piece[...]
     vectors = jnp.concatenate([held[k] for k in range(size)], axis=0)
     vectors_ref[...] = vectors
-    split = pieces_of(vectors, 3)
-    vector_pieces = split[: 2 * vectors.shape[0]]
-    vector_pieces_ref[...] = vector_pieces
+    split = pieces_of(vectors, 2)
+    vector_pieces_ref[...] = split
     norm = jnp.broadcast_to(row_sum(vectors * vectors), norm_ref.shape)
     norm_ref[...] = norm
     spread = jnp.sum(norm, axis=0, keepdims=True) * (1.0 / vectors.shape[0])
     scale_ref[...] = jnp.broadcast_to(1.0 / (1.0 + spread), scale_ref.shape)
     me = flat_index(tensor_size)
-    applied_ref[...] = apply_fisher(split, vectors_ref, vector_pieces, upper_ref, lower_ref, me)
+    applied_ref[...] = apply_fisher(split, vectors_ref, split, upper_ref, lower_ref, me)
 
 
 def start_cg(pieces, prior_pieces, tensor_size):
@@ -259,7 +273,7 @@
     applied = held[...]
     scale = scale_ref[...][:, :1]
     twice = apply_fisher(
-        pieces_of(scale * applied, 3), vectors_ref, vector_pieces_ref[...], upper_ref, lower_ref, me
+        pieces_of(scale * applied, 2), vectors_ref, vector_pieces_ref[...], upper_ref, lower_ref, me
     )
     direction = vectors_ref[...] if first else direction_ref[...]
     residual = direction if first else residual_ref[...]
@@ -314,6 +328,22 @@
     )(*operands)
 
 
+def combine_kernel(curvature_ref, norm_ref, solved_ref, along_ref, scores_ref):
+    step = norm_ref[...] / jnp.sum(curvature_ref[...], axis=0)
+    scores_ref[...] = solved_ref[...] + step[:, :1] * along_ref[...]
+
+
+def combine(curvature, norm, solved, along):
+    return pl.pallas_call(
+        combine_kernel,
+        out_shape=F32(solved.shape),
+        in_specs=[VMEM_SPEC] * 4,
+        out_specs=VMEM_SPEC,
+        compiler_params=PARAMS,
+        name="combine",
+    )(curvature, norm, solved, along)
+
+
 def on_device(dp_size, tensor_size, inputs, in_proj, out_grads, out_proj, prior, queries):
     width = R_IN * R_OUT
     sizes = dp_size, tensor_size
@@ -337,8 +367,7 @@
         state = [applied_rows, *others]
     blocks = gather(state[0], sizes)
     curvature, norm, solved, along = step_cg(blocks, fixed, norm, state, queries, sizes)
-    curvature = jnp.sum(gather(curvature, sizes), axis=0)
-    return solved + (norm / curvature)[:, :1] * along
+    return combine(gather(curvature, sizes), norm, solved, along)
 
 
 def solution(mesh):

time: 82.1 us -> 81.8 us (level)
  transfers between devices with their start and end apart: 8 -> 8, of which waited for: 3 -> 3; matrix products, arithmetic and copies ran while one was open for 0% -> 0% of each run, Pallas kernels for 17% -> 18%
where the time goes in v18:
time: 81.8 us; the launch traced here: 81.6 us
  blocking collectives  37.6 us (46%)
  Pallas kernels  27 us (33%)
  starting transfers between devices  12 us (15%)
  waiting for transfers between devices  4.67 us (6%)
    all_to_all x4, blocking collectives, gather(): lax.all_to_all(value, ('dp', 'tensor'), 0, 0, axis_index_groups=[order])  37.6 us
    pallas_call x2, Pallas kernels, features(): pl.pallas_call(functools.partial(stream_kernel, block), out_shape=pltpu.V...  17.1 us
    ppermute x8, starting transfers between devices, swap(): return lax.ppermute(value, axis, [(i, i ^ bit) for i in range(size)])  12 us
    pallas_call x3, Pallas kernels, step_cg(): pl.pallas_call(functools.partial(step_kernel, sizes, first, last), out_sh...  5 us
    ppermute x8, waiting for transfers between devices, swap(): return lax.ppermute(value, axis, [(i, i ^ bit) for i in range(size)])  4.67 us
    pallas_call x1, Pallas kernels, split_prior(): pl.pallas_call(split_kernel, out_shape=(pltpu.VMEM(prior.shape, jnp.bfloa...  2.32 us
  transfers between devices with their start and end apart: 8, of which 3 were waited for; matrix products, arithmetic and copies ran while one was open for 0% of the time, Pallas kernels for 18%

profile of v18, /device:TPU:0, one launch (start us, length us, event | category | flops | bytes accessed | tf_op | source)
XLA Modules:
  0.0 81.6 jit_solution(15115302023477850050)
XLA Ops:
  0.0 5.1 %in_features.1.refs_0_ = f32[64,512]{1,0:T(8,128)S(1)} custom-call(bf16[512,8192]{1,0:T(8,128)(2,1)} %rows_ref.2, bf16[64,8192]{1,0:T(8,128)(2,1)} %proj_ref.2), custom_call_target="tpu_custom_call" | custom-call | tf_op jit(solution)/shard_map/in_features/pallas_call | solution.py:113
  5.1 4.1 %collective-permute-start.2 = (f32[64,512]{1,0:T(8,128)S(1)}, f32[64,512]{1,0:T(8,128)S(1)}, u32[]{:S(2)}, u32[]{:S(2)}) collective-permute-start(f32[64,512]{1,0:T(8,128)S(1)} %in_features.1.refs_0_), channel_id=1, source_target_pairs={{0,2},{1,3},{2,0},{3,1},{4,6},{5,7},{6,4},{7,5},{8,10},{9,11},{10,... | collective-permute-start | bytes 393224 | tf_op jit(solution)/shard_map/ppermute | solution.py:24
  9.2 1.3 %collective-permute-start.1 = (f32[64,512]{1,0:T(8,128)S(1)}, f32[64,512]{1,0:T(8,128)S(1)}, u32[]{:S(2)}, u32[]{:S(2)}) collective-permute-start(f32[64,512]{1,0:T(8,128)S(1)} %in_features.1.refs_0_), channel_id=1, source_target_pairs={{0,3},{1,2},{2,1},{3,0},{4,7},{5,6},{6,5},{7,4},{8,11},{9,10},{10,... | collective-permute-start | bytes 393224 | tf_op jit(solution)/shard_map/ppermute | solution.py:24
  10.5 0.2 collective-permute-start
  10.7 12.1 %out_features.1.refs_4_ = f32[64,2048]{1,0:T(8,128)S(1)} custom-call(bf16[2048,7168]{1,0:T(8,128)(2,1)} %rows_ref.3, bf16[64,7168]{1,0:T(8,128)(2,1)} %proj_ref.3), custom_call_target="tpu_custom_call" | custom-call | tf_op jit(solution)/shard_map/out_features/pallas_call | solution.py:113
  22.8 0.4 partial_vectors.1
  23.2 0.1 reshape.7
  23.3 2.9 %collective-permute-start.3 = (f32[2,4096]{1,0:T(2,128)S(1)}, f32[2,4096]{1,0:T(2,128)S(1)}, u32[]{:S(2)}, u32[]{:S(2)}) collective-permute-start(f32[2,4096]{1,0:T(2,128)S(1)} %reshape.7), channel_id=1, source_target_pairs={{0,2},{1,3},{2,0},{3,1},{4,6},{5,7},{6,4},{7,5},{8,10},{9,11},{10,... | collective-permute-start | bytes 98312 | tf_op jit(solution)/shard_map/ppermute | solution.py:24
  26.2 2.3 %split_prior.1 = (bf16[256,4096]{1,0:T(8,128)(2,1)S(1)}, bf16[256,4096]{1,0:T(8,128)(2,1)S(1)}) custom-call(f32[256,4096]{1,0:T(8,128)} %prior_ref), custom_call_target="tpu_custom_call" | custom-call | tf_op jit(solution)/shard_map/split_prior/pallas_call | solution.py:147
  28.6 1.5 %collective-permute-start.4 = (f32[2,4096]{1,0:T(2,128)S(1)}, f32[2,4096]{1,0:T(2,128)S(1)}, u32[]{:S(2)}, u32[]{:S(2)}) collective-permute-start(f32[2,4096]{1,0:T(2,128)S(1)} %add.6), channel_id=1, source_target_pairs={{0,1},{1,0},{2,3},{3,2},{4,5},{5,4},{6,7},{7,6},{8,9},{9,8},{10,11... | collective-permute-start | bytes 98312 | tf_op jit(solution)/shard_map/ppermute | solution.py:24
  30.1 2.5 %collective-permute-done.4 = f32[2,4096]{1,0:T(2,128)S(1)} collective-permute-done((f32[2,4096]{1,0:T(2,128)S(1)}, f32[2,4096]{1,0:T(2,128)S(1)}, u32[]{:S(2)}, u32[]{:S(2)}) %collective-permute-start.4) | collective-permute-done | bytes 32800 | tf_op jit(solution)/shard_map/ppermute | solution.py:24
  32.7 1.5 %collective-permute-start.6 = (f32[2,4096]{1,0:T(2,128)S(1)}, f32[2,4096]{1,0:T(2,128)S(1)}, u32[]{:S(2)}, u32[]{:S(2)}) collective-permute-start(f32[2,4096]{1,0:T(2,128)S(1)} %add.7.refs_0_), channel_id=1, source_target_pairs={{0,8},{4,12},{8,0},{12,4},{1,9},{5,13},{9,1},{13,5},{2,10},{6,14},... | collective-permute-start | bytes 98312 | tf_op jit(solution)/shard_map/ppermute | solution.py:24
  34.2 0.3 collective-permute-start.5
  34.5 1.8 %collective-permute-done.7.refs_3_ = f32[2,4096]{1,0:T(2,128)S(1)} collective-permute-done((f32[2,4096]{1,0:T(2,128)S(1)}, f32[2,4096]{1,0:T(2,128)S(1)}, u32[]{:S(2)}, u32[]{:S(2)}) %collective-permute-start.7) | collective-permute-done | bytes 32800 | tf_op jit(solution)/shard_map/ppermute | solution.py:24
  36.3 0.4 collective-permute-done.6.refs_2_
  36.7 1.5 %cg_start.1 = (f32[8,4096]{1,0:T(8,128)S(1)}, bf16[16,4096]{1,0:T(8,128)(2,1)S(1)}, f32[8,128]{1,0:T(8,128)S(1)}, f32[8,256]{1,0:T(8,128)S(1)}, f32[8,128]{1,0:T(8,128)S(1)}) custom-call(f32[2,4096]{1,0:T(2,128)S(1)} %add.7.refs_0_, f32[2,4096]{1,0:T(2,128)S(1)} %collective-permute-done.5.refs_1_, f32[2,4096]{1,0:T(2,128)S(1)} %collective-permute-done.6.refs_2_, ...), custom_call_target="tpu_custom_call" | custom-call | tf_op jit(solution)/shard_map/cg_start/pallas_call | solution.py:247
  38.2 11.0 %all_to_all.20.refs_0_ = f32[16,8,256]{2,1,0:T(8,128)S(1)} all-to-all(f32[16,8,256]{2,1,0:T(8,128)S(1)} %broadcast_in_dim.8), channel_id=1, replica_groups={{5,0,1,2,3,4,6,7,8,9,10,11,12,13,14,15},{21,16,17,18,19,20,22,23,24,25,..., dimensions={0} | all-to-all | bytes 262144 | tf_op jit(solution)/shard_map/all_to_all | solution.py:40
  49.2 1.6 %cg_step.3 = (f32[8,256]{1,0:T(8,128)S(1)}, f32[8,128]{1,0:T(8,128)S(1)}, f32[8,256]{1,0:T(8,128)S(1)}, f32[8,4096]{1,0:T(8,128)S(1)}, f32[8,4096]{1,0:T(8,128)S(1)}, /*index=5*/f32[8,4096]{1,0:T(8,128)S(1)}) custom-call(f32[16,8,256]{2,1,0:T(8,128)S(1)} %all_to_all.20.refs_0_, bf16[256,4096]{1,0:T(8,128)(2,1)S(1)} %get-tuple-element.38.refs_4_.refs_1_, ...), custom_call_target="tpu_custom_call" | custom-call | tf_op jit(solution)/shard_map/cg_step/pallas_call | solution.py:320
  50.7 9.2 %all_to_all.21.refs_0_ = f32[16,8,256]{2,1,0:T(8,128)S(1)} all-to-all(f32[16,8,256]{2,1,0:T(8,128)S(1)} %broadcast_in_dim.9), channel_id=1, replica_groups={{5,0,1,2,3,4,6,7,8,9,10,11,12,13,14,15},{21,16,17,18,19,20,22,23,24,25,..., dimensions={0} | all-to-all | bytes 262144 | tf_op jit(solution)/shard_map/all_to_all | solution.py:40
  60.0 1.6 %cg_step.4 = (f32[8,256]{1,0:T(8,128)S(1)}, f32[8,128]{1,0:T(8,128)S(1)}, f32[8,256]{1,0:T(8,128)S(1)}, f32[8,4096]{1,0:T(8,128)S(1)}, f32[8,4096]{1,0:T(8,128)S(1)}, /*index=5*/f32[8,4096]{1,0:T(8,128)S(1)}) custom-call(f32[16,8,256]{2,1,0:T(8,128)S(1)} %all_to_all.21.refs_0_, bf16[256,4096]{1,0:T(8,128)(2,1)S(1)} %get-tuple-element.38.refs_4_.refs_1_, ...), custom_call_target="tpu_custom_call" | custom-call | tf_op jit(solution)/shard_map/cg_step/pallas_call | solution.py:320
  61.6 9.2 %all_to_all.22.refs_0_ = f32[16,8,256]{2,1,0:T(8,128)S(1)} all-to-all(f32[16,8,256]{2,1,0:T(8,128)S(1)} %broadcast_in_dim.10), channel_id=1, replica_groups={{5,0,1,2,3,4,6,7,8,9,10,11,12,13,14,15},{21,16,17,18,19,20,22,23,24,25,..., dimensions={0} | all-to-all | bytes 262144 | tf_op jit(solution)/shard_map/all_to_all | solution.py:40
  70.8 1.9 %cg_step.5 = (f32[8,128]{1,0:T(8,128)S(1)}, f32[8,128]{1,0:T(8,128)S(1)}, f32[8,32]{1,0:T(8,128)S(1)}, f32[8,32]{1,0:T(8,128)S(1)}) custom-call(f32[16,8,256]{2,1,0:T(8,128)S(1)} %all_to_all.22.refs_0_, bf16[256,4096]{1,0:T(8,128)(2,1)S(1)} %get-tuple-element.38.refs_4_.refs_1_, bf16[256,4096]{1,0:T(8,128)(2,1)S(1)} %get-tuple-element.39.refs_5_.refs_2_, ...), custom_call_target="tpu_custom_call" | custom-call | tf_op jit(solution)/shard_map/cg_step/pallas_call | solution.py:320
  72.7 8.2 %all_to_all.23.curvature_ref = f32[16,8,128]{2,1,0:T(8,128)S(1)} all-to-all(f32[16,8,128]{2,1,0:T(8,128)S(1)} %broadcast_in_dim.11), channel_id=1, replica_groups={{5,0,1,2,3,4,6,7,8,9,10,11,12,13,14,15},{21,16,17,18,19,20,22,23,24,25,..., dimensions={0} | all-to-all | bytes 131072 | tf_op jit(solution)/shard_map/all_to_all | solution.py:40
  80.9 0.7 combine.1
  (14 shorter events, 0.2 us)
Async XLA Ops:
  5.1 17.8 %collective-permute-start.2 = (f32[64,512]{1,0:T(8,128)S(1)}, f32[64,512]{1,0:T(8,128)S(1)}, u32[]{:S(2)}, u32[]{:S(2)}) collective-permute-start(f32[64,512]{1,0:T(8,128)S(1)} %in_features.1.refs_0_), channel_id=1, source_target_pairs={{0,2},{1,3},{2,0},{3,1},{4,6},{5,7},{6,4},{7,5},{8,10},{9,11},{10,... | collective-permute-start | bytes 393224 | tf_op jit(solution)/shard_map/ppermute | solution.py:24
  9.2 13.7 %collective-permute-start.1 = (f32[64,512]{1,0:T(8,128)S(1)}, f32[64,512]{1,0:T(8,128)S(1)}, u32[]{:S(2)}, u32[]{:S(2)}) collective-permute-start(f32[64,512]{1,0:T(8,128)S(1)} %in_features.1.refs_0_), channel_id=1, source_target_pairs={{0,3},{1,2},{2,1},{3,0},{4,7},{5,6},{6,5},{7,4},{8,11},{9,10},{10,... | collective-permute-start | bytes 393224 | tf_op jit(solution)/shard_map/ppermute | solution.py:24
  10.5 12.3 %collective-permute-start = (f32[64,512]{1,0:T(8,128)S(1)}, f32[64,512]{1,0:T(8,128)S(1)}, u32[]{:S(2)}, u32[]{:S(2)}) collective-permute-start(f32[64,512]{1,0:T(8,128)S(1)} %in_features.1.refs_0_), channel_id=1, source_target_pairs={{0,1},{1,0},{2,3},{3,2},{4,5},{5,4},{6,7},{7,6},{8,9},{9,8},{10,11... | collective-permute-start | bytes 393224 | tf_op jit(solution)/shard_map/ppermute | solution.py:24
  23.3 5.2 %collective-permute-start.3 = (f32[2,4096]{1,0:T(2,128)S(1)}, f32[2,4096]{1,0:T(2,128)S(1)}, u32[]{:S(2)}, u32[]{:S(2)}) collective-permute-start(f32[2,4096]{1,0:T(2,128)S(1)} %reshape.7), channel_id=1, source_target_pairs={{0,2},{1,3},{2,0},{3,1},{4,6},{5,7},{6,4},{7,5},{8,10},{9,11},{10,... | collective-permute-start | bytes 98312 | tf_op jit(solution)/shard_map/ppermute | solution.py:24
  28.6 4.0 %collective-permute-start.4 = (f32[2,4096]{1,0:T(2,128)S(1)}, f32[2,4096]{1,0:T(2,128)S(1)}, u32[]{:S(2)}, u32[]{:S(2)}) collective-permute-start(f32[2,4096]{1,0:T(2,128)S(1)} %add.6), channel_id=1, source_target_pairs={{0,1},{1,0},{2,3},{3,2},{4,5},{5,4},{6,7},{7,6},{8,9},{9,8},{10,11... | collective-permute-start | bytes 98312 | tf_op jit(solution)/shard_map/ppermute | solution.py:24
  32.6 3.7 %collective-permute-start.7 = (f32[2,4096]{1,0:T(2,128)S(1)}, f32[2,4096]{1,0:T(2,128)S(1)}, u32[]{:S(2)}, u32[]{:S(2)}) collective-permute-start(f32[2,4096]{1,0:T(2,128)S(1)} %add.7.refs_0_), channel_id=1, source_target_pairs={{0,12},{4,8},{8,4},{12,0},{1,13},{5,9},{9,5},{13,1},{2,14},{6,10},... | collective-permute-start | bytes 98312 | tf_op jit(solution)/shard_map/ppermute | solution.py:24
  32.7 4.0 %collective-permute-start.6 = (f32[2,4096]{1,0:T(2,128)S(1)}, f32[2,4096]{1,0:T(2,128)S(1)}, u32[]{:S(2)}, u32[]{:S(2)}) collective-permute-start(f32[2,4096]{1,0:T(2,128)S(1)} %add.7.refs_0_), channel_id=1, source_target_pairs={{0,8},{4,12},{8,0},{12,4},{1,9},{5,13},{9,1},{13,5},{2,10},{6,14},... | collective-permute-start | bytes 98312 | tf_op jit(solution)/shard_map/ppermute | solution.py:24
  34.2 2.5 %collective-permute-start.5 = (f32[2,4096]{1,0:T(2,128)S(1)}, f32[2,4096]{1,0:T(2,128)S(1)}, u32[]{:S(2)}, u32[]{:S(2)}) collective-permute-start(f32[2,4096]{1,0:T(2,128)S(1)} %add.7.refs_0_), channel_id=1, source_target_pairs={{0,4},{4,0},{8,12},{12,8},{1,5},{5,1},{9,13},{13,9},{2,6},{6,2},{1... | collective-permute-start | bytes 98312 | tf_op jit(solution)/shard_map/ppermute | solution.py:24
  49.2 21.6 %copy-start = (bf16[32,4096]{1,0:T(8,128)(2,1)S(1)}, bf16[32,4096]{1,0:T(8,128)(2,1)}, u32[]{:S(2)}) copy-start(bf16[32,4096]{1,0:T(8,128)(2,1)} %refs_12_.1) | copy-start | bytes 786436

commit v19 on v15

--- a/solution.py
+++ b/solution.py
@@ -12,6 +12,7 @@
 SEQ = 1024
 ITERS = 4
 LANES = 128
+FEW = 4
 NT = (((1,), (1,)), ((), ()))
 HIGHEST = lax.Precision.HIGHEST
 ANY_SPEC = pl.BlockSpec(memory_space=pl.ANY)
@@ -46,6 +47,17 @@
 
 def direct(value, axis, size, order):
     return [value] + [swap(value, axis, size, k) for k in order[1:]]
+
+
+def sum_over(value, axis, size):
+    if size > FEW:
+        for bit in bits(size):
+            value = value + swap(value, axis, size, bit)
+        return value
+    blocks = direct(value, axis, size, order_of(size))
+    while len(blocks) > 1:
+        blocks = [a + b for a, b in zip(blocks[::2], blocks[1::2])]
+    return blocks[0]
 
 
 def in_hbm(value):
@@ -151,7 +163,9 @@
         held[:, pl.ds(start, tokens)] = block[...]
     for s in range(part_ref.shape[0]):
         span = slice(s * SEQ, (s + 1) * SEQ)
-        part_ref[s] = dot_nt(held[:, span], out_ref[:, span]) * (1.0 / SEQ)
+        outs = pieces_of(out_ref[:, span], 2)
+        sums = dot_pieces(pieces_of(held[:, span], 2), outs, R_IN)
+        part_ref[s] = (sums[:, :R_OUT] + sums[:, R_OUT:]) * (1.0 / SEQ)
 
 
 def partial_vectors(blocks, out_local):
@@ -314,19 +328,32 @@
     )(*operands)
 
 
+def combine_kernel(curvature_ref, norm_ref, solved_ref, along_ref, scores_ref):
+    step = norm_ref[...] / jnp.sum(curvature_ref[...], axis=0)
+    scores_ref[...] = solved_ref[...] + step[:, :1] * along_ref[...]
+
+
+def combine(curvature, norm, solved, along):
+    return pl.pallas_call(
+        combine_kernel,
+        out_shape=F32(solved.shape),
+        in_specs=[VMEM_SPEC] * 4,
+        out_specs=VMEM_SPEC,
+        compiler_params=PARAMS,
+        name="combine",
+    )(curvature, norm, solved, along)
+
+
 def on_device(dp_size, tensor_size, inputs, in_proj, out_grads, out_proj, prior, queries):
     width = R_IN * R_OUT
     sizes = dp_size, tensor_size
     in_blocks = direct(features(inputs, in_proj, LANES, 20, "in_features"), "tensor", tensor_size, order_of(tensor_size))
     out_local = features(out_grads, out_proj, 2 * LANES, 44, "out_features")
     partial = partial_vectors(in_blocks, out_local).reshape(-1, width)
-    first, *rest = bits(tensor_size)
     prior, partial = lax.optimization_barrier((prior, partial))
-    partial = partial + swap(partial, "tensor", tensor_size, first)
-    partial, prior_pieces = lax.optimization_barrier((partial, split_prior(prior)))
-    for bit in rest:
-        partial = partial + swap(partial, "tensor", tensor_size, bit)
-    pieces = direct(partial, "dp", dp_size, range(dp_size))
+    own_vectors = sum_over(partial, "tensor", tensor_size)
+    own_vectors, prior_pieces = lax.optimization_barrier((own_vectors, split_prior(prior)))
+    pieces = direct(own_vectors, "dp", dp_size, range(dp_size))
     prior_pieces = [in_vmem(piece) for piece in prior_pieces]
     vectors, vector_pieces, scale, applied_rows, norm = start_cg(pieces, prior_pieces, tensor_size)
     fixed = (*prior_pieces, vectors, vector_pieces, scale)
@@ -337,8 +364,7 @@
         state = [applied_rows, *others]
     blocks = gather(state[0], sizes)
     curvature, norm, solved, along = step_cg(blocks, fixed, norm, state, queries, sizes)
-    curvature = jnp.sum(gather(curvature, sizes), axis=0)
-    return solved + (norm / curvature)[:, :1] * along
+    return combine(gather(curvature, sizes), norm, solved, along)
 
 
 def solution(mesh):

time: 82.1 us -> 80.7 us (0.983)
  blocking collectives: 37.6 us -> 36.7 us
    all_to_all x4, blocking collectives: 37.6 us -> 36.7 us  [gather(): lax.all_to_all(value, ('dp', 'tensor'), 0, 0, axis_index_groups=[order])]
    ppermute x8 -> x9, starting transfers between devices: 12 us -> 11.9 us  [swap(): return lax.ppermute(value, axis, [(i, i ^ bit) for i in range(size)])]
    ppermute x8 -> x9, waiting for transfers between devices: 4.65 us -> 4.66 us  [swap(): return lax.ppermute(value, axis, [(i, i ^ bit) for i in range(size)])]
  transfers between devices with their start and end apart: 8 -> 9, of which waited for: 3 -> 4; matrix products, arithmetic and copies ran while one was open for 0% -> 0% of each run, Pallas kernels for 17% -> 18%
where the time goes in v19:
time: 80.7 us; the launch traced here: 80.4 us
  blocking collectives  36.7 us (45%)
  Pallas kernels  26.8 us (33%)
  starting transfers between devices  11.9 us (15%)
  waiting for transfers between devices  4.66 us (6%)
    all_to_all x4, blocking collectives, gather(): lax.all_to_all(value, ('dp', 'tensor'), 0, 0, axis_index_groups=[order])  36.7 us
    pallas_call x2, Pallas kernels, features(): pl.pallas_call(functools.partial(stream_kernel, block), out_shape=pltpu.V...  16.9 us
    ppermute x9, starting transfers between devices, swap(): return lax.ppermute(value, axis, [(i, i ^ bit) for i in range(size)])  11.9 us
    pallas_call x3, Pallas kernels, step_cg(): pl.pallas_call(functools.partial(step_kernel, sizes, first, last), out_sh...  5.12 us
    ppermute x9, waiting for transfers between devices, swap(): return lax.ppermute(value, axis, [(i, i ^ bit) for i in range(size)])  4.66 us
    pallas_call x1, Pallas kernels, split_prior(): pl.pallas_call(split_kernel, out_shape=(pltpu.VMEM(prior.shape, jnp.bfloa...  2.32 us
  transfers between devices with their start and end apart: 9, of which 4 were waited for; matrix products, arithmetic and copies ran while one was open for 0% of the time, Pallas kernels for 18%

profile of v19, /device:TPU:0, one launch (start us, length us, event | category | flops | bytes accessed | tf_op | source)
XLA Modules:
  0.0 80.4 jit_solution(2701173112279480928)
XLA Ops:
  0.0 5.1 %in_features.1.refs_0_ = f32[64,512]{1,0:T(8,128)S(1)} custom-call(bf16[512,8192]{1,0:T(8,128)(2,1)} %rows_ref.2, bf16[64,8192]{1,0:T(8,128)(2,1)} %proj_ref.2), custom_call_target="tpu_custom_call" | custom-call | tf_op jit(solution)/shard_map/in_features/pallas_call | solution.py:112
  5.1 3.1 %collective-permute-start.2 = (f32[64,512]{1,0:T(8,128)S(1)}, f32[64,512]{1,0:T(8,128)S(1)}, u32[]{:S(2)}, u32[]{:S(2)}) collective-permute-start(f32[64,512]{1,0:T(8,128)S(1)} %in_features.1.refs_0_), channel_id=1, source_target_pairs={{0,1},{1,0},{2,3},{3,2},{4,5},{5,4},{6,7},{7,6},{8,9},{9,8},{10,11... | collective-permute-start | bytes 393224 | tf_op jit(solution)/shard_map/ppermute | solution.py:25
  8.1 2.5 %collective-permute-start.1 = (f32[64,512]{1,0:T(8,128)S(1)}, f32[64,512]{1,0:T(8,128)S(1)}, u32[]{:S(2)}, u32[]{:S(2)}) collective-permute-start(f32[64,512]{1,0:T(8,128)S(1)} %in_features.1.refs_0_), channel_id=1, source_target_pairs={{0,3},{1,2},{2,1},{3,0},{4,7},{5,6},{6,5},{7,4},{8,11},{9,10},{10,... | collective-permute-start | bytes 393224 | tf_op jit(solution)/shard_map/ppermute | solution.py:25
  10.6 0.1 collective-permute-start
  10.7 11.8 %out_features.1.refs_4_ = f32[64,2048]{1,0:T(8,128)S(1)} custom-call(bf16[2048,7168]{1,0:T(8,128)(2,1)} %rows_ref.3, bf16[64,7168]{1,0:T(8,128)(2,1)} %proj_ref.3), custom_call_target="tpu_custom_call" | custom-call | tf_op jit(solution)/shard_map/out_features/pallas_call | solution.py:112
  22.6 0.4 partial_vectors.1
  23.1 1.9 %collective-permute-start.5 = (f32[2,4096]{1,0:T(2,128)S(1)}, f32[2,4096]{1,0:T(2,128)S(1)}, u32[]{:S(2)}, u32[]{:S(2)}) collective-permute-start(f32[2,4096]{1,0:T(2,128)S(1)} %reshape.7), channel_id=1, source_target_pairs={{0,1},{1,0},{2,3},{3,2},{4,5},{5,4},{6,7},{7,6},{8,9},{9,8},{10,11... | collective-permute-start | bytes 98312 | tf_op jit(solution)/shard_map/ppermute | solution.py:25
  25.0 2.5 %collective-permute-start.4 = (f32[2,4096]{1,0:T(2,128)S(1)}, f32[2,4096]{1,0:T(2,128)S(1)}, u32[]{:S(2)}, u32[]{:S(2)}) collective-permute-start(f32[2,4096]{1,0:T(2,128)S(1)} %reshape.7), channel_id=1, source_target_pairs={{0,3},{1,2},{2,1},{3,0},{4,7},{5,6},{6,5},{7,4},{8,11},{9,10},{10,... | collective-permute-start | bytes 98312 | tf_op jit(solution)/shard_map/ppermute | solution.py:25
  27.4 2.3 %split_prior.1 = (bf16[256,4096]{1,0:T(8,128)(2,1)S(1)}, bf16[256,4096]{1,0:T(8,128)(2,1)S(1)}) custom-call(f32[256,4096]{1,0:T(8,128)} %prior_ref), custom_call_target="tpu_custom_call" | custom-call | tf_op jit(solution)/shard_map/split_prior/pallas_call | solution.py:146
  29.8 0.9 %collective-permute-done.4 = f32[2,4096]{1,0:T(2,128)S(1)} collective-permute-done((f32[2,4096]{1,0:T(2,128)S(1)}, f32[2,4096]{1,0:T(2,128)S(1)}, u32[]{:S(2)}, u32[]{:S(2)}) %collective-permute-start.4) | collective-permute-done | bytes 32800 | tf_op jit(solution)/shard_map/ppermute | solution.py:25
  30.7 1.6 %collective-permute-done.3 = f32[2,4096]{1,0:T(2,128)S(1)} collective-permute-done((f32[2,4096]{1,0:T(2,128)S(1)}, f32[2,4096]{1,0:T(2,128)S(1)}, u32[]{:S(2)}, u32[]{:S(2)}) %collective-permute-start.3) | collective-permute-done | bytes 32800 | tf_op jit(solution)/shard_map/ppermute | solution.py:25
  32.4 1.6 %collective-permute-start.7 = (f32[2,4096]{1,0:T(2,128)S(1)}, f32[2,4096]{1,0:T(2,128)S(1)}, u32[]{:S(2)}, u32[]{:S(2)}) collective-permute-start(f32[2,4096]{1,0:T(2,128)S(1)} %add_add_fusion.refs_0_), channel_id=1, source_target_pairs={{0,8},{4,12},{8,0},{12,4},{1,9},{5,13},{9,1},{13,5},{2,10},{6,14},... | collective-permute-start | bytes 98312 | tf_op jit(solution)/shard_map/ppermute | solution.py:25
  33.9 0.3 collective-permute-start.6
  34.2 1.8 %collective-permute-done.8.refs_3_ = f32[2,4096]{1,0:T(2,128)S(1)} collective-permute-done((f32[2,4096]{1,0:T(2,128)S(1)}, f32[2,4096]{1,0:T(2,128)S(1)}, u32[]{:S(2)}, u32[]{:S(2)}) %collective-permute-start.8) | collective-permute-done | bytes 32800 | tf_op jit(solution)/shard_map/ppermute | solution.py:25
  36.0 0.4 collective-permute-done.7.refs_2_
  36.4 1.5 %cg_start.1 = (f32[8,4096]{1,0:T(8,128)S(1)}, bf16[16,4096]{1,0:T(8,128)(2,1)S(1)}, f32[8,128]{1,0:T(8,128)S(1)}, f32[8,256]{1,0:T(8,128)S(1)}, f32[8,128]{1,0:T(8,128)S(1)}) custom-call(f32[2,4096]{1,0:T(2,128)S(1)} %add_add_fusion.refs_0_, f32[2,4096]{1,0:T(2,128)S(1)} %collective-permute-done.6.refs_1_, f32[2,4096]{1,0:T(2,128)S(1)} %collective-permute-done.7.refs_2_, ...), custom_call_target="tpu_custom_call" | custom-call | tf_op jit(solution)/shard_map/cg_start/pallas_call | solution.py:247
  37.9 10.0 %all_to_all.20.refs_0_ = f32[16,8,256]{2,1,0:T(8,128)S(1)} all-to-all(f32[16,8,256]{2,1,0:T(8,128)S(1)} %broadcast_in_dim.8), channel_id=1, replica_groups={{5,0,1,2,3,4,6,7,8,9,10,11,12,13,14,15},{21,16,17,18,19,20,22,23,24,25,..., dimensions={0} | all-to-all | bytes 262144 | tf_op jit(solution)/shard_map/all_to_all | solution.py:41
  47.9 1.6 %cg_step.3 = (f32[8,256]{1,0:T(8,128)S(1)}, f32[8,128]{1,0:T(8,128)S(1)}, f32[8,256]{1,0:T(8,128)S(1)}, f32[8,4096]{1,0:T(8,128)S(1)}, f32[8,4096]{1,0:T(8,128)S(1)}, /*index=5*/f32[8,4096]{1,0:T(8,128)S(1)}) custom-call(f32[16,8,256]{2,1,0:T(8,128)S(1)} %all_to_all.20.refs_0_, bf16[256,4096]{1,0:T(8,128)(2,1)S(1)} %get-tuple-element.38.refs_4_.refs_1_, ...), custom_call_target="tpu_custom_call" | custom-call | tf_op jit(solution)/shard_map/cg_step/pallas_call | solution.py:320
  49.5 9.2 %all_to_all.21.refs_0_ = f32[16,8,256]{2,1,0:T(8,128)S(1)} all-to-all(f32[16,8,256]{2,1,0:T(8,128)S(1)} %broadcast_in_dim.9), channel_id=1, replica_groups={{5,0,1,2,3,4,6,7,8,9,10,11,12,13,14,15},{21,16,17,18,19,20,22,23,24,25,..., dimensions={0} | all-to-all | bytes 262144 | tf_op jit(solution)/shard_map/all_to_all | solution.py:41
  58.7 1.6 %cg_step.4 = (f32[8,256]{1,0:T(8,128)S(1)}, f32[8,128]{1,0:T(8,128)S(1)}, f32[8,256]{1,0:T(8,128)S(1)}, f32[8,4096]{1,0:T(8,128)S(1)}, f32[8,4096]{1,0:T(8,128)S(1)}, /*index=5*/f32[8,4096]{1,0:T(8,128)S(1)}) custom-call(f32[16,8,256]{2,1,0:T(8,128)S(1)} %all_to_all.21.refs_0_, bf16[256,4096]{1,0:T(8,128)(2,1)S(1)} %get-tuple-element.38.refs_4_.refs_1_, ...), custom_call_target="tpu_custom_call" | custom-call | tf_op jit(solution)/shard_map/cg_step/pallas_call | solution.py:320
  60.4 9.2 %all_to_all.22.refs_0_ = f32[16,8,256]{2,1,0:T(8,128)S(1)} all-to-all(f32[16,8,256]{2,1,0:T(8,128)S(1)} %broadcast_in_dim.10), channel_id=1, replica_groups={{5,0,1,2,3,4,6,7,8,9,10,11,12,13,14,15},{21,16,17,18,19,20,22,23,24,25,..., dimensions={0} | all-to-all | bytes 262144 | tf_op jit(solution)/shard_map/all_to_all | solution.py:41
  69.6 1.9 %cg_step.5 = (f32[8,128]{1,0:T(8,128)S(1)}, f32[8,128]{1,0:T(8,128)S(1)}, f32[8,32]{1,0:T(8,128)S(1)}, f32[8,32]{1,0:T(8,128)S(1)}) custom-call(f32[16,8,256]{2,1,0:T(8,128)S(1)} %all_to_all.22.refs_0_, bf16[256,4096]{1,0:T(8,128)(2,1)S(1)} %get-tuple-element.38.refs_4_.refs_1_, bf16[256,4096]{1,0:T(8,128)(2,1)S(1)} %get-tuple-element.39.refs_5_.refs_2_, ...), custom_call_target="tpu_custom_call" | custom-call | tf_op jit(solution)/shard_map/cg_step/pallas_call | solution.py:320
  71.5 8.2 %all_to_all.23.curvature_ref = f32[16,8,128]{2,1,0:T(8,128)S(1)} all-to-all(f32[16,8,128]{2,1,0:T(8,128)S(1)} %broadcast_in_dim.11), channel_id=1, replica_groups={{5,0,1,2,3,4,6,7,8,9,10,11,12,13,14,15},{21,16,17,18,19,20,22,23,24,25,..., dimensions={0} | all-to-all | bytes 131072 | tf_op jit(solution)/shard_map/all_to_all | solution.py:41
  79.7 0.7 combine.1
  (15 shorter events, 0.3 us)
Async XLA Ops:
  5.1 17.5 %collective-permute-start.2 = (f32[64,512]{1,0:T(8,128)S(1)}, f32[64,512]{1,0:T(8,128)S(1)}, u32[]{:S(2)}, u32[]{:S(2)}) collective-permute-start(f32[64,512]{1,0:T(8,128)S(1)} %in_features.1.refs_0_), channel_id=1, source_target_pairs={{0,1},{1,0},{2,3},{3,2},{4,5},{5,4},{6,7},{7,6},{8,9},{9,8},{10,11... | collective-permute-start | bytes 393224 | tf_op jit(solution)/shard_map/ppermute | solution.py:25
  8.1 14.4 %collective-permute-start.1 = (f32[64,512]{1,0:T(8,128)S(1)}, f32[64,512]{1,0:T(8,128)S(1)}, u32[]{:S(2)}, u32[]{:S(2)}) collective-permute-start(f32[64,512]{1,0:T(8,128)S(1)} %in_features.1.refs_0_), channel_id=1, source_target_pairs={{0,3},{1,2},{2,1},{3,0},{4,7},{5,6},{6,5},{7,4},{8,11},{9,10},{10,... | collective-permute-start | bytes 393224 | tf_op jit(solution)/shard_map/ppermute | solution.py:25
  10.6 12.0 %collective-permute-start = (f32[64,512]{1,0:T(8,128)S(1)}, f32[64,512]{1,0:T(8,128)S(1)}, u32[]{:S(2)}, u32[]{:S(2)}) collective-permute-start(f32[64,512]{1,0:T(8,128)S(1)} %in_features.1.refs_0_), channel_id=1, source_target_pairs={{0,2},{1,3},{2,0},{3,1},{4,6},{5,7},{6,4},{7,5},{8,10},{9,11},{10,... | collective-permute-start | bytes 393224 | tf_op jit(solution)/shard_map/ppermute | solution.py:25
  23.1 6.7 %collective-permute-start.5 = (f32[2,4096]{1,0:T(2,128)S(1)}, f32[2,4096]{1,0:T(2,128)S(1)}, u32[]{:S(2)}, u32[]{:S(2)}) collective-permute-start(f32[2,4096]{1,0:T(2,128)S(1)} %reshape.7), channel_id=1, source_target_pairs={{0,1},{1,0},{2,3},{3,2},{4,5},{5,4},{6,7},{7,6},{8,9},{9,8},{10,11... | collective-permute-start | bytes 98312 | tf_op jit(solution)/shard_map/ppermute | solution.py:25
  25.0 5.7 %collective-permute-start.4 = (f32[2,4096]{1,0:T(2,128)S(1)}, f32[2,4096]{1,0:T(2,128)S(1)}, u32[]{:S(2)}, u32[]{:S(2)}) collective-permute-start(f32[2,4096]{1,0:T(2,128)S(1)} %reshape.7), channel_id=1, source_target_pairs={{0,3},{1,2},{2,1},{3,0},{4,7},{5,6},{6,5},{7,4},{8,11},{9,10},{10,... | collective-permute-start | bytes 98312 | tf_op jit(solution)/shard_map/ppermute | solution.py:25
  27.4 4.8 %collective-permute-start.3 = (f32[2,4096]{1,0:T(2,128)S(1)}, f32[2,4096]{1,0:T(2,128)S(1)}, u32[]{:S(2)}, u32[]{:S(2)}) collective-permute-start(f32[2,4096]{1,0:T(2,128)S(1)} %reshape.7), channel_id=1, source_target_pairs={{0,2},{1,3},{2,0},{3,1},{4,6},{5,7},{6,4},{7,5},{8,10},{9,11},{10,... | collective-permute-start | bytes 98312 | tf_op jit(solution)/shard_map/ppermute | solution.py:25
  32.3 3.7 %collective-permute-start.8 = (f32[2,4096]{1,0:T(2,128)S(1)}, f32[2,4096]{1,0:T(2,128)S(1)}, u32[]{:S(2)}, u32[]{:S(2)}) collective-permute-start(f32[2,4096]{1,0:T(2,128)S(1)} %add_add_fusion.refs_0_), channel_id=1, source_target_pairs={{0,12},{4,8},{8,4},{12,0},{1,13},{5,9},{9,5},{13,1},{2,14},{6,10},... | collective-permute-start | bytes 98312 | tf_op jit(solution)/shard_map/ppermute | solution.py:25
  32.4 4.0 %collective-permute-start.7 = (f32[2,4096]{1,0:T(2,128)S(1)}, f32[2,4096]{1,0:T(2,128)S(1)}, u32[]{:S(2)}, u32[]{:S(2)}) collective-permute-start(f32[2,4096]{1,0:T(2,128)S(1)} %add_add_fusion.refs_0_), channel_id=1, source_target_pairs={{0,8},{4,12},{8,0},{12,4},{1,9},{5,13},{9,1},{13,5},{2,10},{6,14},... | collective-permute-start | bytes 98312 | tf_op jit(solution)/shard_map/ppermute | solution.py:25
  33.9 2.5 %collective-permute-start.6 = (f32[2,4096]{1,0:T(2,128)S(1)}, f32[2,4096]{1,0:T(2,128)S(1)}, u32[]{:S(2)}, u32[]{:S(2)}) collective-permute-start(f32[2,4096]{1,0:T(2,128)S(1)} %add_add_fusion.refs_0_), channel_id=1, source_target_pairs={{0,4},{4,0},{8,12},{12,8},{1,5},{5,1},{9,13},{13,9},{2,6},{6,2},{1... | collective-permute-start | bytes 98312 | tf_op jit(solution)/shard_map/ppermute | solution.py:25
  47.9 21.7 %copy-start = (bf16[32,4096]{1,0:T(8,128)(2,1)S(1)}, bf16[32,4096]{1,0:T(8,128)(2,1)}, u32[]{:S(2)}) copy-start(bf16[32,4096]{1,0:T(8,128)(2,1)} %refs_12_.1) | copy-start | bytes 786436

commit v20 on v19

--- a/solution.py
+++ b/solution.py
@@ -81,26 +81,34 @@
     steps = held.shape[0] // block
     firsts = [
         pltpu.make_async_copy(
-            proj_ref.at[:, pl.ds(h * half, half)], proj.at[pl.ds(h * count, count)], sems.at[steps + h]
+            proj_ref.at[:, pl.ds(h * half, half)], proj.at[pl.ds(h * count, count)], sems.at[h]
         )
         for h in range(2)
     ]
 
     def fetch(step):
-        span = pl.ds(pl.multiple_of(step * block, block), block)
-        return pltpu.make_async_copy(rows_ref.at[span], held.at[span], sems.at[step])
+        part = block // 4
+        copies = []
+        for q in range(4):
+            span = pl.ds(pl.multiple_of(step * block + q * part, part), part)
+            copies.append(
+                pltpu.make_async_copy(rows_ref.at[span], held.at[span], sems.at[step * 4 + q + 2])
+            )
+        return copies
 
     for copy in firsts:
         copy.start()
     for step in range(steps):
-        fetch(step).start()
+        for copy in fetch(step):
+            copy.start()
     for copy in firsts:
         copy.wait()
     turned[...] = proj[...].T
 
     @pl.loop(0, steps)
     def _(step):
-        fetch(step).wait()
+        for copy in fetch(step):
+            copy.wait()
         span = pl.ds(pl.multiple_of(step * block, block), block)
         left = jnp.dot(held[span, :half], turned[...], preferred_element_type=jnp.float32)
         right = jnp.dot(held[span, half:], turned[...], preferred_element_type=jnp.float32)
@@ -118,7 +126,7 @@
             pltpu.VMEM(rows.shape, jnp.bfloat16),
             pltpu.VMEM((2 * count, width // 2), jnp.bfloat16),
             pltpu.VMEM((width // 2, 2 * count), jnp.bfloat16),
-            pltpu.SemaphoreType.DMA((rows.shape[0] // block + 2,)),
+            pltpu.SemaphoreType.DMA((rows.shape[0] // block * 4 + 2,)),
         ],
         compiler_params=pltpu.CompilerParams(vmem_limit_bytes=limit * 2**20),
         name=name,

time: 80.7 us -> 80.9 us (level)
  no operation moved by 1% of the time
where the time goes in v20:
time: 80.9 us; the launch traced here: 80.6 us
  blocking collectives  36.7 us (45%)
  Pallas kernels  27.1 us (33%)
  starting transfers between devices  11.9 us (15%)
  waiting for transfers between devices  4.66 us (6%)
    all_to_all x4, blocking collectives, gather(): lax.all_to_all(value, ('dp', 'tensor'), 0, 0, axis_index_groups=[order])  36.7 us
    pallas_call x2, Pallas kernels, features(): pl.pallas_call(functools.partial(stream_kernel, block), out_shape=pltpu.V...  17.1 us
    ppermute x9, starting transfers between devices, swap(): return lax.ppermute(value, axis, [(i, i ^ bit) for i in range(size)])  11.9 us
    pallas_call x3, Pallas kernels, step_cg(): pl.pallas_call(functools.partial(step_kernel, sizes, first, last), out_sh...  5.12 us
    ppermute x9, waiting for transfers between devices, swap(): return lax.ppermute(value, axis, [(i, i ^ bit) for i in range(size)])  4.66 us
    pallas_call x1, Pallas kernels, split_prior(): pl.pallas_call(split_kernel, out_shape=(pltpu.VMEM(prior.shape, jnp.bfloa...  2.32 us
  transfers between devices with their start and end apart: 9, of which 4 were waited for; matrix products, arithmetic and copies ran while one was open for 0% of the time, Pallas kernels for 18%

profile of v20, /device:TPU:0, one launch (start us, length us, event | category | flops | bytes accessed | tf_op | source)
XLA Modules:
  0.0 80.6 jit_solution(9449563209745208235)
XLA Ops:
  0.0 5.1 %in_features.1.refs_0_ = f32[64,512]{1,0:T(8,128)S(1)} custom-call(bf16[512,8192]{1,0:T(8,128)(2,1)} %rows_ref.2, bf16[64,8192]{1,0:T(8,128)(2,1)} %proj_ref.2), custom_call_target="tpu_custom_call" | custom-call | tf_op jit(solution)/shard_map/in_features/pallas_call | solution.py:120
  5.1 3.1 %collective-permute-start.2 = (f32[64,512]{1,0:T(8,128)S(1)}, f32[64,512]{1,0:T(8,128)S(1)}, u32[]{:S(2)}, u32[]{:S(2)}) collective-permute-start(f32[64,512]{1,0:T(8,128)S(1)} %in_features.1.refs_0_), channel_id=1, source_target_pairs={{0,1},{1,0},{2,3},{3,2},{4,5},{5,4},{6,7},{7,6},{8,9},{9,8},{10,11... | collective-permute-start | bytes 393224 | tf_op jit(solution)/shard_map/ppermute | solution.py:25
  8.2 2.5 %collective-permute-start.1 = (f32[64,512]{1,0:T(8,128)S(1)}, f32[64,512]{1,0:T(8,128)S(1)}, u32[]{:S(2)}, u32[]{:S(2)}) collective-permute-start(f32[64,512]{1,0:T(8,128)S(1)} %in_features.1.refs_0_), channel_id=1, source_target_pairs={{0,3},{1,2},{2,1},{3,0},{4,7},{5,6},{6,5},{7,4},{8,11},{9,10},{10,... | collective-permute-start | bytes 393224 | tf_op jit(solution)/shard_map/ppermute | solution.py:25
  10.6 0.1 collective-permute-start
  10.8 12.0 %out_features.1.refs_4_ = f32[64,2048]{1,0:T(8,128)S(1)} custom-call(bf16[2048,7168]{1,0:T(8,128)(2,1)} %rows_ref.3, bf16[64,7168]{1,0:T(8,128)(2,1)} %proj_ref.3), custom_call_target="tpu_custom_call" | custom-call | tf_op jit(solution)/shard_map/out_features/pallas_call | solution.py:120
  22.8 0.4 partial_vectors.1
  23.3 1.9 %collective-permute-start.5 = (f32[2,4096]{1,0:T(2,128)S(1)}, f32[2,4096]{1,0:T(2,128)S(1)}, u32[]{:S(2)}, u32[]{:S(2)}) collective-permute-start(f32[2,4096]{1,0:T(2,128)S(1)} %reshape.7), channel_id=1, source_target_pairs={{0,1},{1,0},{2,3},{3,2},{4,5},{5,4},{6,7},{7,6},{8,9},{9,8},{10,11... | collective-permute-start | bytes 98312 | tf_op jit(solution)/shard_map/ppermute | solution.py:25
  25.2 2.5 %collective-permute-start.4 = (f32[2,4096]{1,0:T(2,128)S(1)}, f32[2,4096]{1,0:T(2,128)S(1)}, u32[]{:S(2)}, u32[]{:S(2)}) collective-permute-start(f32[2,4096]{1,0:T(2,128)S(1)} %reshape.7), channel_id=1, source_target_pairs={{0,3},{1,2},{2,1},{3,0},{4,7},{5,6},{6,5},{7,4},{8,11},{9,10},{10,... | collective-permute-start | bytes 98312 | tf_op jit(solution)/shard_map/ppermute | solution.py:25
  27.7 2.3 %split_prior.1 = (bf16[256,4096]{1,0:T(8,128)(2,1)S(1)}, bf16[256,4096]{1,0:T(8,128)(2,1)S(1)}) custom-call(f32[256,4096]{1,0:T(8,128)} %prior_ref), custom_call_target="tpu_custom_call" | custom-call | tf_op jit(solution)/shard_map/split_prior/pallas_call | solution.py:154
  30.0 0.9 %collective-permute-done.4 = f32[2,4096]{1,0:T(2,128)S(1)} collective-permute-done((f32[2,4096]{1,0:T(2,128)S(1)}, f32[2,4096]{1,0:T(2,128)S(1)}, u32[]{:S(2)}, u32[]{:S(2)}) %collective-permute-start.4) | collective-permute-done | bytes 32800 | tf_op jit(solution)/shard_map/ppermute | solution.py:25
  30.9 1.6 %collective-permute-done.3 = f32[2,4096]{1,0:T(2,128)S(1)} collective-permute-done((f32[2,4096]{1,0:T(2,128)S(1)}, f32[2,4096]{1,0:T(2,128)S(1)}, u32[]{:S(2)}, u32[]{:S(2)}) %collective-permute-start.3) | collective-permute-done | bytes 32800 | tf_op jit(solution)/shard_map/ppermute | solution.py:25
  32.6 1.6 %collective-permute-start.7 = (f32[2,4096]{1,0:T(2,128)S(1)}, f32[2,4096]{1,0:T(2,128)S(1)}, u32[]{:S(2)}, u32[]{:S(2)}) collective-permute-start(f32[2,4096]{1,0:T(2,128)S(1)} %add_add_fusion.refs_0_), channel_id=1, source_target_pairs={{0,8},{4,12},{8,0},{12,4},{1,9},{5,13},{9,1},{13,5},{2,10},{6,14},... | collective-permute-start | bytes 98312 | tf_op jit(solution)/shard_map/ppermute | solution.py:25
  34.2 0.3 collective-permute-start.6
  34.4 1.8 %collective-permute-done.8.refs_3_ = f32[2,4096]{1,0:T(2,128)S(1)} collective-permute-done((f32[2,4096]{1,0:T(2,128)S(1)}, f32[2,4096]{1,0:T(2,128)S(1)}, u32[]{:S(2)}, u32[]{:S(2)}) %collective-permute-start.8) | collective-permute-done | bytes 32800 | tf_op jit(solution)/shard_map/ppermute | solution.py:25
  36.2 0.4 collective-permute-done.7.refs_2_
  36.6 1.5 %cg_start.1 = (f32[8,4096]{1,0:T(8,128)S(1)}, bf16[16,4096]{1,0:T(8,128)(2,1)S(1)}, f32[8,128]{1,0:T(8,128)S(1)}, f32[8,256]{1,0:T(8,128)S(1)}, f32[8,128]{1,0:T(8,128)S(1)}) custom-call(f32[2,4096]{1,0:T(2,128)S(1)} %add_add_fusion.refs_0_, f32[2,4096]{1,0:T(2,128)S(1)} %collective-permute-done.6.refs_1_, f32[2,4096]{1,0:T(2,128)S(1)} %collective-permute-done.7.refs_2_, ...), custom_call_target="tpu_custom_call" | custom-call | tf_op jit(solution)/shard_map/cg_start/pallas_call | solution.py:255
  38.1 10.0 %all_to_all.20.refs_0_ = f32[16,8,256]{2,1,0:T(8,128)S(1)} all-to-all(f32[16,8,256]{2,1,0:T(8,128)S(1)} %broadcast_in_dim.8), channel_id=1, replica_groups={{5,0,1,2,3,4,6,7,8,9,10,11,12,13,14,15},{21,16,17,18,19,20,22,23,24,25,..., dimensions={0} | all-to-all | bytes 262144 | tf_op jit(solution)/shard_map/all_to_all | solution.py:41
  48.1 1.6 %cg_step.3 = (f32[8,256]{1,0:T(8,128)S(1)}, f32[8,128]{1,0:T(8,128)S(1)}, f32[8,256]{1,0:T(8,128)S(1)}, f32[8,4096]{1,0:T(8,128)S(1)}, f32[8,4096]{1,0:T(8,128)S(1)}, /*index=5*/f32[8,4096]{1,0:T(8,128)S(1)}) custom-call(f32[16,8,256]{2,1,0:T(8,128)S(1)} %all_to_all.20.refs_0_, bf16[256,4096]{1,0:T(8,128)(2,1)S(1)} %get-tuple-element.38.refs_4_.refs_1_, ...), custom_call_target="tpu_custom_call" | custom-call | tf_op jit(solution)/shard_map/cg_step/pallas_call | solution.py:328
  49.7 9.2 %all_to_all.21.refs_0_ = f32[16,8,256]{2,1,0:T(8,128)S(1)} all-to-all(f32[16,8,256]{2,1,0:T(8,128)S(1)} %broadcast_in_dim.9), channel_id=1, replica_groups={{5,0,1,2,3,4,6,7,8,9,10,11,12,13,14,15},{21,16,17,18,19,20,22,23,24,25,..., dimensions={0} | all-to-all | bytes 262144 | tf_op jit(solution)/shard_map/all_to_all | solution.py:41
  59.0 1.6 %cg_step.4 = (f32[8,256]{1,0:T(8,128)S(1)}, f32[8,128]{1,0:T(8,128)S(1)}, f32[8,256]{1,0:T(8,128)S(1)}, f32[8,4096]{1,0:T(8,128)S(1)}, f32[8,4096]{1,0:T(8,128)S(1)}, /*index=5*/f32[8,4096]{1,0:T(8,128)S(1)}) custom-call(f32[16,8,256]{2,1,0:T(8,128)S(1)} %all_to_all.21.refs_0_, bf16[256,4096]{1,0:T(8,128)(2,1)S(1)} %get-tuple-element.38.refs_4_.refs_1_, ...), custom_call_target="tpu_custom_call" | custom-call | tf_op jit(solution)/shard_map/cg_step/pallas_call | solution.py:328
  60.6 9.2 %all_to_all.22.refs_0_ = f32[16,8,256]{2,1,0:T(8,128)S(1)} all-to-all(f32[16,8,256]{2,1,0:T(8,128)S(1)} %broadcast_in_dim.10), channel_id=1, replica_groups={{5,0,1,2,3,4,6,7,8,9,10,11,12,13,14,15},{21,16,17,18,19,20,22,23,24,25,..., dimensions={0} | all-to-all | bytes 262144 | tf_op jit(solution)/shard_map/all_to_all | solution.py:41
  69.8 1.9 %cg_step.5 = (f32[8,128]{1,0:T(8,128)S(1)}, f32[8,128]{1,0:T(8,128)S(1)}, f32[8,32]{1,0:T(8,128)S(1)}, f32[8,32]{1,0:T(8,128)S(1)}) custom-call(f32[16,8,256]{2,1,0:T(8,128)S(1)} %all_to_all.22.refs_0_, bf16[256,4096]{1,0:T(8,128)(2,1)S(1)} %get-tuple-element.38.refs_4_.refs_1_, bf16[256,4096]{1,0:T(8,128)(2,1)S(1)} %get-tuple-element.39.refs_5_.refs_2_, ...), custom_call_target="tpu_custom_call" | custom-call | tf_op jit(solution)/shard_map/cg_step/pallas_call | solution.py:328
  71.8 8.2 %all_to_all.23.curvature_ref = f32[16,8,128]{2,1,0:T(8,128)S(1)} all-to-all(f32[16,8,128]{2,1,0:T(8,128)S(1)} %broadcast_in_dim.11), channel_id=1, replica_groups={{5,0,1,2,3,4,6,7,8,9,10,11,12,13,14,15},{21,16,17,18,19,20,22,23,24,25,..., dimensions={0} | all-to-all | bytes 131072 | tf_op jit(solution)/shard_map/all_to_all | solution.py:41
  80.0 0.7 combine.1
  (15 shorter events, 0.3 us)
Async XLA Ops:
  5.1 17.7 %collective-permute-start.2 = (f32[64,512]{1,0:T(8,128)S(1)}, f32[64,512]{1,0:T(8,128)S(1)}, u32[]{:S(2)}, u32[]{:S(2)}) collective-permute-start(f32[64,512]{1,0:T(8,128)S(1)} %in_features.1.refs_0_), channel_id=1, source_target_pairs={{0,1},{1,0},{2,3},{3,2},{4,5},{5,4},{6,7},{7,6},{8,9},{9,8},{10,11... | collective-permute-start | bytes 393224 | tf_op jit(solution)/shard_map/ppermute | solution.py:25
  8.2 14.6 %collective-permute-start.1 = (f32[64,512]{1,0:T(8,128)S(1)}, f32[64,512]{1,0:T(8,128)S(1)}, u32[]{:S(2)}, u32[]{:S(2)}) collective-permute-start(f32[64,512]{1,0:T(8,128)S(1)} %in_features.1.refs_0_), channel_id=1, source_target_pairs={{0,3},{1,2},{2,1},{3,0},{4,7},{5,6},{6,5},{7,4},{8,11},{9,10},{10,... | collective-permute-start | bytes 393224 | tf_op jit(solution)/shard_map/ppermute | solution.py:25
  10.6 12.2 %collective-permute-start = (f32[64,512]{1,0:T(8,128)S(1)}, f32[64,512]{1,0:T(8,128)S(1)}, u32[]{:S(2)}, u32[]{:S(2)}) collective-permute-start(f32[64,512]{1,0:T(8,128)S(1)} %in_features.1.refs_0_), channel_id=1, source_target_pairs={{0,2},{1,3},{2,0},{3,1},{4,6},{5,7},{6,4},{7,5},{8,10},{9,11},{10,... | collective-permute-start | bytes 393224 | tf_op jit(solution)/shard_map/ppermute | solution.py:25
  23.3 6.7 %collective-permute-start.5 = (f32[2,4096]{1,0:T(2,128)S(1)}, f32[2,4096]{1,0:T(2,128)S(1)}, u32[]{:S(2)}, u32[]{:S(2)}) collective-permute-start(f32[2,4096]{1,0:T(2,128)S(1)} %reshape.7), channel_id=1, source_target_pairs={{0,1},{1,0},{2,3},{3,2},{4,5},{5,4},{6,7},{7,6},{8,9},{9,8},{10,11... | collective-permute-start | bytes 98312 | tf_op jit(solution)/shard_map/ppermute | solution.py:25
  25.2 5.7 %collective-permute-start.4 = (f32[2,4096]{1,0:T(2,128)S(1)}, f32[2,4096]{1,0:T(2,128)S(1)}, u32[]{:S(2)}, u32[]{:S(2)}) collective-permute-start(f32[2,4096]{1,0:T(2,128)S(1)} %reshape.7), channel_id=1, source_target_pairs={{0,3},{1,2},{2,1},{3,0},{4,7},{5,6},{6,5},{7,4},{8,11},{9,10},{10,... | collective-permute-start | bytes 98312 | tf_op jit(solution)/shard_map/ppermute | solution.py:25
  27.7 4.8 %collective-permute-start.3 = (f32[2,4096]{1,0:T(2,128)S(1)}, f32[2,4096]{1,0:T(2,128)S(1)}, u32[]{:S(2)}, u32[]{:S(2)}) collective-permute-start(f32[2,4096]{1,0:T(2,128)S(1)} %reshape.7), channel_id=1, source_target_pairs={{0,2},{1,3},{2,0},{3,1},{4,6},{5,7},{6,4},{7,5},{8,10},{9,11},{10,... | collective-permute-start | bytes 98312 | tf_op jit(solution)/shard_map/ppermute | solution.py:25
  32.5 3.7 %collective-permute-start.8 = (f32[2,4096]{1,0:T(2,128)S(1)}, f32[2,4096]{1,0:T(2,128)S(1)}, u32[]{:S(2)}, u32[]{:S(2)}) collective-permute-start(f32[2,4096]{1,0:T(2,128)S(1)} %add_add_fusion.refs_0_), channel_id=1, source_target_pairs={{0,12},{4,8},{8,4},{12,0},{1,13},{5,9},{9,5},{13,1},{2,14},{6,10},... | collective-permute-start | bytes 98312 | tf_op jit(solution)/shard_map/ppermute | solution.py:25
  32.6 4.0 %collective-permute-start.7 = (f32[2,4096]{1,0:T(2,128)S(1)}, f32[2,4096]{1,0:T(2,128)S(1)}, u32[]{:S(2)}, u32[]{:S(2)}) collective-permute-start(f32[2,4096]{1,0:T(2,128)S(1)} %add_add_fusion.refs_0_), channel_id=1, source_target_pairs={{0,8},{4,12},{8,0},{12,4},{1,9},{5,13},{9,1},{13,5},{2,10},{6,14},... | collective-permute-start | bytes 98312 | tf_op jit(solution)/shard_map/ppermute | solution.py:25
  34.2 2.5 %collective-permute-start.6 = (f32[2,4096]{1,0:T(2,128)S(1)}, f32[2,4096]{1,0:T(2,128)S(1)}, u32[]{:S(2)}, u32[]{:S(2)}) collective-permute-start(f32[2,4096]{1,0:T(2,128)S(1)} %add_add_fusion.refs_0_), channel_id=1, source_target_pairs={{0,4},{4,0},{8,12},{12,8},{1,5},{5,1},{9,13},{13,9},{2,6},{6,2},{1... | collective-permute-start | bytes 98312 | tf_op jit(solution)/shard_map/ppermute | solution.py:25
  48.1 21.7 %copy-start = (bf16[32,4096]{1,0:T(8,128)(2,1)S(1)}, bf16[32,4096]{1,0:T(8,128)(2,1)}, u32[]{:S(2)}) copy-start(bf16[32,4096]{1,0:T(8,128)(2,1)} %refs_12_.1) | copy-start | bytes 786436

commit v21 on v19

--- a/solution.py
+++ b/solution.py
@@ -47,6 +47,17 @@
 
 def direct(value, axis, size, order):
     return [value] + [swap(value, axis, size, k) for k in order[1:]]
+
+
+def shifted(value, axis, size):
+    last, first_ones, last_ones = size - 1, [], []
+    for k in reversed(range(1, size)):
+        pairs = [((i + k) % size, i) for i in range(size)]
+        kept = [pair for pair in pairs if pair[1] != last or k == 1]
+        first_ones.append(lax.ppermute(value, axis, kept))
+        if k > 1:
+            last_ones.append(lax.ppermute(value, axis, pairs[last:]))
+    return [value, *reversed(last_ones), *reversed(first_ones)]
 
 
 def sum_over(value, axis, size):
@@ -154,13 +165,24 @@
     )(in_hbm(prior))
 
 
-def partial_kernel(size, *refs):
-    blocks, (out_ref, part_ref, held) = refs[:size], refs[size:]
+def partial_kernel(size, few, *refs):
+    blocks, (out_ref, part_ref, held) = refs[:-3], refs[-3:]
     me = lax.axis_index("tensor")
     tokens = blocks[0].shape[1]
-    for k, block in zip(order_of(size), blocks):
-        start = pl.multiple_of((me ^ k) * tokens, LANES)
-        held[:, pl.ds(start, tokens)] = block[...]
+
+    def place(k, block):
+        source = lax.rem(me + k, size) if few else me ^ k
+        held[:, pl.ds(pl.multiple_of(source * tokens, LANES), tokens)] = block
+
+    place(0, blocks[0][...])
+    rest = blocks[1:]
+    if few:
+        extra, rest = rest[: size - 2], rest[size - 2 :]
+    for k, block in enumerate(rest, 1):
+        block = block[...]
+        if few and k > 1:
+            block = block + extra[k - 2][...]
+        place(k, block)
     for s in range(part_ref.shape[0]):
         span = slice(s * SEQ, (s + 1) * SEQ)
         outs = pieces_of(out_ref[:, span], 2)
@@ -168,10 +190,10 @@
         part_ref[s] = (sums[:, :R_OUT] + sums[:, R_OUT:]) * (1.0 / SEQ)
 
 
-def partial_vectors(blocks, out_local):
+def partial_vectors(blocks, out_local, size, few):
     seq_count = out_local.shape[1] // SEQ
     return pl.pallas_call(
-        functools.partial(partial_kernel, len(blocks)),
+        functools.partial(partial_kernel, size, few),
         out_shape=F32((seq_count, R_IN, R_OUT)),
         in_specs=[VMEM_SPEC] * (len(blocks) + 1),
         out_specs=VMEM_SPEC,
@@ -347,9 +369,11 @@
 def on_device(dp_size, tensor_size, inputs, in_proj, out_grads, out_proj, prior, queries):
     width = R_IN * R_OUT
     sizes = dp_size, tensor_size
-    in_blocks = direct(features(inputs, in_proj, LANES, 20, "in_features"), "tensor", tensor_size, order_of(tensor_size))
+    in_local = features(inputs, in_proj, LANES, 20, "in_features")
+    few = tensor_size <= FEW
+    in_blocks = shifted(in_local, "tensor", tensor_size) if few else direct(in_local, "tensor", tensor_size, range(tensor_size))
     out_local = features(out_grads, out_proj, 2 * LANES, 44, "out_features")
-    partial = partial_vectors(in_blocks, out_local).reshape(-1, width)
+    partial = partial_vectors(in_blocks, out_local, tensor_size, few).reshape(-1, width)
     prior, partial = lax.optimization_barrier((prior, partial))
     own_vectors = sum_over(partial, "tensor", tensor_size)
     own_vectors, prior_pieces = lax.optimization_barrier((own_vectors, split_prior(prior)))

time: 80.7 us -> 88.1 us (1.092)
  starting transfers between devices: 11.9 us -> 18.6 us
    ppermute x0 -> x5, starting transfers between devices: none -> 12.2 us  [the longest x3 10.8 us: shifted(): first_ones.append(lax.ppermute(value, axis, kept))]
    ppermute x9 -> x6, starting transfers between devices: 11.9 us -> 6.39 us  [swap(): return lax.ppermute(value, axis, [(i, i ^ bit) for i in range(size)])]
    ppermute x9 -> x6, waiting for transfers between devices: 4.66 us -> 4.66 us  [swap(): return lax.ppermute(value, axis, [(i, i ^ bit) for i in range(size)])]
  transfers between devices with their start and end apart: 9 -> 11, of which waited for: 4 -> 4; matrix products, arithmetic and copies ran while one was open for 0% -> 0% of each run, Pallas kernels for 18% -> 16%
where the time goes in v21:
time: 88.1 us; the launch traced here: 87.8 us
  blocking collectives  37.3 us (42%)
  Pallas kernels  26.9 us (31%)
  starting transfers between devices  18.6 us (21%)
  waiting for transfers between devices  4.68 us (5%)
    all_to_all x4, blocking collectives, gather(): lax.all_to_all(value, ('dp', 'tensor'), 0, 0, axis_index_groups=[order])  37.3 us
    pallas_call x2, Pallas kernels, features(): pl.pallas_call(functools.partial(stream_kernel, block), out_shape=pltpu.V...  16.9 us
    ppermute x3, starting transfers between devices, shifted(): first_ones.append(lax.ppermute(value, axis, kept))  10.8 us
    ppermute x6, starting transfers between devices, swap(): return lax.ppermute(value, axis, [(i, i ^ bit) for i in range(size)])  6.39 us
    pallas_call x3, Pallas kernels, step_cg(): pl.pallas_call(functools.partial(step_kernel, sizes, first, last), out_sh...  5.12 us
    ppermute x6, waiting for transfers between devices, swap(): return lax.ppermute(value, axis, [(i, i ^ bit) for i in range(size)])  4.66 us
    pallas_call x1, Pallas kernels, split_prior(): pl.pallas_call(split_kernel, out_shape=(pltpu.VMEM(prior.shape, jnp.bfloa...  2.32 us
  transfers between devices with their start and end apart: 11, of which 4 were waited for; matrix products, arithmetic and copies ran while one was open for 0% of the time, Pallas kernels for 16%

profile of v21, /device:TPU:0, one launch (start us, length us, event | category | flops | bytes accessed | tf_op | source)
XLA Modules:
  0.0 87.8 jit_solution(2815222440580054337)
XLA Ops:
  0.0 5.1 %in_features.1.refs_0_ = f32[64,512]{1,0:T(8,128)S(1)} custom-call(bf16[512,8192]{1,0:T(8,128)(2,1)} %rows_ref.2, bf16[64,8192]{1,0:T(8,128)(2,1)} %proj_ref.2), custom_call_target="tpu_custom_call" | custom-call | tf_op jit(solution)/shard_map/in_features/pallas_call | solution.py:123
  5.1 4.9 %collective-permute-start.4 = (f32[64,512]{1,0:T(8,128)S(1)}, f32[64,512]{1,0:T(8,128)S(1)}, u32[]{:S(2)}, u32[]{:S(2)}) collective-permute-start(f32[64,512]{1,0:T(8,128)S(1)} %in_features.1.refs_0_), channel_id=1, source_target_pairs={{3,0},{0,1},{1,2},{7,4},{4,5},{5,6},{11,8},{8,9},{9,10},{15,12},{1... | collective-permute-start | bytes 393224 | tf_op jit(solution)/shard_map/ppermute | solution.py:57
  10.0 2.3 %collective-permute-start.3 = (f32[64,512]{1,0:T(8,128)S(1)}, f32[64,512]{1,0:T(8,128)S(1)}, u32[]{:S(2)}, u32[]{:S(2)}) collective-permute-start(f32[64,512]{1,0:T(8,128)S(1)} %in_features.1.refs_0_), channel_id=1, source_target_pairs={{2,0},{3,1},{0,2},{6,4},{7,5},{4,6},{10,8},{11,9},{8,10},{14,12},{... | collective-permute-start | bytes 393224 | tf_op jit(solution)/shard_map/ppermute | solution.py:57
  12.3 3.6 %collective-permute-start.2 = (f32[64,512]{1,0:T(8,128)S(1)}, f32[64,512]{1,0:T(8,128)S(1)}, u32[]{:S(2)}, u32[]{:S(2)}) collective-permute-start(f32[64,512]{1,0:T(8,128)S(1)} %in_features.1.refs_0_), channel_id=1, source_target_pairs={{1,0},{2,1},{3,2},{0,3},{5,4},{6,5},{7,6},{4,7},{9,8},{10,9},{11,1... | collective-permute-start | bytes 393224 | tf_op jit(solution)/shard_map/ppermute | solution.py:57
  15.9 0.7 collective-permute-start.1
  16.6 0.7 collective-permute-start
  17.3 11.8 %out_features.1.refs_6_ = f32[64,2048]{1,0:T(8,128)S(1)} custom-call(bf16[2048,7168]{1,0:T(8,128)(2,1)} %rows_ref.3, bf16[64,7168]{1,0:T(8,128)(2,1)} %proj_ref.3), custom_call_target="tpu_custom_call" | custom-call | tf_op jit(solution)/shard_map/out_features/pallas_call | solution.py:123
  29.7 2.9 %collective-permute-start.7 = (f32[2,4096]{1,0:T(2,128)S(1)}, f32[2,4096]{1,0:T(2,128)S(1)}, u32[]{:S(2)}, u32[]{:S(2)}) collective-permute-start(f32[2,4096]{1,0:T(2,128)S(1)} %reshape.7), channel_id=1, source_target_pairs={{0,1},{1,0},{2,3},{3,2},{4,5},{5,4},{6,7},{7,6},{8,9},{9,8},{10,11... | collective-permute-start | bytes 98312 | tf_op jit(solution)/shard_map/ppermute | solution.py:25
  32.6 0.8 collective-permute-start.6
  33.4 0.7 collective-permute-start.5
  34.1 2.3 %split_prior.1 = (bf16[256,4096]{1,0:T(8,128)(2,1)S(1)}, bf16[256,4096]{1,0:T(8,128)(2,1)S(1)}) custom-call(f32[256,4096]{1,0:T(8,128)} %prior_ref), custom_call_target="tpu_custom_call" | custom-call | tf_op jit(solution)/shard_map/split_prior/pallas_call | solution.py:157
  36.5 1.9 %collective-permute-done.6 = f32[2,4096]{1,0:T(2,128)S(1)} collective-permute-done((f32[2,4096]{1,0:T(2,128)S(1)}, f32[2,4096]{1,0:T(2,128)S(1)}, u32[]{:S(2)}, u32[]{:S(2)}) %collective-permute-start.6) | collective-permute-done | bytes 32800 | tf_op jit(solution)/shard_map/ppermute | solution.py:25
  38.4 0.5 collective-permute-done.5
  39.1 1.6 %collective-permute-start.9 = (f32[2,4096]{1,0:T(2,128)S(1)}, f32[2,4096]{1,0:T(2,128)S(1)}, u32[]{:S(2)}, u32[]{:S(2)}) collective-permute-start(f32[2,4096]{1,0:T(2,128)S(1)} %add_add_fusion.refs_0_), channel_id=1, source_target_pairs={{0,8},{4,12},{8,0},{12,4},{1,9},{5,13},{9,1},{13,5},{2,10},{6,14},... | collective-permute-start | bytes 98312 | tf_op jit(solution)/shard_map/ppermute | solution.py:25
  40.9 1.8 %collective-permute-done.10.refs_3_ = f32[2,4096]{1,0:T(2,128)S(1)} collective-permute-done((f32[2,4096]{1,0:T(2,128)S(1)}, f32[2,4096]{1,0:T(2,128)S(1)}, u32[]{:S(2)}, u32[]{:S(2)}) %collective-permute-start.10) | collective-permute-done | bytes 32800 | tf_op jit(solution)/shard_map/ppermute | solution.py:25
  43.1 1.5 %cg_start.1 = (f32[8,4096]{1,0:T(8,128)S(1)}, bf16[16,4096]{1,0:T(8,128)(2,1)S(1)}, f32[8,128]{1,0:T(8,128)S(1)}, f32[8,256]{1,0:T(8,128)S(1)}, f32[8,128]{1,0:T(8,128)S(1)}) custom-call(f32[2,4096]{1,0:T(2,128)S(1)} %add_add_fusion.refs_0_, f32[2,4096]{1,0:T(2,128)S(1)} %collective-permute-done.8.refs_1_, f32[2,4096]{1,0:T(2,128)S(1)} %collective-permute-done.9.refs_2_, ...), custom_call_target="tpu_custom_call" | custom-call | tf_op jit(solution)/shard_map/cg_start/pallas_call | solution.py:269
  44.6 10.7 %all_to_all.20.refs_0_ = f32[16,8,256]{2,1,0:T(8,128)S(1)} all-to-all(f32[16,8,256]{2,1,0:T(8,128)S(1)} %broadcast_in_dim.8), channel_id=1, replica_groups={{5,0,1,2,3,4,6,7,8,9,10,11,12,13,14,15},{21,16,17,18,19,20,22,23,24,25,..., dimensions={0} | all-to-all | bytes 262144 | tf_op jit(solution)/shard_map/all_to_all | solution.py:41
  55.3 1.6 %cg_step.3 = (f32[8,256]{1,0:T(8,128)S(1)}, f32[8,128]{1,0:T(8,128)S(1)}, f32[8,256]{1,0:T(8,128)S(1)}, f32[8,4096]{1,0:T(8,128)S(1)}, f32[8,4096]{1,0:T(8,128)S(1)}, /*index=5*/f32[8,4096]{1,0:T(8,128)S(1)}) custom-call(f32[16,8,256]{2,1,0:T(8,128)S(1)} %all_to_all.20.refs_0_, bf16[256,4096]{1,0:T(8,128)(2,1)S(1)} %get-tuple-element.38.refs_4_.refs_1_, ...), custom_call_target="tpu_custom_call" | custom-call | tf_op jit(solution)/shard_map/cg_step/pallas_call | solution.py:342
  56.9 9.2 %all_to_all.21.refs_0_ = f32[16,8,256]{2,1,0:T(8,128)S(1)} all-to-all(f32[16,8,256]{2,1,0:T(8,128)S(1)} %broadcast_in_dim.9), channel_id=1, replica_groups={{5,0,1,2,3,4,6,7,8,9,10,11,12,13,14,15},{21,16,17,18,19,20,22,23,24,25,..., dimensions={0} | all-to-all | bytes 262144 | tf_op jit(solution)/shard_map/all_to_all | solution.py:41
  66.1 1.6 %cg_step.4 = (f32[8,256]{1,0:T(8,128)S(1)}, f32[8,128]{1,0:T(8,128)S(1)}, f32[8,256]{1,0:T(8,128)S(1)}, f32[8,4096]{1,0:T(8,128)S(1)}, f32[8,4096]{1,0:T(8,128)S(1)}, /*index=5*/f32[8,4096]{1,0:T(8,128)S(1)}) custom-call(f32[16,8,256]{2,1,0:T(8,128)S(1)} %all_to_all.21.refs_0_, bf16[256,4096]{1,0:T(8,128)(2,1)S(1)} %get-tuple-element.38.refs_4_.refs_1_, ...), custom_call_target="tpu_custom_call" | custom-call | tf_op jit(solution)/shard_map/cg_step/pallas_call | solution.py:342
  67.7 9.2 %all_to_all.22.refs_0_ = f32[16,8,256]{2,1,0:T(8,128)S(1)} all-to-all(f32[16,8,256]{2,1,0:T(8,128)S(1)} %broadcast_in_dim.10), channel_id=1, replica_groups={{5,0,1,2,3,4,6,7,8,9,10,11,12,13,14,15},{21,16,17,18,19,20,22,23,24,25,..., dimensions={0} | all-to-all | bytes 262144 | tf_op jit(solution)/shard_map/all_to_all | solution.py:41
  77.0 1.9 %cg_step.5 = (f32[8,128]{1,0:T(8,128)S(1)}, f32[8,128]{1,0:T(8,128)S(1)}, f32[8,32]{1,0:T(8,128)S(1)}, f32[8,32]{1,0:T(8,128)S(1)}) custom-call(f32[16,8,256]{2,1,0:T(8,128)S(1)} %all_to_all.22.refs_0_, bf16[256,4096]{1,0:T(8,128)(2,1)S(1)} %get-tuple-element.38.refs_4_.refs_1_, bf16[256,4096]{1,0:T(8,128)(2,1)S(1)} %get-tuple-element.39.refs_5_.refs_2_, ...), custom_call_target="tpu_custom_call" | custom-call | tf_op jit(solution)/shard_map/cg_step/pallas_call | solution.py:342
  78.9 8.2 %all_to_all.23.curvature_ref = f32[16,8,128]{2,1,0:T(8,128)S(1)} all-to-all(f32[16,8,128]{2,1,0:T(8,128)S(1)} %broadcast_in_dim.11), channel_id=1, replica_groups={{5,0,1,2,3,4,6,7,8,9,10,11,12,13,14,15},{21,16,17,18,19,20,22,23,24,25,..., dimensions={0} | all-to-all | bytes 131072 | tf_op jit(solution)/shard_map/all_to_all | solution.py:41
  87.1 0.7 combine.1
  (19 shorter events, 1.4 us)
Async XLA Ops:
  5.1 24.0 %collective-permute-start.4 = (f32[64,512]{1,0:T(8,128)S(1)}, f32[64,512]{1,0:T(8,128)S(1)}, u32[]{:S(2)}, u32[]{:S(2)}) collective-permute-start(f32[64,512]{1,0:T(8,128)S(1)} %in_features.1.refs_0_), channel_id=1, source_target_pairs={{3,0},{0,1},{1,2},{7,4},{4,5},{5,6},{11,8},{8,9},{9,10},{15,12},{1... | collective-permute-start | bytes 393224 | tf_op jit(solution)/shard_map/ppermute | solution.py:57
  10.0 19.1 %collective-permute-start.3 = (f32[64,512]{1,0:T(8,128)S(1)}, f32[64,512]{1,0:T(8,128)S(1)}, u32[]{:S(2)}, u32[]{:S(2)}) collective-permute-start(f32[64,512]{1,0:T(8,128)S(1)} %in_features.1.refs_0_), channel_id=1, source_target_pairs={{2,0},{3,1},{0,2},{6,4},{7,5},{4,6},{10,8},{11,9},{8,10},{14,12},{... | collective-permute-start | bytes 393224 | tf_op jit(solution)/shard_map/ppermute | solution.py:57
  12.3 16.8 %collective-permute-start.2 = (f32[64,512]{1,0:T(8,128)S(1)}, f32[64,512]{1,0:T(8,128)S(1)}, u32[]{:S(2)}, u32[]{:S(2)}) collective-permute-start(f32[64,512]{1,0:T(8,128)S(1)} %in_features.1.refs_0_), channel_id=1, source_target_pairs={{1,0},{2,1},{3,2},{0,3},{5,4},{6,5},{7,6},{4,7},{9,8},{10,9},{11,1... | collective-permute-start | bytes 393224 | tf_op jit(solution)/shard_map/ppermute | solution.py:57
  15.9 13.2 %collective-permute-start.1 = (f32[64,512]{1,0:T(8,128)S(1)}, f32[64,512]{1,0:T(8,128)S(1)}, u32[]{:S(2)}, u32[]{:S(2)}) collective-permute-start(f32[64,512]{1,0:T(8,128)S(1)} %in_features.1.refs_0_), channel_id=1, source_target_pairs={{2,3},{6,7},{10,11},{14,15},{18,19},{22,23},{26,27},{30,31}} | collective-permute-start | bytes 393224 | tf_op jit(solution)/shard_map/ppermute | solution.py:59
  16.6 12.6 %collective-permute-start = (f32[64,512]{1,0:T(8,128)S(1)}, f32[64,512]{1,0:T(8,128)S(1)}, u32[]{:S(2)}, u32[]{:S(2)}) collective-permute-start(f32[64,512]{1,0:T(8,128)S(1)} %in_features.1.refs_0_), channel_id=1, source_target_pairs={{1,3},{5,7},{9,11},{13,15},{17,19},{21,23},{25,27},{29,31}} | collective-permute-start | bytes 393224 | tf_op jit(solution)/shard_map/ppermute | solution.py:59
  29.7 6.8 %collective-permute-start.7 = (f32[2,4096]{1,0:T(2,128)S(1)}, f32[2,4096]{1,0:T(2,128)S(1)}, u32[]{:S(2)}, u32[]{:S(2)}) collective-permute-start(f32[2,4096]{1,0:T(2,128)S(1)} %reshape.7), channel_id=1, source_target_pairs={{0,1},{1,0},{2,3},{3,2},{4,5},{5,4},{6,7},{7,6},{8,9},{9,8},{10,11... | collective-permute-start | bytes 98312 | tf_op jit(solution)/shard_map/ppermute | solution.py:25
  32.6 5.8 %collective-permute-start.6 = (f32[2,4096]{1,0:T(2,128)S(1)}, f32[2,4096]{1,0:T(2,128)S(1)}, u32[]{:S(2)}, u32[]{:S(2)}) collective-permute-start(f32[2,4096]{1,0:T(2,128)S(1)} %reshape.7), channel_id=1, source_target_pairs={{0,3},{1,2},{2,1},{3,0},{4,7},{5,6},{6,5},{7,4},{8,11},{9,10},{10,... | collective-permute-start | bytes 98312 | tf_op jit(solution)/shard_map/ppermute | solution.py:25
  33.4 5.5 %collective-permute-start.5 = (f32[2,4096]{1,0:T(2,128)S(1)}, f32[2,4096]{1,0:T(2,128)S(1)}, u32[]{:S(2)}, u32[]{:S(2)}) collective-permute-start(f32[2,4096]{1,0:T(2,128)S(1)} %reshape.7), channel_id=1, source_target_pairs={{0,2},{1,3},{2,0},{3,1},{4,6},{5,7},{6,4},{7,5},{8,10},{9,11},{10,... | collective-permute-start | bytes 98312 | tf_op jit(solution)/shard_map/ppermute | solution.py:25
  39.0 3.7 %collective-permute-start.10 = (f32[2,4096]{1,0:T(2,128)S(1)}, f32[2,4096]{1,0:T(2,128)S(1)}, u32[]{:S(2)}, u32[]{:S(2)}) collective-permute-start(f32[2,4096]{1,0:T(2,128)S(1)} %add_add_fusion.refs_0_), channel_id=1, source_target_pairs={{0,12},{4,8},{8,4},{12,0},{1,13},{5,9},{9,5},{13,1},{2,14},{6,10},... | collective-permute-start | bytes 98312 | tf_op jit(solution)/shard_map/ppermute | solution.py:25
  39.1 4.0 %collective-permute-start.9 = (f32[2,4096]{1,0:T(2,128)S(1)}, f32[2,4096]{1,0:T(2,128)S(1)}, u32[]{:S(2)}, u32[]{:S(2)}) collective-permute-start(f32[2,4096]{1,0:T(2,128)S(1)} %add_add_fusion.refs_0_), channel_id=1, source_target_pairs={{0,8},{4,12},{8,0},{12,4},{1,9},{5,13},{9,1},{13,5},{2,10},{6,14},... | collective-permute-start | bytes 98312 | tf_op jit(solution)/shard_map/ppermute | solution.py:25
  40.6 2.5 %collective-permute-start.8 = (f32[2,4096]{1,0:T(2,128)S(1)}, f32[2,4096]{1,0:T(2,128)S(1)}, u32[]{:S(2)}, u32[]{:S(2)}) collective-permute-start(f32[2,4096]{1,0:T(2,128)S(1)} %add_add_fusion.refs_0_), channel_id=1, source_target_pairs={{0,4},{4,0},{8,12},{12,8},{1,5},{5,1},{9,13},{13,9},{2,6},{6,2},{1... | collective-permute-start | bytes 98312 | tf_op jit(solution)/shard_map/ppermute | solution.py:25
  55.3 21.7 %copy-start = (bf16[32,4096]{1,0:T(8,128)(2,1)S(1)}, bf16[32,4096]{1,0:T(8,128)(2,1)}, u32[]{:S(2)}) copy-start(bf16[32,4096]{1,0:T(8,128)(2,1)} %refs_12_.1) | copy-start | bytes 786436

commit v22 on v19

--- a/solution.py
+++ b/solution.py
@@ -125,7 +125,7 @@
     )(in_hbm(rows), in_hbm(proj))
 
 
-def split_kernel(prior_ref, upper_ref, lower_ref, held, sems):
+def split_kernel(prior_ref, queries_ref, upper_ref, lower_ref, turned_ref, held, sems):
     chunk = held.shape[1] // sems.shape[0]
     spans = [pl.ds(c * chunk, chunk) for c in range(sems.shape[0])]
     copies = [
@@ -134,6 +134,7 @@
     ]
     for copy in copies:
         copy.start()
+    turned_ref[...] = queries_ref[...].T
     for copy, span in zip(copies, spans):
         copy.wait()
         block = held[:, span]
@@ -142,16 +143,20 @@
         lower_ref[:, span] = (block - upper.astype(jnp.float32)).astype(jnp.bfloat16)
 
 
-def split_prior(prior):
+def split_prior(prior, queries):
     return pl.pallas_call(
         split_kernel,
-        out_shape=(pltpu.VMEM(prior.shape, jnp.bfloat16),) * 2,
-        in_specs=[ANY_SPEC],
-        out_specs=(VMEM_SPEC,) * 2,
+        out_shape=(
+            pltpu.VMEM(prior.shape, jnp.bfloat16),
+            pltpu.VMEM(prior.shape, jnp.bfloat16),
+            pltpu.VMEM(queries.shape[::-1], jnp.bfloat16),
+        ),
+        in_specs=[ANY_SPEC, VMEM_SPEC],
+        out_specs=(VMEM_SPEC,) * 3,
         scratch_shapes=[pltpu.VMEM(prior.shape, jnp.float32), pltpu.SemaphoreType.DMA((8,))],
         compiler_params=PARAMS,
         name="split_prior",
-    )(in_hbm(prior))
+    )(in_hbm(prior), queries)
 
 
 def partial_kernel(size, *refs):
@@ -206,14 +211,16 @@
     return total
 
 
-def apply_fisher(pieces, vectors_ref, vector_pieces, upper_ref, lower_ref, me):
+def apply_fisher(x, vectors_ref, upper_ref, lower_ref, me):
     seqs = vectors_ref.shape[0]
+    pieces = pieces_of(x, 3)
     applied = dot_pieces(pieces, upper_ref[...], seqs)
     applied = applied + dot_pieces(pieces[: 2 * seqs], lower_ref[...], seqs)
-    weights = dot_pieces(pieces, vector_pieces, seqs)
-    weights = (weights[:, :seqs] + weights[:, seqs:]) * (1.0 / seqs)
     own = own_columns(vectors_ref, me, upper_ref.shape[0])
-    return applied + jnp.dot(weights, own, precision=HIGHEST, preferred_element_type=jnp.float32)
+    for s in range(seqs):
+        weight = row_sum(x * vectors_ref[s : s + 1, :]) * (1.0 / seqs)
+        applied = applied + weight * own[s : s + 1, :]
+    return applied
 
 
 def flat_index(tensor_size):
@@ -222,33 +229,29 @@
 
 def start_kernel(size, tensor_size, *refs):
     pieces, refs = refs[:size], refs[size:]
-    upper_ref, lower_ref, vectors_ref, vector_pieces_ref, scale_ref, applied_ref, norm_ref, held = refs
+    upper_ref, lower_ref, vectors_ref, scale_ref, applied_ref, norm_ref, held = refs
     dp = lax.axis_index("dp")
     for k, piece in enumerate(pieces):
         held[dp ^ k] = piece[...]
     vectors = jnp.concatenate([held[k] for k in range(size)], axis=0)
     vectors_ref[...] = vectors
-    split = pieces_of(vectors, 3)
-    vector_pieces = split[: 2 * vectors.shape[0]]
-    vector_pieces_ref[...] = vector_pieces
     norm = jnp.broadcast_to(row_sum(vectors * vectors), norm_ref.shape)
     norm_ref[...] = norm
     spread = jnp.sum(norm, axis=0, keepdims=True) * (1.0 / vectors.shape[0])
     scale_ref[...] = jnp.broadcast_to(1.0 / (1.0 + spread), scale_ref.shape)
     me = flat_index(tensor_size)
-    applied_ref[...] = apply_fisher(split, vectors_ref, vector_pieces, upper_ref, lower_ref, me)
+    applied_ref[...] = apply_fisher(vectors, vectors_ref, upper_ref, lower_ref, me)
 
 
 def start_cg(pieces, prior_pieces, tensor_size):
     size, seqs = len(pieces), len(pieces) * pieces[0].shape[0]
     rows, width = prior_pieces[0].shape
-    vector_pieces = jax.ShapeDtypeStruct((2 * seqs, width), jnp.bfloat16)
     column = F32((seqs, LANES))
     return pl.pallas_call(
         functools.partial(start_kernel, size, tensor_size),
-        out_shape=(F32((seqs, width)), vector_pieces, column, F32((seqs, rows)), column),
+        out_shape=(F32((seqs, width)), column, F32((seqs, rows)), column),
         in_specs=[VMEM_SPEC] * (size + 2),
-        out_specs=(VMEM_SPEC,) * 5,
+        out_specs=(VMEM_SPEC,) * 4,
         scratch_shapes=[pltpu.VMEM((size,) + pieces[0].shape, jnp.float32)],
         compiler_params=PARAMS,
         name="cg_start",
@@ -256,9 +259,8 @@
 
 
 def step_kernel(sizes, first, last, *refs):
-    blocks_ref, upper_ref, lower_ref, vectors_ref, vector_pieces_ref, scale_ref = refs[:6]
-    norm_ref, fisher_direction_ref = refs[6:8]
-    refs = refs[8:]
+    blocks_ref, upper_ref, lower_ref, vectors_ref, scale_ref, norm_ref, fisher_direction_ref = refs[:7]
+    refs = refs[7:]
     if not first:
         fisher_residual_ref, direction_ref, residual_ref, solution_ref = refs[:4]
         refs = refs[4:]
@@ -272,9 +274,7 @@
         held[:, k * rows : (k + 1) * rows] = blocks_ref[i]
     applied = held[...]
     scale = scale_ref[...][:, :1]
-    twice = apply_fisher(
-        pieces_of(scale * applied, 3), vectors_ref, vector_pieces_ref[...], upper_ref, lower_ref, me
-    )
+    twice = apply_fisher(scale * applied, vectors_ref, upper_ref, lower_ref, me)
     direction = vectors_ref[...] if first else direction_ref[...]
     residual = direction if first else residual_ref[...]
     norm = norm_ref[...][:, :1]
@@ -296,7 +296,8 @@
         curvature_out[...] = jnp.broadcast_to(row_sum(own * fisher_direction), curvature_out.shape)
         seqs = direction.shape[0]
         solved = jnp.concatenate([solution, direction], axis=0)
-        scores = dot_pieces(pieces_of(solved, 3), queries_ref[...], 2 * seqs)
+        parts = jnp.dot(pieces_of(solved, 3), queries_ref[...], preferred_element_type=jnp.float32)
+        scores = parts[: 2 * seqs] + parts[2 * seqs : 4 * seqs] + parts[4 * seqs :]
         solved_out[...] = scores[:seqs]
         along_out[...] = scores[seqs:]
     else:
@@ -315,7 +316,7 @@
     out_shape = (rows, column, rows, whole, whole, whole)
     if last:
         operands.append(queries)
-        scores = F32((whole.shape[0], queries.shape[0]))
+        scores = F32((whole.shape[0], queries.shape[1]))
         out_shape = (column, column, scores, scores)
     return pl.pallas_call(
         functools.partial(step_kernel, sizes, first, last),
@@ -352,11 +353,11 @@
     partial = partial_vectors(in_blocks, out_local).reshape(-1, width)
     prior, partial = lax.optimization_barrier((prior, partial))
     own_vectors = sum_over(partial, "tensor", tensor_size)
-    own_vectors, prior_pieces = lax.optimization_barrier((own_vectors, split_prior(prior)))
+    own_vectors, prior_pieces = lax.optimization_barrier((own_vectors, split_prior(prior, queries)))
     pieces = direct(own_vectors, "dp", dp_size, range(dp_size))
-    prior_pieces = [in_vmem(piece) for piece in prior_pieces]
-    vectors, vector_pieces, scale, applied_rows, norm = start_cg(pieces, prior_pieces, tensor_size)
-    fixed = (*prior_pieces, vectors, vector_pieces, scale)
+    *prior_pieces, queries = [in_vmem(piece) for piece in prior_pieces]
+    vectors, scale, applied_rows, norm = start_cg(pieces, prior_pieces, tensor_size)
+    fixed = (*prior_pieces, vectors, scale)
     state = [applied_rows]
     for iteration in range(1, ITERS - 1):
         blocks = gather(state[0], sizes)

time: 80.7 us -> 79.3 us (0.983)
  Pallas kernels: 26.8 us -> 25.7 us
    pallas_call x3, Pallas kernels: 5.12 us -> 3.96 us  [step_cg(): pl.pallas_call(functools.partial(step_kernel, sizes, first, last), out_sh...]
where the time goes in v22:
time: 79.3 us; the launch traced here: 79 us
  blocking collectives  36.6 us (46%)
  Pallas kernels  25.7 us (32%)
  starting transfers between devices  11.9 us (15%)
  waiting for transfers between devices  4.42 us (6%)
    all_to_all x4, blocking collectives, gather(): lax.all_to_all(value, ('dp', 'tensor'), 0, 0, axis_index_groups=[order])  36.6 us
    pallas_call x2, Pallas kernels, features(): pl.pallas_call(functools.partial(stream_kernel, block), out_shape=pltpu.V...  16.9 us
    ppermute x9, starting transfers between devices, swap(): return lax.ppermute(value, axis, [(i, i ^ bit) for i in range(size)])  11.9 us
    ppermute x9, waiting for transfers between devices, swap(): return lax.ppermute(value, axis, [(i, i ^ bit) for i in range(size)])  4.42 us
    pallas_call x3, Pallas kernels, step_cg(): pl.pallas_call(functools.partial(step_kernel, sizes, first, last), out_sh...  3.96 us
    pallas_call x1, Pallas kernels, split_prior(): pl.pallas_call(split_kernel, out_shape=(pltpu.VMEM(prior.shape, jnp.bfloa...  2.56 us
  transfers between devices with their start and end apart: 9, of which 4 were waited for; matrix products, arithmetic and copies ran while one was open for 0% of the time, Pallas kernels for 18%

profile of v22, /device:TPU:0, one launch (start us, length us, event | category | flops | bytes accessed | tf_op | source)
XLA Modules:
  0.0 79.0 jit_solution(18391784908969772649)
XLA Ops:
  0.0 5.1 %in_features.1.refs_0_ = f32[64,512]{1,0:T(8,128)S(1)} custom-call(bf16[512,8192]{1,0:T(8,128)(2,1)} %rows_ref.2, bf16[64,8192]{1,0:T(8,128)(2,1)} %proj_ref.2), custom_call_target="tpu_custom_call" | custom-call | tf_op jit(solution)/shard_map/in_features/pallas_call | solution.py:112
  5.1 3.1 %collective-permute-start.2 = (f32[64,512]{1,0:T(8,128)S(1)}, f32[64,512]{1,0:T(8,128)S(1)}, u32[]{:S(2)}, u32[]{:S(2)}) collective-permute-start(f32[64,512]{1,0:T(8,128)S(1)} %in_features.1.refs_0_), channel_id=1, source_target_pairs={{0,1},{1,0},{2,3},{3,2},{4,5},{5,4},{6,7},{7,6},{8,9},{9,8},{10,11... | collective-permute-start | bytes 393224 | tf_op jit(solution)/shard_map/ppermute | solution.py:25
  8.2 2.5 %collective-permute-start.1 = (f32[64,512]{1,0:T(8,128)S(1)}, f32[64,512]{1,0:T(8,128)S(1)}, u32[]{:S(2)}, u32[]{:S(2)}) collective-permute-start(f32[64,512]{1,0:T(8,128)S(1)} %in_features.1.refs_0_), channel_id=1, source_target_pairs={{0,3},{1,2},{2,1},{3,0},{4,7},{5,6},{6,5},{7,4},{8,11},{9,10},{10,... | collective-permute-start | bytes 393224 | tf_op jit(solution)/shard_map/ppermute | solution.py:25
  10.6 0.1 collective-permute-start
  10.8 11.8 %out_features.1.refs_4_ = f32[64,2048]{1,0:T(8,128)S(1)} custom-call(bf16[2048,7168]{1,0:T(8,128)(2,1)} %rows_ref.3, bf16[64,7168]{1,0:T(8,128)(2,1)} %proj_ref.3), custom_call_target="tpu_custom_call" | custom-call | tf_op jit(solution)/shard_map/out_features/pallas_call | solution.py:112
  22.6 0.4 partial_vectors.1
  23.1 1.9 %collective-permute-start.5 = (f32[2,4096]{1,0:T(2,128)S(1)}, f32[2,4096]{1,0:T(2,128)S(1)}, u32[]{:S(2)}, u32[]{:S(2)}) collective-permute-start(f32[2,4096]{1,0:T(2,128)S(1)} %reshape.7), channel_id=1, source_target_pairs={{0,1},{1,0},{2,3},{3,2},{4,5},{5,4},{6,7},{7,6},{8,9},{9,8},{10,11... | collective-permute-start | bytes 98312 | tf_op jit(solution)/shard_map/ppermute | solution.py:25
  25.0 2.5 %collective-permute-start.4 = (f32[2,4096]{1,0:T(2,128)S(1)}, f32[2,4096]{1,0:T(2,128)S(1)}, u32[]{:S(2)}, u32[]{:S(2)}) collective-permute-start(f32[2,4096]{1,0:T(2,128)S(1)} %reshape.7), channel_id=1, source_target_pairs={{0,3},{1,2},{2,1},{3,0},{4,7},{5,6},{6,5},{7,4},{8,11},{9,10},{10,... | collective-permute-start | bytes 98312 | tf_op jit(solution)/shard_map/ppermute | solution.py:25
  27.5 2.6 %split_prior.1 = (bf16[256,4096]{1,0:T(8,128)(2,1)S(1)}, bf16[256,4096]{1,0:T(8,128)(2,1)S(1)}, bf16[4096,32]{1,0:T(8,128)(2,1)S(1)}) custom-call(f32[256,4096]{1,0:T(8,128)} %prior_ref, bf16[32,4096]{1,0:T(8,128)(2,1)S(1)} %copy-done), custom_call_target="tpu_custom_call" | custom-call | tf_op jit(solution)/shard_map/split_prior/pallas_call | solution.py:147
  30.0 0.7 collective-permute-done.4
  30.7 1.6 %collective-permute-done.3 = f32[2,4096]{1,0:T(2,128)S(1)} collective-permute-done((f32[2,4096]{1,0:T(2,128)S(1)}, f32[2,4096]{1,0:T(2,128)S(1)}, u32[]{:S(2)}, u32[]{:S(2)}) %collective-permute-start.3) | collective-permute-done | bytes 32800 | tf_op jit(solution)/shard_map/ppermute | solution.py:25
  32.4 1.6 %collective-permute-start.7 = (f32[2,4096]{1,0:T(2,128)S(1)}, f32[2,4096]{1,0:T(2,128)S(1)}, u32[]{:S(2)}, u32[]{:S(2)}) collective-permute-start(f32[2,4096]{1,0:T(2,128)S(1)} %add_add_fusion.refs_0_), channel_id=1, source_target_pairs={{0,8},{4,12},{8,0},{12,4},{1,9},{5,13},{9,1},{13,5},{2,10},{6,14},... | collective-permute-start | bytes 98312 | tf_op jit(solution)/shard_map/ppermute | solution.py:25
  33.9 0.3 collective-permute-start.6
  34.2 1.8 %collective-permute-done.8.refs_3_ = f32[2,4096]{1,0:T(2,128)S(1)} collective-permute-done((f32[2,4096]{1,0:T(2,128)S(1)}, f32[2,4096]{1,0:T(2,128)S(1)}, u32[]{:S(2)}, u32[]{:S(2)}) %collective-permute-start.8) | collective-permute-done | bytes 32800 | tf_op jit(solution)/shard_map/ppermute | solution.py:25
  36.0 0.4 collective-permute-done.7.refs_2_
  36.4 1.3 %cg_start.1 = (f32[8,4096]{1,0:T(8,128)S(1)}, f32[8,128]{1,0:T(8,128)S(1)}, f32[8,256]{1,0:T(8,128)S(1)}, f32[8,128]{1,0:T(8,128)S(1)}) custom-call(f32[2,4096]{1,0:T(2,128)S(1)} %add_add_fusion.refs_0_, f32[2,4096]{1,0:T(2,128)S(1)} %collective-permute-done.6.refs_1_, f32[2,4096]{1,0:T(2,128)S(1)} %collective-permute-done.7.refs_2_, ...), custom_call_target="tpu_custom_call" | custom-call | tf_op jit(solution)/shard_map/cg_start/pallas_call | solution.py:250
  37.7 10.0 %all_to_all.20.refs_0_ = f32[16,8,256]{2,1,0:T(8,128)S(1)} all-to-all(f32[16,8,256]{2,1,0:T(8,128)S(1)} %broadcast_in_dim.8), channel_id=1, replica_groups={{5,0,1,2,3,4,6,7,8,9,10,11,12,13,14,15},{21,16,17,18,19,20,22,23,24,25,..., dimensions={0} | all-to-all | bytes 262144 | tf_op jit(solution)/shard_map/all_to_all | solution.py:41
  47.7 1.3 %cg_step.3 = (f32[8,256]{1,0:T(8,128)S(1)}, f32[8,128]{1,0:T(8,128)S(1)}, f32[8,256]{1,0:T(8,128)S(1)}, f32[8,4096]{1,0:T(8,128)S(1)}, f32[8,4096]{1,0:T(8,128)S(1)}, /*index=5*/f32[8,4096]{1,0:T(8,128)S(1)}) custom-call(f32[16,8,256]{2,1,0:T(8,128)S(1)} %all_to_all.20.refs_0_, bf16[256,4096]{1,0:T(8,128)(2,1)S(1)} %get-tuple-element.40.refs_4_.refs_1_, ...), custom_call_target="tpu_custom_call" | custom-call | tf_op jit(solution)/shard_map/cg_step/pallas_call | solution.py:321
  49.0 9.2 %all_to_all.21.refs_0_ = f32[16,8,256]{2,1,0:T(8,128)S(1)} all-to-all(f32[16,8,256]{2,1,0:T(8,128)S(1)} %broadcast_in_dim.9), channel_id=1, replica_groups={{5,0,1,2,3,4,6,7,8,9,10,11,12,13,14,15},{21,16,17,18,19,20,22,23,24,25,..., dimensions={0} | all-to-all | bytes 262144 | tf_op jit(solution)/shard_map/all_to_all | solution.py:41
  58.2 1.3 %cg_step.4 = (f32[8,256]{1,0:T(8,128)S(1)}, f32[8,128]{1,0:T(8,128)S(1)}, f32[8,256]{1,0:T(8,128)S(1)}, f32[8,4096]{1,0:T(8,128)S(1)}, f32[8,4096]{1,0:T(8,128)S(1)}, /*index=5*/f32[8,4096]{1,0:T(8,128)S(1)}) custom-call(f32[16,8,256]{2,1,0:T(8,128)S(1)} %all_to_all.21.refs_0_, bf16[256,4096]{1,0:T(8,128)(2,1)S(1)} %get-tuple-element.40.refs_4_.refs_1_, ...), custom_call_target="tpu_custom_call" | custom-call | tf_op jit(solution)/shard_map/cg_step/pallas_call | solution.py:321
  59.5 9.2 %all_to_all.22.refs_0_ = f32[16,8,256]{2,1,0:T(8,128)S(1)} all-to-all(f32[16,8,256]{2,1,0:T(8,128)S(1)} %broadcast_in_dim.10), channel_id=1, replica_groups={{5,0,1,2,3,4,6,7,8,9,10,11,12,13,14,15},{21,16,17,18,19,20,22,23,24,25,..., dimensions={0} | all-to-all | bytes 262144 | tf_op jit(solution)/shard_map/all_to_all | solution.py:41
  68.7 1.4 %cg_step.5 = (f32[8,128]{1,0:T(8,128)S(1)}, f32[8,128]{1,0:T(8,128)S(1)}, f32[8,32]{1,0:T(8,128)S(1)}, f32[8,32]{1,0:T(8,128)S(1)}) custom-call(f32[16,8,256]{2,1,0:T(8,128)S(1)} %all_to_all.22.refs_0_, bf16[256,4096]{1,0:T(8,128)(2,1)S(1)} %get-tuple-element.40.refs_4_.refs_1_, bf16[256,4096]{1,0:T(8,128)(2,1)S(1)} %get-tuple-element.41.refs_5_.refs_2_, ...), custom_call_target="tpu_custom_call" | custom-call | tf_op jit(solution)/shard_map/cg_step/pallas_call | solution.py:321
  70.2 8.2 %all_to_all.23.curvature_ref = f32[16,8,128]{2,1,0:T(8,128)S(1)} all-to-all(f32[16,8,128]{2,1,0:T(8,128)S(1)} %broadcast_in_dim.11), channel_id=1, replica_groups={{5,0,1,2,3,4,6,7,8,9,10,11,12,13,14,15},{21,16,17,18,19,20,22,23,24,25,..., dimensions={0} | all-to-all | bytes 131072 | tf_op jit(solution)/shard_map/all_to_all | solution.py:41
  78.3 0.7 combine.1
  (15 shorter events, 0.3 us)
Async XLA Ops:
  5.1 22.4 %copy-start = (bf16[32,4096]{1,0:T(8,128)(2,1)S(1)}, bf16[32,4096]{1,0:T(8,128)(2,1)}, u32[]{:S(2)}) copy-start(bf16[32,4096]{1,0:T(8,128)(2,1)} %queries_ref.1) | copy-start | bytes 786436
  5.1 17.5 %collective-permute-start.2 = (f32[64,512]{1,0:T(8,128)S(1)}, f32[64,512]{1,0:T(8,128)S(1)}, u32[]{:S(2)}, u32[]{:S(2)}) collective-permute-start(f32[64,512]{1,0:T(8,128)S(1)} %in_features.1.refs_0_), channel_id=1, source_target_pairs={{0,1},{1,0},{2,3},{3,2},{4,5},{5,4},{6,7},{7,6},{8,9},{9,8},{10,11... | collective-permute-start | bytes 393224 | tf_op jit(solution)/shard_map/ppermute | solution.py:25
  8.2 14.4 %collective-permute-start.1 = (f32[64,512]{1,0:T(8,128)S(1)}, f32[64,512]{1,0:T(8,128)S(1)}, u32[]{:S(2)}, u32[]{:S(2)}) collective-permute-start(f32[64,512]{1,0:T(8,128)S(1)} %in_features.1.refs_0_), channel_id=1, source_target_pairs={{0,3},{1,2},{2,1},{3,0},{4,7},{5,6},{6,5},{7,4},{8,11},{9,10},{10,... | collective-permute-start | bytes 393224 | tf_op jit(solution)/shard_map/ppermute | solution.py:25
  10.6 12.0 %collective-permute-start = (f32[64,512]{1,0:T(8,128)S(1)}, f32[64,512]{1,0:T(8,128)S(1)}, u32[]{:S(2)}, u32[]{:S(2)}) collective-permute-start(f32[64,512]{1,0:T(8,128)S(1)} %in_features.1.refs_0_), channel_id=1, source_target_pairs={{0,2},{1,3},{2,0},{3,1},{4,6},{5,7},{6,4},{7,5},{8,10},{9,11},{10,... | collective-permute-start | bytes 393224 | tf_op jit(solution)/shard_map/ppermute | solution.py:25
  23.1 6.9 %collective-permute-start.5 = (f32[2,4096]{1,0:T(2,128)S(1)}, f32[2,4096]{1,0:T(2,128)S(1)}, u32[]{:S(2)}, u32[]{:S(2)}) collective-permute-start(f32[2,4096]{1,0:T(2,128)S(1)} %reshape.7), channel_id=1, source_target_pairs={{0,1},{1,0},{2,3},{3,2},{4,5},{5,4},{6,7},{7,6},{8,9},{9,8},{10,11... | collective-permute-start | bytes 98312 | tf_op jit(solution)/shard_map/ppermute | solution.py:25
  25.0 5.7 %collective-permute-start.4 = (f32[2,4096]{1,0:T(2,128)S(1)}, f32[2,4096]{1,0:T(2,128)S(1)}, u32[]{:S(2)}, u32[]{:S(2)}) collective-permute-start(f32[2,4096]{1,0:T(2,128)S(1)} %reshape.7), channel_id=1, source_target_pairs={{0,3},{1,2},{2,1},{3,0},{4,7},{5,6},{6,5},{7,4},{8,11},{9,10},{10,... | collective-permute-start | bytes 98312 | tf_op jit(solution)/shard_map/ppermute | solution.py:25
  27.4 4.8 %collective-permute-start.3 = (f32[2,4096]{1,0:T(2,128)S(1)}, f32[2,4096]{1,0:T(2,128)S(1)}, u32[]{:S(2)}, u32[]{:S(2)}) collective-permute-start(f32[2,4096]{1,0:T(2,128)S(1)} %reshape.7), channel_id=1, source_target_pairs={{0,2},{1,3},{2,0},{3,1},{4,6},{5,7},{6,4},{7,5},{8,10},{9,11},{10,... | collective-permute-start | bytes 98312 | tf_op jit(solution)/shard_map/ppermute | solution.py:25
  32.3 3.7 %collective-permute-start.8 = (f32[2,4096]{1,0:T(2,128)S(1)}, f32[2,4096]{1,0:T(2,128)S(1)}, u32[]{:S(2)}, u32[]{:S(2)}) collective-permute-start(f32[2,4096]{1,0:T(2,128)S(1)} %add_add_fusion.refs_0_), channel_id=1, source_target_pairs={{0,12},{4,8},{8,4},{12,0},{1,13},{5,9},{9,5},{13,1},{2,14},{6,10},... | collective-permute-start | bytes 98312 | tf_op jit(solution)/shard_map/ppermute | solution.py:25
  32.4 4.0 %collective-permute-start.7 = (f32[2,4096]{1,0:T(2,128)S(1)}, f32[2,4096]{1,0:T(2,128)S(1)}, u32[]{:S(2)}, u32[]{:S(2)}) collective-permute-start(f32[2,4096]{1,0:T(2,128)S(1)} %add_add_fusion.refs_0_), channel_id=1, source_target_pairs={{0,8},{4,12},{8,0},{12,4},{1,9},{5,13},{9,1},{13,5},{2,10},{6,14},... | collective-permute-start | bytes 98312 | tf_op jit(solution)/shard_map/ppermute | solution.py:25
  33.9 2.5 %collective-permute-start.6 = (f32[2,4096]{1,0:T(2,128)S(1)}, f32[2,4096]{1,0:T(2,128)S(1)}, u32[]{:S(2)}, u32[]{:S(2)}) collective-permute-start(f32[2,4096]{1,0:T(2,128)S(1)} %add_add_fusion.refs_0_), channel_id=1, source_target_pairs={{0,4},{4,0},{8,12},{12,8},{1,5},{5,1},{9,13},{13,9},{2,6},{6,2},{1... | collective-permute-start | bytes 98312 | tf_op jit(solution)/shard_map/ppermute | solution.py:25

commit v23 on v22

--- a/solution.py
+++ b/solution.py
@@ -13,6 +13,7 @@
 ITERS = 4
 LANES = 128
 FEW = 4
+DEPTH = 3
 NT = (((1,), (1,)), ((), ()))
 HIGHEST = lax.Precision.HIGHEST
 ANY_SPEC = pl.BlockSpec(memory_space=pl.ANY)
@@ -31,7 +32,7 @@
 
 def group_order(sizes):
     dp_size, tensor_size = sizes
-    first = min(1, dp_size - 1) * tensor_size + (tensor_size - 1) // 2
+    first = (dp_size - 1) * tensor_size + (tensor_size - 1) // 2
     return [first] + [i for i in range(dp_size * tensor_size) if i != first]
 
 
@@ -92,7 +93,7 @@
 
     for copy in firsts:
         copy.start()
-    for step in range(steps):
+    for step in range(min(DEPTH, steps)):
         fetch(step).start()
     for copy in firsts:
         copy.wait()
@@ -101,6 +102,11 @@
     @pl.loop(0, steps)
     def _(step):
         fetch(step).wait()
+
+        @pl.when(step + DEPTH < steps)
+        def _():
+            fetch(step + DEPTH).start()
+
         span = pl.ds(pl.multiple_of(step * block, block), block)
         left = jnp.dot(held[span, :half], turned[...], preferred_element_type=jnp.float32)
         right = jnp.dot(held[span, half:], turned[...], preferred_element_type=jnp.float32)

time: 79.3 us -> 78.8 us (level)
  no operation moved by 1% of the time
where the time goes in v23:
time: 78.8 us; the launch traced here: 78.5 us
  blocking collectives  36.1 us (46%)
  Pallas kernels  25.7 us (33%)
  starting transfers between devices  11.9 us (15%)
  waiting for transfers between devices  4.42 us (6%)
    all_to_all x4, blocking collectives, gather(): lax.all_to_all(value, ('dp', 'tensor'), 0, 0, axis_index_groups=[order])  36.1 us
    pallas_call x2, Pallas kernels, features(): pl.pallas_call(functools.partial(stream_kernel, block), out_shape=pltpu.V...  16.9 us
    ppermute x9, starting transfers between devices, swap(): return lax.ppermute(value, axis, [(i, i ^ bit) for i in range(size)])  11.9 us
    ppermute x9, waiting for transfers between devices, swap(): return lax.ppermute(value, axis, [(i, i ^ bit) for i in range(size)])  4.42 us
    pallas_call x3, Pallas kernels, step_cg(): pl.pallas_call(functools.partial(step_kernel, sizes, first, last), out_sh...  3.97 us
    pallas_call x1, Pallas kernels, split_prior(): pl.pallas_call(split_kernel, out_shape=(pltpu.VMEM(prior.shape, jnp.bfloa...  2.56 us
  transfers between devices with their start and end apart: 9, of which 4 were waited for; matrix products, arithmetic and copies ran while one was open for 0% of the time, Pallas kernels for 18%

profile of v23, /device:TPU:0, one launch (start us, length us, event | category | flops | bytes accessed | tf_op | source)
XLA Modules:
  0.0 78.5 jit_solution(7601657767586296631)
XLA Ops:
  0.0 5.1 %in_features.1.refs_0_ = f32[64,512]{1,0:T(8,128)S(1)} custom-call(bf16[512,8192]{1,0:T(8,128)(2,1)} %rows_ref.2, bf16[64,8192]{1,0:T(8,128)(2,1)} %proj_ref.2), custom_call_target="tpu_custom_call" | custom-call | tf_op jit(solution)/shard_map/in_features/pallas_call | solution.py:118
  5.1 3.1 %collective-permute-start.2 = (f32[64,512]{1,0:T(8,128)S(1)}, f32[64,512]{1,0:T(8,128)S(1)}, u32[]{:S(2)}, u32[]{:S(2)}) collective-permute-start(f32[64,512]{1,0:T(8,128)S(1)} %in_features.1.refs_0_), channel_id=1, source_target_pairs={{0,1},{1,0},{2,3},{3,2},{4,5},{5,4},{6,7},{7,6},{8,9},{9,8},{10,11... | collective-permute-start | bytes 393224 | tf_op jit(solution)/shard_map/ppermute | solution.py:26
  8.2 2.5 %collective-permute-start.1 = (f32[64,512]{1,0:T(8,128)S(1)}, f32[64,512]{1,0:T(8,128)S(1)}, u32[]{:S(2)}, u32[]{:S(2)}) collective-permute-start(f32[64,512]{1,0:T(8,128)S(1)} %in_features.1.refs_0_), channel_id=1, source_target_pairs={{0,3},{1,2},{2,1},{3,0},{4,7},{5,6},{6,5},{7,4},{8,11},{9,10},{10,... | collective-permute-start | bytes 393224 | tf_op jit(solution)/shard_map/ppermute | solution.py:26
  10.6 0.1 collective-permute-start
  10.8 11.8 %out_features.1.refs_4_ = f32[64,2048]{1,0:T(8,128)S(1)} custom-call(bf16[2048,7168]{1,0:T(8,128)(2,1)} %rows_ref.3, bf16[64,7168]{1,0:T(8,128)(2,1)} %proj_ref.3), custom_call_target="tpu_custom_call" | custom-call | tf_op jit(solution)/shard_map/out_features/pallas_call | solution.py:118
  22.6 0.4 partial_vectors.1
  23.1 1.9 %collective-permute-start.5 = (f32[2,4096]{1,0:T(2,128)S(1)}, f32[2,4096]{1,0:T(2,128)S(1)}, u32[]{:S(2)}, u32[]{:S(2)}) collective-permute-start(f32[2,4096]{1,0:T(2,128)S(1)} %reshape.7), channel_id=1, source_target_pairs={{0,1},{1,0},{2,3},{3,2},{4,5},{5,4},{6,7},{7,6},{8,9},{9,8},{10,11... | collective-permute-start | bytes 98312 | tf_op jit(solution)/shard_map/ppermute | solution.py:26
  25.0 2.5 %collective-permute-start.4 = (f32[2,4096]{1,0:T(2,128)S(1)}, f32[2,4096]{1,0:T(2,128)S(1)}, u32[]{:S(2)}, u32[]{:S(2)}) collective-permute-start(f32[2,4096]{1,0:T(2,128)S(1)} %reshape.7), channel_id=1, source_target_pairs={{0,3},{1,2},{2,1},{3,0},{4,7},{5,6},{6,5},{7,4},{8,11},{9,10},{10,... | collective-permute-start | bytes 98312 | tf_op jit(solution)/shard_map/ppermute | solution.py:26
  27.5 2.6 %split_prior.1 = (bf16[256,4096]{1,0:T(8,128)(2,1)S(1)}, bf16[256,4096]{1,0:T(8,128)(2,1)S(1)}, bf16[4096,32]{1,0:T(8,128)(2,1)S(1)}) custom-call(f32[256,4096]{1,0:T(8,128)} %prior_ref, bf16[32,4096]{1,0:T(8,128)(2,1)S(1)} %copy-done), custom_call_target="tpu_custom_call" | custom-call | tf_op jit(solution)/shard_map/split_prior/pallas_call | solution.py:153
  30.0 0.7 collective-permute-done.4
  30.7 1.6 %collective-permute-done.3 = f32[2,4096]{1,0:T(2,128)S(1)} collective-permute-done((f32[2,4096]{1,0:T(2,128)S(1)}, f32[2,4096]{1,0:T(2,128)S(1)}, u32[]{:S(2)}, u32[]{:S(2)}) %collective-permute-start.3) | collective-permute-done | bytes 32800 | tf_op jit(solution)/shard_map/ppermute | solution.py:26
  32.4 1.6 %collective-permute-start.7 = (f32[2,4096]{1,0:T(2,128)S(1)}, f32[2,4096]{1,0:T(2,128)S(1)}, u32[]{:S(2)}, u32[]{:S(2)}) collective-permute-start(f32[2,4096]{1,0:T(2,128)S(1)} %add_add_fusion.refs_0_), channel_id=1, source_target_pairs={{0,8},{4,12},{8,0},{12,4},{1,9},{5,13},{9,1},{13,5},{2,10},{6,14},... | collective-permute-start | bytes 98312 | tf_op jit(solution)/shard_map/ppermute | solution.py:26
  33.9 0.3 collective-permute-start.6
  34.2 1.8 %collective-permute-done.8.refs_3_ = f32[2,4096]{1,0:T(2,128)S(1)} collective-permute-done((f32[2,4096]{1,0:T(2,128)S(1)}, f32[2,4096]{1,0:T(2,128)S(1)}, u32[]{:S(2)}, u32[]{:S(2)}) %collective-permute-start.8) | collective-permute-done | bytes 32800 | tf_op jit(solution)/shard_map/ppermute | solution.py:26
  36.0 0.4 collective-permute-done.7.refs_2_
  36.4 1.3 %cg_start.1 = (f32[8,4096]{1,0:T(8,128)S(1)}, f32[8,128]{1,0:T(8,128)S(1)}, f32[8,256]{1,0:T(8,128)S(1)}, f32[8,128]{1,0:T(8,128)S(1)}) custom-call(f32[2,4096]{1,0:T(2,128)S(1)} %add_add_fusion.refs_0_, f32[2,4096]{1,0:T(2,128)S(1)} %collective-permute-done.6.refs_1_, f32[2,4096]{1,0:T(2,128)S(1)} %collective-permute-done.7.refs_2_, ...), custom_call_target="tpu_custom_call" | custom-call | tf_op jit(solution)/shard_map/cg_start/pallas_call | solution.py:256
  37.7 9.4 %all_to_all.20.refs_0_ = f32[16,8,256]{2,1,0:T(8,128)S(1)} all-to-all(f32[16,8,256]{2,1,0:T(8,128)S(1)} %broadcast_in_dim.8), channel_id=1, replica_groups={{13,0,1,2,3,4,5,6,7,8,9,10,11,12,14,15},{29,16,17,18,19,20,21,22,23,24,..., dimensions={0} | all-to-all | bytes 262144 | tf_op jit(solution)/shard_map/all_to_all | solution.py:42
  47.1 1.3 %cg_step.3 = (f32[8,256]{1,0:T(8,128)S(1)}, f32[8,128]{1,0:T(8,128)S(1)}, f32[8,256]{1,0:T(8,128)S(1)}, f32[8,4096]{1,0:T(8,128)S(1)}, f32[8,4096]{1,0:T(8,128)S(1)}, /*index=5*/f32[8,4096]{1,0:T(8,128)S(1)}) custom-call(f32[16,8,256]{2,1,0:T(8,128)S(1)} %all_to_all.20.refs_0_, bf16[256,4096]{1,0:T(8,128)(2,1)S(1)} %get-tuple-element.40.refs_4_.refs_1_, ...), custom_call_target="tpu_custom_call" | custom-call | tf_op jit(solution)/shard_map/cg_step/pallas_call | solution.py:327
  48.4 9.2 %all_to_all.21.refs_0_ = f32[16,8,256]{2,1,0:T(8,128)S(1)} all-to-all(f32[16,8,256]{2,1,0:T(8,128)S(1)} %broadcast_in_dim.9), channel_id=1, replica_groups={{13,0,1,2,3,4,5,6,7,8,9,10,11,12,14,15},{29,16,17,18,19,20,21,22,23,24,..., dimensions={0} | all-to-all | bytes 262144 | tf_op jit(solution)/shard_map/all_to_all | solution.py:42
  57.6 1.3 %cg_step.4 = (f32[8,256]{1,0:T(8,128)S(1)}, f32[8,128]{1,0:T(8,128)S(1)}, f32[8,256]{1,0:T(8,128)S(1)}, f32[8,4096]{1,0:T(8,128)S(1)}, f32[8,4096]{1,0:T(8,128)S(1)}, /*index=5*/f32[8,4096]{1,0:T(8,128)S(1)}) custom-call(f32[16,8,256]{2,1,0:T(8,128)S(1)} %all_to_all.21.refs_0_, bf16[256,4096]{1,0:T(8,128)(2,1)S(1)} %get-tuple-element.40.refs_4_.refs_1_, ...), custom_call_target="tpu_custom_call" | custom-call | tf_op jit(solution)/shard_map/cg_step/pallas_call | solution.py:327
  58.9 9.2 %all_to_all.22.refs_0_ = f32[16,8,256]{2,1,0:T(8,128)S(1)} all-to-all(f32[16,8,256]{2,1,0:T(8,128)S(1)} %broadcast_in_dim.10), channel_id=1, replica_groups={{13,0,1,2,3,4,5,6,7,8,9,10,11,12,14,15},{29,16,17,18,19,20,21,22,23,24,..., dimensions={0} | all-to-all | bytes 262144 | tf_op jit(solution)/shard_map/all_to_all | solution.py:42
  68.1 1.4 %cg_step.5 = (f32[8,128]{1,0:T(8,128)S(1)}, f32[8,128]{1,0:T(8,128)S(1)}, f32[8,32]{1,0:T(8,128)S(1)}, f32[8,32]{1,0:T(8,128)S(1)}) custom-call(f32[16,8,256]{2,1,0:T(8,128)S(1)} %all_to_all.22.refs_0_, bf16[256,4096]{1,0:T(8,128)(2,1)S(1)} %get-tuple-element.40.refs_4_.refs_1_, bf16[256,4096]{1,0:T(8,128)(2,1)S(1)} %get-tuple-element.41.refs_5_.refs_2_, ...), custom_call_target="tpu_custom_call" | custom-call | tf_op jit(solution)/shard_map/cg_step/pallas_call | solution.py:327
  69.6 8.3 %all_to_all.23.curvature_ref = f32[16,8,128]{2,1,0:T(8,128)S(1)} all-to-all(f32[16,8,128]{2,1,0:T(8,128)S(1)} %broadcast_in_dim.11), channel_id=1, replica_groups={{13,0,1,2,3,4,5,6,7,8,9,10,11,12,14,15},{29,16,17,18,19,20,21,22,23,24,..., dimensions={0} | all-to-all | bytes 131072 | tf_op jit(solution)/shard_map/all_to_all | solution.py:42
  77.8 0.7 combine.1
  (15 shorter events, 0.3 us)
Async XLA Ops:
  5.1 22.4 %copy-start = (bf16[32,4096]{1,0:T(8,128)(2,1)S(1)}, bf16[32,4096]{1,0:T(8,128)(2,1)}, u32[]{:S(2)}) copy-start(bf16[32,4096]{1,0:T(8,128)(2,1)} %queries_ref.1) | copy-start | bytes 786436
  5.1 17.5 %collective-permute-start.2 = (f32[64,512]{1,0:T(8,128)S(1)}, f32[64,512]{1,0:T(8,128)S(1)}, u32[]{:S(2)}, u32[]{:S(2)}) collective-permute-start(f32[64,512]{1,0:T(8,128)S(1)} %in_features.1.refs_0_), channel_id=1, source_target_pairs={{0,1},{1,0},{2,3},{3,2},{4,5},{5,4},{6,7},{7,6},{8,9},{9,8},{10,11... | collective-permute-start | bytes 393224 | tf_op jit(solution)/shard_map/ppermute | solution.py:26
  8.2 14.4 %collective-permute-start.1 = (f32[64,512]{1,0:T(8,128)S(1)}, f32[64,512]{1,0:T(8,128)S(1)}, u32[]{:S(2)}, u32[]{:S(2)}) collective-permute-start(f32[64,512]{1,0:T(8,128)S(1)} %in_features.1.refs_0_), channel_id=1, source_target_pairs={{0,3},{1,2},{2,1},{3,0},{4,7},{5,6},{6,5},{7,4},{8,11},{9,10},{10,... | collective-permute-start | bytes 393224 | tf_op jit(solution)/shard_map/ppermute | solution.py:26
  10.6 12.0 %collective-permute-start = (f32[64,512]{1,0:T(8,128)S(1)}, f32[64,512]{1,0:T(8,128)S(1)}, u32[]{:S(2)}, u32[]{:S(2)}) collective-permute-start(f32[64,512]{1,0:T(8,128)S(1)} %in_features.1.refs_0_), channel_id=1, source_target_pairs={{0,2},{1,3},{2,0},{3,1},{4,6},{5,7},{6,4},{7,5},{8,10},{9,11},{10,... | collective-permute-start | bytes 393224 | tf_op jit(solution)/shard_map/ppermute | solution.py:26
  23.1 6.9 %collective-permute-start.5 = (f32[2,4096]{1,0:T(2,128)S(1)}, f32[2,4096]{1,0:T(2,128)S(1)}, u32[]{:S(2)}, u32[]{:S(2)}) collective-permute-start(f32[2,4096]{1,0:T(2,128)S(1)} %reshape.7), channel_id=1, source_target_pairs={{0,1},{1,0},{2,3},{3,2},{4,5},{5,4},{6,7},{7,6},{8,9},{9,8},{10,11... | collective-permute-start | bytes 98312 | tf_op jit(solution)/shard_map/ppermute | solution.py:26
  25.0 5.7 %collective-permute-start.4 = (f32[2,4096]{1,0:T(2,128)S(1)}, f32[2,4096]{1,0:T(2,128)S(1)}, u32[]{:S(2)}, u32[]{:S(2)}) collective-permute-start(f32[2,4096]{1,0:T(2,128)S(1)} %reshape.7), channel_id=1, source_target_pairs={{0,3},{1,2},{2,1},{3,0},{4,7},{5,6},{6,5},{7,4},{8,11},{9,10},{10,... | collective-permute-start | bytes 98312 | tf_op jit(solution)/shard_map/ppermute | solution.py:26
  27.4 4.8 %collective-permute-start.3 = (f32[2,4096]{1,0:T(2,128)S(1)}, f32[2,4096]{1,0:T(2,128)S(1)}, u32[]{:S(2)}, u32[]{:S(2)}) collective-permute-start(f32[2,4096]{1,0:T(2,128)S(1)} %reshape.7), channel_id=1, source_target_pairs={{0,2},{1,3},{2,0},{3,1},{4,6},{5,7},{6,4},{7,5},{8,10},{9,11},{10,... | collective-permute-start | bytes 98312 | tf_op jit(solution)/shard_map/ppermute | solution.py:26
  32.3 3.7 %collective-permute-start.8 = (f32[2,4096]{1,0:T(2,128)S(1)}, f32[2,4096]{1,0:T(2,128)S(1)}, u32[]{:S(2)}, u32[]{:S(2)}) collective-permute-start(f32[2,4096]{1,0:T(2,128)S(1)} %add_add_fusion.refs_0_), channel_id=1, source_target_pairs={{0,12},{4,8},{8,4},{12,0},{1,13},{5,9},{9,5},{13,1},{2,14},{6,10},... | collective-permute-start | bytes 98312 | tf_op jit(solution)/shard_map/ppermute | solution.py:26
  32.4 4.0 %collective-permute-start.7 = (f32[2,4096]{1,0:T(2,128)S(1)}, f32[2,4096]{1,0:T(2,128)S(1)}, u32[]{:S(2)}, u32[]{:S(2)}) collective-permute-start(f32[2,4096]{1,0:T(2,128)S(1)} %add_add_fusion.refs_0_), channel_id=1, source_target_pairs={{0,8},{4,12},{8,0},{12,4},{1,9},{5,13},{9,1},{13,5},{2,10},{6,14},... | collective-permute-start | bytes 98312 | tf_op jit(solution)/shard_map/ppermute | solution.py:26
  33.9 2.5 %collective-permute-start.6 = (f32[2,4096]{1,0:T(2,128)S(1)}, f32[2,4096]{1,0:T(2,128)S(1)}, u32[]{:S(2)}, u32[]{:S(2)}) collective-permute-start(f32[2,4096]{1,0:T(2,128)S(1)} %add_add_fusion.refs_0_), channel_id=1, source_target_pairs={{0,4},{4,0},{8,12},{12,8},{1,5},{5,1},{9,13},{13,9},{2,6},{6,2},{1... | collective-permute-start | bytes 98312 | tf_op jit(solution)/shard_map/ppermute | solution.py:26

commit v24 on v23

--- a/solution.py
+++ b/solution.py
@@ -77,7 +77,7 @@
     return jnp.sum(values, axis=1, keepdims=True)
 
 
-def stream_kernel(block, rows_ref, proj_ref, feats_ref, held, proj, turned, sems):
+def stream_kernel(block, by_row, rows_ref, proj_ref, feats_ref, held, proj, turned, sems):
     count, half = proj_ref.shape[0], proj.shape[1]
     steps = held.shape[0] // block
     firsts = [
@@ -110,14 +110,21 @@
         span = pl.ds(pl.multiple_of(step * block, block), block)
         left = jnp.dot(held[span, :half], turned[...], preferred_element_type=jnp.float32)
         right = jnp.dot(held[span, half:], turned[...], preferred_element_type=jnp.float32)
-        feats_ref[:, span] = left.T[:count] + right.T[count:]
-
-
-def features(rows, proj, block, limit, name):
+        lane = lax.broadcasted_iota(jnp.int32, left.shape, 1)
+        both = jnp.where(lane < count, left, right)
+        if by_row:
+            feats_ref[span, :] = both
+        else:
+            both = both.T
+            feats_ref[:, span] = both[:count] + both[count:]
+
+
+def features(rows, proj, block, by_row, limit, name):
     count, width = proj.shape
-    return pl.pallas_call(
-        functools.partial(stream_kernel, block),
-        out_shape=pltpu.VMEM((count, rows.shape[0]), jnp.float32),
+    shape = (rows.shape[0], 2 * count) if by_row else (count, rows.shape[0])
+    return pl.pallas_call(
+        functools.partial(stream_kernel, block, by_row),
+        out_shape=pltpu.VMEM(shape, jnp.float32),
         in_specs=[ANY_SPEC] * 2,
         out_specs=VMEM_SPEC,
         scratch_shapes=[
@@ -174,19 +181,24 @@
         held[:, pl.ds(start, tokens)] = block[...]
     for s in range(part_ref.shape[0]):
         span = slice(s * SEQ, (s + 1) * SEQ)
-        outs = pieces_of(out_ref[:, span], 2)
-        sums = dot_pieces(pieces_of(held[:, span], 2), outs, R_IN)
+        ins, sums = pieces_of(held[:, span], 2), 0.0
+        outs = out_ref[span, :]
+        for _ in range(2):
+            piece = outs.astype(jnp.bfloat16)
+            outs = outs - piece.astype(jnp.float32)
+            sums = sums + jnp.dot(ins, piece, preferred_element_type=jnp.float32)
+        sums = sums[:R_IN] + sums[R_IN:]
         part_ref[s] = (sums[:, :R_OUT] + sums[:, R_OUT:]) * (1.0 / SEQ)
 
 
 def partial_vectors(blocks, out_local):
-    seq_count = out_local.shape[1] // SEQ
+    seq_count = out_local.shape[0] // SEQ
     return pl.pallas_call(
         functools.partial(partial_kernel, len(blocks)),
         out_shape=F32((seq_count, R_IN, R_OUT)),
         in_specs=[VMEM_SPEC] * (len(blocks) + 1),
         out_specs=VMEM_SPEC,
-        scratch_shapes=[pltpu.VMEM(out_local.shape, jnp.float32)],
+        scratch_shapes=[pltpu.VMEM((R_IN, out_local.shape[0]), jnp.float32)],
         compiler_params=PARAMS,
         name="partial_vectors",
     )(*blocks, out_local)
@@ -354,8 +366,8 @@
 def on_device(dp_size, tensor_size, inputs, in_proj, out_grads, out_proj, prior, queries):
     width = R_IN * R_OUT
     sizes = dp_size, tensor_size
-    in_blocks = direct(features(inputs, in_proj, LANES, 20, "in_features"), "tensor", tensor_size, order_of(tensor_size))
-    out_local = features(out_grads, out_proj, 2 * LANES, 44, "out_features")
+    in_blocks = direct(features(inputs, in_proj, LANES, False, 20, "in_features"), "tensor", tensor_size, order_of(tensor_size))
+    out_local = features(out_grads, out_proj, 2 * LANES, True, 44, "out_features")
     partial = partial_vectors(in_blocks, out_local).reshape(-1, width)
     prior, partial = lax.optimization_barrier((prior, partial))
     own_vectors = sum_over(partial, "tensor", tensor_size)

time: 78.8 us -> 78.5 us (level)
  transfers between devices with their start and end apart: 9 -> 9, of which waited for: 4 -> 5; matrix products, arithmetic and copies ran while one was open for 0% -> 0% of each run, Pallas kernels for 18% -> 18%
where the time goes in v24:
time: 78.5 us; the launch traced here: 78.2 us
  blocking collectives  36.1 us (46%)
  Pallas kernels  25.4 us (32%)
  starting transfers between devices  11.7 us (15%)
  waiting for transfers between devices  4.67 us (6%)
    all_to_all x4, blocking collectives, gather(): lax.all_to_all(value, ('dp', 'tensor'), 0, 0, axis_index_groups=[order])  36.1 us
    pallas_call x2, Pallas kernels, features(): pl.pallas_call(functools.partial(stream_kernel, block, by_row), out_shape...  16.4 us
    ppermute x9, starting transfers between devices, swap(): return lax.ppermute(value, axis, [(i, i ^ bit) for i in range(size)])  11.7 us
    ppermute x9, waiting for transfers between devices, swap(): return lax.ppermute(value, axis, [(i, i ^ bit) for i in range(size)])  4.67 us
    pallas_call x3, Pallas kernels, step_cg(): pl.pallas_call(functools.partial(step_kernel, sizes, first, last), out_sh...  3.97 us
    pallas_call x1, Pallas kernels, split_prior(): pl.pallas_call(split_kernel, out_shape=(pltpu.VMEM(prior.shape, jnp.bfloa...  2.56 us
  transfers between devices with their start and end apart: 9, of which 5 were waited for; matrix products, arithmetic and copies ran while one was open for 0% of the time, Pallas kernels for 18%

profile of v24, /device:TPU:0, one launch (start us, length us, event | category | flops | bytes accessed | tf_op | source)
XLA Modules:
  0.0 78.2 jit_solution(5948513798798012733)
XLA Ops:
  0.0 5.1 %in_features.1.refs_0_ = f32[64,512]{1,0:T(8,128)S(1)} custom-call(bf16[512,8192]{1,0:T(8,128)(2,1)} %rows_ref.2, bf16[64,8192]{1,0:T(8,128)(2,1)} %proj_ref.2), custom_call_target="tpu_custom_call" | custom-call | tf_op jit(solution)/shard_map/in_features/pallas_call | solution.py:125
  5.1 3.1 %collective-permute-start.2 = (f32[64,512]{1,0:T(8,128)S(1)}, f32[64,512]{1,0:T(8,128)S(1)}, u32[]{:S(2)}, u32[]{:S(2)}) collective-permute-start(f32[64,512]{1,0:T(8,128)S(1)} %in_features.1.refs_0_), channel_id=1, source_target_pairs={{0,1},{1,0},{2,3},{3,2},{4,5},{5,4},{6,7},{7,6},{8,9},{9,8},{10,11... | collective-permute-start | bytes 393224 | tf_op jit(solution)/shard_map/ppermute | solution.py:26
  8.2 2.5 %collective-permute-start.1 = (f32[64,512]{1,0:T(8,128)S(1)}, f32[64,512]{1,0:T(8,128)S(1)}, u32[]{:S(2)}, u32[]{:S(2)}) collective-permute-start(f32[64,512]{1,0:T(8,128)S(1)} %in_features.1.refs_0_), channel_id=1, source_target_pairs={{0,3},{1,2},{2,1},{3,0},{4,7},{5,6},{6,5},{7,4},{8,11},{9,10},{10,... | collective-permute-start | bytes 393224 | tf_op jit(solution)/shard_map/ppermute | solution.py:26
  10.8 11.4 %out_features.1.refs_4_ = f32[2048,128]{1,0:T(8,128)S(1)} custom-call(bf16[2048,7168]{1,0:T(8,128)(2,1)} %rows_ref.3, bf16[64,7168]{1,0:T(8,128)(2,1)} %proj_ref.3), custom_call_target="tpu_custom_call" | custom-call | tf_op jit(solution)/shard_map/out_features/pallas_call | solution.py:125
  22.1 0.2 collective-permute-done.refs_1_
  22.4 0.5 partial_vectors.1
  23.0 1.6 %collective-permute-start.5 = (f32[2,4096]{1,0:T(2,128)S(1)}, f32[2,4096]{1,0:T(2,128)S(1)}, u32[]{:S(2)}, u32[]{:S(2)}) collective-permute-start(f32[2,4096]{1,0:T(2,128)S(1)} %reshape.7), channel_id=1, source_target_pairs={{0,1},{1,0},{2,3},{3,2},{4,5},{5,4},{6,7},{7,6},{8,9},{9,8},{10,11... | collective-permute-start | bytes 98312 | tf_op jit(solution)/shard_map/ppermute | solution.py:26
  24.7 2.5 %collective-permute-start.4 = (f32[2,4096]{1,0:T(2,128)S(1)}, f32[2,4096]{1,0:T(2,128)S(1)}, u32[]{:S(2)}, u32[]{:S(2)}) collective-permute-start(f32[2,4096]{1,0:T(2,128)S(1)} %reshape.7), channel_id=1, source_target_pairs={{0,3},{1,2},{2,1},{3,0},{4,7},{5,6},{6,5},{7,4},{8,11},{9,10},{10,... | collective-permute-start | bytes 98312 | tf_op jit(solution)/shard_map/ppermute | solution.py:26
  27.1 2.6 %split_prior.1 = (bf16[256,4096]{1,0:T(8,128)(2,1)S(1)}, bf16[256,4096]{1,0:T(8,128)(2,1)S(1)}, bf16[4096,32]{1,0:T(8,128)(2,1)S(1)}) custom-call(f32[256,4096]{1,0:T(8,128)} %prior_ref, bf16[32,4096]{1,0:T(8,128)(2,1)S(1)} %copy-done), custom_call_target="tpu_custom_call" | custom-call | tf_op jit(solution)/shard_map/split_prior/pallas_call | solution.py:160
  29.7 0.7 collective-permute-done.4
  30.4 1.6 %collective-permute-done.3 = f32[2,4096]{1,0:T(2,128)S(1)} collective-permute-done((f32[2,4096]{1,0:T(2,128)S(1)}, f32[2,4096]{1,0:T(2,128)S(1)}, u32[]{:S(2)}, u32[]{:S(2)}) %collective-permute-start.3) | collective-permute-done | bytes 32800 | tf_op jit(solution)/shard_map/ppermute | solution.py:26
  32.1 1.6 %collective-permute-start.7 = (f32[2,4096]{1,0:T(2,128)S(1)}, f32[2,4096]{1,0:T(2,128)S(1)}, u32[]{:S(2)}, u32[]{:S(2)}) collective-permute-start(f32[2,4096]{1,0:T(2,128)S(1)} %add_add_fusion.refs_0_), channel_id=1, source_target_pairs={{0,8},{4,12},{8,0},{12,4},{1,9},{5,13},{9,1},{13,5},{2,10},{6,14},... | collective-permute-start | bytes 98312 | tf_op jit(solution)/shard_map/ppermute | solution.py:26
  33.6 0.3 collective-permute-start.6
  33.9 1.8 %collective-permute-done.8.refs_3_ = f32[2,4096]{1,0:T(2,128)S(1)} collective-permute-done((f32[2,4096]{1,0:T(2,128)S(1)}, f32[2,4096]{1,0:T(2,128)S(1)}, u32[]{:S(2)}, u32[]{:S(2)}) %collective-permute-start.8) | collective-permute-done | bytes 32800 | tf_op jit(solution)/shard_map/ppermute | solution.py:26
  35.7 0.4 collective-permute-done.7.refs_2_
  36.1 1.3 %cg_start.1 = (f32[8,4096]{1,0:T(8,128)S(1)}, f32[8,128]{1,0:T(8,128)S(1)}, f32[8,256]{1,0:T(8,128)S(1)}, f32[8,128]{1,0:T(8,128)S(1)}) custom-call(f32[2,4096]{1,0:T(2,128)S(1)} %add_add_fusion.refs_0_, f32[2,4096]{1,0:T(2,128)S(1)} %collective-permute-done.6.refs_1_, f32[2,4096]{1,0:T(2,128)S(1)} %collective-permute-done.7.refs_2_, ...), custom_call_target="tpu_custom_call" | custom-call | tf_op jit(solution)/shard_map/cg_start/pallas_call | solution.py:268
  37.4 9.4 %all_to_all.20.refs_0_ = f32[16,8,256]{2,1,0:T(8,128)S(1)} all-to-all(f32[16,8,256]{2,1,0:T(8,128)S(1)} %broadcast_in_dim.8), channel_id=1, replica_groups={{13,0,1,2,3,4,5,6,7,8,9,10,11,12,14,15},{29,16,17,18,19,20,21,22,23,24,..., dimensions={0} | all-to-all | bytes 262144 | tf_op jit(solution)/shard_map/all_to_all | solution.py:42
  46.7 1.3 %cg_step.3 = (f32[8,256]{1,0:T(8,128)S(1)}, f32[8,128]{1,0:T(8,128)S(1)}, f32[8,256]{1,0:T(8,128)S(1)}, f32[8,4096]{1,0:T(8,128)S(1)}, f32[8,4096]{1,0:T(8,128)S(1)}, /*index=5*/f32[8,4096]{1,0:T(8,128)S(1)}) custom-call(f32[16,8,256]{2,1,0:T(8,128)S(1)} %all_to_all.20.refs_0_, bf16[256,4096]{1,0:T(8,128)(2,1)S(1)} %get-tuple-element.40.refs_4_.refs_1_, ...), custom_call_target="tpu_custom_call" | custom-call | tf_op jit(solution)/shard_map/cg_step/pallas_call | solution.py:339
  48.1 9.2 %all_to_all.21.refs_0_ = f32[16,8,256]{2,1,0:T(8,128)S(1)} all-to-all(f32[16,8,256]{2,1,0:T(8,128)S(1)} %broadcast_in_dim.9), channel_id=1, replica_groups={{13,0,1,2,3,4,5,6,7,8,9,10,11,12,14,15},{29,16,17,18,19,20,21,22,23,24,..., dimensions={0} | all-to-all | bytes 262144 | tf_op jit(solution)/shard_map/all_to_all | solution.py:42
  57.3 1.3 %cg_step.4 = (f32[8,256]{1,0:T(8,128)S(1)}, f32[8,128]{1,0:T(8,128)S(1)}, f32[8,256]{1,0:T(8,128)S(1)}, f32[8,4096]{1,0:T(8,128)S(1)}, f32[8,4096]{1,0:T(8,128)S(1)}, /*index=5*/f32[8,4096]{1,0:T(8,128)S(1)}) custom-call(f32[16,8,256]{2,1,0:T(8,128)S(1)} %all_to_all.21.refs_0_, bf16[256,4096]{1,0:T(8,128)(2,1)S(1)} %get-tuple-element.40.refs_4_.refs_1_, ...), custom_call_target="tpu_custom_call" | custom-call | tf_op jit(solution)/shard_map/cg_step/pallas_call | solution.py:339
  58.6 9.2 %all_to_all.22.refs_0_ = f32[16,8,256]{2,1,0:T(8,128)S(1)} all-to-all(f32[16,8,256]{2,1,0:T(8,128)S(1)} %broadcast_in_dim.10), channel_id=1, replica_groups={{13,0,1,2,3,4,5,6,7,8,9,10,11,12,14,15},{29,16,17,18,19,20,21,22,23,24,..., dimensions={0} | all-to-all | bytes 262144 | tf_op jit(solution)/shard_map/all_to_all | solution.py:42
  67.8 1.4 %cg_step.5 = (f32[8,128]{1,0:T(8,128)S(1)}, f32[8,128]{1,0:T(8,128)S(1)}, f32[8,32]{1,0:T(8,128)S(1)}, f32[8,32]{1,0:T(8,128)S(1)}) custom-call(f32[16,8,256]{2,1,0:T(8,128)S(1)} %all_to_all.22.refs_0_, bf16[256,4096]{1,0:T(8,128)(2,1)S(1)} %get-tuple-element.40.refs_4_.refs_1_, bf16[256,4096]{1,0:T(8,128)(2,1)S(1)} %get-tuple-element.41.refs_5_.refs_2_, ...), custom_call_target="tpu_custom_call" | custom-call | tf_op jit(solution)/shard_map/cg_step/pallas_call | solution.py:339
  69.2 8.3 %all_to_all.23.curvature_ref = f32[16,8,128]{2,1,0:T(8,128)S(1)} all-to-all(f32[16,8,128]{2,1,0:T(8,128)S(1)} %broadcast_in_dim.11), channel_id=1, replica_groups={{13,0,1,2,3,4,5,6,7,8,9,10,11,12,14,15},{29,16,17,18,19,20,21,22,23,24,..., dimensions={0} | all-to-all | bytes 131072 | tf_op jit(solution)/shard_map/all_to_all | solution.py:42
  77.5 0.7 combine.1
  (15 shorter events, 0.4 us)
Async XLA Ops:
  5.1 22.1 %copy-start = (bf16[32,4096]{1,0:T(8,128)(2,1)S(1)}, bf16[32,4096]{1,0:T(8,128)(2,1)}, u32[]{:S(2)}) copy-start(bf16[32,4096]{1,0:T(8,128)(2,1)} %queries_ref.1) | copy-start | bytes 786436
  5.1 17.1 %collective-permute-start.2 = (f32[64,512]{1,0:T(8,128)S(1)}, f32[64,512]{1,0:T(8,128)S(1)}, u32[]{:S(2)}, u32[]{:S(2)}) collective-permute-start(f32[64,512]{1,0:T(8,128)S(1)} %in_features.1.refs_0_), channel_id=1, source_target_pairs={{0,1},{1,0},{2,3},{3,2},{4,5},{5,4},{6,7},{7,6},{8,9},{9,8},{10,11... | collective-permute-start | bytes 393224 | tf_op jit(solution)/shard_map/ppermute | solution.py:26
  8.2 14.0 %collective-permute-start.1 = (f32[64,512]{1,0:T(8,128)S(1)}, f32[64,512]{1,0:T(8,128)S(1)}, u32[]{:S(2)}, u32[]{:S(2)}) collective-permute-start(f32[64,512]{1,0:T(8,128)S(1)} %in_features.1.refs_0_), channel_id=1, source_target_pairs={{0,3},{1,2},{2,1},{3,0},{4,7},{5,6},{6,5},{7,4},{8,11},{9,10},{10,... | collective-permute-start | bytes 393224 | tf_op jit(solution)/shard_map/ppermute | solution.py:26
  10.6 11.8 %collective-permute-start = (f32[64,512]{1,0:T(8,128)S(1)}, f32[64,512]{1,0:T(8,128)S(1)}, u32[]{:S(2)}, u32[]{:S(2)}) collective-permute-start(f32[64,512]{1,0:T(8,128)S(1)} %in_features.1.refs_0_), channel_id=1, source_target_pairs={{0,2},{1,3},{2,0},{3,1},{4,6},{5,7},{6,4},{7,5},{8,10},{9,11},{10,... | collective-permute-start | bytes 393224 | tf_op jit(solution)/shard_map/ppermute | solution.py:26
  23.0 6.7 %collective-permute-start.5 = (f32[2,4096]{1,0:T(2,128)S(1)}, f32[2,4096]{1,0:T(2,128)S(1)}, u32[]{:S(2)}, u32[]{:S(2)}) collective-permute-start(f32[2,4096]{1,0:T(2,128)S(1)} %reshape.7), channel_id=1, source_target_pairs={{0,1},{1,0},{2,3},{3,2},{4,5},{5,4},{6,7},{7,6},{8,9},{9,8},{10,11... | collective-permute-start | bytes 98312 | tf_op jit(solution)/shard_map/ppermute | solution.py:26
  24.7 5.7 %collective-permute-start.4 = (f32[2,4096]{1,0:T(2,128)S(1)}, f32[2,4096]{1,0:T(2,128)S(1)}, u32[]{:S(2)}, u32[]{:S(2)}) collective-permute-start(f32[2,4096]{1,0:T(2,128)S(1)} %reshape.7), channel_id=1, source_target_pairs={{0,3},{1,2},{2,1},{3,0},{4,7},{5,6},{6,5},{7,4},{8,11},{9,10},{10,... | collective-permute-start | bytes 98312 | tf_op jit(solution)/shard_map/ppermute | solution.py:26
  27.1 4.8 %collective-permute-start.3 = (f32[2,4096]{1,0:T(2,128)S(1)}, f32[2,4096]{1,0:T(2,128)S(1)}, u32[]{:S(2)}, u32[]{:S(2)}) collective-permute-start(f32[2,4096]{1,0:T(2,128)S(1)} %reshape.7), channel_id=1, source_target_pairs={{0,2},{1,3},{2,0},{3,1},{4,6},{5,7},{6,4},{7,5},{8,10},{9,11},{10,... | collective-permute-start | bytes 98312 | tf_op jit(solution)/shard_map/ppermute | solution.py:26
  32.0 3.7 %collective-permute-start.8 = (f32[2,4096]{1,0:T(2,128)S(1)}, f32[2,4096]{1,0:T(2,128)S(1)}, u32[]{:S(2)}, u32[]{:S(2)}) collective-permute-start(f32[2,4096]{1,0:T(2,128)S(1)} %add_add_fusion.refs_0_), channel_id=1, source_target_pairs={{0,12},{4,8},{8,4},{12,0},{1,13},{5,9},{9,5},{13,1},{2,14},{6,10},... | collective-permute-start | bytes 98312 | tf_op jit(solution)/shard_map/ppermute | solution.py:26
  32.1 4.0 %collective-permute-start.7 = (f32[2,4096]{1,0:T(2,128)S(1)}, f32[2,4096]{1,0:T(2,128)S(1)}, u32[]{:S(2)}, u32[]{:S(2)}) collective-permute-start(f32[2,4096]{1,0:T(2,128)S(1)} %add_add_fusion.refs_0_), channel_id=1, source_target_pairs={{0,8},{4,12},{8,0},{12,4},{1,9},{5,13},{9,1},{13,5},{2,10},{6,14},... | collective-permute-start | bytes 98312 | tf_op jit(solution)/shard_map/ppermute | solution.py:26
  33.6 2.5 %collective-permute-start.6 = (f32[2,4096]{1,0:T(2,128)S(1)}, f32[2,4096]{1,0:T(2,128)S(1)}, u32[]{:S(2)}, u32[]{:S(2)}) collective-permute-start(f32[2,4096]{1,0:T(2,128)S(1)} %add_add_fusion.refs_0_), channel_id=1, source_target_pairs={{0,4},{4,0},{8,12},{12,8},{1,5},{5,1},{9,13},{13,9},{2,6},{6,2},{1... | collective-permute-start | bytes 98312 | tf_op jit(solution)/shard_map/ppermute | solution.py:26

commit v25 on v24

--- a/solution.py
+++ b/solution.py
@@ -274,6 +274,15 @@
         compiler_params=PARAMS,
         name="cg_start",
     )(*pieces, *prior_pieces)
+
+
+def diagonal(shape):
+    return lax.broadcasted_iota(jnp.int32, shape, 0) == lax.broadcasted_iota(jnp.int32, shape, 1)
+
+
+def on_lanes(column):
+    here = diagonal((column.shape[0], LANES))
+    return jnp.sum(jnp.where(here, column, 0.0), axis=0, keepdims=True)
 
 
 def step_kernel(sizes, first, last, *refs):
@@ -307,11 +316,11 @@
     fisher_direction = fisher_direction_ref[...]
     fisher_residual = (fisher_direction if first else fisher_residual_ref[...]) - (step / scale) * twice
     fisher_direction = fisher_residual + share * fisher_direction
-    norm_out[...] = jnp.broadcast_to(norm_next, norm_out.shape)
+    norm_out[...] = on_lanes(norm_next) if last else jnp.broadcast_to(norm_next, norm_out.shape)
     if last:
         held[...] = direction
         own = own_columns(held, me, rows)
-        curvature_out[...] = jnp.broadcast_to(row_sum(own * fisher_direction), curvature_out.shape)
+        curvature_out[...] = on_lanes(row_sum(own * fisher_direction))
         seqs = direction.shape[0]
         solved = jnp.concatenate([solution, direction], axis=0)
         parts = jnp.dot(pieces_of(solved, 3), queries_ref[...], preferred_element_type=jnp.float32)
@@ -335,7 +344,7 @@
     if last:
         operands.append(queries)
         scores = F32((whole.shape[0], queries.shape[1]))
-        out_shape = (column, column, scores, scores)
+        out_shape = (F32((1, LANES)), F32((1, LANES)), scores, scores)
     return pl.pallas_call(
         functools.partial(step_kernel, sizes, first, last),
         out_shape=out_shape,
@@ -349,7 +358,9 @@
 
 def combine_kernel(curvature_ref, norm_ref, solved_ref, along_ref, scores_ref):
     step = norm_ref[...] / jnp.sum(curvature_ref[...], axis=0)
-    scores_ref[...] = solved_ref[...] + step[:, :1] * along_ref[...]
+    here = diagonal((solved_ref.shape[0], LANES))
+    step = row_sum(jnp.where(here, step, 0.0))
+    scores_ref[...] = solved_ref[...] + step * along_ref[...]
 
 
 def combine(curvature, norm, solved, along):

time: 78.5 us -> 78.1 us (level)
  no operation moved by 1% of the time
where the time goes in v25:
time: 78.1 us; the launch traced here: 77.8 us
  blocking collectives  35.7 us (46%)
  Pallas kernels  25.4 us (33%)
  starting transfers between devices  11.7 us (15%)
  waiting for transfers between devices  4.67 us (6%)
    all_to_all x4, blocking collectives, gather(): lax.all_to_all(value, ('dp', 'tensor'), 0, 0, axis_index_groups=[order])  35.7 us
    pallas_call x2, Pallas kernels, features(): pl.pallas_call(functools.partial(stream_kernel, block, by_row), out_shape...  16.4 us
    ppermute x9, starting transfers between devices, swap(): return lax.ppermute(value, axis, [(i, i ^ bit) for i in range(size)])  11.7 us
    ppermute x9, waiting for transfers between devices, swap(): return lax.ppermute(value, axis, [(i, i ^ bit) for i in range(size)])  4.67 us
    pallas_call x3, Pallas kernels, step_cg(): pl.pallas_call(functools.partial(step_kernel, sizes, first, last), out_sh...  3.97 us
    pallas_call x1, Pallas kernels, split_prior(): pl.pallas_call(split_kernel, out_shape=(pltpu.VMEM(prior.shape, jnp.bfloa...  2.56 us
  transfers between devices with their start and end apart: 9, of which 5 were waited for; matrix products, arithmetic and copies ran while one was open for 0% of the time, Pallas kernels for 18%

profile of v25, /device:TPU:0, one launch (start us, length us, event | category | flops | bytes accessed | tf_op | source)
XLA Modules:
  0.0 77.8 jit_solution(6570957372043652235)
XLA Ops:
  0.0 5.1 %in_features.1.refs_0_ = f32[64,512]{1,0:T(8,128)S(1)} custom-call(bf16[512,8192]{1,0:T(8,128)(2,1)} %rows_ref.2, bf16[64,8192]{1,0:T(8,128)(2,1)} %proj_ref.2), custom_call_target="tpu_custom_call" | custom-call | tf_op jit(solution)/shard_map/in_features/pallas_call | solution.py:125
  5.1 3.1 %collective-permute-start.2 = (f32[64,512]{1,0:T(8,128)S(1)}, f32[64,512]{1,0:T(8,128)S(1)}, u32[]{:S(2)}, u32[]{:S(2)}) collective-permute-start(f32[64,512]{1,0:T(8,128)S(1)} %in_features.1.refs_0_), channel_id=1, source_target_pairs={{0,1},{1,0},{2,3},{3,2},{4,5},{5,4},{6,7},{7,6},{8,9},{9,8},{10,11... | collective-permute-start | bytes 393224 | tf_op jit(solution)/shard_map/ppermute | solution.py:26
  8.2 2.5 %collective-permute-start.1 = (f32[64,512]{1,0:T(8,128)S(1)}, f32[64,512]{1,0:T(8,128)S(1)}, u32[]{:S(2)}, u32[]{:S(2)}) collective-permute-start(f32[64,512]{1,0:T(8,128)S(1)} %in_features.1.refs_0_), channel_id=1, source_target_pairs={{0,3},{1,2},{2,1},{3,0},{4,7},{5,6},{6,5},{7,4},{8,11},{9,10},{10,... | collective-permute-start | bytes 393224 | tf_op jit(solution)/shard_map/ppermute | solution.py:26
  10.8 11.4 %out_features.1.refs_4_ = f32[2048,128]{1,0:T(8,128)S(1)} custom-call(bf16[2048,7168]{1,0:T(8,128)(2,1)} %rows_ref.3, bf16[64,7168]{1,0:T(8,128)(2,1)} %proj_ref.3), custom_call_target="tpu_custom_call" | custom-call | tf_op jit(solution)/shard_map/out_features/pallas_call | solution.py:125
  22.1 0.2 collective-permute-done.refs_1_
  22.4 0.5 partial_vectors.1
  23.0 1.6 %collective-permute-start.5 = (f32[2,4096]{1,0:T(2,128)S(1)}, f32[2,4096]{1,0:T(2,128)S(1)}, u32[]{:S(2)}, u32[]{:S(2)}) collective-permute-start(f32[2,4096]{1,0:T(2,128)S(1)} %reshape.9), channel_id=1, source_target_pairs={{0,1},{1,0},{2,3},{3,2},{4,5},{5,4},{6,7},{7,6},{8,9},{9,8},{10,11... | collective-permute-start | bytes 98312 | tf_op jit(solution)/shard_map/ppermute | solution.py:26
  24.7 2.5 %collective-permute-start.4 = (f32[2,4096]{1,0:T(2,128)S(1)}, f32[2,4096]{1,0:T(2,128)S(1)}, u32[]{:S(2)}, u32[]{:S(2)}) collective-permute-start(f32[2,4096]{1,0:T(2,128)S(1)} %reshape.9), channel_id=1, source_target_pairs={{0,3},{1,2},{2,1},{3,0},{4,7},{5,6},{6,5},{7,4},{8,11},{9,10},{10,... | collective-permute-start | bytes 98312 | tf_op jit(solution)/shard_map/ppermute | solution.py:26
  27.1 2.6 %split_prior.1 = (bf16[256,4096]{1,0:T(8,128)(2,1)S(1)}, bf16[256,4096]{1,0:T(8,128)(2,1)S(1)}, bf16[4096,32]{1,0:T(8,128)(2,1)S(1)}) custom-call(f32[256,4096]{1,0:T(8,128)} %prior_ref, bf16[32,4096]{1,0:T(8,128)(2,1)S(1)} %copy-done), custom_call_target="tpu_custom_call" | custom-call | tf_op jit(solution)/shard_map/split_prior/pallas_call | solution.py:160
  29.7 0.7 collective-permute-done.4
  30.4 1.6 %collective-permute-done.3 = f32[2,4096]{1,0:T(2,128)S(1)} collective-permute-done((f32[2,4096]{1,0:T(2,128)S(1)}, f32[2,4096]{1,0:T(2,128)S(1)}, u32[]{:S(2)}, u32[]{:S(2)}) %collective-permute-start.3) | collective-permute-done | bytes 32800 | tf_op jit(solution)/shard_map/ppermute | solution.py:26
  32.1 1.6 %collective-permute-start.7 = (f32[2,4096]{1,0:T(2,128)S(1)}, f32[2,4096]{1,0:T(2,128)S(1)}, u32[]{:S(2)}, u32[]{:S(2)}) collective-permute-start(f32[2,4096]{1,0:T(2,128)S(1)} %add_add_fusion.refs_0_), channel_id=1, source_target_pairs={{0,8},{4,12},{8,0},{12,4},{1,9},{5,13},{9,1},{13,5},{2,10},{6,14},... | collective-permute-start | bytes 98312 | tf_op jit(solution)/shard_map/ppermute | solution.py:26
  33.6 0.3 collective-permute-start.6
  33.9 1.8 %collective-permute-done.8.refs_3_ = f32[2,4096]{1,0:T(2,128)S(1)} collective-permute-done((f32[2,4096]{1,0:T(2,128)S(1)}, f32[2,4096]{1,0:T(2,128)S(1)}, u32[]{:S(2)}, u32[]{:S(2)}) %collective-permute-start.8) | collective-permute-done | bytes 32800 | tf_op jit(solution)/shard_map/ppermute | solution.py:26
  35.7 0.4 collective-permute-done.7.refs_2_
  36.1 1.3 %cg_start.1 = (f32[8,4096]{1,0:T(8,128)S(1)}, f32[8,128]{1,0:T(8,128)S(1)}, f32[8,256]{1,0:T(8,128)S(1)}, f32[8,128]{1,0:T(8,128)S(1)}) custom-call(f32[2,4096]{1,0:T(2,128)S(1)} %add_add_fusion.refs_0_, f32[2,4096]{1,0:T(2,128)S(1)} %collective-permute-done.6.refs_1_, f32[2,4096]{1,0:T(2,128)S(1)} %collective-permute-done.7.refs_2_, ...), custom_call_target="tpu_custom_call" | custom-call | tf_op jit(solution)/shard_map/cg_start/pallas_call | solution.py:268
  37.4 9.4 %all_to_all.20.refs_0_ = f32[16,8,256]{2,1,0:T(8,128)S(1)} all-to-all(f32[16,8,256]{2,1,0:T(8,128)S(1)} %broadcast_in_dim.10), channel_id=1, replica_groups={{13,0,1,2,3,4,5,6,7,8,9,10,11,12,14,15},{29,16,17,18,19,20,21,22,23,24,..., dimensions={0} | all-to-all | bytes 262144 | tf_op jit(solution)/shard_map/all_to_all | solution.py:42
  46.7 1.3 %cg_step.3 = (f32[8,256]{1,0:T(8,128)S(1)}, f32[8,128]{1,0:T(8,128)S(1)}, f32[8,256]{1,0:T(8,128)S(1)}, f32[8,4096]{1,0:T(8,128)S(1)}, f32[8,4096]{1,0:T(8,128)S(1)}, /*index=5*/f32[8,4096]{1,0:T(8,128)S(1)}) custom-call(f32[16,8,256]{2,1,0:T(8,128)S(1)} %all_to_all.20.refs_0_, bf16[256,4096]{1,0:T(8,128)(2,1)S(1)} %get-tuple-element.40.refs_4_.refs_1_, ...), custom_call_target="tpu_custom_call" | custom-call | tf_op jit(solution)/shard_map/cg_step/pallas_call | solution.py:348
  48.1 9.2 %all_to_all.21.refs_0_ = f32[16,8,256]{2,1,0:T(8,128)S(1)} all-to-all(f32[16,8,256]{2,1,0:T(8,128)S(1)} %broadcast_in_dim.11), channel_id=1, replica_groups={{13,0,1,2,3,4,5,6,7,8,9,10,11,12,14,15},{29,16,17,18,19,20,21,22,23,24,..., dimensions={0} | all-to-all | bytes 262144 | tf_op jit(solution)/shard_map/all_to_all | solution.py:42
  57.3 1.3 %cg_step.4 = (f32[8,256]{1,0:T(8,128)S(1)}, f32[8,128]{1,0:T(8,128)S(1)}, f32[8,256]{1,0:T(8,128)S(1)}, f32[8,4096]{1,0:T(8,128)S(1)}, f32[8,4096]{1,0:T(8,128)S(1)}, /*index=5*/f32[8,4096]{1,0:T(8,128)S(1)}) custom-call(f32[16,8,256]{2,1,0:T(8,128)S(1)} %all_to_all.21.refs_0_, bf16[256,4096]{1,0:T(8,128)(2,1)S(1)} %get-tuple-element.40.refs_4_.refs_1_, ...), custom_call_target="tpu_custom_call" | custom-call | tf_op jit(solution)/shard_map/cg_step/pallas_call | solution.py:348
  58.6 9.2 %all_to_all.22.refs_0_ = f32[16,8,256]{2,1,0:T(8,128)S(1)} all-to-all(f32[16,8,256]{2,1,0:T(8,128)S(1)} %broadcast_in_dim.12), channel_id=1, replica_groups={{13,0,1,2,3,4,5,6,7,8,9,10,11,12,14,15},{29,16,17,18,19,20,21,22,23,24,..., dimensions={0} | all-to-all | bytes 262144 | tf_op jit(solution)/shard_map/all_to_all | solution.py:42
  67.8 1.4 %cg_step.5 = (f32[1,128]{1,0:T(1,128)S(1)}, f32[1,128]{1,0:T(1,128)S(1)}, f32[8,32]{1,0:T(8,128)S(1)}, f32[8,32]{1,0:T(8,128)S(1)}) custom-call(f32[16,8,256]{2,1,0:T(8,128)S(1)} %all_to_all.22.refs_0_, bf16[256,4096]{1,0:T(8,128)(2,1)S(1)} %get-tuple-element.40.refs_4_.refs_1_, bf16[256,4096]{1,0:T(8,128)(2,1)S(1)} %get-tuple-element.41.refs_5_.refs_2_, ...), custom_call_target="tpu_custom_call" | custom-call | tf_op jit(solution)/shard_map/cg_step/pallas_call | solution.py:348
  69.2 7.9 %all_to_all.23.curvature_ref = f32[16,1,128]{2,1,0:T(1,128)S(1)} all-to-all(f32[16,1,128]{2,1,0:T(1,128)S(1)} %broadcast_in_dim.14), channel_id=1, replica_groups={{13,0,1,2,3,4,5,6,7,8,9,10,11,12,14,15},{29,16,17,18,19,20,21,22,23,24,..., dimensions={0} | all-to-all | bytes 16384 | tf_op jit(solution)/shard_map/all_to_all | solution.py:42
  77.1 0.7 combine.1
  (15 shorter events, 0.4 us)
Async XLA Ops:
  5.1 22.1 %copy-start = (bf16[32,4096]{1,0:T(8,128)(2,1)S(1)}, bf16[32,4096]{1,0:T(8,128)(2,1)}, u32[]{:S(2)}) copy-start(bf16[32,4096]{1,0:T(8,128)(2,1)} %queries_ref.1) | copy-start | bytes 786436
  5.1 17.1 %collective-permute-start.2 = (f32[64,512]{1,0:T(8,128)S(1)}, f32[64,512]{1,0:T(8,128)S(1)}, u32[]{:S(2)}, u32[]{:S(2)}) collective-permute-start(f32[64,512]{1,0:T(8,128)S(1)} %in_features.1.refs_0_), channel_id=1, source_target_pairs={{0,1},{1,0},{2,3},{3,2},{4,5},{5,4},{6,7},{7,6},{8,9},{9,8},{10,11... | collective-permute-start | bytes 393224 | tf_op jit(solution)/shard_map/ppermute | solution.py:26
  8.2 14.0 %collective-permute-start.1 = (f32[64,512]{1,0:T(8,128)S(1)}, f32[64,512]{1,0:T(8,128)S(1)}, u32[]{:S(2)}, u32[]{:S(2)}) collective-permute-start(f32[64,512]{1,0:T(8,128)S(1)} %in_features.1.refs_0_), channel_id=1, source_target_pairs={{0,3},{1,2},{2,1},{3,0},{4,7},{5,6},{6,5},{7,4},{8,11},{9,10},{10,... | collective-permute-start | bytes 393224 | tf_op jit(solution)/shard_map/ppermute | solution.py:26
  10.6 11.8 %collective-permute-start = (f32[64,512]{1,0:T(8,128)S(1)}, f32[64,512]{1,0:T(8,128)S(1)}, u32[]{:S(2)}, u32[]{:S(2)}) collective-permute-start(f32[64,512]{1,0:T(8,128)S(1)} %in_features.1.refs_0_), channel_id=1, source_target_pairs={{0,2},{1,3},{2,0},{3,1},{4,6},{5,7},{6,4},{7,5},{8,10},{9,11},{10,... | collective-permute-start | bytes 393224 | tf_op jit(solution)/shard_map/ppermute | solution.py:26
  23.0 6.7 %collective-permute-start.5 = (f32[2,4096]{1,0:T(2,128)S(1)}, f32[2,4096]{1,0:T(2,128)S(1)}, u32[]{:S(2)}, u32[]{:S(2)}) collective-permute-start(f32[2,4096]{1,0:T(2,128)S(1)} %reshape.9), channel_id=1, source_target_pairs={{0,1},{1,0},{2,3},{3,2},{4,5},{5,4},{6,7},{7,6},{8,9},{9,8},{10,11... | collective-permute-start | bytes 98312 | tf_op jit(solution)/shard_map/ppermute | solution.py:26
  24.7 5.7 %collective-permute-start.4 = (f32[2,4096]{1,0:T(2,128)S(1)}, f32[2,4096]{1,0:T(2,128)S(1)}, u32[]{:S(2)}, u32[]{:S(2)}) collective-permute-start(f32[2,4096]{1,0:T(2,128)S(1)} %reshape.9), channel_id=1, source_target_pairs={{0,3},{1,2},{2,1},{3,0},{4,7},{5,6},{6,5},{7,4},{8,11},{9,10},{10,... | collective-permute-start | bytes 98312 | tf_op jit(solution)/shard_map/ppermute | solution.py:26
  27.1 4.8 %collective-permute-start.3 = (f32[2,4096]{1,0:T(2,128)S(1)}, f32[2,4096]{1,0:T(2,128)S(1)}, u32[]{:S(2)}, u32[]{:S(2)}) collective-permute-start(f32[2,4096]{1,0:T(2,128)S(1)} %reshape.9), channel_id=1, source_target_pairs={{0,2},{1,3},{2,0},{3,1},{4,6},{5,7},{6,4},{7,5},{8,10},{9,11},{10,... | collective-permute-start | bytes 98312 | tf_op jit(solution)/shard_map/ppermute | solution.py:26
  32.0 3.7 %collective-permute-start.8 = (f32[2,4096]{1,0:T(2,128)S(1)}, f32[2,4096]{1,0:T(2,128)S(1)}, u32[]{:S(2)}, u32[]{:S(2)}) collective-permute-start(f32[2,4096]{1,0:T(2,128)S(1)} %add_add_fusion.refs_0_), channel_id=1, source_target_pairs={{0,12},{4,8},{8,4},{12,0},{1,13},{5,9},{9,5},{13,1},{2,14},{6,10},... | collective-permute-start | bytes 98312 | tf_op jit(solution)/shard_map/ppermute | solution.py:26
  32.1 4.0 %collective-permute-start.7 = (f32[2,4096]{1,0:T(2,128)S(1)}, f32[2,4096]{1,0:T(2,128)S(1)}, u32[]{:S(2)}, u32[]{:S(2)}) collective-permute-start(f32[2,4096]{1,0:T(2,128)S(1)} %add_add_fusion.refs_0_), channel_id=1, source_target_pairs={{0,8},{4,12},{8,0},{12,4},{1,9},{5,13},{9,1},{13,5},{2,10},{6,14},... | collective-permute-start | bytes 98312 | tf_op jit(solution)/shard_map/ppermute | solution.py:26
  33.6 2.5 %collective-permute-start.6 = (f32[2,4096]{1,0:T(2,128)S(1)}, f32[2,4096]{1,0:T(2,128)S(1)}, u32[]{:S(2)}, u32[]{:S(2)}) collective-permute-start(f32[2,4096]{1,0:T(2,128)S(1)} %add_add_fusion.refs_0_), channel_id=1, source_target_pairs={{0,4},{4,0},{8,12},{12,8},{1,5},{5,1},{9,13},{13,9},{2,6},{6,2},{1... | collective-permute-start | bytes 98312 | tf_op jit(solution)/shard_map/ppermute | solution.py:26

commit v26 on v25

--- a/solution.py
+++ b/solution.py
@@ -13,7 +13,7 @@
 ITERS = 4
 LANES = 128
 FEW = 4
-DEPTH = 3
+DEPTH = 6
 NT = (((1,), (1,)), ((), ()))
 HIGHEST = lax.Precision.HIGHEST
 ANY_SPEC = pl.BlockSpec(memory_space=pl.ANY)
@@ -378,7 +378,7 @@
     width = R_IN * R_OUT
     sizes = dp_size, tensor_size
     in_blocks = direct(features(inputs, in_proj, LANES, False, 20, "in_features"), "tensor", tensor_size, order_of(tensor_size))
-    out_local = features(out_grads, out_proj, 2 * LANES, True, 44, "out_features")
+    out_local = features(out_grads, out_proj, LANES, True, 44, "out_features")
     partial = partial_vectors(in_blocks, out_local).reshape(-1, width)
     prior, partial = lax.optimization_barrier((prior, partial))
     own_vectors = sum_over(partial, "tensor", tensor_size)

time: 78.1 us -> 78.8 us (level)
  transfers between devices with their start and end apart: 9 -> 9, of which waited for: 5 -> 4; matrix products, arithmetic and copies ran while one was open for 0% -> 0% of each run, Pallas kernels for 18% -> 19%
where the time goes in v26:
time: 78.8 us; the launch traced here: 78.5 us
  blocking collectives  35.7 us (45%)
  Pallas kernels  26.1 us (33%)
  starting transfers between devices  11.9 us (15%)
  waiting for transfers between devices  4.42 us (6%)
    all_to_all x4, blocking collectives, gather(): lax.all_to_all(value, ('dp', 'tensor'), 0, 0, axis_index_groups=[order])  35.7 us
    pallas_call x2, Pallas kernels, features(): pl.pallas_call(functools.partial(stream_kernel, block, by_row), out_shape...  17.1 us
    ppermute x9, starting transfers between devices, swap(): return lax.ppermute(value, axis, [(i, i ^ bit) for i in range(size)])  11.9 us
    ppermute x9, waiting for transfers between devices, swap(): return lax.ppermute(value, axis, [(i, i ^ bit) for i in range(size)])  4.42 us
    pallas_call x3, Pallas kernels, step_cg(): pl.pallas_call(functools.partial(step_kernel, sizes, first, last), out_sh...  3.97 us
    pallas_call x1, Pallas kernels, split_prior(): pl.pallas_call(split_kernel, out_shape=(pltpu.VMEM(prior.shape, jnp.bfloa...  2.56 us
  transfers between devices with their start and end apart: 9, of which 4 were waited for; matrix products, arithmetic and copies ran while one was open for 0% of the time, Pallas kernels for 19%

profile of v26, /device:TPU:0, one launch (start us, length us, event | category | flops | bytes accessed | tf_op | source)
XLA Modules:
  0.0 78.5 jit_solution(7603036035451893528)
XLA Ops:
  0.0 5.1 %in_features.1.refs_0_ = f32[64,512]{1,0:T(8,128)S(1)} custom-call(bf16[512,8192]{1,0:T(8,128)(2,1)} %rows_ref.2, bf16[64,8192]{1,0:T(8,128)(2,1)} %proj_ref.2), custom_call_target="tpu_custom_call" | custom-call | tf_op jit(solution)/shard_map/in_features/pallas_call | solution.py:125
  5.1 3.1 %collective-permute-start.2 = (f32[64,512]{1,0:T(8,128)S(1)}, f32[64,512]{1,0:T(8,128)S(1)}, u32[]{:S(2)}, u32[]{:S(2)}) collective-permute-start(f32[64,512]{1,0:T(8,128)S(1)} %in_features.1.refs_0_), channel_id=1, source_target_pairs={{0,1},{1,0},{2,3},{3,2},{4,5},{5,4},{6,7},{7,6},{8,9},{9,8},{10,11... | collective-permute-start | bytes 393224 | tf_op jit(solution)/shard_map/ppermute | solution.py:26
  8.2 2.5 %collective-permute-start.1 = (f32[64,512]{1,0:T(8,128)S(1)}, f32[64,512]{1,0:T(8,128)S(1)}, u32[]{:S(2)}, u32[]{:S(2)}) collective-permute-start(f32[64,512]{1,0:T(8,128)S(1)} %in_features.1.refs_0_), channel_id=1, source_target_pairs={{0,3},{1,2},{2,1},{3,0},{4,7},{5,6},{6,5},{7,4},{8,11},{9,10},{10,... | collective-permute-start | bytes 393224 | tf_op jit(solution)/shard_map/ppermute | solution.py:26
  10.6 0.1 collective-permute-start
  10.8 12.0 %out_features.1.refs_4_ = f32[2048,128]{1,0:T(8,128)S(1)} custom-call(bf16[2048,7168]{1,0:T(8,128)(2,1)} %rows_ref.3, bf16[64,7168]{1,0:T(8,128)(2,1)} %proj_ref.3), custom_call_target="tpu_custom_call" | custom-call | tf_op jit(solution)/shard_map/out_features/pallas_call | solution.py:125
  22.8 0.5 partial_vectors.1
  23.5 1.9 %collective-permute-start.5 = (f32[2,4096]{1,0:T(2,128)S(1)}, f32[2,4096]{1,0:T(2,128)S(1)}, u32[]{:S(2)}, u32[]{:S(2)}) collective-permute-start(f32[2,4096]{1,0:T(2,128)S(1)} %reshape.9), channel_id=1, source_target_pairs={{0,1},{1,0},{2,3},{3,2},{4,5},{5,4},{6,7},{7,6},{8,9},{9,8},{10,11... | collective-permute-start | bytes 98312 | tf_op jit(solution)/shard_map/ppermute | solution.py:26
  25.4 2.5 %collective-permute-start.4 = (f32[2,4096]{1,0:T(2,128)S(1)}, f32[2,4096]{1,0:T(2,128)S(1)}, u32[]{:S(2)}, u32[]{:S(2)}) collective-permute-start(f32[2,4096]{1,0:T(2,128)S(1)} %reshape.9), channel_id=1, source_target_pairs={{0,3},{1,2},{2,1},{3,0},{4,7},{5,6},{6,5},{7,4},{8,11},{9,10},{10,... | collective-permute-start | bytes 98312 | tf_op jit(solution)/shard_map/ppermute | solution.py:26
  27.8 2.6 %split_prior.1 = (bf16[256,4096]{1,0:T(8,128)(2,1)S(1)}, bf16[256,4096]{1,0:T(8,128)(2,1)S(1)}, bf16[4096,32]{1,0:T(8,128)(2,1)S(1)}) custom-call(f32[256,4096]{1,0:T(8,128)} %prior_ref, bf16[32,4096]{1,0:T(8,128)(2,1)S(1)} %copy-done), custom_call_target="tpu_custom_call" | custom-call | tf_op jit(solution)/shard_map/split_prior/pallas_call | solution.py:160
  30.4 0.7 collective-permute-done.4
  31.1 1.6 %collective-permute-done.3 = f32[2,4096]{1,0:T(2,128)S(1)} collective-permute-done((f32[2,4096]{1,0:T(2,128)S(1)}, f32[2,4096]{1,0:T(2,128)S(1)}, u32[]{:S(2)}, u32[]{:S(2)}) %collective-permute-start.3) | collective-permute-done | bytes 32800 | tf_op jit(solution)/shard_map/ppermute | solution.py:26
  32.8 1.6 %collective-permute-start.7 = (f32[2,4096]{1,0:T(2,128)S(1)}, f32[2,4096]{1,0:T(2,128)S(1)}, u32[]{:S(2)}, u32[]{:S(2)}) collective-permute-start(f32[2,4096]{1,0:T(2,128)S(1)} %add_add_fusion.refs_0_), channel_id=1, source_target_pairs={{0,8},{4,12},{8,0},{12,4},{1,9},{5,13},{9,1},{13,5},{2,10},{6,14},... | collective-permute-start | bytes 98312 | tf_op jit(solution)/shard_map/ppermute | solution.py:26
  34.3 0.3 collective-permute-start.6
  34.6 1.8 %collective-permute-done.8.refs_3_ = f32[2,4096]{1,0:T(2,128)S(1)} collective-permute-done((f32[2,4096]{1,0:T(2,128)S(1)}, f32[2,4096]{1,0:T(2,128)S(1)}, u32[]{:S(2)}, u32[]{:S(2)}) %collective-permute-start.8) | collective-permute-done | bytes 32800 | tf_op jit(solution)/shard_map/ppermute | solution.py:26
  36.4 0.4 collective-permute-done.7.refs_2_
  36.8 1.3 %cg_start.1 = (f32[8,4096]{1,0:T(8,128)S(1)}, f32[8,128]{1,0:T(8,128)S(1)}, f32[8,256]{1,0:T(8,128)S(1)}, f32[8,128]{1,0:T(8,128)S(1)}) custom-call(f32[2,4096]{1,0:T(2,128)S(1)} %add_add_fusion.refs_0_, f32[2,4096]{1,0:T(2,128)S(1)} %collective-permute-done.6.refs_1_, f32[2,4096]{1,0:T(2,128)S(1)} %collective-permute-done.7.refs_2_, ...), custom_call_target="tpu_custom_call" | custom-call | tf_op jit(solution)/shard_map/cg_start/pallas_call | solution.py:268
  38.1 9.4 %all_to_all.20.refs_0_ = f32[16,8,256]{2,1,0:T(8,128)S(1)} all-to-all(f32[16,8,256]{2,1,0:T(8,128)S(1)} %broadcast_in_dim.10), channel_id=1, replica_groups={{13,0,1,2,3,4,5,6,7,8,9,10,11,12,14,15},{29,16,17,18,19,20,21,22,23,24,..., dimensions={0} | all-to-all | bytes 262144 | tf_op jit(solution)/shard_map/all_to_all | solution.py:42
  47.4 1.3 %cg_step.3 = (f32[8,256]{1,0:T(8,128)S(1)}, f32[8,128]{1,0:T(8,128)S(1)}, f32[8,256]{1,0:T(8,128)S(1)}, f32[8,4096]{1,0:T(8,128)S(1)}, f32[8,4096]{1,0:T(8,128)S(1)}, /*index=5*/f32[8,4096]{1,0:T(8,128)S(1)}) custom-call(f32[16,8,256]{2,1,0:T(8,128)S(1)} %all_to_all.20.refs_0_, bf16[256,4096]{1,0:T(8,128)(2,1)S(1)} %get-tuple-element.40.refs_4_.refs_1_, ...), custom_call_target="tpu_custom_call" | custom-call | tf_op jit(solution)/shard_map/cg_step/pallas_call | solution.py:348
  48.7 9.2 %all_to_all.21.refs_0_ = f32[16,8,256]{2,1,0:T(8,128)S(1)} all-to-all(f32[16,8,256]{2,1,0:T(8,128)S(1)} %broadcast_in_dim.11), channel_id=1, replica_groups={{13,0,1,2,3,4,5,6,7,8,9,10,11,12,14,15},{29,16,17,18,19,20,21,22,23,24,..., dimensions={0} | all-to-all | bytes 262144 | tf_op jit(solution)/shard_map/all_to_all | solution.py:42
  58.0 1.3 %cg_step.4 = (f32[8,256]{1,0:T(8,128)S(1)}, f32[8,128]{1,0:T(8,128)S(1)}, f32[8,256]{1,0:T(8,128)S(1)}, f32[8,4096]{1,0:T(8,128)S(1)}, f32[8,4096]{1,0:T(8,128)S(1)}, /*index=5*/f32[8,4096]{1,0:T(8,128)S(1)}) custom-call(f32[16,8,256]{2,1,0:T(8,128)S(1)} %all_to_all.21.refs_0_, bf16[256,4096]{1,0:T(8,128)(2,1)S(1)} %get-tuple-element.40.refs_4_.refs_1_, ...), custom_call_target="tpu_custom_call" | custom-call | tf_op jit(solution)/shard_map/cg_step/pallas_call | solution.py:348
  59.3 9.2 %all_to_all.22.refs_0_ = f32[16,8,256]{2,1,0:T(8,128)S(1)} all-to-all(f32[16,8,256]{2,1,0:T(8,128)S(1)} %broadcast_in_dim.12), channel_id=1, replica_groups={{13,0,1,2,3,4,5,6,7,8,9,10,11,12,14,15},{29,16,17,18,19,20,21,22,23,24,..., dimensions={0} | all-to-all | bytes 262144 | tf_op jit(solution)/shard_map/all_to_all | solution.py:42
  68.5 1.4 %cg_step.5 = (f32[1,128]{1,0:T(1,128)S(1)}, f32[1,128]{1,0:T(1,128)S(1)}, f32[8,32]{1,0:T(8,128)S(1)}, f32[8,32]{1,0:T(8,128)S(1)}) custom-call(f32[16,8,256]{2,1,0:T(8,128)S(1)} %all_to_all.22.refs_0_, bf16[256,4096]{1,0:T(8,128)(2,1)S(1)} %get-tuple-element.40.refs_4_.refs_1_, bf16[256,4096]{1,0:T(8,128)(2,1)S(1)} %get-tuple-element.41.refs_5_.refs_2_, ...), custom_call_target="tpu_custom_call" | custom-call | tf_op jit(solution)/shard_map/cg_step/pallas_call | solution.py:348
  69.9 7.9 %all_to_all.23.curvature_ref = f32[16,1,128]{2,1,0:T(1,128)S(1)} all-to-all(f32[16,1,128]{2,1,0:T(1,128)S(1)} %broadcast_in_dim.14), channel_id=1, replica_groups={{13,0,1,2,3,4,5,6,7,8,9,10,11,12,14,15},{29,16,17,18,19,20,21,22,23,24,..., dimensions={0} | all-to-all | bytes 16384 | tf_op jit(solution)/shard_map/all_to_all | solution.py:42
  77.8 0.7 combine.1
  (15 shorter events, 0.3 us)
Async XLA Ops:
  5.1 22.8 %copy-start = (bf16[32,4096]{1,0:T(8,128)(2,1)S(1)}, bf16[32,4096]{1,0:T(8,128)(2,1)}, u32[]{:S(2)}) copy-start(bf16[32,4096]{1,0:T(8,128)(2,1)} %queries_ref.1) | copy-start | bytes 786436
  5.1 17.7 %collective-permute-start.2 = (f32[64,512]{1,0:T(8,128)S(1)}, f32[64,512]{1,0:T(8,128)S(1)}, u32[]{:S(2)}, u32[]{:S(2)}) collective-permute-start(f32[64,512]{1,0:T(8,128)S(1)} %in_features.1.refs_0_), channel_id=1, source_target_pairs={{0,1},{1,0},{2,3},{3,2},{4,5},{5,4},{6,7},{7,6},{8,9},{9,8},{10,11... | collective-permute-start | bytes 393224 | tf_op jit(solution)/shard_map/ppermute | solution.py:26
  8.2 14.7 %collective-permute-start.1 = (f32[64,512]{1,0:T(8,128)S(1)}, f32[64,512]{1,0:T(8,128)S(1)}, u32[]{:S(2)}, u32[]{:S(2)}) collective-permute-start(f32[64,512]{1,0:T(8,128)S(1)} %in_features.1.refs_0_), channel_id=1, source_target_pairs={{0,3},{1,2},{2,1},{3,0},{4,7},{5,6},{6,5},{7,4},{8,11},{9,10},{10,... | collective-permute-start | bytes 393224 | tf_op jit(solution)/shard_map/ppermute | solution.py:26
  10.6 12.2 %collective-permute-start = (f32[64,512]{1,0:T(8,128)S(1)}, f32[64,512]{1,0:T(8,128)S(1)}, u32[]{:S(2)}, u32[]{:S(2)}) collective-permute-start(f32[64,512]{1,0:T(8,128)S(1)} %in_features.1.refs_0_), channel_id=1, source_target_pairs={{0,2},{1,3},{2,0},{3,1},{4,6},{5,7},{6,4},{7,5},{8,10},{9,11},{10,... | collective-permute-start | bytes 393224 | tf_op jit(solution)/shard_map/ppermute | solution.py:26
  23.5 6.9 %collective-permute-start.5 = (f32[2,4096]{1,0:T(2,128)S(1)}, f32[2,4096]{1,0:T(2,128)S(1)}, u32[]{:S(2)}, u32[]{:S(2)}) collective-permute-start(f32[2,4096]{1,0:T(2,128)S(1)} %reshape.9), channel_id=1, source_target_pairs={{0,1},{1,0},{2,3},{3,2},{4,5},{5,4},{6,7},{7,6},{8,9},{9,8},{10,11... | collective-permute-start | bytes 98312 | tf_op jit(solution)/shard_map/ppermute | solution.py:26
  25.4 5.7 %collective-permute-start.4 = (f32[2,4096]{1,0:T(2,128)S(1)}, f32[2,4096]{1,0:T(2,128)S(1)}, u32[]{:S(2)}, u32[]{:S(2)}) collective-permute-start(f32[2,4096]{1,0:T(2,128)S(1)} %reshape.9), channel_id=1, source_target_pairs={{0,3},{1,2},{2,1},{3,0},{4,7},{5,6},{6,5},{7,4},{8,11},{9,10},{10,... | collective-permute-start | bytes 98312 | tf_op jit(solution)/shard_map/ppermute | solution.py:26
  27.8 4.8 %collective-permute-start.3 = (f32[2,4096]{1,0:T(2,128)S(1)}, f32[2,4096]{1,0:T(2,128)S(1)}, u32[]{:S(2)}, u32[]{:S(2)}) collective-permute-start(f32[2,4096]{1,0:T(2,128)S(1)} %reshape.9), channel_id=1, source_target_pairs={{0,2},{1,3},{2,0},{3,1},{4,6},{5,7},{6,4},{7,5},{8,10},{9,11},{10,... | collective-permute-start | bytes 98312 | tf_op jit(solution)/shard_map/ppermute | solution.py:26
  32.7 3.7 %collective-permute-start.8 = (f32[2,4096]{1,0:T(2,128)S(1)}, f32[2,4096]{1,0:T(2,128)S(1)}, u32[]{:S(2)}, u32[]{:S(2)}) collective-permute-start(f32[2,4096]{1,0:T(2,128)S(1)} %add_add_fusion.refs_0_), channel_id=1, source_target_pairs={{0,12},{4,8},{8,4},{12,0},{1,13},{5,9},{9,5},{13,1},{2,14},{6,10},... | collective-permute-start | bytes 98312 | tf_op jit(solution)/shard_map/ppermute | solution.py:26
  32.8 4.0 %collective-permute-start.7 = (f32[2,4096]{1,0:T(2,128)S(1)}, f32[2,4096]{1,0:T(2,128)S(1)}, u32[]{:S(2)}, u32[]{:S(2)}) collective-permute-start(f32[2,4096]{1,0:T(2,128)S(1)} %add_add_fusion.refs_0_), channel_id=1, source_target_pairs={{0,8},{4,12},{8,0},{12,4},{1,9},{5,13},{9,1},{13,5},{2,10},{6,14},... | collective-permute-start | bytes 98312 | tf_op jit(solution)/shard_map/ppermute | solution.py:26
  34.3 2.5 %collective-permute-start.6 = (f32[2,4096]{1,0:T(2,128)S(1)}, f32[2,4096]{1,0:T(2,128)S(1)}, u32[]{:S(2)}, u32[]{:S(2)}) collective-permute-start(f32[2,4096]{1,0:T(2,128)S(1)} %add_add_fusion.refs_0_), channel_id=1, source_target_pairs={{0,4},{4,0},{8,12},{12,8},{1,5},{5,1},{9,13},{13,9},{2,6},{6,2},{1... | collective-permute-start | bytes 98312 | tf_op jit(solution)/shard_map/ppermute | solution.py:26

commit v27 on v25

--- a/solution.py
+++ b/solution.py
@@ -55,7 +55,7 @@
         for bit in bits(size):
             value = value + swap(value, axis, size, bit)
         return value
-    blocks = direct(value, axis, size, order_of(size))
+    blocks = direct(value, axis, size, range(size))
     while len(blocks) > 1:
         blocks = [a + b for a, b in zip(blocks[::2], blocks[1::2])]
     return blocks[0]

time: 78.1 us -> 77.3 us (0.990)
  waiting for transfers between devices: 4.67 us -> 3.21 us
    ppermute x9, waiting for transfers between devices: 4.67 us -> 3.21 us  [swap(): return lax.ppermute(value, axis, [(i, i ^ bit) for i in range(size)])]
  transfers between devices with their start and end apart: 9 -> 9, of which waited for: 5 -> 4; matrix products, arithmetic and copies ran while one was open for 0% -> 0% of each run, Pallas kernels for 18% -> 18%
where the time goes in v27:
time: 77.3 us; the launch traced here: 77 us
  blocking collectives  36 us (47%)
  Pallas kernels  25.4 us (33%)
  starting transfers between devices  12.1 us (16%)
  waiting for transfers between devices  3.21 us (4%)
    all_to_all x4, blocking collectives, gather(): lax.all_to_all(value, ('dp', 'tensor'), 0, 0, axis_index_groups=[order])  36 us
    pallas_call x2, Pallas kernels, features(): pl.pallas_call(functools.partial(stream_kernel, block, by_row), out_shape...  16.4 us
    ppermute x9, starting transfers between devices, swap(): return lax.ppermute(value, axis, [(i, i ^ bit) for i in range(size)])  12.1 us
    pallas_call x3, Pallas kernels, step_cg(): pl.pallas_call(functools.partial(step_kernel, sizes, first, last), out_sh...  3.97 us
    ppermute x9, waiting for transfers between devices, swap(): return lax.ppermute(value, axis, [(i, i ^ bit) for i in range(size)])  3.21 us
    pallas_call x1, Pallas kernels, split_prior(): pl.pallas_call(split_kernel, out_shape=(pltpu.VMEM(prior.shape, jnp.bfloa...  2.56 us
  transfers between devices with their start and end apart: 9, of which 4 were waited for; matrix products, arithmetic and copies ran while one was open for 0% of the time, Pallas kernels for 18%

profile of v27, /device:TPU:0, one launch (start us, length us, event | category | flops | bytes accessed | tf_op | source)
XLA Modules:
  0.0 77.0 jit_solution(17607276512988086549)
XLA Ops:
  0.0 5.1 %in_features.1.refs_0_ = f32[64,512]{1,0:T(8,128)S(1)} custom-call(bf16[512,8192]{1,0:T(8,128)(2,1)} %rows_ref.2, bf16[64,8192]{1,0:T(8,128)(2,1)} %proj_ref.2), custom_call_target="tpu_custom_call" | custom-call | tf_op jit(solution)/shard_map/in_features/pallas_call | solution.py:125
  5.1 3.1 %collective-permute-start.2 = (f32[64,512]{1,0:T(8,128)S(1)}, f32[64,512]{1,0:T(8,128)S(1)}, u32[]{:S(2)}, u32[]{:S(2)}) collective-permute-start(f32[64,512]{1,0:T(8,128)S(1)} %in_features.1.refs_0_), channel_id=1, source_target_pairs={{0,1},{1,0},{2,3},{3,2},{4,5},{5,4},{6,7},{7,6},{8,9},{9,8},{10,11... | collective-permute-start | bytes 393224 | tf_op jit(solution)/shard_map/ppermute | solution.py:26
  8.2 2.5 %collective-permute-start.1 = (f32[64,512]{1,0:T(8,128)S(1)}, f32[64,512]{1,0:T(8,128)S(1)}, u32[]{:S(2)}, u32[]{:S(2)}) collective-permute-start(f32[64,512]{1,0:T(8,128)S(1)} %in_features.1.refs_0_), channel_id=1, source_target_pairs={{0,3},{1,2},{2,1},{3,0},{4,7},{5,6},{6,5},{7,4},{8,11},{9,10},{10,... | collective-permute-start | bytes 393224 | tf_op jit(solution)/shard_map/ppermute | solution.py:26
  10.8 11.4 %out_features.1.refs_4_ = f32[2048,128]{1,0:T(8,128)S(1)} custom-call(bf16[2048,7168]{1,0:T(8,128)(2,1)} %rows_ref.3, bf16[64,7168]{1,0:T(8,128)(2,1)} %proj_ref.3), custom_call_target="tpu_custom_call" | custom-call | tf_op jit(solution)/shard_map/out_features/pallas_call | solution.py:125
  22.1 0.2 collective-permute-done.refs_1_
  22.4 0.5 partial_vectors.1
  23.0 2.8 %collective-permute-start.5 = (f32[2,4096]{1,0:T(2,128)S(1)}, f32[2,4096]{1,0:T(2,128)S(1)}, u32[]{:S(2)}, u32[]{:S(2)}) collective-permute-start(f32[2,4096]{1,0:T(2,128)S(1)} %reshape.9), channel_id=1, source_target_pairs={{0,3},{1,2},{2,1},{3,0},{4,7},{5,6},{6,5},{7,4},{8,11},{9,10},{10,... | collective-permute-start | bytes 98312 | tf_op jit(solution)/shard_map/ppermute | solution.py:26
  25.8 0.3 collective-permute-start.4
  26.1 1.4 %collective-permute-start.3 = (f32[2,4096]{1,0:T(2,128)S(1)}, f32[2,4096]{1,0:T(2,128)S(1)}, u32[]{:S(2)}, u32[]{:S(2)}) collective-permute-start(f32[2,4096]{1,0:T(2,128)S(1)} %reshape.9), channel_id=1, source_target_pairs={{0,1},{1,0},{2,3},{3,2},{4,5},{5,4},{6,7},{7,6},{8,9},{9,8},{10,11... | collective-permute-start | bytes 98312 | tf_op jit(solution)/shard_map/ppermute | solution.py:26
  27.5 2.6 %split_prior.1 = (bf16[256,4096]{1,0:T(8,128)(2,1)S(1)}, bf16[256,4096]{1,0:T(8,128)(2,1)S(1)}, bf16[4096,32]{1,0:T(8,128)(2,1)S(1)}) custom-call(f32[256,4096]{1,0:T(8,128)} %prior_ref, bf16[32,4096]{1,0:T(8,128)(2,1)S(1)} %copy-done), custom_call_target="tpu_custom_call" | custom-call | tf_op jit(solution)/shard_map/split_prior/pallas_call | solution.py:160
  30.1 0.8 %collective-permute-done.4 = f32[2,4096]{1,0:T(2,128)S(1)} collective-permute-done((f32[2,4096]{1,0:T(2,128)S(1)}, f32[2,4096]{1,0:T(2,128)S(1)}, u32[]{:S(2)}, u32[]{:S(2)}) %collective-permute-start.4) | collective-permute-done | bytes 32800 | tf_op jit(solution)/shard_map/ppermute | solution.py:26
  31.0 1.6 %collective-permute-start.7 = (f32[2,4096]{1,0:T(2,128)S(1)}, f32[2,4096]{1,0:T(2,128)S(1)}, u32[]{:S(2)}, u32[]{:S(2)}) collective-permute-start(f32[2,4096]{1,0:T(2,128)S(1)} %add_add_fusion.refs_0_), channel_id=1, source_target_pairs={{0,8},{4,12},{8,0},{12,4},{1,9},{5,13},{9,1},{13,5},{2,10},{6,14},... | collective-permute-start | bytes 98312 | tf_op jit(solution)/shard_map/ppermute | solution.py:26
  32.5 0.3 collective-permute-start.6
  32.8 1.8 %collective-permute-done.8.refs_3_ = f32[2,4096]{1,0:T(2,128)S(1)} collective-permute-done((f32[2,4096]{1,0:T(2,128)S(1)}, f32[2,4096]{1,0:T(2,128)S(1)}, u32[]{:S(2)}, u32[]{:S(2)}) %collective-permute-start.8) | collective-permute-done | bytes 32800 | tf_op jit(solution)/shard_map/ppermute | solution.py:26
  34.6 0.4 collective-permute-done.7.refs_2_
  35.0 1.3 %cg_start.1 = (f32[8,4096]{1,0:T(8,128)S(1)}, f32[8,128]{1,0:T(8,128)S(1)}, f32[8,256]{1,0:T(8,128)S(1)}, f32[8,128]{1,0:T(8,128)S(1)}) custom-call(f32[2,4096]{1,0:T(2,128)S(1)} %add_add_fusion.refs_0_, f32[2,4096]{1,0:T(2,128)S(1)} %collective-permute-done.6.refs_1_, f32[2,4096]{1,0:T(2,128)S(1)} %collective-permute-done.7.refs_2_, ...), custom_call_target="tpu_custom_call" | custom-call | tf_op jit(solution)/shard_map/cg_start/pallas_call | solution.py:268
  36.3 9.7 %all_to_all.20.refs_0_ = f32[16,8,256]{2,1,0:T(8,128)S(1)} all-to-all(f32[16,8,256]{2,1,0:T(8,128)S(1)} %broadcast_in_dim.10), channel_id=1, replica_groups={{13,0,1,2,3,4,5,6,7,8,9,10,11,12,14,15},{29,16,17,18,19,20,21,22,23,24,..., dimensions={0} | all-to-all | bytes 262144 | tf_op jit(solution)/shard_map/all_to_all | solution.py:42
  46.0 1.3 %cg_step.3 = (f32[8,256]{1,0:T(8,128)S(1)}, f32[8,128]{1,0:T(8,128)S(1)}, f32[8,256]{1,0:T(8,128)S(1)}, f32[8,4096]{1,0:T(8,128)S(1)}, f32[8,4096]{1,0:T(8,128)S(1)}, /*index=5*/f32[8,4096]{1,0:T(8,128)S(1)}) custom-call(f32[16,8,256]{2,1,0:T(8,128)S(1)} %all_to_all.20.refs_0_, bf16[256,4096]{1,0:T(8,128)(2,1)S(1)} %get-tuple-element.40.refs_4_.refs_1_, ...), custom_call_target="tpu_custom_call" | custom-call | tf_op jit(solution)/shard_map/cg_step/pallas_call | solution.py:348
  47.3 9.2 %all_to_all.21.refs_0_ = f32[16,8,256]{2,1,0:T(8,128)S(1)} all-to-all(f32[16,8,256]{2,1,0:T(8,128)S(1)} %broadcast_in_dim.11), channel_id=1, replica_groups={{13,0,1,2,3,4,5,6,7,8,9,10,11,12,14,15},{29,16,17,18,19,20,21,22,23,24,..., dimensions={0} | all-to-all | bytes 262144 | tf_op jit(solution)/shard_map/all_to_all | solution.py:42
  56.5 1.3 %cg_step.4 = (f32[8,256]{1,0:T(8,128)S(1)}, f32[8,128]{1,0:T(8,128)S(1)}, f32[8,256]{1,0:T(8,128)S(1)}, f32[8,4096]{1,0:T(8,128)S(1)}, f32[8,4096]{1,0:T(8,128)S(1)}, /*index=5*/f32[8,4096]{1,0:T(8,128)S(1)}) custom-call(f32[16,8,256]{2,1,0:T(8,128)S(1)} %all_to_all.21.refs_0_, bf16[256,4096]{1,0:T(8,128)(2,1)S(1)} %get-tuple-element.40.refs_4_.refs_1_, ...), custom_call_target="tpu_custom_call" | custom-call | tf_op jit(solution)/shard_map/cg_step/pallas_call | solution.py:348
  57.8 9.2 %all_to_all.22.refs_0_ = f32[16,8,256]{2,1,0:T(8,128)S(1)} all-to-all(f32[16,8,256]{2,1,0:T(8,128)S(1)} %broadcast_in_dim.12), channel_id=1, replica_groups={{13,0,1,2,3,4,5,6,7,8,9,10,11,12,14,15},{29,16,17,18,19,20,21,22,23,24,..., dimensions={0} | all-to-all | bytes 262144 | tf_op jit(solution)/shard_map/all_to_all | solution.py:42
  67.0 1.4 %cg_step.5 = (f32[1,128]{1,0:T(1,128)S(1)}, f32[1,128]{1,0:T(1,128)S(1)}, f32[8,32]{1,0:T(8,128)S(1)}, f32[8,32]{1,0:T(8,128)S(1)}) custom-call(f32[16,8,256]{2,1,0:T(8,128)S(1)} %all_to_all.22.refs_0_, bf16[256,4096]{1,0:T(8,128)(2,1)S(1)} %get-tuple-element.40.refs_4_.refs_1_, bf16[256,4096]{1,0:T(8,128)(2,1)S(1)} %get-tuple-element.41.refs_5_.refs_2_, ...), custom_call_target="tpu_custom_call" | custom-call | tf_op jit(solution)/shard_map/cg_step/pallas_call | solution.py:348
  68.5 7.9 %all_to_all.23.curvature_ref = f32[16,1,128]{2,1,0:T(1,128)S(1)} all-to-all(f32[16,1,128]{2,1,0:T(1,128)S(1)} %broadcast_in_dim.14), channel_id=1, replica_groups={{13,0,1,2,3,4,5,6,7,8,9,10,11,12,14,15},{29,16,17,18,19,20,21,22,23,24,..., dimensions={0} | all-to-all | bytes 16384 | tf_op jit(solution)/shard_map/all_to_all | solution.py:42
  76.3 0.7 combine.1
  (15 shorter events, 0.4 us)
Async XLA Ops:
  5.1 22.4 %copy-start = (bf16[32,4096]{1,0:T(8,128)(2,1)S(1)}, bf16[32,4096]{1,0:T(8,128)(2,1)}, u32[]{:S(2)}) copy-start(bf16[32,4096]{1,0:T(8,128)(2,1)} %queries_ref.1) | copy-start | bytes 786436
  5.1 17.1 %collective-permute-start.2 = (f32[64,512]{1,0:T(8,128)S(1)}, f32[64,512]{1,0:T(8,128)S(1)}, u32[]{:S(2)}, u32[]{:S(2)}) collective-permute-start(f32[64,512]{1,0:T(8,128)S(1)} %in_features.1.refs_0_), channel_id=1, source_target_pairs={{0,1},{1,0},{2,3},{3,2},{4,5},{5,4},{6,7},{7,6},{8,9},{9,8},{10,11... | collective-permute-start | bytes 393224 | tf_op jit(solution)/shard_map/ppermute | solution.py:26
  8.2 14.0 %collective-permute-start.1 = (f32[64,512]{1,0:T(8,128)S(1)}, f32[64,512]{1,0:T(8,128)S(1)}, u32[]{:S(2)}, u32[]{:S(2)}) collective-permute-start(f32[64,512]{1,0:T(8,128)S(1)} %in_features.1.refs_0_), channel_id=1, source_target_pairs={{0,3},{1,2},{2,1},{3,0},{4,7},{5,6},{6,5},{7,4},{8,11},{9,10},{10,... | collective-permute-start | bytes 393224 | tf_op jit(solution)/shard_map/ppermute | solution.py:26
  10.6 11.8 %collective-permute-start = (f32[64,512]{1,0:T(8,128)S(1)}, f32[64,512]{1,0:T(8,128)S(1)}, u32[]{:S(2)}, u32[]{:S(2)}) collective-permute-start(f32[64,512]{1,0:T(8,128)S(1)} %in_features.1.refs_0_), channel_id=1, source_target_pairs={{0,2},{1,3},{2,0},{3,1},{4,6},{5,7},{6,4},{7,5},{8,10},{9,11},{10,... | collective-permute-start | bytes 393224 | tf_op jit(solution)/shard_map/ppermute | solution.py:26
  23.0 7.0 %collective-permute-start.5 = (f32[2,4096]{1,0:T(2,128)S(1)}, f32[2,4096]{1,0:T(2,128)S(1)}, u32[]{:S(2)}, u32[]{:S(2)}) collective-permute-start(f32[2,4096]{1,0:T(2,128)S(1)} %reshape.9), channel_id=1, source_target_pairs={{0,3},{1,2},{2,1},{3,0},{4,7},{5,6},{6,5},{7,4},{8,11},{9,10},{10,... | collective-permute-start | bytes 98312 | tf_op jit(solution)/shard_map/ppermute | solution.py:26
  25.8 5.0 %collective-permute-start.4 = (f32[2,4096]{1,0:T(2,128)S(1)}, f32[2,4096]{1,0:T(2,128)S(1)}, u32[]{:S(2)}, u32[]{:S(2)}) collective-permute-start(f32[2,4096]{1,0:T(2,128)S(1)} %reshape.9), channel_id=1, source_target_pairs={{0,2},{1,3},{2,0},{3,1},{4,6},{5,7},{6,4},{7,5},{8,10},{9,11},{10,... | collective-permute-start | bytes 98312 | tf_op jit(solution)/shard_map/ppermute | solution.py:26
  26.1 4.7 %collective-permute-start.3 = (f32[2,4096]{1,0:T(2,128)S(1)}, f32[2,4096]{1,0:T(2,128)S(1)}, u32[]{:S(2)}, u32[]{:S(2)}) collective-permute-start(f32[2,4096]{1,0:T(2,128)S(1)} %reshape.9), channel_id=1, source_target_pairs={{0,1},{1,0},{2,3},{3,2},{4,5},{5,4},{6,7},{7,6},{8,9},{9,8},{10,11... | collective-permute-start | bytes 98312 | tf_op jit(solution)/shard_map/ppermute | solution.py:26
  30.9 3.7 %collective-permute-start.8 = (f32[2,4096]{1,0:T(2,128)S(1)}, f32[2,4096]{1,0:T(2,128)S(1)}, u32[]{:S(2)}, u32[]{:S(2)}) collective-permute-start(f32[2,4096]{1,0:T(2,128)S(1)} %add_add_fusion.refs_0_), channel_id=1, source_target_pairs={{0,12},{4,8},{8,4},{12,0},{1,13},{5,9},{9,5},{13,1},{2,14},{6,10},... | collective-permute-start | bytes 98312 | tf_op jit(solution)/shard_map/ppermute | solution.py:26
  31.0 4.0 %collective-permute-start.7 = (f32[2,4096]{1,0:T(2,128)S(1)}, f32[2,4096]{1,0:T(2,128)S(1)}, u32[]{:S(2)}, u32[]{:S(2)}) collective-permute-start(f32[2,4096]{1,0:T(2,128)S(1)} %add_add_fusion.refs_0_), channel_id=1, source_target_pairs={{0,8},{4,12},{8,0},{12,4},{1,9},{5,13},{9,1},{13,5},{2,10},{6,14},... | collective-permute-start | bytes 98312 | tf_op jit(solution)/shard_map/ppermute | solution.py:26
  32.5 2.5 %collective-permute-start.6 = (f32[2,4096]{1,0:T(2,128)S(1)}, f32[2,4096]{1,0:T(2,128)S(1)}, u32[]{:S(2)}, u32[]{:S(2)}) collective-permute-start(f32[2,4096]{1,0:T(2,128)S(1)} %add_add_fusion.refs_0_), channel_id=1, source_target_pairs={{0,4},{4,0},{8,12},{12,8},{1,5},{5,1},{9,13},{13,9},{2,6},{6,2},{1... | collective-permute-start | bytes 98312 | tf_op jit(solution)/shard_map/ppermute | solution.py:26

commit v28 on v27

--- a/solution.py
+++ b/solution.py
@@ -32,7 +32,7 @@
 
 def group_order(sizes):
     dp_size, tensor_size = sizes
-    first = (dp_size - 1) * tensor_size + (tensor_size - 1) // 2
+    first = (dp_size - 1) * tensor_size + tensor_size // 2
     return [first] + [i for i in range(dp_size * tensor_size) if i != first]
 
 

time: 77.3 us -> 76.8 us (level)
  no operation moved by 1% of the time
where the time goes in v28:
time: 76.8 us; the launch traced here: 76.5 us
  blocking collectives  35.5 us (46%)
  Pallas kernels  25.4 us (33%)
  starting transfers between devices  12.1 us (16%)
  waiting for transfers between devices  3.21 us (4%)
    all_to_all x4, blocking collectives, gather(): lax.all_to_all(value, ('dp', 'tensor'), 0, 0, axis_index_groups=[order])  35.5 us
    pallas_call x2, Pallas kernels, features(): pl.pallas_call(functools.partial(stream_kernel, block, by_row), out_shape...  16.4 us
    ppermute x9, starting transfers between devices, swap(): return lax.ppermute(value, axis, [(i, i ^ bit) for i in range(size)])  12.1 us
    pallas_call x3, Pallas kernels, step_cg(): pl.pallas_call(functools.partial(step_kernel, sizes, first, last), out_sh...  3.97 us
    ppermute x9, waiting for transfers between devices, swap(): return lax.ppermute(value, axis, [(i, i ^ bit) for i in range(size)])  3.21 us
    pallas_call x1, Pallas kernels, split_prior(): pl.pallas_call(split_kernel, out_shape=(pltpu.VMEM(prior.shape, jnp.bfloa...  2.56 us
  transfers between devices with their start and end apart: 9, of which 4 were waited for; matrix products, arithmetic and copies ran while one was open for 0% of the time, Pallas kernels for 18%

profile of v28, /device:TPU:0, one launch (start us, length us, event | category | flops | bytes accessed | tf_op | source)
XLA Modules:
  0.0 76.5 jit_solution(14877889411996779690)
XLA Ops:
  0.0 5.1 %in_features.1.refs_0_ = f32[64,512]{1,0:T(8,128)S(1)} custom-call(bf16[512,8192]{1,0:T(8,128)(2,1)} %rows_ref.2, bf16[64,8192]{1,0:T(8,128)(2,1)} %proj_ref.2), custom_call_target="tpu_custom_call" | custom-call | tf_op jit(solution)/shard_map/in_features/pallas_call | solution.py:125
  5.1 3.1 %collective-permute-start.2 = (f32[64,512]{1,0:T(8,128)S(1)}, f32[64,512]{1,0:T(8,128)S(1)}, u32[]{:S(2)}, u32[]{:S(2)}) collective-permute-start(f32[64,512]{1,0:T(8,128)S(1)} %in_features.1.refs_0_), channel_id=1, source_target_pairs={{0,1},{1,0},{2,3},{3,2},{4,5},{5,4},{6,7},{7,6},{8,9},{9,8},{10,11... | collective-permute-start | bytes 393224 | tf_op jit(solution)/shard_map/ppermute | solution.py:26
  8.2 2.5 %collective-permute-start.1 = (f32[64,512]{1,0:T(8,128)S(1)}, f32[64,512]{1,0:T(8,128)S(1)}, u32[]{:S(2)}, u32[]{:S(2)}) collective-permute-start(f32[64,512]{1,0:T(8,128)S(1)} %in_features.1.refs_0_), channel_id=1, source_target_pairs={{0,3},{1,2},{2,1},{3,0},{4,7},{5,6},{6,5},{7,4},{8,11},{9,10},{10,... | collective-permute-start | bytes 393224 | tf_op jit(solution)/shard_map/ppermute | solution.py:26
  10.8 11.4 %out_features.1.refs_4_ = f32[2048,128]{1,0:T(8,128)S(1)} custom-call(bf16[2048,7168]{1,0:T(8,128)(2,1)} %rows_ref.3, bf16[64,7168]{1,0:T(8,128)(2,1)} %proj_ref.3), custom_call_target="tpu_custom_call" | custom-call | tf_op jit(solution)/shard_map/out_features/pallas_call | solution.py:125
  22.1 0.2 collective-permute-done.refs_1_
  22.4 0.5 partial_vectors.1
  23.0 2.8 %collective-permute-start.5 = (f32[2,4096]{1,0:T(2,128)S(1)}, f32[2,4096]{1,0:T(2,128)S(1)}, u32[]{:S(2)}, u32[]{:S(2)}) collective-permute-start(f32[2,4096]{1,0:T(2,128)S(1)} %reshape.9), channel_id=1, source_target_pairs={{0,3},{1,2},{2,1},{3,0},{4,7},{5,6},{6,5},{7,4},{8,11},{9,10},{10,... | collective-permute-start | bytes 98312 | tf_op jit(solution)/shard_map/ppermute | solution.py:26
  25.8 0.3 collective-permute-start.4
  26.1 1.4 %collective-permute-start.3 = (f32[2,4096]{1,0:T(2,128)S(1)}, f32[2,4096]{1,0:T(2,128)S(1)}, u32[]{:S(2)}, u32[]{:S(2)}) collective-permute-start(f32[2,4096]{1,0:T(2,128)S(1)} %reshape.9), channel_id=1, source_target_pairs={{0,1},{1,0},{2,3},{3,2},{4,5},{5,4},{6,7},{7,6},{8,9},{9,8},{10,11... | collective-permute-start | bytes 98312 | tf_op jit(solution)/shard_map/ppermute | solution.py:26
  27.5 2.6 %split_prior.1 = (bf16[256,4096]{1,0:T(8,128)(2,1)S(1)}, bf16[256,4096]{1,0:T(8,128)(2,1)S(1)}, bf16[4096,32]{1,0:T(8,128)(2,1)S(1)}) custom-call(f32[256,4096]{1,0:T(8,128)} %prior_ref, bf16[32,4096]{1,0:T(8,128)(2,1)S(1)} %copy-done), custom_call_target="tpu_custom_call" | custom-call | tf_op jit(solution)/shard_map/split_prior/pallas_call | solution.py:160
  30.1 0.8 %collective-permute-done.4 = f32[2,4096]{1,0:T(2,128)S(1)} collective-permute-done((f32[2,4096]{1,0:T(2,128)S(1)}, f32[2,4096]{1,0:T(2,128)S(1)}, u32[]{:S(2)}, u32[]{:S(2)}) %collective-permute-start.4) | collective-permute-done | bytes 32800 | tf_op jit(solution)/shard_map/ppermute | solution.py:26
  31.0 1.6 %collective-permute-start.7 = (f32[2,4096]{1,0:T(2,128)S(1)}, f32[2,4096]{1,0:T(2,128)S(1)}, u32[]{:S(2)}, u32[]{:S(2)}) collective-permute-start(f32[2,4096]{1,0:T(2,128)S(1)} %add_add_fusion.refs_0_), channel_id=1, source_target_pairs={{0,8},{4,12},{8,0},{12,4},{1,9},{5,13},{9,1},{13,5},{2,10},{6,14},... | collective-permute-start | bytes 98312 | tf_op jit(solution)/shard_map/ppermute | solution.py:26
  32.5 0.3 collective-permute-start.6
  32.8 1.8 %collective-permute-done.8.refs_3_ = f32[2,4096]{1,0:T(2,128)S(1)} collective-permute-done((f32[2,4096]{1,0:T(2,128)S(1)}, f32[2,4096]{1,0:T(2,128)S(1)}, u32[]{:S(2)}, u32[]{:S(2)}) %collective-permute-start.8) | collective-permute-done | bytes 32800 | tf_op jit(solution)/shard_map/ppermute | solution.py:26
  34.6 0.4 collective-permute-done.7.refs_2_
  35.0 1.3 %cg_start.1 = (f32[8,4096]{1,0:T(8,128)S(1)}, f32[8,128]{1,0:T(8,128)S(1)}, f32[8,256]{1,0:T(8,128)S(1)}, f32[8,128]{1,0:T(8,128)S(1)}) custom-call(f32[2,4096]{1,0:T(2,128)S(1)} %add_add_fusion.refs_0_, f32[2,4096]{1,0:T(2,128)S(1)} %collective-permute-done.6.refs_1_, f32[2,4096]{1,0:T(2,128)S(1)} %collective-permute-done.7.refs_2_, ...), custom_call_target="tpu_custom_call" | custom-call | tf_op jit(solution)/shard_map/cg_start/pallas_call | solution.py:268
  36.3 9.2 %all_to_all.20.refs_0_ = f32[16,8,256]{2,1,0:T(8,128)S(1)} all-to-all(f32[16,8,256]{2,1,0:T(8,128)S(1)} %broadcast_in_dim.10), channel_id=1, replica_groups={{14,0,1,2,3,4,5,6,7,8,9,10,11,12,13,15},{30,16,17,18,19,20,21,22,23,24,..., dimensions={0} | all-to-all | bytes 262144 | tf_op jit(solution)/shard_map/all_to_all | solution.py:42
  45.5 1.3 %cg_step.3 = (f32[8,256]{1,0:T(8,128)S(1)}, f32[8,128]{1,0:T(8,128)S(1)}, f32[8,256]{1,0:T(8,128)S(1)}, f32[8,4096]{1,0:T(8,128)S(1)}, f32[8,4096]{1,0:T(8,128)S(1)}, /*index=5*/f32[8,4096]{1,0:T(8,128)S(1)}) custom-call(f32[16,8,256]{2,1,0:T(8,128)S(1)} %all_to_all.20.refs_0_, bf16[256,4096]{1,0:T(8,128)(2,1)S(1)} %get-tuple-element.40.refs_4_.refs_1_, ...), custom_call_target="tpu_custom_call" | custom-call | tf_op jit(solution)/shard_map/cg_step/pallas_call | solution.py:348
  46.8 9.2 %all_to_all.21.refs_0_ = f32[16,8,256]{2,1,0:T(8,128)S(1)} all-to-all(f32[16,8,256]{2,1,0:T(8,128)S(1)} %broadcast_in_dim.11), channel_id=1, replica_groups={{14,0,1,2,3,4,5,6,7,8,9,10,11,12,13,15},{30,16,17,18,19,20,21,22,23,24,..., dimensions={0} | all-to-all | bytes 262144 | tf_op jit(solution)/shard_map/all_to_all | solution.py:42
  56.0 1.3 %cg_step.4 = (f32[8,256]{1,0:T(8,128)S(1)}, f32[8,128]{1,0:T(8,128)S(1)}, f32[8,256]{1,0:T(8,128)S(1)}, f32[8,4096]{1,0:T(8,128)S(1)}, f32[8,4096]{1,0:T(8,128)S(1)}, /*index=5*/f32[8,4096]{1,0:T(8,128)S(1)}) custom-call(f32[16,8,256]{2,1,0:T(8,128)S(1)} %all_to_all.21.refs_0_, bf16[256,4096]{1,0:T(8,128)(2,1)S(1)} %get-tuple-element.40.refs_4_.refs_1_, ...), custom_call_target="tpu_custom_call" | custom-call | tf_op jit(solution)/shard_map/cg_step/pallas_call | solution.py:348
  57.3 9.2 %all_to_all.22.refs_0_ = f32[16,8,256]{2,1,0:T(8,128)S(1)} all-to-all(f32[16,8,256]{2,1,0:T(8,128)S(1)} %broadcast_in_dim.12), channel_id=1, replica_groups={{14,0,1,2,3,4,5,6,7,8,9,10,11,12,13,15},{30,16,17,18,19,20,21,22,23,24,..., dimensions={0} | all-to-all | bytes 262144 | tf_op jit(solution)/shard_map/all_to_all | solution.py:42
  66.6 1.4 %cg_step.5 = (f32[1,128]{1,0:T(1,128)S(1)}, f32[1,128]{1,0:T(1,128)S(1)}, f32[8,32]{1,0:T(8,128)S(1)}, f32[8,32]{1,0:T(8,128)S(1)}) custom-call(f32[16,8,256]{2,1,0:T(8,128)S(1)} %all_to_all.22.refs_0_, bf16[256,4096]{1,0:T(8,128)(2,1)S(1)} %get-tuple-element.40.refs_4_.refs_1_, bf16[256,4096]{1,0:T(8,128)(2,1)S(1)} %get-tuple-element.41.refs_5_.refs_2_, ...), custom_call_target="tpu_custom_call" | custom-call | tf_op jit(solution)/shard_map/cg_step/pallas_call | solution.py:348
  68.0 7.9 %all_to_all.23.curvature_ref = f32[16,1,128]{2,1,0:T(1,128)S(1)} all-to-all(f32[16,1,128]{2,1,0:T(1,128)S(1)} %broadcast_in_dim.14), channel_id=1, replica_groups={{14,0,1,2,3,4,5,6,7,8,9,10,11,12,13,15},{30,16,17,18,19,20,21,22,23,24,..., dimensions={0} | all-to-all | bytes 16384 | tf_op jit(solution)/shard_map/all_to_all | solution.py:42
  75.8 0.7 combine.1
  (15 shorter events, 0.4 us)
Async XLA Ops:
  5.1 22.4 %copy-start = (bf16[32,4096]{1,0:T(8,128)(2,1)S(1)}, bf16[32,4096]{1,0:T(8,128)(2,1)}, u32[]{:S(2)}) copy-start(bf16[32,4096]{1,0:T(8,128)(2,1)} %queries_ref.1) | copy-start | bytes 786436
  5.1 17.1 %collective-permute-start.2 = (f32[64,512]{1,0:T(8,128)S(1)}, f32[64,512]{1,0:T(8,128)S(1)}, u32[]{:S(2)}, u32[]{:S(2)}) collective-permute-start(f32[64,512]{1,0:T(8,128)S(1)} %in_features.1.refs_0_), channel_id=1, source_target_pairs={{0,1},{1,0},{2,3},{3,2},{4,5},{5,4},{6,7},{7,6},{8,9},{9,8},{10,11... | collective-permute-start | bytes 393224 | tf_op jit(solution)/shard_map/ppermute | solution.py:26
  8.2 14.0 %collective-permute-start.1 = (f32[64,512]{1,0:T(8,128)S(1)}, f32[64,512]{1,0:T(8,128)S(1)}, u32[]{:S(2)}, u32[]{:S(2)}) collective-permute-start(f32[64,512]{1,0:T(8,128)S(1)} %in_features.1.refs_0_), channel_id=1, source_target_pairs={{0,3},{1,2},{2,1},{3,0},{4,7},{5,6},{6,5},{7,4},{8,11},{9,10},{10,... | collective-permute-start | bytes 393224 | tf_op jit(solution)/shard_map/ppermute | solution.py:26
  10.6 11.8 %collective-permute-start = (f32[64,512]{1,0:T(8,128)S(1)}, f32[64,512]{1,0:T(8,128)S(1)}, u32[]{:S(2)}, u32[]{:S(2)}) collective-permute-start(f32[64,512]{1,0:T(8,128)S(1)} %in_features.1.refs_0_), channel_id=1, source_target_pairs={{0,2},{1,3},{2,0},{3,1},{4,6},{5,7},{6,4},{7,5},{8,10},{9,11},{10,... | collective-permute-start | bytes 393224 | tf_op jit(solution)/shard_map/ppermute | solution.py:26
  23.0 7.0 %collective-permute-start.5 = (f32[2,4096]{1,0:T(2,128)S(1)}, f32[2,4096]{1,0:T(2,128)S(1)}, u32[]{:S(2)}, u32[]{:S(2)}) collective-permute-start(f32[2,4096]{1,0:T(2,128)S(1)} %reshape.9), channel_id=1, source_target_pairs={{0,3},{1,2},{2,1},{3,0},{4,7},{5,6},{6,5},{7,4},{8,11},{9,10},{10,... | collective-permute-start | bytes 98312 | tf_op jit(solution)/shard_map/ppermute | solution.py:26
  25.8 5.0 %collective-permute-start.4 = (f32[2,4096]{1,0:T(2,128)S(1)}, f32[2,4096]{1,0:T(2,128)S(1)}, u32[]{:S(2)}, u32[]{:S(2)}) collective-permute-start(f32[2,4096]{1,0:T(2,128)S(1)} %reshape.9), channel_id=1, source_target_pairs={{0,2},{1,3},{2,0},{3,1},{4,6},{5,7},{6,4},{7,5},{8,10},{9,11},{10,... | collective-permute-start | bytes 98312 | tf_op jit(solution)/shard_map/ppermute | solution.py:26
  26.1 4.7 %collective-permute-start.3 = (f32[2,4096]{1,0:T(2,128)S(1)}, f32[2,4096]{1,0:T(2,128)S(1)}, u32[]{:S(2)}, u32[]{:S(2)}) collective-permute-start(f32[2,4096]{1,0:T(2,128)S(1)} %reshape.9), channel_id=1, source_target_pairs={{0,1},{1,0},{2,3},{3,2},{4,5},{5,4},{6,7},{7,6},{8,9},{9,8},{10,11... | collective-permute-start | bytes 98312 | tf_op jit(solution)/shard_map/ppermute | solution.py:26
  30.9 3.7 %collective-permute-start.8 = (f32[2,4096]{1,0:T(2,128)S(1)}, f32[2,4096]{1,0:T(2,128)S(1)}, u32[]{:S(2)}, u32[]{:S(2)}) collective-permute-start(f32[2,4096]{1,0:T(2,128)S(1)} %add_add_fusion.refs_0_), channel_id=1, source_target_pairs={{0,12},{4,8},{8,4},{12,0},{1,13},{5,9},{9,5},{13,1},{2,14},{6,10},... | collective-permute-start | bytes 98312 | tf_op jit(solution)/shard_map/ppermute | solution.py:26
  31.0 4.0 %collective-permute-start.7 = (f32[2,4096]{1,0:T(2,128)S(1)}, f32[2,4096]{1,0:T(2,128)S(1)}, u32[]{:S(2)}, u32[]{:S(2)}) collective-permute-start(f32[2,4096]{1,0:T(2,128)S(1)} %add_add_fusion.refs_0_), channel_id=1, source_target_pairs={{0,8},{4,12},{8,0},{12,4},{1,9},{5,13},{9,1},{13,5},{2,10},{6,14},... | collective-permute-start | bytes 98312 | tf_op jit(solution)/shard_map/ppermute | solution.py:26
  32.5 2.5 %collective-permute-start.6 = (f32[2,4096]{1,0:T(2,128)S(1)}, f32[2,4096]{1,0:T(2,128)S(1)}, u32[]{:S(2)}, u32[]{:S(2)}) collective-permute-start(f32[2,4096]{1,0:T(2,128)S(1)} %add_add_fusion.refs_0_), channel_id=1, source_target_pairs={{0,4},{4,0},{8,12},{12,8},{1,5},{5,1},{9,13},{13,9},{2,6},{6,2},{1... | collective-permute-start | bytes 98312 | tf_op jit(solution)/shard_map/ppermute | solution.py:26

commit v29 on v28

--- a/solution.py
+++ b/solution.py
@@ -169,7 +169,7 @@
         scratch_shapes=[pltpu.VMEM(prior.shape, jnp.float32), pltpu.SemaphoreType.DMA((8,))],
         compiler_params=PARAMS,
         name="split_prior",
-    )(in_hbm(prior), queries)
+    )(prior, queries)
 
 
 def partial_kernel(size, *refs):

time: 76.8 us -> 77.6 us (1.010)
  local copies, waits for them, and re-layouts: 0.14 us -> 2.33 us
  Pallas kernels: 25.4 us -> 24.4 us
    unnamed x2 -> x4, local copies, waits for them, and re-layouts: 0.01 us -> 2.19 us
    pallas_call x1, Pallas kernels: 2.56 us -> 1.6 us  [split_prior(): pl.pallas_call(split_kernel, out_shape=(pltpu.VMEM(prior.shape, jnp.bfloa...]
  transfers between devices with their start and end apart: 9 -> 9, of which waited for: 4 -> 3; matrix products, arithmetic and copies ran while one was open for 0% -> 0% of each run, Pallas kernels for 18% -> 17%
where the time goes in v29:
time: 77.6 us; the launch traced here: 77.3 us
  blocking collectives  35.9 us (46%)
  Pallas kernels  24.4 us (31%)
  starting transfers between devices  12.1 us (16%)
  waiting for transfers between devices  2.44 us (3%)
  local copies, waits for them, and re-layouts  2.33 us (3%)
    all_to_all x4, blocking collectives, gather(): lax.all_to_all(value, ('dp', 'tensor'), 0, 0, axis_index_groups=[order])  35.9 us
    pallas_call x2, Pallas kernels, features(): pl.pallas_call(functools.partial(stream_kernel, block, by_row), out_shape...  16.4 us
    ppermute x9, starting transfers between devices, swap(): return lax.ppermute(value, axis, [(i, i ^ bit) for i in range(size)])  12.1 us
    pallas_call x3, Pallas kernels, step_cg(): pl.pallas_call(functools.partial(step_kernel, sizes, first, last), out_sh...  3.95 us
    ppermute x9, waiting for transfers between devices, swap(): return lax.ppermute(value, axis, [(i, i ^ bit) for i in range(size)])  2.44 us
    unnamed x4, local copies, waits for them, and re-layouts  2.19 us
    pallas_call x1, Pallas kernels, split_prior(): pl.pallas_call(split_kernel, out_shape=(pltpu.VMEM(prior.shape, jnp.bfloa...  1.6 us
  transfers between devices with their start and end apart: 9, of which 3 were waited for; matrix products, arithmetic and copies ran while one was open for 0% of the time, Pallas kernels for 17%

profile of v29, /device:TPU:0, one launch (start us, length us, event | category | flops | bytes accessed | tf_op | source)
XLA Modules:
  0.0 77.3 jit_solution(13620797153830148035)
XLA Ops:
  0.0 5.1 %in_features.1.refs_0_ = f32[64,512]{1,0:T(8,128)S(1)} custom-call(bf16[512,8192]{1,0:T(8,128)(2,1)} %rows_ref.2, bf16[64,8192]{1,0:T(8,128)(2,1)} %proj_ref.2), custom_call_target="tpu_custom_call" | custom-call | tf_op jit(solution)/shard_map/in_features/pallas_call | solution.py:125
  5.1 3.1 %collective-permute-start.2 = (f32[64,512]{1,0:T(8,128)S(1)}, f32[64,512]{1,0:T(8,128)S(1)}, u32[]{:S(2)}, u32[]{:S(2)}) collective-permute-start(f32[64,512]{1,0:T(8,128)S(1)} %in_features.1.refs_0_), channel_id=1, source_target_pairs={{0,1},{1,0},{2,3},{3,2},{4,5},{5,4},{6,7},{7,6},{8,9},{9,8},{10,11... | collective-permute-start | bytes 393224 | tf_op jit(solution)/shard_map/ppermute | solution.py:26
  8.2 2.5 %collective-permute-start.1 = (f32[64,512]{1,0:T(8,128)S(1)}, f32[64,512]{1,0:T(8,128)S(1)}, u32[]{:S(2)}, u32[]{:S(2)}) collective-permute-start(f32[64,512]{1,0:T(8,128)S(1)} %in_features.1.refs_0_), channel_id=1, source_target_pairs={{0,3},{1,2},{2,1},{3,0},{4,7},{5,6},{6,5},{7,4},{8,11},{9,10},{10,... | collective-permute-start | bytes 393224 | tf_op jit(solution)/shard_map/ppermute | solution.py:26
  10.8 11.4 %out_features.1.refs_4_ = f32[2048,128]{1,0:T(8,128)S(1)} custom-call(bf16[2048,7168]{1,0:T(8,128)(2,1)} %rows_ref.3, bf16[64,7168]{1,0:T(8,128)(2,1)} %proj_ref.3), custom_call_target="tpu_custom_call" | custom-call | tf_op jit(solution)/shard_map/out_features/pallas_call | solution.py:125
  22.1 0.2 collective-permute-done.refs_1_
  22.4 0.5 partial_vectors.1
  23.0 2.8 %collective-permute-start.5 = (f32[2,4096]{1,0:T(2,128)S(1)}, f32[2,4096]{1,0:T(2,128)S(1)}, u32[]{:S(2)}, u32[]{:S(2)}) collective-permute-start(f32[2,4096]{1,0:T(2,128)S(1)} %reshape.9), channel_id=1, source_target_pairs={{0,3},{1,2},{2,1},{3,0},{4,7},{5,6},{6,5},{7,4},{8,11},{9,10},{10,... | collective-permute-start | bytes 98312 | tf_op jit(solution)/shard_map/ppermute | solution.py:26
  25.8 0.3 collective-permute-start.4
  26.1 1.4 %collective-permute-start.3 = (f32[2,4096]{1,0:T(2,128)S(1)}, f32[2,4096]{1,0:T(2,128)S(1)}, u32[]{:S(2)}, u32[]{:S(2)}) collective-permute-start(f32[2,4096]{1,0:T(2,128)S(1)} %reshape.9), channel_id=1, source_target_pairs={{0,1},{1,0},{2,3},{3,2},{4,5},{5,4},{6,7},{7,6},{8,9},{9,8},{10,11... | collective-permute-start | bytes 98312 | tf_op jit(solution)/shard_map/ppermute | solution.py:26
  27.5 2.2 %copy-done = f32[256,4096]{1,0:T(8,128)S(1)} copy-done((f32[256,4096]{1,0:T(8,128)S(1)}, f32[256,4096]{1,0:T(8,128)}, u32[]{:S(2)}) %copy-start) | copy-done | bytes 4194328
  29.7 1.6 %split_prior.1 = (bf16[256,4096]{1,0:T(8,128)(2,1)S(1)}, bf16[256,4096]{1,0:T(8,128)(2,1)S(1)}, bf16[4096,32]{1,0:T(8,128)(2,1)S(1)}) custom-call(f32[256,4096]{1,0:T(8,128)S(1)} %copy-done, bf16[32,4096]{1,0:T(8,128)(2,1)S(1)} %copy-done.1), custom_call_target="tpu_custom_call" | custom-call | tf_op jit(solution)/shard_map/split_prior/pallas_call | solution.py:160
  31.4 1.6 %collective-permute-start.7 = (f32[2,4096]{1,0:T(2,128)S(1)}, f32[2,4096]{1,0:T(2,128)S(1)}, u32[]{:S(2)}, u32[]{:S(2)}) collective-permute-start(f32[2,4096]{1,0:T(2,128)S(1)} %add_add_fusion.refs_0_), channel_id=1, source_target_pairs={{0,8},{4,12},{8,0},{12,4},{1,9},{5,13},{9,1},{13,5},{2,10},{6,14},... | collective-permute-start | bytes 98312 | tf_op jit(solution)/shard_map/ppermute | solution.py:26
  33.0 0.3 collective-permute-start.6
  33.3 1.8 %collective-permute-done.8.refs_3_ = f32[2,4096]{1,0:T(2,128)S(1)} collective-permute-done((f32[2,4096]{1,0:T(2,128)S(1)}, f32[2,4096]{1,0:T(2,128)S(1)}, u32[]{:S(2)}, u32[]{:S(2)}) %collective-permute-start.8) | collective-permute-done | bytes 32800 | tf_op jit(solution)/shard_map/ppermute | solution.py:26
  35.1 0.4 collective-permute-done.7.refs_2_
  35.5 1.2 %cg_start.1 = (f32[8,4096]{1,0:T(8,128)S(1)}, f32[8,128]{1,0:T(8,128)S(1)}, f32[8,256]{1,0:T(8,128)S(1)}, f32[8,128]{1,0:T(8,128)S(1)}) custom-call(f32[2,4096]{1,0:T(2,128)S(1)} %add_add_fusion.refs_0_, f32[2,4096]{1,0:T(2,128)S(1)} %collective-permute-done.6.refs_1_, f32[2,4096]{1,0:T(2,128)S(1)} %collective-permute-done.7.refs_2_, ...), custom_call_target="tpu_custom_call" | custom-call | tf_op jit(solution)/shard_map/cg_start/pallas_call | solution.py:268
  36.7 9.6 %all_to_all.20.refs_0_ = f32[16,8,256]{2,1,0:T(8,128)S(1)} all-to-all(f32[16,8,256]{2,1,0:T(8,128)S(1)} %broadcast_in_dim.10), channel_id=1, replica_groups={{14,0,1,2,3,4,5,6,7,8,9,10,11,12,13,15},{30,16,17,18,19,20,21,22,23,24,..., dimensions={0} | all-to-all | bytes 262144 | tf_op jit(solution)/shard_map/all_to_all | solution.py:42
  46.3 1.3 %cg_step.3 = (f32[8,256]{1,0:T(8,128)S(1)}, f32[8,128]{1,0:T(8,128)S(1)}, f32[8,256]{1,0:T(8,128)S(1)}, f32[8,4096]{1,0:T(8,128)S(1)}, f32[8,4096]{1,0:T(8,128)S(1)}, /*index=5*/f32[8,4096]{1,0:T(8,128)S(1)}) custom-call(f32[16,8,256]{2,1,0:T(8,128)S(1)} %all_to_all.20.refs_0_, bf16[256,4096]{1,0:T(8,128)(2,1)S(1)} %get-tuple-element.40.refs_4_.refs_1_, ...), custom_call_target="tpu_custom_call" | custom-call | tf_op jit(solution)/shard_map/cg_step/pallas_call | solution.py:348
  47.6 9.2 %all_to_all.21.refs_0_ = f32[16,8,256]{2,1,0:T(8,128)S(1)} all-to-all(f32[16,8,256]{2,1,0:T(8,128)S(1)} %broadcast_in_dim.11), channel_id=1, replica_groups={{14,0,1,2,3,4,5,6,7,8,9,10,11,12,13,15},{30,16,17,18,19,20,21,22,23,24,..., dimensions={0} | all-to-all | bytes 262144 | tf_op jit(solution)/shard_map/all_to_all | solution.py:42
  56.8 1.3 %cg_step.4 = (f32[8,256]{1,0:T(8,128)S(1)}, f32[8,128]{1,0:T(8,128)S(1)}, f32[8,256]{1,0:T(8,128)S(1)}, f32[8,4096]{1,0:T(8,128)S(1)}, f32[8,4096]{1,0:T(8,128)S(1)}, /*index=5*/f32[8,4096]{1,0:T(8,128)S(1)}) custom-call(f32[16,8,256]{2,1,0:T(8,128)S(1)} %all_to_all.21.refs_0_, bf16[256,4096]{1,0:T(8,128)(2,1)S(1)} %get-tuple-element.40.refs_4_.refs_1_, ...), custom_call_target="tpu_custom_call" | custom-call | tf_op jit(solution)/shard_map/cg_step/pallas_call | solution.py:348
  58.1 9.2 %all_to_all.22.refs_0_ = f32[16,8,256]{2,1,0:T(8,128)S(1)} all-to-all(f32[16,8,256]{2,1,0:T(8,128)S(1)} %broadcast_in_dim.12), channel_id=1, replica_groups={{14,0,1,2,3,4,5,6,7,8,9,10,11,12,13,15},{30,16,17,18,19,20,21,22,23,24,..., dimensions={0} | all-to-all | bytes 262144 | tf_op jit(solution)/shard_map/all_to_all | solution.py:42
  67.4 1.4 %cg_step.5 = (f32[1,128]{1,0:T(1,128)S(1)}, f32[1,128]{1,0:T(1,128)S(1)}, f32[8,32]{1,0:T(8,128)S(1)}, f32[8,32]{1,0:T(8,128)S(1)}) custom-call(f32[16,8,256]{2,1,0:T(8,128)S(1)} %all_to_all.22.refs_0_, bf16[256,4096]{1,0:T(8,128)(2,1)S(1)} %get-tuple-element.40.refs_4_.refs_1_, bf16[256,4096]{1,0:T(8,128)(2,1)S(1)} %get-tuple-element.41.refs_5_.refs_2_, ...), custom_call_target="tpu_custom_call" | custom-call | tf_op jit(solution)/shard_map/cg_step/pallas_call | solution.py:348
  68.8 7.9 %all_to_all.23.curvature_ref = f32[16,1,128]{2,1,0:T(1,128)S(1)} all-to-all(f32[16,1,128]{2,1,0:T(1,128)S(1)} %broadcast_in_dim.14), channel_id=1, replica_groups={{14,0,1,2,3,4,5,6,7,8,9,10,11,12,13,15},{30,16,17,18,19,20,21,22,23,24,..., dimensions={0} | all-to-all | bytes 16384 | tf_op jit(solution)/shard_map/all_to_all | solution.py:42
  76.6 0.7 combine.1
  (17 shorter events, 0.4 us)
Async XLA Ops:
  5.1 22.4 %copy-start.1 = (bf16[32,4096]{1,0:T(8,128)(2,1)S(1)}, bf16[32,4096]{1,0:T(8,128)(2,1)}, u32[]{:S(2)}) copy-start(bf16[32,4096]{1,0:T(8,128)(2,1)} %queries_ref.1) | copy-start | bytes 786436
  5.1 17.1 %collective-permute-start.2 = (f32[64,512]{1,0:T(8,128)S(1)}, f32[64,512]{1,0:T(8,128)S(1)}, u32[]{:S(2)}, u32[]{:S(2)}) collective-permute-start(f32[64,512]{1,0:T(8,128)S(1)} %in_features.1.refs_0_), channel_id=1, source_target_pairs={{0,1},{1,0},{2,3},{3,2},{4,5},{5,4},{6,7},{7,6},{8,9},{9,8},{10,11... | collective-permute-start | bytes 393224 | tf_op jit(solution)/shard_map/ppermute | solution.py:26
  8.2 14.0 %collective-permute-start.1 = (f32[64,512]{1,0:T(8,128)S(1)}, f32[64,512]{1,0:T(8,128)S(1)}, u32[]{:S(2)}, u32[]{:S(2)}) collective-permute-start(f32[64,512]{1,0:T(8,128)S(1)} %in_features.1.refs_0_), channel_id=1, source_target_pairs={{0,3},{1,2},{2,1},{3,0},{4,7},{5,6},{6,5},{7,4},{8,11},{9,10},{10,... | collective-permute-start | bytes 393224 | tf_op jit(solution)/shard_map/ppermute | solution.py:26
  10.6 11.8 %collective-permute-start = (f32[64,512]{1,0:T(8,128)S(1)}, f32[64,512]{1,0:T(8,128)S(1)}, u32[]{:S(2)}, u32[]{:S(2)}) collective-permute-start(f32[64,512]{1,0:T(8,128)S(1)} %in_features.1.refs_0_), channel_id=1, source_target_pairs={{0,2},{1,3},{2,0},{3,1},{4,6},{5,7},{6,4},{7,5},{8,10},{9,11},{10,... | collective-permute-start | bytes 393224 | tf_op jit(solution)/shard_map/ppermute | solution.py:26
  23.0 8.3 %collective-permute-start.5 = (f32[2,4096]{1,0:T(2,128)S(1)}, f32[2,4096]{1,0:T(2,128)S(1)}, u32[]{:S(2)}, u32[]{:S(2)}) collective-permute-start(f32[2,4096]{1,0:T(2,128)S(1)} %reshape.9), channel_id=1, source_target_pairs={{0,3},{1,2},{2,1},{3,0},{4,7},{5,6},{6,5},{7,4},{8,11},{9,10},{10,... | collective-permute-start | bytes 98312 | tf_op jit(solution)/shard_map/ppermute | solution.py:26
  25.8 5.5 %collective-permute-start.4 = (f32[2,4096]{1,0:T(2,128)S(1)}, f32[2,4096]{1,0:T(2,128)S(1)}, u32[]{:S(2)}, u32[]{:S(2)}) collective-permute-start(f32[2,4096]{1,0:T(2,128)S(1)} %reshape.9), channel_id=1, source_target_pairs={{0,2},{1,3},{2,0},{3,1},{4,6},{5,7},{6,4},{7,5},{8,10},{9,11},{10,... | collective-permute-start | bytes 98312 | tf_op jit(solution)/shard_map/ppermute | solution.py:26
  26.1 5.2 %collective-permute-start.3 = (f32[2,4096]{1,0:T(2,128)S(1)}, f32[2,4096]{1,0:T(2,128)S(1)}, u32[]{:S(2)}, u32[]{:S(2)}) collective-permute-start(f32[2,4096]{1,0:T(2,128)S(1)} %reshape.9), channel_id=1, source_target_pairs={{0,1},{1,0},{2,3},{3,2},{4,5},{5,4},{6,7},{7,6},{8,9},{9,8},{10,11... | collective-permute-start | bytes 98312 | tf_op jit(solution)/shard_map/ppermute | solution.py:26
  27.5 2.2 %copy-start = (f32[256,4096]{1,0:T(8,128)S(1)}, f32[256,4096]{1,0:T(8,128)}, u32[]{:S(2)}) copy-start(f32[256,4096]{1,0:T(8,128)} %prior_ref) | copy-start | bytes 12582916
  31.4 3.7 %collective-permute-start.8 = (f32[2,4096]{1,0:T(2,128)S(1)}, f32[2,4096]{1,0:T(2,128)S(1)}, u32[]{:S(2)}, u32[]{:S(2)}) collective-permute-start(f32[2,4096]{1,0:T(2,128)S(1)} %add_add_fusion.refs_0_), channel_id=1, source_target_pairs={{0,12},{4,8},{8,4},{12,0},{1,13},{5,9},{9,5},{13,1},{2,14},{6,10},... | collective-permute-start | bytes 98312 | tf_op jit(solution)/shard_map/ppermute | solution.py:26
  31.4 4.0 %collective-permute-start.7 = (f32[2,4096]{1,0:T(2,128)S(1)}, f32[2,4096]{1,0:T(2,128)S(1)}, u32[]{:S(2)}, u32[]{:S(2)}) collective-permute-start(f32[2,4096]{1,0:T(2,128)S(1)} %add_add_fusion.refs_0_), channel_id=1, source_target_pairs={{0,8},{4,12},{8,0},{12,4},{1,9},{5,13},{9,1},{13,5},{2,10},{6,14},... | collective-permute-start | bytes 98312 | tf_op jit(solution)/shard_map/ppermute | solution.py:26
  33.0 2.5 %collective-permute-start.6 = (f32[2,4096]{1,0:T(2,128)S(1)}, f32[2,4096]{1,0:T(2,128)S(1)}, u32[]{:S(2)}, u32[]{:S(2)}) collective-permute-start(f32[2,4096]{1,0:T(2,128)S(1)} %add_add_fusion.refs_0_), channel_id=1, source_target_pairs={{0,4},{4,0},{8,12},{12,8},{1,5},{5,1},{9,13},{13,9},{2,6},{6,2},{1... | collective-permute-start | bytes 98312 | tf_op jit(solution)/shard_map/ppermute | solution.py:26
